TPU v7x, 32 devices: a whole 2x2x4 slice. The times are simulated.
32 devices in a mesh: wide: 8 (over y, x, core), narrow: 4 (over z).
Axes of the slice: x: 2, y: 2, z: 4, core: 2. Of those that a mesh axis runs over, the one named last changes fastest.
Arguments:
- tokens: bfloat16 [8192, 768], P(('wide', 'narrow')), may hold values from -6 to 6
- cotangent: bfloat16 [8192, 768], P(('wide', 'narrow')), may hold values from -6 to 6
- horizons: int32 [8], P('wide'), may hold values from 1024 to 2048
- qkv_weight: bfloat16 [2, 768, 2304], replicated, may hold values from -0.21875 to 0.21875
- out_weight: bfloat16 [2, 768, 768], replicated, may hold values from -1.75 to 1.75
- ffn_in_weight: bfloat16 [2, 768, 3072], replicated, may hold values from -0.21875 to 0.21875
- ffn_out_weight: bfloat16 [2, 3072, 768], replicated, may hold values from -0.109375 to 0.109375
- qkv_bias: bfloat16 [2, 2304], replicated, may hold values from -1 to 1
- ffn_in_bias: bfloat16 [2, 3072], replicated, may hold values from -1.5 to 1.5
- model_biases: bfloat16 [2, 4, 768], replicated, may hold values from -1.5 to 1.5
- norm_gains: bfloat16 [2, 2, 768], replicated, may hold values from 0.5 to 1.5
Outputs:
- output: bfloat16 [8192, 768], P(('wide', 'narrow'))
- input_grad: float32 [8192, 768], P(('wide', 'narrow'))
- grad_qkv_weight: float32 [2, 768, 2304], P(None, 'wide', 'narrow')
- grad_out_weight: float32 [2, 768, 768], P(None, 'wide', 'narrow')
- grad_ffn_in_weight: float32 [2, 768, 3072], P(None, 'wide', 'narrow')
- grad_ffn_out_weight: float32 [2, 3072, 768], P(None, 'wide', 'narrow')
- grad_qkv_bias: float32 [2, 2304], P(None, 'narrow')
- grad_ffn_in_bias: float32 [2, 3072], P(None, 'narrow')
- grad_model_biases: float32 [2, 4, 768], P(None, None, 'narrow')
- grad_norm_gains: float32 [2, 2, 768], P(None, None, 'narrow')
All inputs are finite; a program needn't handle non-finite values.
Results may differ from a plain program's by a relative error of at most 0.014.
Values may be sent and summed in bfloat16 or wider, within the bound.
No kernel may reach another device: no remote copies, remote signals or barrier semaphores. Data moves between devices by JAX's collectives and lax.ppermute only.
A program may use at most 576 MiB of HBM per device.

v0:
```python
import math

import jax
import jax.numpy as jnp
from jax import lax
from jax.sharding import PartitionSpec as P

D = 768
HEADS = 12
HEAD_DIM = 64
LAYERS = 2
SEQ_LEN = 1024
STRETCH = 64


PRECISE = lax.Precision.HIGHEST
NORM_EPS = 1e-05


def linear_mix(query, key_in, value_in, horizon_block):
    seq_count = query.shape[0]
    length = query.shape[1]
    head_count = query.shape[2]
    head_width = query.shape[3]
    block_count = length // STRETCH
    places = jnp.arange(length, dtype=jnp.float32)
    angles = 0.5 * math.pi * places[None, :] / horizon_block.astype(jnp.float32)[:, None]
    cosine = jnp.cos(angles)[:, :, None, None]
    sine = jnp.sin(angles)[:, :, None, None]
    query_feat = jax.nn.softplus(query)
    key_feat = jax.nn.softplus(key_in)
    query_both = jnp.concatenate([query_feat * cosine, query_feat * sine], axis=-1)
    key_both = jnp.concatenate([key_feat * cosine, key_feat * sine], axis=-1)
    block_shape = (seq_count, block_count, STRETCH, head_count, 2 * head_width)
    query_both = query_both.reshape(block_shape)
    key_both = key_both.reshape(block_shape)
    value_blocks = value_in.reshape(seq_count, block_count, STRETCH, head_count, head_width)
    states = jnp.einsum("sbjhf,sbjhe->sbhfe", key_both, value_blocks, precision=PRECISE)
    totals = jnp.sum(key_both, axis=2)
    states_before = jnp.cumsum(
        jnp.concatenate([jnp.zeros_like(states[:, :1]), states[:, :-1]], axis=1), axis=1
    )
    totals_before = jnp.cumsum(
        jnp.concatenate([jnp.zeros_like(totals[:, :1]), totals[:, :-1]], axis=1), axis=1
    )
    inter_num = jnp.einsum("sbihf,sbhfe->sbihe", query_both, states_before, precision=PRECISE)
    inter_den = jnp.einsum("sbihf,sbhf->sbih", query_both, totals_before, precision=PRECISE)
    scores = jnp.einsum("sbihf,sbjhf->sbhij", query_both, key_both, precision=PRECISE)
    causal = jnp.arange(STRETCH)[:, None] >= jnp.arange(STRETCH)[None, :]
    scores = jnp.where(causal, scores, 0.0)
    intra_num = jnp.einsum("sbhij,sbjhe->sbihe", scores, value_blocks, precision=PRECISE)
    intra_den = jnp.einsum("sbhij->sbih", scores)
    numerator = inter_num + intra_num
    denominator = inter_den + intra_den
    return (numerator / denominator[..., None]).reshape(seq_count, length, head_count, head_width)


def mix_back(kept_heads, grad_heads, horizon_block, seq_group):
    total_rows = kept_heads.shape[0]
    head_count = kept_heads.shape[2]
    whole_seq = kept_heads.astype(jnp.float32).reshape(seq_group, SEQ_LEN, head_count, 3, HEAD_DIM)

    def local_mix(query, key_in, value_in):
        return linear_mix(query, key_in, value_in, horizon_block)

    result, pullback = jax.vjp(
        local_mix, whole_seq[:, :, :, 0], whole_seq[:, :, :, 1], whole_seq[:, :, :, 2]
    )
    grads_all = pullback(
        grad_heads.astype(jnp.float32).reshape(seq_group, SEQ_LEN, head_count, HEAD_DIM)
    )
    stacked = jnp.stack(grads_all, axis=3)
    return stacked.reshape(total_rows, 1, head_count, 3 * HEAD_DIM).astype(jnp.bfloat16)


def matmul_low(left, right):
    return jnp.dot(left, right, preferred_element_type=jnp.float32)


def left_outer(left, right):
    return lax.dot_general(
        left, right, (((0,), (0,)), ((), ())), preferred_element_type=jnp.float32
    )


def right_back(left, right):
    return lax.dot_general(
        left, right, (((1,), (1,)), ((), ())), preferred_element_type=jnp.float32
    )


def norm_apply(total, gain_vec, bias_vec):
    row_mean = jnp.mean(total, axis=-1, keepdims=True)
    centred = total - row_mean
    inv_scale = lax.rsqrt(jnp.mean(centred * centred, axis=-1, keepdims=True) + NORM_EPS)
    normal = centred * inv_scale
    return (normal * gain_vec + bias_vec, normal, inv_scale)


def norm_back(upstream, normal, inv_scale, gain_vec):
    grad_normal = upstream * gain_vec
    inner_one = jnp.mean(grad_normal, axis=-1, keepdims=True)
    inner_two = jnp.mean(grad_normal * normal, axis=-1, keepdims=True)
    grad_total = inv_scale * (grad_normal - inner_one - normal * inner_two)
    return (grad_total, jnp.sum(upstream * normal, axis=0), jnp.sum(upstream, axis=0))


def gelu_slope(values):
    return 0.5 * (1.0 + lax.erf(values * (1.0 / math.sqrt(2.0)))) + values * jnp.exp(
        -0.5 * values * values
    ) * (1.0 / math.sqrt(2.0 * math.pi))


def shards(
    tokens,
    cotangent,
    horizons,
    qkv_weight,
    out_weight,
    ffn_in_weight,
    ffn_out_weight,
    qkv_bias,
    ffn_in_bias,
    model_biases,
    norm_gains,
):
    groups = lax.axis_size("narrow")
    tok_rows = tokens.shape[0]
    seq_group = horizons.shape[0]
    heads_dev = HEADS // groups
    gains_all = norm_gains.astype(jnp.float32)
    biases_all = model_biases.astype(jnp.float32)
    current = tokens.astype(jnp.float32)
    saved = []
    for layer_at in range(LAYERS):
        inputs_low = current.astype(jnp.bfloat16)
        packed = matmul_low(inputs_low, qkv_weight[layer_at]) + qkv_bias[layer_at].astype(
            jnp.float32
        )
        packed = packed.astype(jnp.bfloat16).reshape(tok_rows, groups, heads_dev, 3 * HEAD_DIM)
        received = lax.all_to_all(packed, "narrow", split_axis=1, concat_axis=0, tiled=True)
        head_count = received.shape[2]
        whole_seq = received.astype(jnp.float32).reshape(
            seq_group, SEQ_LEN, head_count, 3, HEAD_DIM
        )
        result = linear_mix(
            whole_seq[:, :, :, 0], whole_seq[:, :, :, 1], whole_seq[:, :, :, 2], horizons
        )
        mixed_heads = result.reshape(received.shape[0], 1, head_count, HEAD_DIM).astype(
            jnp.bfloat16
        )
        kept_heads = received
        mixed_tok = lax.all_to_all(
            mixed_heads, "narrow", split_axis=0, concat_axis=1, tiled=True
        ).reshape(tok_rows, D)
        branch = matmul_low(mixed_tok, out_weight[layer_at]) + biases_all[layer_at, 0]
        middle, normal_one, scale_one = norm_apply(
            current + branch, gains_all[layer_at, 0], biases_all[layer_at, 2]
        )
        middle_low = middle.astype(jnp.bfloat16)
        pre_act = matmul_low(middle_low, ffn_in_weight[layer_at]) + ffn_in_bias[layer_at].astype(
            jnp.float32
        )
        hidden = jax.nn.gelu(pre_act, approximate=False).astype(jnp.bfloat16)
        branch_two = matmul_low(hidden, ffn_out_weight[layer_at]) + biases_all[layer_at, 1]
        current, normal_two, scale_two = norm_apply(
            middle + branch_two, gains_all[layer_at, 1], biases_all[layer_at, 3]
        )
        saved.append(
            (
                inputs_low,
                kept_heads,
                mixed_tok,
                normal_one,
                scale_one,
                middle_low,
                pre_act,
                normal_two,
                scale_two,
            )
        )
    output = current.astype(jnp.bfloat16)
    gradient = cotangent.astype(jnp.float32)
    layer_terms = [None] * LAYERS
    for layer_at in reversed(range(LAYERS)):
        (
            inputs_low,
            kept_heads,
            mixed_tok,
            normal_one,
            scale_one,
            middle_low,
            pre_act,
            normal_two,
            scale_two,
        ) = saved[layer_at]
        grad_two, gain_two, shift_two = norm_back(
            gradient, normal_two, scale_two, gains_all[layer_at, 1]
        )
        grad_branch_two = grad_two.astype(jnp.bfloat16)
        hidden = jax.nn.gelu(pre_act, approximate=False).astype(jnp.bfloat16)
        term_ffn_out = left_outer(hidden, grad_branch_two)
        grad_pre = (
            right_back(grad_branch_two, ffn_out_weight[layer_at]) * gelu_slope(pre_act)
        ).astype(jnp.bfloat16)
        term_ffn_in = left_outer(middle_low, grad_pre)
        grad_middle = grad_two + right_back(grad_pre, ffn_in_weight[layer_at])
        grad_one, gain_one, shift_one = norm_back(
            grad_middle, normal_one, scale_one, gains_all[layer_at, 0]
        )
        grad_branch = grad_one.astype(jnp.bfloat16)
        term_out = left_outer(mixed_tok, grad_branch)
        grad_mixed = (
            right_back(grad_branch, out_weight[layer_at])
            .astype(jnp.bfloat16)
            .reshape(tok_rows, groups, heads_dev, HEAD_DIM)
        )
        grad_heads = lax.all_to_all(grad_mixed, "narrow", split_axis=1, concat_axis=0, tiled=True)
        grad_packed_heads = mix_back(kept_heads, grad_heads, horizons, seq_group)
        grad_packed = lax.all_to_all(
            grad_packed_heads, "narrow", split_axis=0, concat_axis=1, tiled=True
        ).reshape(tok_rows, 3 * D)
        term_qkv = left_outer(inputs_low, grad_packed)
        gradient = grad_one + right_back(grad_packed, qkv_weight[layer_at])
        bias_rows = jnp.stack(
            [
                jnp.sum(grad_branch.astype(jnp.float32), axis=0),
                jnp.sum(grad_branch_two.astype(jnp.float32), axis=0),
                shift_one,
                shift_two,
            ]
        )
        layer_terms[layer_at] = (
            term_qkv,
            term_out,
            term_ffn_in,
            term_ffn_out,
            jnp.sum(grad_packed.astype(jnp.float32), axis=0),
            jnp.sum(grad_pre.astype(jnp.float32), axis=0),
            bias_rows,
            jnp.stack([gain_one, gain_two]),
        )
    terms = tuple(
        (
            jnp.stack([layer_terms[layer_at][member_at] for layer_at in range(LAYERS)])
            for member_at in range(8)
        )
    )
    shares = (
        lax.psum_scatter(
            terms[0].astype(jnp.bfloat16), "narrow", scatter_dimension=2, tiled=True
        ).astype(jnp.float32),
        lax.psum_scatter(
            terms[1].astype(jnp.bfloat16), "narrow", scatter_dimension=2, tiled=True
        ).astype(jnp.float32),
        lax.psum_scatter(
            terms[2].astype(jnp.bfloat16), "narrow", scatter_dimension=2, tiled=True
        ).astype(jnp.float32),
        lax.psum_scatter(
            terms[3].astype(jnp.bfloat16), "narrow", scatter_dimension=2, tiled=True
        ).astype(jnp.float32),
        lax.psum_scatter(
            terms[4].astype(jnp.bfloat16), "narrow", scatter_dimension=1, tiled=True
        ).astype(jnp.float32),
        lax.psum_scatter(
            terms[5].astype(jnp.bfloat16), "narrow", scatter_dimension=1, tiled=True
        ).astype(jnp.float32),
        lax.psum_scatter(
            terms[6].astype(jnp.bfloat16), "narrow", scatter_dimension=2, tiled=True
        ).astype(jnp.float32),
        lax.psum_scatter(
            terms[7].astype(jnp.bfloat16), "narrow", scatter_dimension=2, tiled=True
        ).astype(jnp.float32),
    )
    matrix_sums = (
        lax.psum_scatter(shares[0], "wide", scatter_dimension=1, tiled=True),
        lax.psum_scatter(shares[1], "wide", scatter_dimension=1, tiled=True),
        lax.psum_scatter(shares[2], "wide", scatter_dimension=1, tiled=True),
        lax.psum_scatter(shares[3], "wide", scatter_dimension=1, tiled=True),
    )
    small_shares = (shares[4], shares[5], shares[6], shares[7])
    small_sums = lax.psum(
        (small_shares[0], small_shares[1], small_shares[2], small_shares[3]), "wide"
    )
    return (
        output,
        gradient,
        matrix_sums[0],
        matrix_sums[1],
        matrix_sums[2],
        matrix_sums[3],
        small_sums[0],
        small_sums[1],
        small_sums[2],
        small_sums[3],
    )


def solution(mesh):
    placed = (
        P(("wide", "narrow"), None),
        P(("wide", "narrow"), None),
        P("wide"),
        P(),
        P(),
        P(),
        P(),
        P(),
        P(),
        P(),
        P(),
    )
    return jax.shard_map(
        shards,
        mesh=mesh,
        in_specs=placed,
        out_specs=(
            P(("wide", "narrow"), None),
            P(("wide", "narrow"), None),
            P(None, "wide", "narrow"),
            P(None, "wide", "narrow"),
            P(None, "wide", "narrow"),
            P(None, "wide", "narrow"),
            P(None, "narrow"),
            P(None, "narrow"),
            P(None, None, "narrow"),
            P(None, None, "narrow"),
        ),
        check_vma=False,
    )
```

profile of v0, /device:TPU:0, one launch (start us, length us, event | category | flops | bytes accessed | tf_op | source)
XLA Modules:
  0.0 1514.3 jit_solution(6990319254359068592)
XLA Ops:
  8.0 3.2 fusion.48
  12.7 6.5 all-to-all-start
  20.6 27.1 %all-to-all-done = bf16[256,4,3,192]{0,3,2,1:T(8,128)(2,1)S(1)} async-done(((bf16[256,4,3,192]{0,3,2,1:T(8,128)(2,1)}), bf16[256,4,3,192]{0,3,2,1:T(8,128)(2,1)S(1)}, u32[]{:S(2)}, u32[]{:S(2)}) %all-to-all-start) | async-done | bytes 1179680 | tf_op jit(solution)/shard_map/all_to_all | solution.py:141
  59.6 3.2 copy.411
  66.3 3.3 copy.405
  69.6 3.2 fusion.212
  77.5 3.2 fusion.324
  87.1 4.5 all-to-all-start.1
  92.3 10.6 all-to-all-done.1
  108.9 11.6 fusion.58
  125.7 3.5 all-to-all-start.2
  129.9 26.0 %all-to-all-done.2 = bf16[256,4,3,192]{0,3,2,1:T(8,128)(2,1)S(1)} async-done(((bf16[256,4,3,192]{0,3,2,1:T(8,128)(2,1)}), bf16[256,4,3,192]{0,3,2,1:T(8,128)(2,1)S(1)}, u32[]{:S(2)}, u32[]{:S(2)}) %all-to-all-start.2) | async-done | bytes 1179680 | tf_op jit(solution)/shard_map/all_to_all | solution.py:141
  168.0 3.2 copy.431
  173.8 3.2 copy.425
  177.0 3.5 fusion.216
  198.3 3.9 all-to-all-start.3
  202.2 4.9 fusion.261
  213.9 3.8 fusion.330
  229.7 10.0 fusion.61
  252.8 5.1 all-to-all-start.4
  260.5 3.7 fusion.199
  264.2 4.2 all-to-all-done.4
  276.5 3.5 fusion.91
  292.5 3.6 add_bitcast_fusion.1
  322.6 3.7 all-to-all-start.5
  328.5 3.6 fusion.21
  332.0 40.5 %all-to-all-done.5 = bf16[1024,1,3,192]{3,2,1,0:T(4,128)(2,1)S(1)} async-done(((bf16[1024,1,3,192]{3,2,1,0:T(4,128)(2,1)}), bf16[1024,1,3,192]{3,2,1,0:T(4,128)(2,1)S(1)}, u32[]{:S(2)}, u32[]{:S(2)}) %all-to-all-start.5) | async-done | bytes 1179680 | tf_op jit(solution)/shard_map/all_to_all | solution.py:220
  377.7 4.0 multiply_reduce_fusion.1
  383.2 3.8 fusion.20
  387.0 4.6 fusion.333
  396.6 4.6 copy.521
  401.1 8.3 pad_maximum_fusion.1
  409.4 24.6 %copy.522 = bf16[2,3072,768]{1,0,2:T(2,128)(2,1)} copy(bf16[2,3072,768]{2,1,0:T(8,128)(2,1)} %pad_maximum_fusion.1) | data formatting | bytes 18874368 | tf_op jit(solution)/shard_map/stack | solution.py:245
  443.8 3.7 fusion.331
  452.5 3.5 all-to-all-start.6
  458.6 3.8 fusion.190
  462.4 16.8 %all-to-all-done.6 = bf16[256,4,3,64]{0,3,2,1:T(8,128)(2,1)S(1)} async-done(((bf16[256,4,3,64]{0,3,2,1:T(8,128)(2,1)}), bf16[256,4,3,64]{0,3,2,1:T(8,128)(2,1)S(1)}, u32[]{:S(2)}, u32[]{:S(2)}) %all-to-all-start.6) | async-done | bytes 393248 | tf_op jit(solution)/shard_map/all_to_all | solution.py:218
  483.5 4.3 fusion.90
  494.9 3.4 add_bitcast_fusion
  526.9 3.4 fusion.265
  533.1 3.8 all-to-all-start.7
  537.0 4.3 fusion.17
  541.3 99.0 %all-to-all-done.7 = bf16[1024,1,3,192]{3,2,1,0:T(4,128)(2,1)S(1)} async-done(((bf16[1024,1,3,192]{3,2,1,0:T(4,128)(2,1)}), bf16[1024,1,3,192]{3,2,1,0:T(4,128)(2,1)S(1)}, u32[]{:S(2)}, u32[]{:S(2)}) %all-to-all-start.7) | async-done | bytes 1179680 | tf_op jit(solution)/shard_map/all_to_all | solution.py:220
  641.6 3.9 copy.556
  648.4 3.4 pad_maximum_fusion.2
  653.0 5.3 fusion.19
  658.4 3.7 fusion.18
  662.0 8.3 pad_maximum_fusion
  680.3 207.5 %all-reduce.14.cloned.1.call-done = (bf16[2,768,768]{1,0,2:T(2,128)(2,1)}, bf16[2,3072,768]{1,0,2:T(2,128)(2,1)}) async-done(((bf16[2,768,768]{1,0,2:T(2,128)(2,1)}, bf16[2,3072,768]{1,0,2:T(2,128)(2,1)}), (bf16[2,768,768]{1,0,2:T(2,128)(2,1)}, bf16[2,3072,768]{1,0,2:T(2,128)(2,1)})) %all-reduce.14.cloned.1.call-update) | async-done | bytes 11796496
  889.2 36.6 %copy.557 = f32[2,768,192]{0,2,1:T(8,128)} copy(f32[2,768,192]{1,0,2:T(2,128)S(1)} %dynamic-slice_convert_fusion.1) | data formatting | bytes 2359296
  925.8 52.2 %reshape.1107 = f32[768,384]{1,0:T(8,128)} reshape(f32[768,192,2]{2,1,0:T(8,128)} %bitcast.168) | data formatting | bytes 2359296
  978.1 34.4 %reduce-scatter.22.cloned.1.call-done = bf16[2,768,576]{1,2,0:T(8,128)(2,1)} async-done(((bf16[2,768,2304]{1,2,0:T(8,128)(2,1)}), bf16[2,768,576]{1,2,0:T(8,128)(2,1)}) %reduce-scatter.22.cloned.1.call-update) | async-done | bytes 1769488 | tf_op jit(solution)/shard_map/reduce_scatter | solution.py:250
  1012.5 6.8 copy.520
  1019.4 5.5 dynamic-slice_convert_fusion
  1024.9 141.3 %copy.559 = f32[2,3072,192]{0,2,1:T(8,128)} copy(f32[2,3072,192]{1,0,2:T(2,128)} %dynamic-slice_convert_fusion) | data formatting | bytes 9437184
  1166.2 203.4 %reshape.1109 = f32[3072,384]{1,0:T(8,128)} reshape(f32[3072,192,2]{2,1,0:T(8,128)} %bitcast.171) | data formatting | bytes 9437184
  1369.7 4.4 convert_element_type.306
  1379.1 4.1 fusion.158
  1384.2 24.7 %all-reduce.7 = (f32[2,576]{1,0:T(2,128)}, f32[2,768]{1,0:T(2,128)}, f32[2,4,192]{2,1,0:T(4,128)}, f32[2,2,192]{2,1,0:T(2,128)}) all-reduce(bf16[2,576]{1,0:T(2,128)(2,1)S(1)} %copy.562, bf16[2,768]{1,0:T(2,128)(2,1)S(1)} %copy.564, bf16[2,4,192]{2,1,0:T(4,128)(2,1)S(1)} %copy.566, ...), channel_id=1, replica_groups=mesh['wide'=8,'narrow'=4] {'wide'}, use_global_device_ids=true, to_apply=%region_49.51 | all-reduce | flops 4992 | bytes 29952 | tf_op jit(solution)/shard_map/psum | solution.py:282
  1408.9 11.7 reshape.1108
  1420.7 7.0 copy.526
  1429.6 16.3 %reduce-scatter.30.cloned.1.call-done = f32[384,384]{1,0:T(8,128)} async-done(((f32[3072,384]{1,0:T(8,128)}), f32[384,384]{1,0:T(8,128)}) %reduce-scatter.30.cloned.1.call-update) | async-done | bytes 589840
  1445.9 40.1 %reshape.1110 = f32[384,192,2]{2,1,0:T(8,128)} reshape(f32[384,384]{1,0:T(8,128)} %reduce-scatter.30.cloned.1.call-done) | data formatting | bytes 1179648
  1486.0 21.5 %copy.527 = f32[2,384,192]{1,2,0:T(8,128)} copy(f32[2,384,192]{0,2,1:T(8,128)} %bitcast.618) | data formatting | bytes 1179648
  (557 shorter events, 251.6 us)
Async XLA Ops:
  12.7 7.1 copy-start.111
  12.7 7.1 copy-start.100
  12.7 35.0 %all-to-all-start = ((bf16[256,4,3,192]{0,3,2,1:T(8,128)(2,1)}), bf16[256,4,3,192]{0,3,2,1:T(8,128)(2,1)S(1)}, u32[]{:S(2)}, u32[]{:S(2)}) async-start(bf16[256,4,3,192]{0,3,2,1:T(8,128)(2,1)} %bitcast.1), calls=%async_computation | async-start | bytes 2359296 | tf_op jit(solution)/shard_map/all_to_all | solution.py:141
  20.6 100.0 %copy-start.74 = (f32[768]{0:T(1024)}, f32[768]{0:T(1024)S(1)}, u32[]{:S(2)}) copy-start(f32[768]{0:T(1024)S(1)} %get-tuple-element.97) | copy-start | bytes 9220
  20.6 101.8 %copy-start.96 = (f32[768]{0:T(1024)}, f32[768]{0:T(1024)S(1)}, u32[]{:S(2)}) copy-start(f32[768]{0:T(1024)S(1)} %get-tuple-element.205) | copy-start | bytes 9220
  20.6 101.8 %copy-start.117 = (f32[768]{0:T(1024)}, f32[768]{0:T(1024)S(1)}, u32[]{:S(2)}) copy-start(f32[768]{0:T(1024)S(1)} %get-tuple-element.95) | copy-start | bytes 9220
  53.1 9.6 copy-start.8
  56.6 27.1 %copy-start = (bf16[16,64,3,64]{3,1,2,0:T(8,128)(2,1)}, bf16[16,64,3,64]{3,1,2,0:T(8,128)(2,1)S(1)}, u32[]{:S(2)}) copy-start(bf16[16,64,3,64]{3,1,2,0:T(8,128)(2,1)S(1)} %copy.495) | copy-start | bytes 1179652
  85.7 6.0 copy-start.84
  87.1 15.8 %all-to-all-start.1 = ((bf16[4,2,24576]{2,1,0:T(2,128)(2,1)}), bf16[4,2,24576]{2,1,0:T(2,128)(2,1)}, u32[]{:S(2)}, u32[]{:S(2)}) async-start(bf16[4,2,24576]{2,1,0:T(2,128)(2,1)} %reshape.1136), calls=%async_computation.1 | async-start | bytes 786432 | tf_op jit(solution)/shard_map/all_to_all | solution.py:153
  92.3 14.6 copy-start.54
  106.9 13.8 slice-start.3
  106.9 16.2 %slice-start.15 = ((s8[7077888]{0:T(1024)(128)(4,1)}), s8[4194304]{0:T(1024)(128)(4,1)S(1)}, s32[]{:S(2)}) async-start(s8[7077888]{0:T(1024)(128)(4,1)} %bitcast.692), calls=%async_computation.43 | async-start | bytes 8388608
  108.6 12.0 copy-start.22
  108.7 11.9 copy-start.86
  108.9 11.7 copy-start.91
  108.9 11.7 slice-start.4
  108.9 11.7 slice-start.5
  108.9 14.1 slice-start.16
  125.7 30.2 %all-to-all-start.2 = ((bf16[256,4,3,192]{0,3,2,1:T(8,128)(2,1)}), bf16[256,4,3,192]{0,3,2,1:T(8,128)(2,1)S(1)}, u32[]{:S(2)}, u32[]{:S(2)}) async-start(bf16[256,4,3,192]{0,3,2,1:T(8,128)(2,1)} %bitcast.27), calls=%async_computation.2 | async-start | bytes 2359296 | tf_op jit(solution)/shard_map/all_to_all | solution.py:141
  160.4 41.8 %copy-start.6 = (f32[1,1024,3,3,64]{1,4,2,3,0:T(8,128)}, f32[1,1024,3,3,64]{1,4,2,3,0:T(8,128)S(1)}, u32[]{:S(2)}) copy-start(f32[1,1024,3,3,64]{1,4,2,3,0:T(8,128)S(1)} %copy_convert_fusion) | copy-start | bytes 7077892
  163.9 27.4 %copy-start.3 = (bf16[16,64,3,64]{3,1,2,0:T(8,128)(2,1)}, bf16[16,64,3,64]{3,1,2,0:T(8,128)(2,1)S(1)}, u32[]{:S(2)}) copy-start(bf16[16,64,3,64]{3,1,2,0:T(8,128)(2,1)S(1)} %copy.457) | copy-start | bytes 1179652
  195.9 6.3 copy-start.80
  195.9 6.3 copy-start.82
  198.3 25.3 %all-to-all-start.3 = ((bf16[4,2,24576]{2,1,0:T(2,128)(2,1)}), bf16[4,2,24576]{2,1,0:T(2,128)(2,1)S(1)}, u32[]{:S(2)}, u32[]{:S(2)}) async-start(bf16[4,2,24576]{2,1,0:T(2,128)(2,1)} %reshape.1138), calls=%async_computation.3 | async-start | bytes 786432 | tf_op jit(solution)/shard_map/all_to_all | solution.py:153
  227.0 12.7 slice-start.6
  229.3 20.2 %copy-start.25 = (f32[256,768]{1,0:T(8,128)}, f32[256,768]{1,0:T(8,128)S(1)}, u32[]{:S(2)}) copy-start(f32[256,768]{1,0:T(8,128)S(1)} %get-tuple-element.184) | copy-start | bytes 2359300
  229.3 20.2 %copy-start.89 = (f32[256]{0:T(256)}, f32[256]{0:T(256)S(1)}, u32[]{:S(2)}) copy-start(f32[256]{0:T(256)S(1)} %broadcast_multiply_fusion.11) | copy-start | bytes 3076
  229.6 20.0 %copy-start.94 = (f32[256]{0:T(256)}, f32[256]{0:T(256)S(1)}, u32[]{:S(2)}) copy-start(f32[256]{0:T(256)S(1)} %add_rsqrt_fusion.1) | copy-start | bytes 3076
  229.6 10.1 copy-start.119
  229.6 10.1 slice-start.7
  229.6 10.1 slice-start.8
  241.4 5.9 slice-start.9
  252.8 15.7 %all-to-all-start.4 = ((bf16[256,4,3,64]{0,3,2,1:T(8,128)(2,1)}), bf16[256,4,3,64]{0,3,2,1:T(8,128)(2,1)S(1)}, u32[]{:S(2)}, u32[]{:S(2)}) async-start(bf16[256,4,3,64]{0,3,2,1:T(8,128)(2,1)} %bitcast.51), calls=%async_computation.4 | async-start | bytes 786432 | tf_op jit(solution)/shard_map/all_to_all | solution.py:218
  322.6 49.9 %all-to-all-start.5 = ((bf16[1024,1,3,192]{3,2,1,0:T(4,128)(2,1)}), bf16[1024,1,3,192]{3,2,1,0:T(4,128)(2,1)S(1)}, u32[]{:S(2)}, u32[]{:S(2)}) async-start(bf16[1024,1,3,192]{3,2,1,0:T(4,128)(2,1)} %copy.477), calls=%async_computation.5 | async-start | bytes 4194304 | tf_op jit(solution)/shard_map/all_to_all | solution.py:220
  326.4 561.4 %all-reduce.14.cloned.1.call-start = ((), (), s32[]{:S(2)}) async-start(), calls=%async_computation.27 | async-start | bytes 23592960
  375.5 6.3 copy-start.19
  383.2 8.5 slice-start.12
  387.0 4.6 copy-start.23
  387.0 4.6 copy-start.87
  387.0 4.6 copy-start.92
  387.0 4.6 slice-start.13
  387.0 4.6 slice-start.14
  441.2 6.3 copy-start.69
  443.8 5.0 copy-start.1
  452.5 26.7 %all-to-all-start.6 = ((bf16[256,4,3,64]{0,3,2,1:T(8,128)(2,1)}), bf16[256,4,3,64]{0,3,2,1:T(8,128)(2,1)S(1)}, u32[]{:S(2)}, u32[]{:S(2)}) async-start(bf16[256,4,3,64]{0,3,2,1:T(8,128)(2,1)} %bitcast.102), calls=%async_computation.6 | async-start | bytes 786432 | tf_op jit(solution)/shard_map/all_to_all | solution.py:218
  533.1 107.2 %all-to-all-start.7 = ((bf16[1024,1,3,192]{3,2,1,0:T(4,128)(2,1)}), bf16[1024,1,3,192]{3,2,1,0:T(4,128)(2,1)S(1)}, u32[]{:S(2)}, u32[]{:S(2)}) async-start(bf16[1024,1,3,192]{3,2,1,0:T(4,128)(2,1)} %copy.516), calls=%async_computation.7 | async-start | bytes 4194304 | tf_op jit(solution)/shard_map/all_to_all | solution.py:220
  536.9 475.6 %reduce-scatter.22.cloned.1.call-start = ((), (), s32[]{:S(2)}) async-start(), calls=%async_computation.17 | async-start | bytes 8847360 | tf_op jit(solution)/shard_map/reduce_scatter | solution.py:250
  651.9 6.5 copy-start.24
  651.9 6.4 copy-start.75
  651.9 6.4 copy-start.88
  651.9 6.4 copy-start.93
  651.9 717.7 %reduce-scatter.24.cloned.1.call-start = ((), (), s32[]{:S(2)}) async-start(), calls=%async_computation.18 | async-start | bytes 11796480 | tf_op jit(solution)/shard_map/reduce_scatter | solution.py:256
  653.0 5.4 copy-start.63
  670.4 705.6 %reduce-scatter.38.cloned.1.call-start = ((), (), s32[]{:S(2)}) async-start(), calls=%async_computation.25 | async-start | bytes 245760
  673.9 703.1 %reduce-scatter.34.cloned.1.call-start = ((), (), s32[]{:S(2)}) async-start(), calls=%async_computation.23 | async-start | bytes 983040
  676.1 702.0 %reduce-scatter.36.cloned.1.call-start = ((), (), s32[]{:S(2)}) async-start(), calls=%async_computation.24 | async-start | bytes 245760
  677.8 705.5 %reduce-scatter.32.cloned.1.call-start = ((), (), s32[]{:S(2)}) async-start(), calls=%async_computation.22 | async-start | bytes 737280
  680.2 728.7 %reduce-scatter.28.cloned.1.call-start = ((), (), s32[]{:S(2)}) async-start(), calls=%async_computation.20 | async-start | bytes 1327104
  978.1 449.6 %all-reduce.12.cloned.1.call-start = ((), (), s32[]{:S(2)}) async-start(), calls=%async_computation.26 | async-start | bytes 7864320
  1019.3 426.6 %reduce-scatter.30.cloned.1.call-start = ((), (), s32[]{:S(2)}) async-start(), calls=%async_computation.21 | async-start | bytes 5308416
  1369.6 137.9 %reduce-scatter.26.cloned.1.call-start = ((), (), s32[]{:S(2)}) async-start(), calls=%async_computation.19 | async-start | bytes 5308416 | tf_op jit(solution)/shard_map/reduce_scatter | solution.py:278
  1374.1 5.0 copy-start.29
  1374.1 5.0 copy-start.32
  (101 other events, 224.8 us)
Sparse Core Ops, SparseCore 0:
  434.2 453.4 all-reduce.13
  890.0 122.4 reduce-scatter.21
  1014.8 161.7 reduce-scatter.23
  1179.3 20.2 reduce-scatter.37
  1201.9 21.4 reduce-scatter.33
  1226.2 18.6 reduce-scatter.35
  1247.7 20.2 reduce-scatter.31
  1271.2 35.1 reduce-scatter.27
  1310.1 78.0 all-reduce.11
  1391.9 53.9 reduce-scatter.29
  1449.9 53.8 reduce-scatter.25
where the time goes:
time: 1530 us; the launch traced here: 1510 us
  local copies, waits for them, and re-layouts  696 us (45%)
  waiting for transfers between devices  482 us (32%)
  matrix products  173 us (11%)
  other arithmetic  84 us (5%)
  starting transfers between devices  35.1 us (2%)
  blocking collectives  24.7 us (2%)
  between operations  18.6 us (1%)
    unnamed x323, local copies, waits for them, and re-layouts  569 us
    unnamed x19, waiting for transfers between devices  224 us
    all_to_all x2, waiting for transfers between devices, shards(): lax.all_to_all(grad_packed_heads, 'narrow', split_axis=0, concat_axis=1,...  139 us
    all_to_all x2, waiting for transfers between devices, shards(): lax.all_to_all(packed, 'narrow', split_axis=1, concat_axis=0, tiled=True)  53.1 us
    reduce_scatter x1, waiting for transfers between devices, shards(): lax.psum_scatter(terms[0].astype(jnp.bfloat16), 'narrow', scatter_dimensi...  34.4 us
    dot_general x8, matrix products, matmul_low(): return jnp.dot(left, right, preferred_element_type=jnp.float32)  33.2 us
  transfers between devices with their start and end apart: 19, of which 10 were waited for; matrix products, arithmetic and copies ran while one was open for 45% of the time, Pallas kernels for 0%

commit v1 on v0

v1 whole, which is shorter than its diff:
```python
import functools
import math

import jax
import jax.numpy as jnp
from jax import lax
from jax.experimental import pallas as pl
from jax.experimental.pallas import tpu as pltpu
from jax.sharding import PartitionSpec as P

D = 768
HEADS = 12
HEAD_DIM = 64
FF = 3072
LAYERS = 2
PAIRS = HEADS // 2
NORM_EPS = 1e-05
LANES = 128
STATE_ROWS = PAIRS * LANES + LANES

BF = jnp.bfloat16
F32 = jnp.float32
VMEM = pl.BlockSpec(memory_space=pltpu.VMEM)
SMEM = pl.BlockSpec(memory_space=pltpu.SMEM)
ANY = pl.BlockSpec(memory_space=pl.ANY)


def nn(a, b):
    return lax.dot_general(a, b, (((1,), (0,)), ((), ())), preferred_element_type=F32)


def nt(a, b):
    return lax.dot_general(a, b, (((1,), (1,)), ((), ())), preferred_element_type=F32)


def tn(a, b):
    return lax.dot_general(a, b, (((0,), (0,)), ((), ())), preferred_element_type=F32)


def low(v):
    return v.astype(BF)


def softplus(u):
    return jnp.maximum(u, 0.0) + jnp.log1p(jnp.exp(-jnp.abs(u)))


def sigmoid(u):
    return 1.0 / (1.0 + jnp.exp(-u))


def swap(v):
    return pltpu.roll(v, HEAD_DIM, 1)


def left_half(rows):
    return lax.broadcasted_iota(jnp.int32, (rows, LANES), 1) < HEAD_DIM


def tile(v, at):
    return v[:, at * LANES : (at + 1) * LANES]


def row_mean(v):
    return jnp.mean(v, axis=-1, keepdims=True)


def norm_apply(total, gain, shift):
    centred = total - row_mean(total)
    scale = lax.rsqrt(row_mean(centred * centred) + NORM_EPS)
    normal = centred * scale
    return normal * gain + shift, normal, scale


def norm_back(upstream, normal, scale, gain):
    grad = upstream * gain
    return scale * (grad - row_mean(grad) - normal * row_mean(grad * normal))


def column_sum(v):
    return jnp.sum(v, axis=0, keepdims=True)


def spread(v, rows):
    return jnp.broadcast_to(v, (rows, LANES))


def vector(ref, layer, row=None):
    if row is None:
        return ref[...].astype(F32)[layer : layer + 1]
    return ref[layer].astype(F32)[row : row + 1]


def call(kernel, outs, in_specs, scratch, flops, byte_count, **more):
    return pl.pallas_call(
        kernel,
        out_shape=outs,
        in_specs=in_specs,
        out_specs=jax.tree.map(lambda _: VMEM, outs),
        scratch_shapes=scratch,
        compiler_params=pltpu.CompilerParams(vmem_limit_bytes=48 * 1024 * 1024),
        cost_estimate=pl.CostEstimate(
            flops=int(flops), bytes_accessed=int(byte_count), transcendentals=0
        ),
        **more,
    )


def shape(*dims, dtype=F32):
    return jax.ShapeDtypeStruct(dims, dtype)


def project_kernel(layer, x_ref, w_hbm, b_ref, cs_ref, packed_ref, xt_ref, st_ref, wbuf, sems):
    parts = wbuf.shape[0]
    copies = [
        pltpu.make_async_copy(w_hbm.at[layer, :, pl.ds(D * j, D)], wbuf.at[j], sems.at[j])
        for j in range(parts)
    ]
    for copy in copies:
        copy.start()
    rows = x_ref.shape[0]
    x = x_ref[...].astype(F32)
    xb = low(x)
    xt_ref[...] = low(x.T)
    cs = cs_ref[...]
    lo = left_half(rows)
    lo_state = left_half(LANES)
    lane = lax.broadcasted_iota(jnp.int32, (LANES, LANES), 1)
    bias = vector(b_ref, layer)
    totals = jnp.zeros((LANES, LANES), F32)
    for j in range(parts):
        copies[j].wait()
        pk = low(nn(xb, wbuf[j]) + bias[:, D * j : D * (j + 1)])
        packed_ref[:, D * j : D * (j + 1)] = pk
        pf = pk.astype(F32)
        for p in range(2):
            t0, t1, t2 = (tile(pf, 3 * p + i) for i in range(3))
            sp0 = softplus(t0)
            sp2 = softplus(t2)
            kf0 = low(jnp.where(lo, swap(sp0), sp0) * cs)
            kf1 = low(jnp.where(lo, sp2, swap(sp2)) * cs)
            s0 = tn(kf0, low(jnp.where(lo, t1, 1.0)))
            s1 = tn(kf1, low(jnp.where(lo, 1.0, t2)))
            pair = 2 * j + p
            st_ref[pair * LANES : (pair + 1) * LANES, :] = low(jnp.where(lo_state, s0, s1))
            totals = jnp.where(lane == HEAD_DIM + 2 * pair, s0, totals)
            totals = jnp.where(lane == 2 * pair + 1, s1, totals)
    st_ref[PAIRS * LANES :, :] = low(totals)


def project(layer, x, w, b, cs):
    rows = x.shape[0]
    return call(
        functools.partial(project_kernel, layer),
        (
            shape(rows, 3 * D, dtype=BF),
            shape(D, rows, dtype=BF),
            shape(STATE_ROWS, LANES, dtype=BF),
        ),
        [VMEM, ANY, VMEM, VMEM],
        [pltpu.VMEM((3, D, D), BF), pltpu.SemaphoreType.DMA((3,))],
        2 * rows * D * 3 * D,
        2 * D * 3 * D,
    )(x, w, b, cs)


def inside_kernel(packed_ref, cm_ref, num_ref, den_ref, sq_ref):
    rows = packed_ref.shape[0]
    lo = left_half(rows)
    cm = cm_ref[...]
    for pair in range(PAIRS):
        at = pair * 3 * LANES
        t0, t1, t2 = (
            packed_ref[:, at + i * LANES : at + (i + 1) * LANES].astype(F32) for i in range(3)
        )
        sp0, sp1, sp2 = softplus(t0), softplus(t1), softplus(t2)
        a0 = nt(low(jnp.where(lo, sp0, 0.0)), low(swap(sp0)))
        a1 = nt(low(jnp.where(lo, 0.0, sp1)), low(swap(sp2)))
        n0 = nn(low(a0 * cm), low(jnp.where(lo, t1, 1.0)))
        n1 = nn(low(a1 * cm), low(jnp.where(lo, 1.0, t2)))
        here = slice(pair * LANES, (pair + 1) * LANES)
        num_ref[:, here] = jnp.where(lo, n0, n1)
        den_ref[:, here] = swap(jnp.where(lo, n1, n0))
        sq_ref[:, here] = low(jnp.where(lo, sp0, sp1))


def inside(packed, cm):
    rows = packed.shape[0]
    return call(
        inside_kernel,
        (shape(rows, D), shape(rows, D), shape(rows, D, dtype=BF)),
        [VMEM, VMEM],
        [],
        4 * HEADS * rows * rows * LANES,
        rows * D * 16,
    )(packed, cm)


def totals_column(totals, head, rows):
    at = head + (HEAD_DIM if head % 2 == 0 else 0)
    return jnp.broadcast_to(totals[:, at : at + 1], (rows, LANES))


def layer_kernel(
    layer,
    shifts,
    *refs,
):
    recv = refs[:shifts]
    (
        x_ref,
        num_ref,
        den_ref,
        sq_ref,
        cs_ref,
        wo_hbm,
        w1_hbm,
        w2_hbm,
        bf_ref,
        mb_ref,
        ng_ref,
        before_ref,
        mixed_ref,
        mixt_ref,
        inv_ref,
        n1_ref,
        r1_ref,
        midt_ref,
        hid_ref,
        slope_ref,
        n2_ref,
        r2_ref,
        s_ref,
        wo,
        w1,
        w2,
        sems,
    ) = refs[shifts:]
    parts = w1.shape[0]
    co = pltpu.make_async_copy(wo_hbm.at[layer], wo, sems.at[2 * parts])
    c1 = [
        pltpu.make_async_copy(w1_hbm.at[layer, :, pl.ds(D * j, D)], w1.at[j], sems.at[j])
        for j in range(parts)
    ]
    c2 = [
        pltpu.make_async_copy(
            w2_hbm.at[layer, pl.ds(D * j, D), :], w2.at[j], sems.at[parts + j]
        )
        for j in range(parts)
    ]
    co.start()
    for j in range(parts):
        c1[j].start()
        c2[j].start()
    rows = x_ref.shape[0]
    lo = left_half(rows)
    lo_state = left_half(LANES)
    cs = cs_ref[...]
    before = recv[0][...].astype(F32)
    for other in recv[1:]:
        before = before + other[...].astype(F32)
    before_ref[...] = low(before)
    totals = before[PAIRS * LANES :]
    for pair in range(PAIRS):
        here = slice(pair * LANES, (pair + 1) * LANES)
        sq = sq_ref[:, here].astype(F32)
        other = swap(sq)
        state = before[here]
        n0 = nn(
            low(jnp.where(lo, sq, other) * cs),
            low(jnp.where(lo_state, state, totals_column(totals, 2 * pair, LANES))),
        )
        n1 = nn(
            low(jnp.where(lo, other, sq) * cs),
            low(jnp.where(lo_state, totals_column(totals, 2 * pair + 1, LANES), state)),
        )
        num = num_ref[:, here] + jnp.where(lo, n0, n1)
        inv = 1.0 / (den_ref[:, here] + swap(jnp.where(lo, n1, n0)))
        mixed = num * inv
        inv_ref[:, here] = inv
        mixed_ref[:, here] = low(mixed)
        mixt_ref[here, :] = low(mixed.T)
    co.wait()
    x = x_ref[...].astype(F32)
    branch = nn(mixed_ref[...], wo[...]) + vector(mb_ref, layer, 0)
    middle, n1, r1 = norm_apply(x + branch, vector(ng_ref, layer, 0), vector(mb_ref, layer, 2))
    n1_ref[...] = n1
    r1_ref[...] = spread(r1, rows)
    midt_ref[...] = low(middle.T)
    mid = low(middle)
    bias = vector(bf_ref, layer)
    total = middle + vector(mb_ref, layer, 1)
    for j in range(parts):
        here = slice(D * j, D * (j + 1))
        c1[j].wait()
        pre = nn(mid, w1[j]) + bias[:, here]
        cdf = 0.5 * (1.0 + lax.erf(pre * (1.0 / math.sqrt(2.0))))
        hid = low(pre * cdf)
        hid_ref[:, here] = hid
        slope_ref[:, here] = low(
            cdf + pre * jnp.exp(-0.5 * pre * pre) * (1.0 / math.sqrt(2.0 * math.pi))
        )
        c2[j].wait()
        total = total + nn(hid, w2[j])
    s_next, n2, r2 = norm_apply(total, vector(ng_ref, layer, 1), vector(mb_ref, layer, 3))
    n2_ref[...] = n2
    r2_ref[...] = spread(r2, rows)
    s_ref[...] = s_next.astype(s_ref.dtype)


def layer_forward(layer, recv, x, num, den, sq, cs, wo, w1, w2, bf, mb, ng, out_type):
    rows = x.shape[0]
    parts = FF // D
    return call(
        functools.partial(layer_kernel, layer, len(recv)),
        (
            shape(STATE_ROWS, LANES, dtype=BF),
            shape(rows, D, dtype=BF),
            shape(D, rows, dtype=BF),
            shape(rows, D),
            shape(rows, D),
            shape(rows, LANES),
            shape(D, rows, dtype=BF),
            shape(rows, FF, dtype=BF),
            shape(rows, FF, dtype=BF),
            shape(rows, D),
            shape(rows, LANES),
            shape(rows, D, dtype=out_type),
        ),
        [VMEM] * (len(recv) + 5) + [ANY] * 3 + [VMEM] * 3,
        [
            pltpu.VMEM((D, D), BF),
            pltpu.VMEM((parts, D, D), BF),
            pltpu.VMEM((parts, D, D), BF),
            pltpu.SemaphoreType.DMA((2 * parts + 1,)),
        ],
        2 * rows * D * (D + 2 * FF),
        2 * D * (D + 2 * FF),
    )(*recv, x, num, den, sq, cs, wo, w1, w2, bf, mb, ng)


def back_kernel(
    layer,
    gs_ref,
    n2_ref,
    r2_ref,
    slope_ref,
    n1_ref,
    r1_ref,
    mixed_ref,
    inv_ref,
    sq_ref,
    cs_ref,
    wo_hbm,
    w1_hbm,
    w2_hbm,
    ng_ref,
    gb2t_ref,
    gpre_ref,
    gb1_ref,
    gz1_ref,
    u_ref,
    dd_ref,
    st_ref,
    sums_ref,
    wo,
    w1,
    w2,
    sems,
):
    parts = w1.shape[0]
    co = pltpu.make_async_copy(wo_hbm.at[layer], wo, sems.at[2 * parts])
    c1 = [
        pltpu.make_async_copy(w1_hbm.at[layer, :, pl.ds(D * j, D)], w1.at[j], sems.at[j])
        for j in range(parts)
    ]
    c2 = [
        pltpu.make_async_copy(
            w2_hbm.at[layer, pl.ds(D * j, D), :], w2.at[j], sems.at[parts + j]
        )
        for j in range(parts)
    ]
    for j in range(parts):
        c2[j].start()
        c1[j].start()
    co.start()
    rows = gs_ref.shape[0]
    lo = left_half(rows)
    lo_state = left_half(LANES)
    cs = cs_ref[...]
    lane = lax.broadcasted_iota(jnp.int32, (LANES, LANES), 1)
    sublane = lax.broadcasted_iota(jnp.int32, (LANES, LANES), 0)
    same = low(jnp.where((lane < HEAD_DIM) == (sublane < HEAD_DIM), 1.0, 0.0))
    gs = gs_ref[...].astype(F32)
    n2 = n2_ref[...]
    gz2 = norm_back(gs, n2, r2_ref[:, :1], vector(ng_ref, layer, 1))
    gb2 = low(gz2)
    gb2t_ref[...] = low(gz2.T)
    sums_ref[...] = jnp.zeros(sums_ref.shape, F32)
    sums_ref[5:6, :] = column_sum(gb2.astype(F32))
    sums_ref[7:8, :] = column_sum(gs)
    sums_ref[9:10, :] = column_sum(gs * n2)
    gmid = gz2
    for j in range(parts):
        here = slice(D * j, D * (j + 1))
        c2[j].wait()
        gpre = low(nt(gb2, w2[j]) * slope_ref[:, here].astype(F32))
        gpre_ref[:, here] = gpre
        sums_ref[j : j + 1, :] = column_sum(gpre.astype(F32))
        c1[j].wait()
        gmid = gmid + nt(gpre, w1[j])
    n1 = n1_ref[...]
    gz1 = norm_back(gmid, n1, r1_ref[:, :1], vector(ng_ref, layer, 0))
    gb1 = low(gz1)
    gz1_ref[...] = gz1
    gb1_ref[...] = gb1
    sums_ref[4:5, :] = column_sum(gb1.astype(F32))
    sums_ref[6:7, :] = column_sum(gmid)
    sums_ref[8:9, :] = column_sum(gmid * n1)
    co.wait()
    gmixed = low(nt(gb1, wo[...])).astype(F32)
    totals = jnp.zeros((LANES, LANES), F32)
    for pair in range(PAIRS):
        here = slice(pair * LANES, (pair + 1) * LANES)
        u = gmixed[:, here] * inv_ref[:, here]
        dd = -nn(low(u * mixed_ref[:, here].astype(F32)), same)
        u_ref[:, here] = low(u)
        dd_ref[:, here] = low(dd)
        ds = swap(dd)
        sq = sq_ref[:, here].astype(F32)
        other = swap(sq)
        s0 = tn(low(jnp.where(lo, sq, other) * cs), low(jnp.where(lo, u, ds)))
        s1 = tn(low(jnp.where(lo, other, sq) * cs), low(jnp.where(lo, ds, u)))
        st_ref[here, :] = low(jnp.where(lo_state, s0, s1))
        totals = jnp.where(lane == HEAD_DIM + 2 * pair, s0, totals)
        totals = jnp.where(lane == 2 * pair + 1, s1, totals)
    st_ref[PAIRS * LANES :, :] = low(totals)


def layer_back(layer, gs, n2, r2, slope, n1, r1, mixed, inv, sq, cs, wo, w1, w2, ng):
    rows = gs.shape[0]
    parts = FF // D
    return call(
        functools.partial(back_kernel, layer),
        (
            shape(D, rows, dtype=BF),
            shape(rows, FF, dtype=BF),
            shape(rows, D, dtype=BF),
            shape(rows, D),
            shape(rows, D, dtype=BF),
            shape(rows, D, dtype=BF),
            shape(STATE_ROWS, LANES, dtype=BF),
            shape(16, D),
        ),
        [VMEM] * 10 + [ANY] * 3 + [VMEM],
        [
            pltpu.VMEM((D, D), BF),
            pltpu.VMEM((parts, D, D), BF),
            pltpu.VMEM((parts, D, D), BF),
            pltpu.SemaphoreType.DMA((2 * parts + 1,)),
        ],
        2 * rows * D * (D + 2 * FF),
        2 * D * (D + 2 * FF),
    )(gs, n2, r2, slope, n1, r1, mixed, inv, sq, cs, wo, w1, w2, ng)


def mix_back_kernel(layer, shifts, *refs):
    recv = refs[:shifts]
    (
        spot_ref,
        packed_ref,
        u_ref,
        dd_ref,
        before_ref,
        cs_ref,
        cm_ref,
        gb1_ref,
        gz1_ref,
        w_hbm,
        gpk_ref,
        gcol_ref,
        gs_ref,
        sums_ref,
        wbuf,
        sems,
    ) = refs[shifts:]
    parts = wbuf.shape[0]
    copies = [
        pltpu.make_async_copy(w_hbm.at[layer, :, pl.ds(D * j, D)], wbuf.at[j], sems.at[j])
        for j in range(parts)
    ]
    for copy in copies:
        copy.start()
    rows = packed_ref.shape[0]
    lo = left_half(rows)
    lo_state = left_half(LANES)
    one_left = lax.broadcasted_iota(jnp.int32, (rows, LANES), 1) == 0
    one_right = lax.broadcasted_iota(jnp.int32, (rows, LANES), 1) == HEAD_DIM
    col_left = lax.broadcasted_iota(jnp.int32, (LANES, LANES), 1) == 0
    col_right = lax.broadcasted_iota(jnp.int32, (LANES, LANES), 1) == HEAD_DIM
    cs = cs_ref[...]
    cm = cm_ref[...]
    later = recv[0][...].astype(F32)
    for other in recv[1:]:
        later = later + other[...].astype(F32)
    before = before_ref[...].astype(F32)
    before_totals = before[PAIRS * LANES :]
    later_totals = later[PAIRS * LANES :]
    for pair in range(PAIRS):
        here = slice(pair * LANES, (pair + 1) * LANES)
        at = pair * 3 * LANES
        t0, t1, t2 = (
            packed_ref[:, at + i * LANES : at + (i + 1) * LANES].astype(F32) for i in range(3)
        )
        sp0, sp1, sp2 = softplus(t0), softplus(t1), softplus(t2)
        sw0 = swap(sp0)
        sw1 = swap(sp1)
        sw2 = swap(sp2)
        q0 = low(jnp.where(lo, sp0, 0.0))
        k0 = low(jnp.where(lo, sw0, 0.0))
        q1 = low(jnp.where(lo, 0.0, sp1))
        k1 = low(jnp.where(lo, 0.0, sw2))
        kf0 = low(jnp.where(lo, sw0, sp0) * cs)
        kf1 = low(jnp.where(lo, sp2, sw2) * cs)
        v0 = low(jnp.where(lo, t1, jnp.where(one_right, 1.0, 0.0)))
        v1 = low(jnp.where(lo, jnp.where(one_left, 1.0, 0.0), t2))
        u = u_ref[:, here]
        uf = u.astype(F32)
        ds = swap(dd_ref[:, here].astype(F32))
        u0 = low(jnp.where(lo, uf, ds))
        u1 = low(jnp.where(lo, ds, uf))
        p0 = low(nt(q0, k0) * cm)
        p1 = low(nt(q1, k1) * cm)
        d0 = low(nt(u0, v0) * cm)
        d1 = low(nt(u1, v1) * cm)
        state = before[here]
        after = later[here]
        after_low = low(after)
        s0 = low(
            jnp.where(
                lo_state,
                state,
                jnp.where(col_right, totals_column(before_totals, 2 * pair, LANES), 0.0),
            )
        )
        s1 = low(
            jnp.where(
                lo_state,
                jnp.where(col_left, totals_column(before_totals, 2 * pair + 1, LANES), 0.0),
                state,
            )
        )
        r0 = low(
            jnp.where(
                lo_state,
                after,
                jnp.where(col_right, totals_column(later_totals, 2 * pair, LANES), 0.0),
            )
        )
        r1 = low(
            jnp.where(
                lo_state,
                jnp.where(col_left, totals_column(later_totals, 2 * pair + 1, LANES), 0.0),
                after,
            )
        )
        eq0 = nt(u0, s0) * cs
        eq1 = nt(u1, s1) * cs
        ek0 = nt(v0, r0) * cs
        ek1 = nt(v1, r1) * cs
        eq0 = eq0 + swap(eq0)
        eq1 = eq1 + swap(eq1)
        ek0 = ek0 + swap(ek0)
        ek1 = ek1 + swap(ek1)
        dq = jnp.where(lo, eq0 + nn(d0, k0), eq1 + nn(d1, k1))
        dk = jnp.where(lo, ek0 + tn(d0, q0), ek1 + tn(d1, q1))
        dv = jnp.where(
            lo,
            tn(p0, u) + nn(kf0, after_low),
            tn(p1, u) + nn(kf1, after_low),
        )
        dks = swap(dk)
        gpk_ref[:, at : at + LANES] = low(jnp.where(lo, dq, dks) * sigmoid(t0))
        gpk_ref[:, at + LANES : at + 2 * LANES] = low(jnp.where(lo, dv, dq * sigmoid(t1)))
        gpk_ref[:, at + 2 * LANES : at + 3 * LANES] = low(
            jnp.where(lo, dks * sigmoid(t2), dv)
        )
    grad = gz1_ref[...]
    for j in range(parts):
        here = slice(D * j, D * (j + 1))
        copies[j].wait()
        gpk = gpk_ref[:, here]
        sums_ref[j : j + 1, :] = column_sum(gpk.astype(F32))
        grad = grad + nt(gpk, wbuf[j])
    gs_ref[...] = grad
    near = spot_ref[3]
    far = spot_ref[4]
    gpk = gpk_ref[...].astype(F32)
    gb1 = gb1_ref[...].astype(F32)
    for low_bit in range(2):
        slot = low_bit ^ near
        for source, start in ((gb1, 0), (gpk, D // 2)):
            width = source.shape[1] // 4
            first = source[:, low_bit * width : (low_bit + 1) * width]
            second = source[:, (low_bit + 2) * width : (low_bit + 3) * width]
            both = jnp.concatenate(
                [jnp.where(far == 0, first, second), jnp.where(far == 0, second, first)], axis=1
            )
            gcol_ref[slot, :, start : start + 2 * width] = low(both)


def mix_back(layer, recv, spot, packed, u, dd, before, cs, cm, gb1, gz1, w):
    rows = packed.shape[0]
    return call(
        functools.partial(mix_back_kernel, layer, len(recv)),
        (
            shape(rows, 3 * D, dtype=BF),
            shape(2, rows, 2 * D, dtype=BF),
            shape(rows, D),
            shape(3, D),
        ),
        [VMEM] * len(recv) + [SMEM] + [VMEM] * 8 + [ANY],
        [pltpu.VMEM((3, D, D), BF), pltpu.SemaphoreType.DMA((3,))],
        2 * rows * D * 3 * D + 12 * HEADS * rows * rows * LANES,
        2 * D * 3 * D,
    )(*recv, spot, packed, u, dd, before, cs, cm, gb1, gz1, w)


def ffn_block(spot, midt, gpre, gb2t, hid, put):
    near = spot[3]
    far = spot[4]
    grad_in = nn(midt[0], gpre[...])
    grad_out = nn(gb2t[...], hid[...])
    for n in range(4):
        slot = (n % 2) ^ near
        half = (n // 2) ^ far
        put(0, slot, half, grad_in[:, D * n : D * (n + 1)])
        put(1, slot, half, grad_out[(D // 4) * n : (D // 4) * (n + 1)])


def ffn_send_kernel(spot, midt, gpre, gb2t, hid, out):
    def put(kind, slot, half, value):
        if kind == 0:
            out[0, slot, pl.ds(half * 96, 96), :] = low(value)
        else:
            out[0, slot, pl.ds(192, 192), pl.ds(half * 384, 384)] = low(value)

    ffn_block(spot, midt, gpre, gb2t, hid, put)


def ffn_keep_kernel(spot, midt, gpre, gb2t, hid, got, send0, keep0, send1, keep1):
    across = pl.program_id(0)
    along = pl.program_id(1)
    near = spot[3]
    far = spot[4]
    grad_in = nn(midt[0], gpre[...])
    grad_out = nn(gb2t[...], hid[...])

    def fill_in(target):
        for n in range(4):
            slot = (n % 2) ^ near
            rows = pl.ds(((n // 2) ^ far) * 96, 96)
            target[0, slot, rows, :] = low(
                grad_in[:, D * n : D * (n + 1)] + got[0, slot, rows, :].astype(F32)
            )

    def fill_out(target):
        for n in range(4):
            slot = (n % 2) ^ near
            lanes = pl.ds(pl.multiple_of(((n // 2) ^ far) * 384, 384), 384)
            target[0, slot, :, lanes] = low(
                grad_out[192 * n : 192 * (n + 1)] + got[0, slot, pl.ds(192, 192), lanes].astype(F32)
            )

    @pl.when(across == 0)
    def _():
        fill_in(keep0)

    @pl.when(across == 1)
    def _():
        fill_in(send0)

    @pl.when(along == 0)
    def _():
        fill_out(keep1)

    @pl.when(along == 1)
    def _():
        fill_out(send1)


def mix_send_kernel(spot, xt, mixt, gcol, out):
    for slot in range(2):
        out[0, slot, :, : D // 2] = low(nn(mixt[0], gcol[slot, :, : D // 2]))
        out[0, slot, :, D // 2 :] = low(nn(xt[0], gcol[slot, :, D // 2 :]))


def mix_keep_kernel(spot, xt, mixt, gcol, got, send0, keep0, send1, keep1):
    across = pl.program_id(0)
    along = pl.program_id(1)
    half = send0.shape[2]
    full = [
        (
            nn(mixt[0], gcol[slot, :, : D // 2]) + got[0, slot, :, : D // 2].astype(F32),
            nn(xt[0], gcol[slot, :, D // 2 :]) + got[0, slot, :, D // 2 :].astype(F32),
        )
        for slot in range(2)
    ]

    def fill(target, rows):
        for slot in range(2):
            target[0, slot, :, : D // 2] = low(full[slot][0][rows])
            target[0, slot, :, D // 2 :] = low(full[slot][1][rows])

    first = slice(0, half)
    second = slice(half, 2 * half)

    @pl.when(across == 0)
    def _():
        fill(keep0, first)

    @pl.when(across == 1)
    def _():
        fill(send0, first)

    @pl.when(along == 0)
    def _():
        fill(keep1, second)

    @pl.when(along == 1)
    def _():
        fill(send1, second)


def owner(same_core):
    def index(across, along, spot):
        core = spot[0] if same_core else 1 - spot[0]
        return ((spot[1] ^ along) * 2 + (spot[2] ^ across)) * 2 + core

    return index


def grad_specs(block, index):
    def rows_of(_):
        return pl.BlockSpec((1, D // 8, _), lambda a, b, s: (index(a, b, s), 0, 0))

    def whole(*dims):
        return pl.BlockSpec(dims, lambda a, b, s: (0,) * len(dims))

    return rows_of, whole


def grad_call(kind, spot, operands, got):
    keep = got is not None
    index = owner(keep)
    rows_of, whole = grad_specs(None, index)
    tokens = operands[0].shape[1]
    if kind == "ffn":
        midt, gpre, gb2t, hid = operands
        operands = (midt.reshape(8, D // 8, tokens), gpre, gb2t, hid)
        in_specs = [
            rows_of(tokens),
            whole(tokens, FF),
            whole(D, tokens),
            pl.BlockSpec((tokens, FF // 8), lambda a, b, s: (0, index(a, b, s))),
        ]
        rows, columns = 384, D
        kernel = ffn_keep_kernel if keep else ffn_send_kernel
        flops = 2 * tokens * D * FF
    else:
        xt, mixt, gcol = operands
        operands = (xt.reshape(8, D // 8, tokens), mixt.reshape(8, D // 8, tokens), gcol)
        in_specs = [rows_of(tokens), rows_of(tokens), whole(2, tokens, 2 * D)]
        rows, columns = 96, 2 * D
        kernel = mix_keep_kernel if keep else mix_send_kernel
        flops = 2 * tokens * D * 2 * D
    block = pl.BlockSpec((1, 2, rows, columns), lambda a, b, s: (2 * a + b, 0, 0, 0))
    if keep:
        in_specs.append(block)
        operands = operands + (got,)

        def half(at):
            return pl.BlockSpec(
                (1, 2, rows // 2, columns), lambda a, b, s: (at(a, b), 0, 0, 0)
            )

        out_specs = (
            half(lambda a, b: a * b),
            half(lambda a, b: jnp.where(a == 0, b, 1)),
            half(lambda a, b: a),
            half(lambda a, b: a),
        )
        outs = (shape(2, 2, rows // 2, columns, dtype=BF),) * 4
    else:
        out_specs = block
        outs = shape(4, 2, rows, columns, dtype=BF)
    return pl.pallas_call(
        kernel,
        out_shape=outs,
        grid_spec=pltpu.PrefetchScalarGridSpec(
            num_scalar_prefetch=1, grid=(2, 2), in_specs=in_specs, out_specs=out_specs
        ),
        compiler_params=pltpu.CompilerParams(vmem_limit_bytes=48 * 1024 * 1024),
        cost_estimate=pl.CostEstimate(
            flops=int(flops), bytes_accessed=int(4 * 2 * rows * columns * 2 * 2), transcendentals=0
        ),
    )(spot, *operands)


def wide_swap(v, bit):
    size = lax.axis_size("wide")
    return lax.ppermute(v, "wide", [(i, i ^ bit) for i in range(size)])


def narrow_swap(v, bit):
    size = lax.axis_size("narrow")
    return lax.ppermute(v, "narrow", [(i, i ^ bit) for i in range(size)])


def wide_add(v):
    return v.astype(F32)


def reduce_group(kind, spot, operands):
    sent = grad_call(kind, spot, operands, None)
    got = wide_swap(sent, 1)
    send0, keep0, send1, keep1 = grad_call(kind, spot, operands, got)
    got0 = wide_swap(send0, 2)
    got1 = wide_swap(send1, 4)
    next0 = wide_swap(low(wide_add(keep0[1]) + wide_add(got0[1])), 4)
    next1 = wide_swap(low(wide_add(keep1[1]) + wide_add(got1[1])), 2)
    sum0 = wide_add(keep0[0]) + wide_add(got0[0]) + wide_add(next0)
    sum1 = wide_add(keep1[0]) + wide_add(got1[0]) + wide_add(next1)
    full = jnp.concatenate([sum0, sum1], axis=1)
    near = narrow_swap(low(full[1]), 1)
    total = full[0] + wide_add(near)
    if kind == "ffn":
        mine = (total[:96], total[192:, :384])
        other = jnp.concatenate([total[96:192, :384], total[96:192, 384:], total[192:, 384:]], axis=0)
        far = wide_add(narrow_swap(low(other), 2))
        grad_in = mine[0] + jnp.concatenate([far[:96], far[96:192]], axis=1)
        grad_out = (mine[1] + far[192:]).T
        return grad_in, grad_out
    quarter = D // 4
    mine = jnp.concatenate([total[:, :quarter], total[:, 2 * quarter : 5 * quarter]], axis=1)
    other = jnp.concatenate([total[:, quarter : 2 * quarter], total[:, 5 * quarter :]], axis=1)
    both = mine + wide_add(narrow_swap(low(other), 2))
    return both[:, quarter:], both[:, :quarter]


def reduce_plain(left, right):
    term = low(tn(left, right))
    part = lax.psum_scatter(term, "narrow", scatter_dimension=1, tiled=True)
    return lax.psum_scatter(part.astype(F32), "wide", scatter_dimension=0, tiled=True)


def travel(state, step):
    size = lax.axis_size("narrow")
    got = []
    for shift in range(1, size):
        pairs = [(i, i + step * shift) for i in range(size) if 0 <= i + step * shift < size]
        got.append(lax.ppermute(state, "narrow", pairs))
    return got


def shards(
    tokens,
    cotangent,
    horizons,
    qkv_weight,
    out_weight,
    ffn_in_weight,
    ffn_out_weight,
    qkv_bias,
    ffn_in_bias,
    model_biases,
    norm_gains,
):
    rows = tokens.shape[0]
    wide = lax.axis_size("wide")
    narrow = lax.axis_size("narrow")
    wide_at = lax.axis_index("wide")
    narrow_at = lax.axis_index("narrow")
    spot = jnp.stack(
        [wide_at % 2, (wide_at // 4) % 2, (wide_at // 2) % 2, narrow_at % 2, (narrow_at // 2) % 2]
    ).astype(jnp.int32)
    step = 0.5 * math.pi / horizons[0].astype(F32)
    places = (narrow_at * rows + jnp.arange(rows)).astype(F32) * step
    cs = jnp.concatenate(
        [
            jnp.broadcast_to(jnp.cos(places)[:, None], (rows, HEAD_DIM)),
            jnp.broadcast_to(jnp.sin(places)[:, None], (rows, HEAD_DIM)),
        ],
        axis=1,
    )
    apart = jnp.arange(rows)[:, None] - jnp.arange(rows)[None, :]
    cm = jnp.where(apart >= 0, jnp.cos(apart.astype(F32) * step), 0.0)

    x = tokens
    saved = []
    for layer in range(LAYERS):
        packed, xt, state = project(layer, x, qkv_weight, qkv_bias, cs)
        recv = travel(state, 1)
        num, den, sq = inside(packed, cm)
        out_type = BF if layer == LAYERS - 1 else F32
        before, mixed, mixt, inv, n1, r1, midt, hid, slope, n2, r2, x_next = layer_forward(
            layer,
            recv,
            x,
            num,
            den,
            sq,
            cs,
            out_weight,
            ffn_in_weight,
            ffn_out_weight,
            ffn_in_bias,
            model_biases,
            norm_gains,
            out_type,
        )
        saved.append((packed, xt, sq, before, mixed, mixt, inv, n1, r1, midt, hid, slope, n2, r2))
        x = x_next
    output = x
    gs = cotangent
    layer_grads = [None] * LAYERS
    layer_sums = [None] * LAYERS
    for layer in reversed(range(LAYERS)):
        packed, xt, sq, before, mixed, mixt, inv, n1, r1, midt, hid, slope, n2, r2 = saved[layer]
        gb2t, gpre, gb1, gz1, u, dd, state, sums = layer_back(
            layer,
            gs,
            n2,
            r2,
            slope,
            n1,
            r1,
            mixed,
            inv,
            sq,
            cs,
            out_weight,
            ffn_in_weight,
            ffn_out_weight,
            norm_gains,
        )
        recv = travel(state, -1)
        if wide == 8 and narrow == 4:
            grad_in, grad_out = reduce_group("ffn", spot, (midt, gpre, gb2t, hid))
        else:
            grad_in = reduce_plain(midt.T, gpre)
            grad_out = reduce_plain(hid, gb2t.T)
        gpk, gcol, gs, gpk_sums = mix_back(
            layer, recv, spot, packed, u, dd, before, cs, cm, gb1, gz1, qkv_weight
        )
        if wide == 8 and narrow == 4:
            grad_qkv, grad_o = reduce_group("mix", spot, (xt, mixt, gcol))
        else:
            grad_qkv = reduce_plain(xt.T, gpk)
            grad_o = reduce_plain(mixt.T, gb1)
        layer_grads[layer] = (grad_qkv, grad_o, grad_in, grad_out)
        layer_sums[layer] = jnp.concatenate([sums[:10], gpk_sums], axis=0)
    sums = jnp.stack(layer_sums)
    if wide == 8 and narrow == 4:
        for bit in (1, 2, 4):
            sums = sums + wide_swap(sums, bit)
        for bit in (1, 2):
            sums = sums + narrow_swap(sums, bit)
    else:
        sums = lax.psum(sums, ("wide", "narrow"))

    def columns(v):
        width = v.shape[-1] // narrow
        return lax.dynamic_slice_in_dim(v, narrow_at * width, width, axis=v.ndim - 1)

    grads = [jnp.stack([layer_grads[l][k] for l in range(LAYERS)]) for k in range(4)]
    return (
        output,
        gs,
        grads[0],
        grads[1],
        grads[2],
        grads[3],
        columns(sums[:, 10:13].reshape(LAYERS, 3 * D)),
        columns(sums[:, 0:4].reshape(LAYERS, FF)),
        columns(sums[:, 4:8]),
        columns(sums[:, 8:10]),
    )


def solution(mesh):
    rows = P(("wide", "narrow"), None)
    placed = (rows, rows, P("wide")) + (P(),) * 8
    return jax.shard_map(
        shards,
        mesh=mesh,
        in_specs=placed,
        out_specs=(rows, rows)
        + (P(None, "wide", "narrow"),) * 4
        + (P(None, "narrow"),) * 2
        + (P(None, None, "narrow"),) * 2,
        check_vma=False,
    )
```

time: 1530 us -> 410 us (0.27)
  local copies, waits for them, and re-layouts: 696 us -> 36.4 us
  waiting for transfers between devices: 482 us -> 173 us
  matrix products: 173 us -> 0 us
  Pallas kernels: 0 us -> 113 us
  other arithmetic: 84 us -> 13.4 us
  starting transfers between devices: 35.1 us -> 66.9 us
  blocking collectives: 24.7 us -> 0 us
  between operations: 18.6 us -> 2.82 us
    unnamed x323 -> x143, local copies, waits for them, and re-layouts: 569 us -> 32.7 us
    all_to_all x8 -> x0, waiting for transfers between devices: 224 us -> none  [the longest x2 139 us: shards(): lax.all_to_all(grad_packed_heads, 'narrow', split_axis=0, concat_axis=1,...]
    unnamed x19 -> x0, waiting for transfers between devices: 224 us -> none
    ppermute x0 -> x45, waiting for transfers between devices: none -> 173 us  [the longest x23 86.7 us: wide_swap(): return lax.ppermute(v, 'wide', [(i, i ^ bit) for i in range(size)])]
    dot_general x62 -> x0, matrix products: 173 us -> none  [the longest x8 33.2 us: matmul_low(): return jnp.dot(left, right, preferred_element_type=jnp.float32)]
    pallas_call x0 -> x18, Pallas kernels: none -> 113 us  [the longest x8 37.8 us: grad_call(): pl.pallas_call(kernel, out_shape=outs, grid_spec=pltpu.PrefetchScalarGrid...]
    ppermute x0 -> x45, starting transfers between devices: none -> 66.9 us  [the longest x12 34.1 us: travel(): got.append(lax.ppermute(state, 'narrow', pairs))]
    another operation x26 -> x5, local copies, waits for them, and re-layouts: 37.4 us -> 0.34 us  [the longest x4 0.25 us: shards(): jnp.stack([layer_grads[l][k] for l in range(LAYERS)])]
  transfers between devices with their start and end apart: 19 -> 45, of which waited for: 10 -> 26; matrix products, arithmetic and copies ran while one was open for 45% -> 4% of each run, Pallas kernels for 0% -> 14%
where the time goes in v1:
time: 410 us; the launch traced here: 406 us
  waiting for transfers between devices  173 us (42%)
  Pallas kernels  113 us (28%)
  starting transfers between devices  66.9 us (16%)
  local copies, waits for them, and re-layouts  36.4 us (9%)
  other arithmetic  13.4 us (3%)
    ppermute x23, waiting for transfers between devices, wide_swap(): return lax.ppermute(v, 'wide', [(i, i ^ bit) for i in range(size)])  86.7 us
    ppermute x12, waiting for transfers between devices, travel(): got.append(lax.ppermute(state, 'narrow', pairs))  47.2 us
    ppermute x10, waiting for transfers between devices, narrow_swap(): return lax.ppermute(v, 'narrow', [(i, i ^ bit) for i in range(size)])  39.3 us
    pallas_call x8, Pallas kernels, grad_call(): pl.pallas_call(kernel, out_shape=outs, grid_spec=pltpu.PrefetchScalarGrid...  37.8 us
    ppermute x12, starting transfers between devices, travel(): got.append(lax.ppermute(state, 'narrow', pairs))  34.1 us
    unnamed x143, local copies, waits for them, and re-layouts  32.7 us
    ppermute x23, starting transfers between devices, wide_swap(): return lax.ppermute(v, 'wide', [(i, i ^ bit) for i in range(size)])  23.8 us
    pallas_call x2, Pallas kernels, layer_forward(): call(functools.partial(layer_kernel, layer, len(recv)), (shape(STATE_ROWS...  21.5 us
  transfers between devices with their start and end apart: 45, of which 26 were waited for; matrix products, arithmetic and copies ran while one was open for 4% of the time, Pallas kernels for 14%

profile of v1, /device:TPU:0, one launch (start us, length us, event | category | flops | bytes accessed | tf_op | source)
XLA Modules:
  0.0 405.8 jit_solution(4350783636908565931)
XLA Ops:
  3.4 4.2 %shard_map.186 = (bf16[256,2304]{1,0:T(8,128)(2,1)S(1)}, bf16[768,256]{1,0:T(8,128)(2,1)S(1)}, bf16[896,128]{1,0:T(8,128)(2,1)S(1)}) custom-call(bf16[256,768]{1,0:T(8,128)(2,1)S(1)} %copy-done.18, bf16[2,768,2304]{2,1,0:T(8,128)(2,1)} %refs_12_.7, bf16[2,2304]{1,0:T(2,128)(2,1)S(1)} %copy-done.67, f32[256,128]{1,0:T(8,128)S(1)} %pad_maximum_fusion.12.cs_ref.refs_7_.refs_8_), custom_call_target="tpu_custom_call" | custom-call | flops 905969664 | bytes 3538944 | tf_op jit(solution)/shard_map/pallas_call | solution.py:153
  8.3 5.1 %collective-permute-start = (bf16[896,128]{1,0:T(8,128)(2,1)S(1)}, bf16[896,128]{1,0:T(8,128)(2,1)S(1)}, u32[]{:S(2)}, u32[]{:S(2)}) collective-permute-start(bf16[896,128]{1,0:T(8,128)(2,1)S(1)} %get-tuple-element.84), channel_id=1, source_target_pairs={{0,1},{1,2},{2,3},{4,5},{5,6},{6,7},{8,9},{9,10},{10,11},{12,13},{... | collective-permute-start | bytes 688136 | tf_op jit(solution)/shard_map/ppermute | solution.py:862
  13.4 4.5 %collective-permute-start.1 = (bf16[896,128]{1,0:T(8,128)(2,1)S(1)}, bf16[896,128]{1,0:T(8,128)(2,1)S(1)}, u32[]{:S(2)}, u32[]{:S(2)}) collective-permute-start(bf16[896,128]{1,0:T(8,128)(2,1)S(1)} %get-tuple-element.84), channel_id=1, source_target_pairs={{0,2},{1,3},{4,6},{5,7},{8,10},{9,11},{12,14},{13,15},{16,18},{17,... | collective-permute-start | bytes 688136 | tf_op jit(solution)/shard_map/ppermute | solution.py:862
  20.1 2.3 shard_map.187
  24.1 4.0 collective-permute-done.2.refs_2_
  28.1 10.8 %shard_map.188 = (bf16[896,128]{1,0:T(8,128)(2,1)S(1)}, bf16[256,768]{1,0:T(8,128)(2,1)S(1)}, bf16[768,256]{1,0:T(8,128)(2,1)S(1)}, f32[256,768]{1,0:T(8,128)S(1...) custom-call(bf16[896,128]{1,0:T(8,128)(2,1)S(1)} %collective-permute, ...), custom_call_target="tpu_custom_call" | custom-call | flops 2717908992 | bytes 10616832 | tf_op jit(solution)/shard_map/pallas_call | solution.py:314
  41.6 1.7 copy-done.8
  43.3 4.2 %shard_map.189 = (bf16[256,2304]{1,0:T(8,128)(2,1)S(1)}, bf16[768,256]{1,0:T(8,128)(2,1)S(1)}, bf16[896,128]{1,0:T(8,128)(2,1)S(1)}) custom-call(f32[256,768]{1,0:T(8,128)S(1)} %copy-done.8, bf16[2,768,2304]{2,1,0:T(8,128)(2,1)} %refs_12_.7, bf16[2,2304]{1,0:T(2,128)(2,1)S(1)} %copy-done.68, f32[256,128]{1,0:T(8,128)S(1)} %pad_maximum_fusion.12.cs_ref.refs_7_.refs_8_), custom_call_target="tpu_custom_call" | custom-call | flops 905969664 | bytes 3538944 | tf_op jit(solution)/shard_map/pallas_call | solution.py:153
  47.5 8.5 %collective-permute-start.3 = (bf16[896,128]{1,0:T(8,128)(2,1)S(1)}, bf16[896,128]{1,0:T(8,128)(2,1)S(1)}, u32[]{:S(2)}, u32[]{:S(2)}) collective-permute-start(bf16[896,128]{1,0:T(8,128)(2,1)S(1)} %get-tuple-element.90), channel_id=1, source_target_pairs={{0,1},{1,2},{2,3},{4,5},{5,6},{6,7},{8,9},{9,10},{10,11},{12,13},{... | collective-permute-start | bytes 688136 | tf_op jit(solution)/shard_map/ppermute | solution.py:862
  56.1 5.3 %collective-permute-start.4 = (bf16[896,128]{1,0:T(8,128)(2,1)S(1)}, bf16[896,128]{1,0:T(8,128)(2,1)S(1)}, u32[]{:S(2)}, u32[]{:S(2)}) collective-permute-start(bf16[896,128]{1,0:T(8,128)(2,1)S(1)} %get-tuple-element.90), channel_id=1, source_target_pairs={{0,2},{1,3},{4,6},{5,7},{8,10},{9,11},{12,14},{13,15},{16,18},{17,... | collective-permute-start | bytes 688136 | tf_op jit(solution)/shard_map/ppermute | solution.py:862
  62.9 2.3 shard_map.190
  68.0 2.0 collective-permute-done.5.refs_2_
  70.0 10.7 %shard_map.191 = (bf16[896,128]{1,0:T(8,128)(2,1)S(1)}, bf16[256,768]{1,0:T(8,128)(2,1)S(1)}, bf16[768,256]{1,0:T(8,128)(2,1)S(1)}, f32[256,768]{1,0:T(8,128)S(1...) custom-call(bf16[896,128]{1,0:T(8,128)(2,1)S(1)} %collective-permute, ...), custom_call_target="tpu_custom_call" | custom-call | flops 2717908992 | bytes 10616832 | tf_op jit(solution)/shard_map/pallas_call | solution.py:314
  83.1 11.5 %shard_map.192 = (bf16[768,256]{1,0:T(8,128)(2,1)S(1)}, bf16[256,3072]{1,0:T(8,128)(2,1)}, bf16[256,768]{1,0:T(8,128)(2,1)S(1)}, f32[256,768]{1,0:T(8,128)S(1)},...) custom-call(bf16[256,768]{1,0:T(8,128)(2,1)S(1)} %copy-done.49, ...), custom_call_target="tpu_custom_call" | custom-call | flops 2717908992 | bytes 10616832 | tf_op jit(solution)/shard_map/pallas_call | solution.py:443
  103.1 8.4 %collective-permute-done.6.refs_0_ = bf16[896,128]{1,0:T(8,128)(2,1)S(1)} collective-permute-done((bf16[896,128]{1,0:T(8,128)(2,1)}, bf16[896,128]{1,0:T(8,128)(2,1)S(1)}, u32[]{:S(2)}, u32[]{:S(2)}) %collective-permute-start.6) | collective-permute-done | bytes 229408 | tf_op jit(solution)/shard_map/ppermute | solution.py:862
  112.1 14.5 %collective-permute-done.7.refs_1_ = bf16[896,128]{1,0:T(8,128)(2,1)} collective-permute-done((bf16[896,128]{1,0:T(8,128)(2,1)}, bf16[896,128]{1,0:T(8,128)(2,1)}, u32[]{:S(2)}, u32[]{:S(2)}) %collective-permute-start.7) | collective-permute-done | bytes 229408 | tf_op jit(solution)/shard_map/ppermute | solution.py:862
  132.7 9.5 %shard_map.193 = (bf16[256,2304]{1,0:T(8,128)(2,1)}, bf16[2,256,1536]{2,1,0:T(8,128)(2,1)}, f32[256,768]{1,0:T(8,128)S(1)}, f32[3,768]{1,0:T(4,128)S(1)}) custom-call(bf16[896,128]{1,0:T(8,128)(2,1)S(1)} %copy-done.57, bf16[896,128]{1,0:T(8,128)(2,1)} %collective-permute-done.7.refs_1_, bf16[896,128]{1,0:T(8,128)(2,1)} %collective-permute-done.8.refs_2_, ...), custom_call_target="tpu_custom_call" | custom-call | flops 2113929216 | bytes 3538944 | tf_op jit(solution)/shard_map/pallas_call | solution.py:614
  143.6 3.5 shard_map.198
  147.2 9.9 %shard_map.194 = (bf16[768,256]{1,0:T(8,128)(2,1)S(1)}, bf16[256,3072]{1,0:T(8,128)(2,1)}, bf16[256,768]{1,0:T(8,128)(2,1)S(1)}, f32[256,768]{1,0:T(8,128)S(1)},...) custom-call(f32[256,768]{1,0:T(8,128)S(1)} %get-tuple-element.109.gs, ...), custom_call_target="tpu_custom_call" | custom-call | flops 2717908992 | bytes 10616832 | tf_op jit(solution)/shard_map/pallas_call | solution.py:443
  161.8 14.9 %collective-permute-done.10.refs_1_ = bf16[896,128]{1,0:T(8,128)(2,1)S(1)} collective-permute-done((bf16[896,128]{1,0:T(8,128)(2,1)S(1)}, bf16[896,128]{1,0:T(8,128)(2,1)S(1)}, u32[]{:S(2)}, u32[]{:S(2)}) %collective-permute-start.10) | collective-permute-done | bytes 229408 | tf_op jit(solution)/shard_map/ppermute | solution.py:862
  176.6 3.5 collective-permute-done.9.refs_0_
  180.1 10.1 %shard_map.195 = (bf16[256,2304]{1,0:T(8,128)(2,1)}, bf16[2,256,1536]{2,1,0:T(8,128)(2,1)}, f32[256,768]{1,0:T(8,128)}, f32[3,768]{1,0:T(4,128)S(1)}) custom-call(bf16[896,128]{1,0:T(8,128)(2,1)S(1)} %collective-permute-done.9.refs_0_, bf16[896,128]{1,0:T(8,128)(2,1)S(1)} %collective-permute-done.10.refs_1_, ...), custom_call_target="tpu_custom_call" | custom-call | flops 2113929216 | bytes 3538944 | tf_op jit(solution)/shard_map/pallas_call | solution.py:614
  191.6 3.6 shard_map.196
  195.9 3.7 collective-permute-done.40
  199.6 1.6 collective-permute-start.41
  201.1 3.6 collective-permute-done.41
  205.4 1.5 collective-permute-start.42
  206.9 3.4 collective-permute-done.42
  211.3 2.1 collective-permute-start.43
  215.3 4.7 %shard_map.202 = bf16[4,2,384,768]{3,2,1,0:T(8,128)(2,1)} custom-call(s32[5]{0:T(128)S(1)} %stack.68.refs_3_.spot, bf16[8,96,256]{2,1,0:T(8,128)(2,1)S(1)} %bitcast.106, bf16[256,3072]{1,0:T(8,128)(2,1)S(1)} %copy-done.6, bf16[768,256]{1,0:T(8,128)(2,1)S(1)} %copy-done.14, bf16[256,3072]{1,0:T(8,128)(2,1)S(1)} %copy-done.5), custom_call_target="tpu_custom_call" | custom-call | flops 1207959552 | bytes 9437184 | tf_op jit(solution)/shard_map/pallas_call | solution.py:797
  220.2 4.6 %shard_map.200 = bf16[4,2,384,768]{3,2,1,0:T(8,128)(2,1)} custom-call(s32[5]{0:T(128)S(1)} %stack.68.refs_3_.spot, bf16[8,96,256]{2,1,0:T(8,128)(2,1)S(1)} %bitcast.104, bf16[256,3072]{1,0:T(8,128)(2,1)S(1)} %copy-done.7, bf16[768,256]{1,0:T(8,128)(2,1)S(1)} %copy-done.17, bf16[256,3072]{1,0:T(8,128)(2,1)S(1)} %copy-done.4), custom_call_target="tpu_custom_call" | custom-call | flops 1207959552 | bytes 9437184 | tf_op jit(solution)/shard_map/pallas_call | solution.py:797
  225.3 2.5 collective-permute-done.44
  227.9 4.2 %shard_map.199 = (bf16[2,2,48,1536]{3,2,1,0:T(8,128)(2,1)S(1)}, bf16[2,2,48,1536]{3,2,1,0:T(8,128)(2,1)S(1)}, bf16[2,2,48,1536]{3,2,1,0:T(8,128)(2,1)S(1)}, bf16[2,2,48,1536]{3,2,1,0:T(8,128)(2,1)S(1)}) custom-call(s32[5]{0:T(128)S(1)} %stack.68.refs_3_.spot, bf16[8,96,256]{2,1,0:T(8,128)(2,1)S(1)} %bitcast.113, bf16[8,96,256]{2,1,0:T(8,128)(2,1)S(1)} %bitcast.115, ...), custom_call_target="tpu_custom_call" | custom-call | flops 603979776 | bytes 4718592 | tf_op jit(solution)/shard_map/pallas_call | solution.py:797
  232.1 1.6 collective-permute-start.20
  235.7 1.5 collective-permute-start.22
  237.9 4.1 %shard_map.197 = (bf16[2,2,48,1536]{3,2,1,0:T(8,128)(2,1)S(1)}, bf16[2,2,48,1536]{3,2,1,0:T(8,128)(2,1)S(1)}, bf16[2,2,48,1536]{3,2,1,0:T(8,128)(2,1)S(1)}, bf16[2,2,48,1536]{3,2,1,0:T(8,128)(2,1)S(1)}) custom-call(s32[5]{0:T(128)S(1)} %stack.68.refs_3_.spot, bf16[8,96,256]{2,1,0:T(8,128)(2,1)S(1)} %bitcast.109, bf16[8,96,256]{2,1,0:T(8,128)(2,1)S(1)} %bitcast.111, ...), custom_call_target="tpu_custom_call" | custom-call | flops 603979776 | bytes 4718592 | tf_op jit(solution)/shard_map/pallas_call | solution.py:797
  242.6 5.8 %collective-permute-done.20 = bf16[2,2,48,1536]{3,2,1,0:T(8,128)(2,1)S(1)} collective-permute-done((bf16[2,2,48,1536]{3,2,1,0:T(8,128)(2,1)S(1)}, bf16[2,2,48,1536]{3,2,1,0:T(8,128)(2,1)S(1)}, u32[]{:S(2)}, u32[]{:S(2)}) %collective-permute-start.20) | collective-permute-done | bytes 589856 | tf_op jit(solution)/shard_map/ppermute | solution.py:812
  248.4 1.5 collective-permute-start.15
  249.9 1.9 collective-permute-done.22
  251.9 1.5 collective-permute-start.21
  253.5 6.6 %collective-permute-done.13 = bf16[2,2,48,1536]{3,2,1,0:T(8,128)(2,1)S(1)} collective-permute-done((bf16[2,2,48,1536]{3,2,1,0:T(8,128)(2,1)S(1)}, bf16[2,2,48,1536]{3,2,1,0:T(8,128)(2,1)S(1)}, u32[]{:S(2)}, u32[]{:S(2)}) %collective-permute-start.13) | collective-permute-done | bytes 589856 | tf_op jit(solution)/shard_map/ppermute | solution.py:812
  261.7 2.9 collective-permute-done.15
  264.6 1.5 collective-permute-start.14
  266.2 4.7 %collective-permute-done.21 = bf16[2,48,1536]{2,1,0:T(8,128)(2,1)S(1)} collective-permute-done((bf16[2,48,1536]{2,1,0:T(8,128)(2,1)S(1)}, bf16[2,48,1536]{2,1,0:T(8,128)(2,1)S(1)}, u32[]{:S(2)}, u32[]{:S(2)}) %collective-permute-start.21) | collective-permute-done | bytes 294944 | tf_op jit(solution)/shard_map/ppermute | solution.py:812
  272.8 3.2 collective-permute-done.14
  276.1 1.6 collective-permute-done.16
  277.8 4.2 %collective-permute-done.24 = bf16[96,1536]{1,0:T(8,128)(2,1)S(1)} collective-permute-done((bf16[96,1536]{1,0:T(8,128)(2,1)S(1)}, bf16[96,1536]{1,0:T(8,128)(2,1)S(1)}, u32[]{:S(2)}, u32[]{:S(2)}) %collective-permute-start.24) | collective-permute-done | bytes 294944 | tf_op jit(solution)/shard_map/ppermute | solution.py:817
  282.5 1.8 collective-permute-start.17
  284.4 4.2 %collective-permute-done.25 = bf16[96,768]{1,0:T(8,128)(2,1)S(1)} collective-permute-done((bf16[96,768]{1,0:T(8,128)(2,1)S(1)}, bf16[96,768]{1,0:T(8,128)(2,1)S(1)}, u32[]{:S(2)}, u32[]{:S(2)}) %collective-permute-start.25) | collective-permute-done | bytes 147488 | tf_op jit(solution)/shard_map/ppermute | solution.py:817
  288.9 6.5 %shard_map.203 = (bf16[2,2,192,768]{3,2,1,0:T(8,128)(2,1)S(1)}, bf16[2,2,192,768]{3,2,1,0:T(8,128)(2,1)S(1)}, bf16[2,2,192,768]{3,2,1,0:T(8,128)(2,1)S(1)}, bf16[2,2,192,768]{3,2,1,0:T(8,128)(2,1)S(1)}) custom-call(s32[5]{0:T(128)S(1)} %stack.68.refs_3_.spot, bf16[8,96,256]{2,1,0:T(8,128)(2,1)S(1)} %bitcast.107, bf16[256,3072]{1,0:T(8,128)(2,1)} %get-tuple-element.147.gpre, ...), custom_call_target="tpu_custom_call" | custom-call | flops 1207959552 | bytes 9437184 | tf_op jit(solution)/shard_map/pallas_call | solution.py:797
  296.0 1.6 collective-permute-start.36
  297.6 2.2 copy-done.69
  299.8 6.5 %shard_map.201 = (bf16[2,2,192,768]{3,2,1,0:T(8,128)(2,1)S(1)}, bf16[2,2,192,768]{3,2,1,0:T(8,128)(2,1)S(1)}, bf16[2,2,192,768]{3,2,1,0:T(8,128)(2,1)S(1)}, bf16[2,2,192,768]{3,2,1,0:T(8,128)(2,1)S(1)}) custom-call(s32[5]{0:T(128)S(1)} %stack.68.refs_3_.spot, bf16[8,96,256]{2,1,0:T(8,128)(2,1)S(1)} %bitcast.105, bf16[256,3072]{1,0:T(8,128)(2,1)} %get-tuple-element.139.gpre, ...), custom_call_target="tpu_custom_call" | custom-call | flops 1207959552 | bytes 9437184 | tf_op jit(solution)/shard_map/pallas_call | solution.py:797
  306.3 2.1 collective-permute-start.27
  309.2 15.3 %collective-permute-done.34 = bf16[2,2,192,768]{3,2,1,0:T(8,128)(2,1)} collective-permute-done((bf16[2,2,192,768]{3,2,1,0:T(8,128)(2,1)S(1)}, bf16[2,2,192,768]{3,2,1,0:T(8,128)(2,1)}, u32[]{:S(2)}, u32[]{:S(2)}) %collective-permute-start.34) | collective-permute-done | bytes 1179680 | tf_op jit(solution)/shard_map/ppermute | solution.py:812
  325.7 1.6 collective-permute-start.35
  328.6 21.1 %collective-permute-done.27 = bf16[2,2,192,768]{3,2,1,0:T(8,128)(2,1)S(1)} collective-permute-done((bf16[2,2,192,768]{3,2,1,0:T(8,128)(2,1)S(1)}, bf16[2,2,192,768]{3,2,1,0:T(8,128)(2,1)S(1)}, u32[]{:S(2)}, u32[]{:S(2)}) %collective-permute-start.27) | collective-permute-done | bytes 1179680 | tf_op jit(solution)/shard_map/ppermute | solution.py:812
  349.8 1.6 collective-permute-start.28
  352.4 10.0 %collective-permute-done.35 = bf16[2,192,768]{2,1,0:T(8,128)(2,1)S(1)} collective-permute-done((bf16[2,192,768]{2,1,0:T(8,128)(2,1)S(1)}, bf16[2,192,768]{2,1,0:T(8,128)(2,1)S(1)}, u32[]{:S(2)}, u32[]{:S(2)}) %collective-permute-start.35) | collective-permute-done | bytes 589856 | tf_op jit(solution)/shard_map/ppermute | solution.py:812
  365.9 2.8 collective-permute-done.28
  371.6 9.4 %collective-permute-done.38 = bf16[384,768]{1,0:T(8,128)(2,1)S(1)} collective-permute-done((bf16[384,768]{1,0:T(8,128)(2,1)S(1)}, bf16[384,768]{1,0:T(8,128)(2,1)S(1)}, u32[]{:S(2)}, u32[]{:S(2)}) %collective-permute-start.38) | collective-permute-done | bytes 589856 | tf_op jit(solution)/shard_map/ppermute | solution.py:817
  381.2 3.0 collective-permute-start.39
  384.2 9.4 %collective-permute-done.31 = bf16[384,768]{1,0:T(8,128)(2,1)S(1)} collective-permute-done((bf16[384,768]{1,0:T(8,128)(2,1)S(1)}, bf16[384,768]{1,0:T(8,128)(2,1)S(1)}, u32[]{:S(2)}, u32[]{:S(2)}) %collective-permute-start.31) | collective-permute-done | bytes 589856 | tf_op jit(solution)/shard_map/ppermute | solution.py:817
  394.1 9.6 %collective-permute-done.32 = bf16[384,384]{1,0:T(8,128)(2,1)S(1)} collective-permute-done((bf16[384,384]{1,0:T(8,128)(2,1)S(1)}, bf16[384,384]{1,0:T(8,128)(2,1)S(1)}, u32[]{:S(2)}, u32[]{:S(2)}) %collective-permute-start.32) | collective-permute-done | bytes 294944 | tf_op jit(solution)/shard_map/ppermute | solution.py:817
  (265 shorter events, 65.0 us)
Async XLA Ops:
  8.3 19.8 %copy-start.19 = (bf16[256,768]{1,0:T(8,128)(2,1)S(1)}, bf16[256,768]{1,0:T(8,128)(2,1)}, u32[]{:S(2)}) copy-start(bf16[256,768]{1,0:T(8,128)(2,1)} %refs_3_.1) | copy-start | bytes 1179652
  8.3 19.8 %copy-start.62 = (bf16[2,2,768]{2,1,0:T(2,128)(2,1)S(1)}, bf16[2,2,768]{2,1,0:T(2,128)(2,1)}, u32[]{:S(2)}) copy-start(bf16[2,2,768]{2,1,0:T(2,128)(2,1)} %ng_ref.3) | copy-start | bytes 18436
  8.3 19.8 %copy-start.63 = (bf16[2,3072]{1,0:T(2,128)(2,1)S(1)}, bf16[2,3072]{1,0:T(2,128)(2,1)}, u32[]{:S(2)}) copy-start(bf16[2,3072]{1,0:T(2,128)(2,1)} %refs_11_.3) | copy-start | bytes 36868
  8.3 19.8 %copy-start.64 = (bf16[2,4,768]{2,1,0:T(4,128)(2,1)S(1)}, bf16[2,4,768]{2,1,0:T(4,128)(2,1)}, u32[]{:S(2)}) copy-start(bf16[2,4,768]{2,1,0:T(4,128)(2,1)} %refs_12_.5) | copy-start | bytes 36868
  8.3 15.8 %collective-permute-start = (bf16[896,128]{1,0:T(8,128)(2,1)S(1)}, bf16[896,128]{1,0:T(8,128)(2,1)S(1)}, u32[]{:S(2)}, u32[]{:S(2)}) collective-permute-start(bf16[896,128]{1,0:T(8,128)(2,1)S(1)} %get-tuple-element.84), channel_id=1, source_target_pairs={{0,1},{1,2},{2,3},{4,5},{5,6},{6,7},{8,9},{9,10},{10,11},{12,13},{... | collective-permute-start | bytes 688136 | tf_op jit(solution)/shard_map/ppermute | solution.py:862
  13.4 10.7 %collective-permute-start.1 = (bf16[896,128]{1,0:T(8,128)(2,1)S(1)}, bf16[896,128]{1,0:T(8,128)(2,1)S(1)}, u32[]{:S(2)}, u32[]{:S(2)}) collective-permute-start(bf16[896,128]{1,0:T(8,128)(2,1)S(1)} %get-tuple-element.84), channel_id=1, source_target_pairs={{0,2},{1,3},{4,6},{5,7},{8,10},{9,11},{12,14},{13,15},{16,18},{17,... | collective-permute-start | bytes 688136 | tf_op jit(solution)/shard_map/ppermute | solution.py:862
  17.9 10.2 %collective-permute-start.2 = (bf16[896,128]{1,0:T(8,128)(2,1)S(1)}, bf16[896,128]{1,0:T(8,128)(2,1)S(1)}, u32[]{:S(2)}, u32[]{:S(2)}) collective-permute-start(bf16[896,128]{1,0:T(8,128)(2,1)S(1)} %get-tuple-element.84), channel_id=1, source_target_pairs={{0,3},{4,7},{8,11},{12,15},{16,19},{20,23},{24,27},{28,31}} | collective-permute-start | bytes 688136 | tf_op jit(solution)/shard_map/ppermute | solution.py:862
  28.1 13.4 %copy-start.68 = (bf16[2,2304]{1,0:T(2,128)(2,1)S(1)}, bf16[2,2304]{1,0:T(2,128)(2,1)}, u32[]{:S(2)}) copy-start(bf16[2,2304]{1,0:T(2,128)(2,1)} %b_ref.3) | copy-start | bytes 27652
  47.5 94.7 %copy-start.26 = (bf16[768,256]{1,0:T(8,128)(2,1)}, bf16[768,256]{1,0:T(8,128)(2,1)S(1)}, u32[]{:S(2)}) copy-start(bf16[768,256]{1,0:T(8,128)(2,1)S(1)} %get-tuple-element.131) | copy-start | bytes 1179652
  47.5 22.5 %copy-start.9 = (f32[256,768]{1,0:T(8,128)S(1)}, f32[256,768]{1,0:T(8,128)}, u32[]{:S(2)}) copy-start(f32[256,768]{1,0:T(8,128)} %get-tuple-element.89.x_ref.refs_3_) | copy-start | bytes 2359300
  47.5 20.5 %collective-permute-start.3 = (bf16[896,128]{1,0:T(8,128)(2,1)S(1)}, bf16[896,128]{1,0:T(8,128)(2,1)S(1)}, u32[]{:S(2)}, u32[]{:S(2)}) collective-permute-start(bf16[896,128]{1,0:T(8,128)(2,1)S(1)} %get-tuple-element.90), channel_id=1, source_target_pairs={{0,1},{1,2},{2,3},{4,5},{5,6},{6,7},{8,9},{9,10},{10,11},{12,13},{... | collective-permute-start | bytes 688136 | tf_op jit(solution)/shard_map/ppermute | solution.py:862
  56.1 12.0 %collective-permute-start.4 = (bf16[896,128]{1,0:T(8,128)(2,1)S(1)}, bf16[896,128]{1,0:T(8,128)(2,1)S(1)}, u32[]{:S(2)}, u32[]{:S(2)}) collective-permute-start(bf16[896,128]{1,0:T(8,128)(2,1)S(1)} %get-tuple-element.90), channel_id=1, source_target_pairs={{0,2},{1,3},{4,6},{5,7},{8,10},{9,11},{12,14},{13,15},{16,18},{17,... | collective-permute-start | bytes 688136 | tf_op jit(solution)/shard_map/ppermute | solution.py:862
  61.4 8.6 %collective-permute-start.5 = (bf16[896,128]{1,0:T(8,128)(2,1)S(1)}, bf16[896,128]{1,0:T(8,128)(2,1)S(1)}, u32[]{:S(2)}, u32[]{:S(2)}) collective-permute-start(bf16[896,128]{1,0:T(8,128)(2,1)S(1)} %get-tuple-element.90), channel_id=1, source_target_pairs={{0,3},{4,7},{8,11},{12,15},{16,19},{20,23},{24,27},{28,31}} | collective-permute-start | bytes 688136 | tf_op jit(solution)/shard_map/ppermute | solution.py:862
  70.0 13.1 %copy-start.49 = (bf16[256,768]{1,0:T(8,128)(2,1)S(1)}, bf16[256,768]{1,0:T(8,128)(2,1)}, u32[]{:S(2)}) copy-start(bf16[256,768]{1,0:T(8,128)(2,1)} %gs_ref.1) | copy-start | bytes 1179652
  83.1 59.1 %copy-start.28 = (bf16[768,256]{1,0:T(8,128)(2,1)}, bf16[768,256]{1,0:T(8,128)(2,1)S(1)}, u32[]{:S(2)}) copy-start(bf16[768,256]{1,0:T(8,128)(2,1)S(1)} %get-tuple-element.132) | copy-start | bytes 1179652
  99.0 12.4 %collective-permute-start.6 = (bf16[896,128]{1,0:T(8,128)(2,1)}, bf16[896,128]{1,0:T(8,128)(2,1)S(1)}, u32[]{:S(2)}, u32[]{:S(2)}) collective-permute-start(bf16[896,128]{1,0:T(8,128)(2,1)} %get-tuple-element.103), channel_id=1, source_target_pairs={{1,0},{2,1},{3,2},{5,4},{6,5},{7,6},{9,8},{10,9},{11,10},{13,12},{... | collective-permute-start | bytes 688136 | tf_op jit(solution)/shard_map/ppermute | solution.py:862
  100.3 26.3 %collective-permute-start.7 = (bf16[896,128]{1,0:T(8,128)(2,1)}, bf16[896,128]{1,0:T(8,128)(2,1)}, u32[]{:S(2)}, u32[]{:S(2)}) collective-permute-start(bf16[896,128]{1,0:T(8,128)(2,1)} %get-tuple-element.103), channel_id=1, source_target_pairs={{2,0},{3,1},{6,4},{7,5},{10,8},{11,9},{14,12},{15,13},{18,16},{19,... | collective-permute-start | bytes 688136 | tf_op jit(solution)/shard_map/ppermute | solution.py:862
  101.6 25.0 %collective-permute-start.8 = (bf16[896,128]{1,0:T(8,128)(2,1)}, bf16[896,128]{1,0:T(8,128)(2,1)}, u32[]{:S(2)}, u32[]{:S(2)}) collective-permute-start(bf16[896,128]{1,0:T(8,128)(2,1)} %get-tuple-element.103), channel_id=1, source_target_pairs={{3,0},{7,4},{11,8},{15,12},{19,16},{23,20},{27,24},{31,28}} | collective-permute-start | bytes 688136 | tf_op jit(solution)/shard_map/ppermute | solution.py:862
  147.2 80.7 %collective-permute-start.19 = (bf16[4,2,96,1536]{3,2,1,0:T(8,128)(2,1)}, bf16[4,2,96,1536]{3,2,1,0:T(8,128)(2,1)}, u32[]{:S(2)}, u32[]{:S(2)}) collective-permute-start(bf16[4,2,96,1536]{3,2,1,0:T(8,128)(2,1)} %shard_map.198), channel_id=1, source_target_pairs={{0,4},{4,0},{8,12},{12,8},{16,20},{20,16},{24,28},{28,24},{1,5},{5... | collective-permute-start | bytes 7077896 | tf_op jit(solution)/shard_map/ppermute | solution.py:812
  147.2 32.9 %copy-start.53 = (bf16[896,128]{1,0:T(8,128)(2,1)S(1)}, bf16[896,128]{1,0:T(8,128)(2,1)}, u32[]{:S(2)}) copy-start(bf16[896,128]{1,0:T(8,128)(2,1)} %copy-done.52) | copy-start | bytes 688132
  157.9 18.7 %collective-permute-start.10 = (bf16[896,128]{1,0:T(8,128)(2,1)S(1)}, bf16[896,128]{1,0:T(8,128)(2,1)S(1)}, u32[]{:S(2)}, u32[]{:S(2)}) collective-permute-start(bf16[896,128]{1,0:T(8,128)(2,1)S(1)} %get-tuple-element.117), channel_id=1, source_target_pairs={{2,0},{3,1},{6,4},{7,5},{10,8},{11,9},{14,12},{15,13},{18,16},{19,... | collective-permute-start | bytes 688136 | tf_op jit(solution)/shard_map/ppermute | solution.py:862
  159.2 17.5 %collective-permute-start.11 = (bf16[896,128]{1,0:T(8,128)(2,1)S(1)}, bf16[896,128]{1,0:T(8,128)(2,1)S(1)}, u32[]{:S(2)}, u32[]{:S(2)}) collective-permute-start(bf16[896,128]{1,0:T(8,128)(2,1)S(1)} %get-tuple-element.117), channel_id=1, source_target_pairs={{3,0},{7,4},{11,8},{15,12},{19,16},{23,20},{27,24},{31,28}} | collective-permute-start | bytes 688136 | tf_op jit(solution)/shard_map/ppermute | solution.py:862
  160.5 19.6 %collective-permute-start.9 = (bf16[896,128]{1,0:T(8,128)(2,1)S(1)}, bf16[896,128]{1,0:T(8,128)(2,1)S(1)}, u32[]{:S(2)}, u32[]{:S(2)}) collective-permute-start(bf16[896,128]{1,0:T(8,128)(2,1)S(1)} %get-tuple-element.117), channel_id=1, source_target_pairs={{1,0},{2,1},{3,2},{5,4},{6,5},{7,6},{9,8},{10,9},{11,10},{13,12},{... | collective-permute-start | bytes 688136 | tf_op jit(solution)/shard_map/ppermute | solution.py:862
  180.1 10.1 %copy-start.21 = (bf16[768,256]{1,0:T(8,128)(2,1)S(1)}, bf16[768,256]{1,0:T(8,128)(2,1)}, u32[]{:S(2)}) copy-start(bf16[768,256]{1,0:T(8,128)(2,1)} %copy-done.20) | copy-start | bytes 1179652
  180.1 10.1 %copy-start.24 = (bf16[768,256]{1,0:T(8,128)(2,1)S(1)}, bf16[768,256]{1,0:T(8,128)(2,1)}, u32[]{:S(2)}) copy-start(bf16[768,256]{1,0:T(8,128)(2,1)} %copy-done.23) | copy-start | bytes 1179652
  191.6 21.7 %copy-start.5 = (bf16[256,3072]{1,0:T(8,128)(2,1)S(1)}, bf16[256,3072]{1,0:T(8,128)(2,1)}, u32[]{:S(2)}) copy-start(bf16[256,3072]{1,0:T(8,128)(2,1)} %get-tuple-element.149.hid) | copy-start | bytes 4718596
  191.6 21.7 %copy-start.6 = (bf16[256,3072]{1,0:T(8,128)(2,1)S(1)}, bf16[256,3072]{1,0:T(8,128)(2,1)}, u32[]{:S(2)}) copy-start(bf16[256,3072]{1,0:T(8,128)(2,1)} %get-tuple-element.147.gpre) | copy-start | bytes 4718596
  195.2 42.6 %collective-permute-start.12 = (bf16[4,2,96,1536]{3,2,1,0:T(8,128)(2,1)}, bf16[4,2,96,1536]{3,2,1,0:T(8,128)(2,1)}, u32[]{:S(2)}, u32[]{:S(2)}) collective-permute-start(bf16[4,2,96,1536]{3,2,1,0:T(8,128)(2,1)} %shard_map.196), channel_id=1, source_target_pairs={{0,4},{4,0},{8,12},{12,8},{16,20},{20,16},{24,28},{28,24},{1,5},{5... | collective-permute-start | bytes 7077896 | tf_op jit(solution)/shard_map/ppermute | solution.py:812
  195.3 4.2 %collective-permute-start.40 = (f32[2,13,768]{2,1,0:T(8,128)S(1)}, f32[2,13,768]{2,1,0:T(8,128)S(1)}, u32[]{:S(2)}, u32[]{:S(2)}) collective-permute-start(f32[2,13,768]{2,1,0:T(8,128)S(1)} %pad_maximum_fusion.13), channel_id=1, source_target_pairs={{0,4},{4,0},{8,12},{12,8},{16,20},{20,16},{24,28},{28,24},{1,5},{5... | collective-permute-start | bytes 239624 | tf_op jit(solution)/shard_map/ppermute | solution.py:812
  199.6 5.1 %collective-permute-start.41 = (f32[2,13,768]{2,1,0:T(8,128)S(1)}, f32[2,13,768]{2,1,0:T(8,128)S(1)}, u32[]{:S(2)}, u32[]{:S(2)}) collective-permute-start(f32[2,13,768]{2,1,0:T(8,128)S(1)} %fusion.35), channel_id=1, source_target_pairs={{0,8},{4,12},{8,0},{12,4},{16,24},{20,28},{24,16},{28,20},{1,9},{5... | collective-permute-start | bytes 239624 | tf_op jit(solution)/shard_map/ppermute | solution.py:812
  205.4 4.9 %collective-permute-start.42 = (f32[2,13,768]{2,1,0:T(8,128)}, f32[2,13,768]{2,1,0:T(8,128)}, u32[]{:S(2)}, u32[]{:S(2)}) collective-permute-start(f32[2,13,768]{2,1,0:T(8,128)} %fusion.47), channel_id=1, source_target_pairs={{0,16},{4,20},{8,24},{12,28},{16,0},{20,4},{24,8},{28,12},{1,17},{... | collective-permute-start | bytes 239624 | tf_op jit(solution)/shard_map/ppermute | solution.py:812
  211.3 8.8 %collective-permute-start.43 = (f32[2,13,768]{2,1,0:T(8,128)S(1)}, f32[2,13,768]{2,1,0:T(8,128)S(1)}, u32[]{:S(2)}, u32[]{:S(2)}) collective-permute-start(f32[2,13,768]{2,1,0:T(8,128)S(1)} %add.242), channel_id=1, source_target_pairs={{0,1},{1,0},{2,3},{3,2},{4,5},{5,4},{6,7},{7,6},{8,9},{9,8},{10,11... | collective-permute-start | bytes 239624 | tf_op jit(solution)/shard_map/ppermute | solution.py:817
  220.0 68.8 %collective-permute-start.33 = (bf16[4,2,384,768]{3,2,1,0:T(8,128)(2,1)}, bf16[4,2,384,768]{3,2,1,0:T(8,128)(2,1)}, u32[]{:S(2)}, u32[]{:S(2)}) collective-permute-start(bf16[4,2,384,768]{3,2,1,0:T(8,128)(2,1)} %shard_map.202), channel_id=1, source_target_pairs={{0,4},{4,0},{8,12},{12,8},{16,20},{20,16},{24,28},{28,24},{1,5},{5... | collective-permute-start | bytes 14155784 | tf_op jit(solution)/shard_map/ppermute | solution.py:812
  220.1 7.7 %collective-permute-start.44 = (f32[2,13,768]{2,1,0:T(8,128)S(1)}, f32[2,13,768]{2,1,0:T(8,128)S(1)}, u32[]{:S(2)}, u32[]{:S(2)}) collective-permute-start(f32[2,13,768]{2,1,0:T(8,128)S(1)} %add.243), channel_id=1, source_target_pairs={{0,2},{1,3},{2,0},{3,1},{4,6},{5,7},{6,4},{7,5},{8,10},{9,11},{10,... | collective-permute-start | bytes 239624 | tf_op jit(solution)/shard_map/ppermute | solution.py:817
  220.2 7.7 %copy-start.1 = (bf16[2,256,1536]{2,1,0:T(8,128)(2,1)S(1)}, bf16[2,256,1536]{2,1,0:T(8,128)(2,1)}, u32[]{:S(2)}) copy-start(bf16[2,256,1536]{2,1,0:T(8,128)(2,1)} %get-tuple-element.133.gcol) | copy-start | bytes 4718596
  220.2 7.7 %copy-start.27 = (bf16[768,256]{1,0:T(8,128)(2,1)S(1)}, bf16[768,256]{1,0:T(8,128)(2,1)}, u32[]{:S(2)}) copy-start(bf16[768,256]{1,0:T(8,128)(2,1)} %copy-done.26) | copy-start | bytes 1179652
  224.8 72.8 %collective-permute-start.26 = (bf16[4,2,384,768]{3,2,1,0:T(8,128)(2,1)}, bf16[4,2,384,768]{3,2,1,0:T(8,128)(2,1)S(1)}, u32[]{:S(2)}, u32[]{:S(2)}) collective-permute-start(bf16[4,2,384,768]{3,2,1,0:T(8,128)(2,1)} %shard_map.200), channel_id=1, source_target_pairs={{0,4},{4,0},{8,12},{12,8},{16,20},{20,16},{24,28},{28,24},{1,5},{5... | collective-permute-start | bytes 14155784 | tf_op jit(solution)/shard_map/ppermute | solution.py:812
  227.8 10.0 %copy-start.22 = (bf16[768,256]{1,0:T(8,128)(2,1)S(1)}, bf16[768,256]{1,0:T(8,128)(2,1)}, u32[]{:S(2)}) copy-start(bf16[768,256]{1,0:T(8,128)(2,1)} %copy-done.20) | copy-start | bytes 1179652
  227.8 10.0 %copy-start.25 = (bf16[768,256]{1,0:T(8,128)(2,1)S(1)}, bf16[768,256]{1,0:T(8,128)(2,1)}, u32[]{:S(2)}) copy-start(bf16[768,256]{1,0:T(8,128)(2,1)} %copy-done.23) | copy-start | bytes 1179652
  227.9 10.0 %copy-start.3 = (bf16[2,256,1536]{2,1,0:T(8,128)(2,1)S(1)}, bf16[2,256,1536]{2,1,0:T(8,128)(2,1)}, u32[]{:S(2)}) copy-start(bf16[2,256,1536]{2,1,0:T(8,128)(2,1)} %get-tuple-element.126.gcol) | copy-start | bytes 4718596
  232.1 16.2 %collective-permute-start.20 = (bf16[2,2,48,1536]{3,2,1,0:T(8,128)(2,1)S(1)}, bf16[2,2,48,1536]{3,2,1,0:T(8,128)(2,1)S(1)}, u32[]{:S(2)}, u32[]{:S(2)}) collective-permute-start(bf16[2,2,48,1536]{3,2,1,0:T(8,128)(2,1)S(1)} %get-tuple-element.135), channel_id=1, source_target_pairs={{0,8},{4,12},{8,0},{12,4},{16,24},{20,28},{24,16},{28,20},{1,9},{5... | collective-permute-start | bytes 1769480 | tf_op jit(solution)/shard_map/ppermute | solution.py:812
  235.7 16.2 %collective-permute-start.22 = (bf16[2,2,48,1536]{3,2,1,0:T(8,128)(2,1)S(1)}, bf16[2,2,48,1536]{3,2,1,0:T(8,128)(2,1)S(1)}, u32[]{:S(2)}, u32[]{:S(2)}) collective-permute-start(bf16[2,2,48,1536]{3,2,1,0:T(8,128)(2,1)S(1)} %get-tuple-element.137), channel_id=1, source_target_pairs={{0,16},{4,20},{8,24},{12,28},{16,0},{20,4},{24,8},{28,12},{1,17},{... | collective-permute-start | bytes 1769480 | tf_op jit(solution)/shard_map/ppermute | solution.py:812
  242.0 18.1 %collective-permute-start.13 = (bf16[2,2,48,1536]{3,2,1,0:T(8,128)(2,1)S(1)}, bf16[2,2,48,1536]{3,2,1,0:T(8,128)(2,1)S(1)}, u32[]{:S(2)}, u32[]{:S(2)}) collective-permute-start(bf16[2,2,48,1536]{3,2,1,0:T(8,128)(2,1)S(1)} %get-tuple-element.128), channel_id=1, source_target_pairs={{0,8},{4,12},{8,0},{12,4},{16,24},{20,28},{24,16},{28,20},{1,9},{5... | collective-permute-start | bytes 1769480 | tf_op jit(solution)/shard_map/ppermute | solution.py:812
  248.4 16.3 %collective-permute-start.15 = (bf16[2,2,48,1536]{3,2,1,0:T(8,128)(2,1)S(1)}, bf16[2,2,48,1536]{3,2,1,0:T(8,128)(2,1)S(1)}, u32[]{:S(2)}, u32[]{:S(2)}) collective-permute-start(bf16[2,2,48,1536]{3,2,1,0:T(8,128)(2,1)S(1)} %get-tuple-element.130), channel_id=1, source_target_pairs={{0,16},{4,20},{8,24},{12,28},{16,0},{20,4},{24,8},{28,12},{1,17},{... | collective-permute-start | bytes 1769480 | tf_op jit(solution)/shard_map/ppermute | solution.py:812
  251.9 19.1 %collective-permute-start.21 = (bf16[2,48,1536]{2,1,0:T(8,128)(2,1)S(1)}, bf16[2,48,1536]{2,1,0:T(8,128)(2,1)S(1)}, u32[]{:S(2)}, u32[]{:S(2)}) collective-permute-start(bf16[2,48,1536]{2,1,0:T(8,128)(2,1)S(1)} %fusion.24), channel_id=1, source_target_pairs={{0,16},{4,20},{8,24},{12,28},{16,0},{20,4},{24,8},{28,12},{1,17},{... | collective-permute-start | bytes 884744 | tf_op jit(solution)/shard_map/ppermute | solution.py:812
  260.1 12.4 %collective-permute-start.23 = (bf16[2,48,1536]{2,1,0:T(8,128)(2,1)S(1)}, bf16[2,48,1536]{2,1,0:T(8,128)(2,1)S(1)}, u32[]{:S(2)}, u32[]{:S(2)}) collective-permute-start(bf16[2,48,1536]{2,1,0:T(8,128)(2,1)S(1)} %fusion.25), channel_id=1, source_target_pairs={{0,8},{4,12},{8,0},{12,4},{16,24},{20,28},{24,16},{28,20},{1,9},{5... | collective-permute-start | bytes 884744 | tf_op jit(solution)/shard_map/ppermute | solution.py:812
  264.6 11.3 %collective-permute-start.14 = (bf16[2,48,1536]{2,1,0:T(8,128)(2,1)S(1)}, bf16[2,48,1536]{2,1,0:T(8,128)(2,1)S(1)}, u32[]{:S(2)}, u32[]{:S(2)}) collective-permute-start(bf16[2,48,1536]{2,1,0:T(8,128)(2,1)S(1)} %fusion.22), channel_id=1, source_target_pairs={{0,16},{4,20},{8,24},{12,28},{16,0},{20,4},{24,8},{28,12},{1,17},{... | collective-permute-start | bytes 884744 | tf_op jit(solution)/shard_map/ppermute | solution.py:812
  270.9 6.7 %collective-permute-start.16 = (bf16[2,48,1536]{2,1,0:T(8,128)(2,1)S(1)}, bf16[2,48,1536]{2,1,0:T(8,128)(2,1)S(1)}, u32[]{:S(2)}, u32[]{:S(2)}) collective-permute-start(bf16[2,48,1536]{2,1,0:T(8,128)(2,1)S(1)} %fusion.23), channel_id=1, source_target_pairs={{0,8},{4,12},{8,0},{12,4},{16,24},{20,28},{24,16},{28,20},{1,9},{5... | collective-permute-start | bytes 884744 | tf_op jit(solution)/shard_map/ppermute | solution.py:812
  272.7 9.3 %collective-permute-start.24 = (bf16[96,1536]{1,0:T(8,128)(2,1)S(1)}, bf16[96,1536]{1,0:T(8,128)(2,1)S(1)}, u32[]{:S(2)}, u32[]{:S(2)}) collective-permute-start(bf16[96,1536]{1,0:T(8,128)(2,1)S(1)} %fusion.27), channel_id=1, source_target_pairs={{0,1},{1,0},{2,3},{3,2},{4,5},{5,4},{6,7},{7,6},{8,9},{9,8},{10,11... | collective-permute-start | bytes 884744 | tf_op jit(solution)/shard_map/ppermute | solution.py:817
  282.4 6.2 %collective-permute-start.25 = (bf16[96,768]{1,0:T(8,128)(2,1)S(1)}, bf16[96,768]{1,0:T(8,128)(2,1)S(1)}, u32[]{:S(2)}, u32[]{:S(2)}) collective-permute-start(bf16[96,768]{1,0:T(8,128)(2,1)S(1)} %pad_maximum_fusion.11), channel_id=1, source_target_pairs={{0,2},{1,3},{2,0},{3,1},{4,6},{5,7},{6,4},{7,5},{8,10},{9,11},{10,... | collective-permute-start | bytes 442376 | tf_op jit(solution)/shard_map/ppermute | solution.py:817
  282.5 13.0 %collective-permute-start.17 = (bf16[96,1536]{1,0:T(8,128)(2,1)S(1)}, bf16[96,1536]{1,0:T(8,128)(2,1)S(1)}, u32[]{:S(2)}, u32[]{:S(2)}) collective-permute-start(bf16[96,1536]{1,0:T(8,128)(2,1)S(1)} %fusion.26), channel_id=1, source_target_pairs={{0,1},{1,0},{2,3},{3,2},{4,5},{5,4},{6,7},{7,6},{8,9},{9,8},{10,11... | collective-permute-start | bytes 884744 | tf_op jit(solution)/shard_map/ppermute | solution.py:817
  295.4 29.1 %collective-permute-start.34 = (bf16[2,2,192,768]{3,2,1,0:T(8,128)(2,1)S(1)}, bf16[2,2,192,768]{3,2,1,0:T(8,128)(2,1)}, u32[]{:S(2)}, u32[]{:S(2)}) collective-permute-start(bf16[2,2,192,768]{3,2,1,0:T(8,128)(2,1)S(1)} %get-tuple-element.151), channel_id=1, source_target_pairs={{0,8},{4,12},{8,0},{12,4},{16,24},{20,28},{24,16},{28,20},{1,9},{5... | collective-permute-start | bytes 3538952 | tf_op jit(solution)/shard_map/ppermute | solution.py:812
  295.9 12.5 %collective-permute-start.18 = (bf16[96,768]{1,0:T(8,128)(2,1)S(1)}, bf16[96,768]{1,0:T(8,128)(2,1)S(1)}, u32[]{:S(2)}, u32[]{:S(2)}) collective-permute-start(bf16[96,768]{1,0:T(8,128)(2,1)S(1)} %pad_maximum_fusion.10), channel_id=1, source_target_pairs={{0,2},{1,3},{2,0},{3,1},{4,6},{5,7},{6,4},{7,5},{8,10},{9,11},{10,... | collective-permute-start | bytes 442376 | tf_op jit(solution)/shard_map/ppermute | solution.py:817
  296.0 31.3 %collective-permute-start.36 = (bf16[2,2,192,768]{3,2,1,0:T(8,128)(2,1)S(1)}, bf16[2,2,192,768]{3,2,1,0:T(8,128)(2,1)}, u32[]{:S(2)}, u32[]{:S(2)}) collective-permute-start(bf16[2,2,192,768]{3,2,1,0:T(8,128)(2,1)S(1)} %get-tuple-element.153), channel_id=1, source_target_pairs={{0,16},{4,20},{8,24},{12,28},{16,0},{20,4},{24,8},{28,12},{1,17},{... | collective-permute-start | bytes 3538952 | tf_op jit(solution)/shard_map/ppermute | solution.py:812
  306.3 43.4 %collective-permute-start.27 = (bf16[2,2,192,768]{3,2,1,0:T(8,128)(2,1)S(1)}, bf16[2,2,192,768]{3,2,1,0:T(8,128)(2,1)S(1)}, u32[]{:S(2)}, u32[]{:S(2)}) collective-permute-start(bf16[2,2,192,768]{3,2,1,0:T(8,128)(2,1)S(1)} %get-tuple-element.143), channel_id=1, source_target_pairs={{0,8},{4,12},{8,0},{12,4},{16,24},{20,28},{24,16},{28,20},{1,9},{5... | collective-permute-start | bytes 3538952 | tf_op jit(solution)/shard_map/ppermute | solution.py:812
  308.5 42.9 %collective-permute-start.29 = (bf16[2,2,192,768]{3,2,1,0:T(8,128)(2,1)S(1)}, bf16[2,2,192,768]{3,2,1,0:T(8,128)(2,1)S(1)}, u32[]{:S(2)}, u32[]{:S(2)}) collective-permute-start(bf16[2,2,192,768]{3,2,1,0:T(8,128)(2,1)S(1)} %get-tuple-element.145), channel_id=1, source_target_pairs={{0,16},{4,20},{8,24},{12,28},{16,0},{20,4},{24,8},{28,12},{1,17},{... | collective-permute-start | bytes 3538952 | tf_op jit(solution)/shard_map/ppermute | solution.py:812
  325.7 36.7 %collective-permute-start.35 = (bf16[2,192,768]{2,1,0:T(8,128)(2,1)S(1)}, bf16[2,192,768]{2,1,0:T(8,128)(2,1)S(1)}, u32[]{:S(2)}, u32[]{:S(2)}) collective-permute-start(bf16[2,192,768]{2,1,0:T(8,128)(2,1)S(1)} %fusion.10), channel_id=1, source_target_pairs={{0,16},{4,20},{8,24},{12,28},{16,0},{20,4},{24,8},{28,12},{1,17},{... | collective-permute-start | bytes 1769480 | tf_op jit(solution)/shard_map/ppermute | solution.py:812
  328.5 35.2 %collective-permute-start.37 = (bf16[2,192,768]{2,1,0:T(8,128)(2,1)S(1)}, bf16[2,192,768]{2,1,0:T(8,128)(2,1)S(1)}, u32[]{:S(2)}, u32[]{:S(2)}) collective-permute-start(bf16[2,192,768]{2,1,0:T(8,128)(2,1)S(1)} %fusion.11), channel_id=1, source_target_pairs={{0,8},{4,12},{8,0},{12,4},{16,24},{20,28},{24,16},{28,20},{1,9},{5... | collective-permute-start | bytes 1769480 | tf_op jit(solution)/shard_map/ppermute | solution.py:812
  349.8 18.9 %collective-permute-start.28 = (bf16[2,192,768]{2,1,0:T(8,128)(2,1)S(1)}, bf16[2,192,768]{2,1,0:T(8,128)(2,1)S(1)}, u32[]{:S(2)}, u32[]{:S(2)}) collective-permute-start(bf16[2,192,768]{2,1,0:T(8,128)(2,1)S(1)} %fusion.8), channel_id=1, source_target_pairs={{0,16},{4,20},{8,24},{12,28},{16,0},{20,4},{24,8},{28,12},{1,17},{... | collective-permute-start | bytes 1769480 | tf_op jit(solution)/shard_map/ppermute | solution.py:812
  351.5 17.4 %collective-permute-start.30 = (bf16[2,192,768]{2,1,0:T(8,128)(2,1)S(1)}, bf16[2,192,768]{2,1,0:T(8,128)(2,1)S(1)}, u32[]{:S(2)}, u32[]{:S(2)}) collective-permute-start(bf16[2,192,768]{2,1,0:T(8,128)(2,1)S(1)} %fusion.9), channel_id=1, source_target_pairs={{0,8},{4,12},{8,0},{12,4},{16,24},{20,28},{24,16},{28,20},{1,9},{5... | collective-permute-start | bytes 1769480 | tf_op jit(solution)/shard_map/ppermute | solution.py:812
  365.0 16.0 %collective-permute-start.38 = (bf16[384,768]{1,0:T(8,128)(2,1)S(1)}, bf16[384,768]{1,0:T(8,128)(2,1)S(1)}, u32[]{:S(2)}, u32[]{:S(2)}) collective-permute-start(bf16[384,768]{1,0:T(8,128)(2,1)S(1)} %fusion.19), channel_id=1, source_target_pairs={{0,1},{1,0},{2,3},{3,2},{4,5},{5,4},{6,7},{7,6},{8,9},{9,8},{10,11... | collective-permute-start | bytes 1769480 | tf_op jit(solution)/shard_map/ppermute | solution.py:817
  369.2 24.4 %collective-permute-start.31 = (bf16[384,768]{1,0:T(8,128)(2,1)S(1)}, bf16[384,768]{1,0:T(8,128)(2,1)S(1)}, u32[]{:S(2)}, u32[]{:S(2)}) collective-permute-start(bf16[384,768]{1,0:T(8,128)(2,1)S(1)} %fusion.18), channel_id=1, source_target_pairs={{0,1},{1,0},{2,3},{3,2},{4,5},{5,4},{6,7},{7,6},{8,9},{9,8},{10,11... | collective-permute-start | bytes 1769480 | tf_op jit(solution)/shard_map/ppermute | solution.py:817
  381.2 12.7 %collective-permute-start.39 = (bf16[384,384]{1,0:T(8,128)(2,1)S(1)}, bf16[384,384]{1,0:T(8,128)(2,1)S(1)}, u32[]{:S(2)}, u32[]{:S(2)}) collective-permute-start(bf16[384,384]{1,0:T(8,128)(2,1)S(1)} %pad_maximum_fusion.8), channel_id=1, source_target_pairs={{0,2},{1,3},{2,0},{3,1},{4,6},{5,7},{6,4},{7,5},{8,10},{9,11},{10,... | collective-permute-start | bytes 884744 | tf_op jit(solution)/shard_map/ppermute | solution.py:817
  393.9 9.8 %collective-permute-start.32 = (bf16[384,384]{1,0:T(8,128)(2,1)S(1)}, bf16[384,384]{1,0:T(8,128)(2,1)S(1)}, u32[]{:S(2)}, u32[]{:S(2)}) collective-permute-start(bf16[384,384]{1,0:T(8,128)(2,1)S(1)} %pad_maximum_fusion.7), channel_id=1, source_target_pairs={{0,2},{1,3},{2,0},{3,1},{4,6},{5,7},{6,4},{7,5},{8,10},{9,11},{10,... | collective-permute-start | bytes 884744 | tf_op jit(solution)/shard_map/ppermute | solution.py:817
  (51 other events, 118.7 us)

commit v2 on v0

v2 whole, which is shorter than its diff:
```python
import math

import jax
import jax.numpy as jnp
from jax import lax
from jax.experimental import pallas as pl
from jax.experimental.pallas import tpu as pltpu
from jax.sharding import PartitionSpec as P

D = 768
HEADS = 12
HEAD_DIM = 64
FF = 3072
LAYERS = 2
PAIRS = HEADS // 2
NORM_EPS = 1e-05
LANES = 128
STATE_ROWS = PAIRS * LANES + 16

BF = jnp.bfloat16
F32 = jnp.float32


def nn(a, b):
    return lax.dot_general(a, b, (((1,), (0,)), ((), ())), preferred_element_type=F32)


def nt(a, b):
    return lax.dot_general(a, b, (((1,), (1,)), ((), ())), preferred_element_type=F32)


def tn(a, b):
    return lax.dot_general(a, b, (((0,), (0,)), ((), ())), preferred_element_type=F32)


def low(v):
    return v.astype(BF)


def up(v):
    return v.astype(F32)


def beside(a, b):
    return jnp.concatenate([a, b], axis=1)


def above(a, b):
    return jnp.concatenate([a, b], axis=0)


def softplus(u):
    return jnp.maximum(u, 0.0) + jnp.log1p(jnp.exp(-jnp.abs(u)))


def sigmoid(u):
    return 1.0 / (1.0 + jnp.exp(-u))


def swap(v):
    return pltpu.roll(v, HEAD_DIM, 1)


def lane_of(rows):
    return lax.broadcasted_iota(jnp.int32, (rows, LANES), 1)


def row_mean(v):
    return jnp.mean(v, axis=-1, keepdims=True)


def norm_apply(total, gain, shift):
    centred = total - row_mean(total)
    scale = lax.rsqrt(row_mean(centred * centred) + NORM_EPS)
    normal = centred * scale
    return normal * gain + shift, normal, scale


def norm_back(upstream, normal, scale, gain):
    grad = upstream * gain
    return scale * (grad - row_mean(grad) - normal * row_mean(grad * normal))


def column_sum(v):
    return jnp.sum(v, axis=0, keepdims=True)


def shape(*dims, dtype=F32):
    return jax.ShapeDtypeStruct(dims, dtype)


class Box(dict):
    __getattr__ = dict.__getitem__
    __setattr__ = dict.__setitem__


class Refs:
    def __init__(self):
        self.refs = Box()
        self.copies = Box()
        self.flushes = Box()

    def __getitem__(self, name):
        for copy in self.copies.pop(name, []):
            if copy is not None:
                copy.wait()
        return self.refs[name]

    def __getattr__(self, name):
        return self[name]

    def part(self, name, at):
        copies = self.copies.get(name)
        if copies and copies[at] is not None:
            copies[at].wait()
            copies[at] = None
        return self.refs[name].at[at]

    def done(self, name):
        if name in self.flushes:
            self.flushes[name].start()


def in_hbm(array):
    return pltpu.with_memory_space_constraint(array, pltpu.HBM)


def in_vmem(array):
    return pltpu.with_memory_space_constraint(array, pltpu.VMEM)


def whole_cut(ref):
    return ref


def run(body, ins, outs, deps=(), scratch=None, limit=20, flops=0, nbytes=0):
    scratch = scratch or Box()
    in_names = list(ins)
    out_names = list(outs)
    operands, in_specs, out_shapes, out_specs, scratch_shapes = [], [], [], [], []
    vmem = pl.BlockSpec(memory_space=pltpu.VMEM)
    hbm = pl.BlockSpec(memory_space=pltpu.HBM)
    smem = pl.BlockSpec(memory_space=pltpu.SMEM)
    for name in in_names:
        mode, array = ins[name][:2]
        operands.append(Box(d=in_hbm, v=in_vmem).get(mode, whole_cut)(array))
        in_specs.append(Box(v=vmem, s=smem, d=hbm)[mode])
    fetch_names = [name for name in out_names if outs[name][0] == "f"]
    for name in fetch_names:
        operands.append(in_hbm(outs[name][1]))
        in_specs.append(hbm)
    for dep in deps:
        operands.append(in_vmem(dep))
        in_specs.append(vmem)
    copy_count = 0
    plan = []
    for name in in_names:
        if ins[name][0] == "d":
            array = ins[name][1]
            cuts, block = ins[name][2] if len(ins[name]) > 2 else (None, array.shape)
            scratch_shapes.append(
                pltpu.VMEM(block if cuts is None else (len(cuts),) + block, array.dtype)
            )
            plan.append((name, cuts))
            copy_count += 1 if cuts is None else len(cuts)
    for name in out_names:
        mode = outs[name][0]
        if mode == "f":
            array, cuts, block = outs[name][1:]
            out_shapes.append(pltpu.VMEM((len(cuts),) + block, array.dtype))
            copy_count += len(cuts)
        else:
            given = outs[name][1]
            space = pltpu.HBM if mode == "h" else pltpu.VMEM
            out_shapes.append(space(given.shape, given.dtype))
            if mode == "h":
                scratch_shapes.append(pltpu.VMEM(outs[name][1].shape, outs[name][1].dtype))
                copy_count += 1
        out_specs.append(hbm if mode == "h" else vmem)
    out_shapes.append(pltpu.VMEM((8, LANES), F32))
    out_specs.append(vmem)
    for spec in scratch.values():
        scratch_shapes.append(spec)
    scratch_shapes.append(pltpu.SemaphoreType.DMA((max(copy_count, 1),)))

    def kernel(*refs):
        refs = list(refs)
        sems = refs.pop()
        used = [0]

        def make(source, target):
            copy = pltpu.make_async_copy(source, target, sems.at[used[0]])
            used[0] += 1
            return copy

        n_in, n_fetch, n_out = len(in_names), len(fetch_names), len(out_names)
        in_refs = dict(zip(in_names, refs[:n_in]))
        fetch_refs = dict(zip(fetch_names, refs[n_in : n_in + n_fetch]))
        rest = refs[n_in + n_fetch + len(deps) :]
        out_refs = dict(zip(out_names, rest[:n_out]))
        token = rest[n_out]
        spare = rest[n_out + 1 :]
        io = Refs()
        for name in in_names:
            io.refs[name] = in_refs[name]
        for name, cuts in plan:
            buffer = spare.pop(0)
            io.refs[name] = buffer
            if cuts is None:
                io.copies[name] = [make(in_refs[name], buffer)]
            else:
                io.copies[name] = [
                    make(cut(in_refs[name]), buffer.at[at]) for at, cut in enumerate(cuts)
                ]
            for copy in io.copies[name]:
                copy.start()
        fetches = []
        for name in out_names:
            mode = outs[name][0]
            if mode == "f":
                for at, cut in enumerate(outs[name][2]):
                    fetches.append(make(cut(fetch_refs[name]), out_refs[name].at[at]))
                io.refs[name] = out_refs[name]
            elif mode == "h":
                buffer = spare.pop(0)
                io.refs[name] = buffer
                io.flushes[name] = make(buffer, out_refs[name])
            else:
                io.refs[name] = out_refs[name]
        for name in scratch:
            io.refs[name] = spare.pop(0)
        for copy in fetches:
            copy.start()
        token[...] = jnp.zeros(token.shape, F32)
        body(io)
        for name in list(io.copies):
            io[name]
        for copy in fetches:
            copy.wait()
        for copy in io.flushes.values():
            copy.wait()

    cost = COSTS[min(Counter.at, len(COSTS) - 1)]
    Counter.at += 1
    results = pl.pallas_call(
        kernel,
        out_shape=tuple(out_shapes),
        in_specs=in_specs,
        out_specs=tuple(out_specs),
        scratch_shapes=scratch_shapes,
        compiler_params=pltpu.CompilerParams(vmem_limit_bytes=limit * 1024 * 1024),
        cost_estimate=pl.CostEstimate(
            flops=int(cost * 10**9), bytes_accessed=10**8, transcendentals=0
        ),
    )(*operands)
    return Box(zip(out_names, results)), results[-1]


def columns_of(layer, parts):
    return [lambda ref, j=j: ref.at[layer, :, pl.ds(D * j, D)] for j in range(parts)], (D, D)


def rows_of(layer, parts):
    return [lambda ref, j=j: ref.at[layer, pl.ds(D * j, D), :] for j in range(parts)], (D, D)


def layer_of(layer, block):
    return [lambda ref: ref.at[layer]], block


COSTS = [120, 10, 15, 60, 0.3, 30, 30, 120, 0.3, 0.3, 1, 30, 120, 3, 10, 6, 15, 6, 1, 6, 3, 0.3, 22, 30, 22, 22, 3, 6, 22, 10, 120, 3, 10, 0.3, 3, 10, 120, 3, 10, 60, 0.3, 30, 0.3]


class Counter:
    at = 0


def project(layer, x, x_mode, wq, vecs, cs, long, deps):
    rows = x.shape[0]

    def body(io):
        x_in = up(io.x[...])
        xb = low(x_in)
        io.xt[...] = low(x_in.T)
        io.done("xt")
        lane = lane_of(rows)
        lo = lane < HEAD_DIM
        lane_state = lane_of(LANES)
        lo_state = lane_state < HEAD_DIM
        totals = jnp.zeros((LANES, LANES), F32)
        for j in range(3):
            w = io.part("wq", j)
            bias = vector(io, "qkv_bias", layer)[:, D * j : D * (j + 1)]
            pk = low(nn(xb, w[...]) + bias)
            io.packed[:, D * j : D * (j + 1)] = pk
            if long:
                io.kept[:, D * j : D * (j + 1)] = pk
            pf = up(pk)
            cs_now = io.cs[...]
            for p in range(2):
                t0, t1, t2 = (
                    pf[:, (3 * p + i) * LANES : (3 * p + i + 1) * LANES] for i in range(3)
                )
                sp0 = softplus(t0)
                sp2 = softplus(t2)
                kf0 = low(jnp.where(lo, swap(sp0), sp0) * cs_now)
                kf1 = low(jnp.where(lo, sp2, swap(sp2)) * cs_now)
                s0 = tn(kf0, low(jnp.where(lo, t1, 1.0)))
                s1 = tn(kf1, low(jnp.where(lo, 1.0, t2)))
                pair = 2 * j + p
                io.state[pair * LANES : (pair + 1) * LANES, :] = low(
                    jnp.where(lo_state, s0, s1)
                )
                totals = jnp.where(lane_state == 2 * pair, swap(s0), totals)
                totals = jnp.where(lane_state == 2 * pair + 1, s1, totals)
        io.state[PAIRS * LANES :, :] = low(totals.T[:16])
        if long:
            io.done("kept")

    outs = Box(
        packed=("v", shape(rows, 3 * D, dtype=BF)),
        xt=("h", shape(D, rows, dtype=BF)),
        state=("v", shape(STATE_ROWS, LANES, dtype=BF)),
    )
    if long:
        outs.kept = ("h", shape(rows, 3 * D, dtype=BF))
    return run(
        body,
        Box(x=(x_mode, x), wq=wq, cs=("d", cs), **vecs),
        outs,
        deps,
        flops=2 * rows * D * 3 * D,
        nbytes=2 * D * 3 * D,
    )


def inside(packed, cm, long, fetches, deps):
    rows = packed.shape[0]

    def body(io):
        lo = lane_of(rows) < HEAD_DIM
        for pair in range(PAIRS):
            at = pair * 3 * LANES
            t0, t1, t2 = (
                up(io.packed[:, at + i * LANES : at + (i + 1) * LANES]) for i in range(3)
            )
            sp0, sp1, sp2 = softplus(t0), softplus(t1), softplus(t2)
            a0 = nt(low(jnp.where(lo, sp0, 0.0)), low(swap(sp0)))
            a1 = nt(low(jnp.where(lo, 0.0, sp1)), low(swap(sp2)))
            mask = io.cm[...]
            n0 = nn(low(a0 * mask), low(jnp.where(lo, t1, 1.0)))
            n1 = nn(low(a1 * mask), low(jnp.where(lo, 1.0, t2)))
            here = slice(pair * LANES, (pair + 1) * LANES)
            io.num[:, here] = jnp.where(lo, n0, n1)
            io.den[:, here] = swap(jnp.where(lo, n1, n0))
            sq = low(jnp.where(lo, sp0, sp1))
            io.sq[:, here] = sq
            if long:
                io.sq_kept[:, here] = sq

    outs = Box(
        num=("v", shape(rows, D)),
        den=("v", shape(rows, D)),
        sq=("v", shape(rows, D, dtype=BF)),
    )
    if long:
        outs.sq_kept = ("h", shape(rows, D, dtype=BF))

    def body_all(io):
        body(io)
        if long:
            io.done("sq_kept")

    outs.update(fetches)
    return run(
        body_all,
        Box(packed=("v", packed), cm=("d", cm)),
        outs,
        deps,
        flops=4 * HEADS * rows * rows * LANES,
        nbytes=rows * D * 16,
    )


def sum_states(io, count):
    total = up(io.recv0[...])
    for at in range(1, count):
        total = total + up(io["recv%d" % at][...])
    return total


def vector(io, name, layer):
    return up(io[name][...])[layer : layer + 1]


def state_totals(total):
    return jnp.concatenate(
        [total[PAIRS * LANES :], jnp.zeros((LANES - 16, LANES), F32)], axis=0
    ).T


def totals_column(totals, head):
    return jnp.broadcast_to(totals[:, head : head + 1], (LANES, LANES))


def diagonal(a, b):
    zero = jnp.zeros((LANES, LANES), BF)
    return above(beside(a, zero), beside(zero, b))


def second_norm_back(io, gs, n2, r2, gain):
    gz2 = norm_back(gs, n2, r2, gain)
    gb2 = low(gz2)
    io.gz2[...] = gz2
    io.gb2[...] = gb2
    io.gb2t[...] = low(gz2.T)
    io.sums_a[...] = jnp.zeros((8, D), F32)
    io.sums_a[0:1, :] = column_sum(up(gb2))
    io.sums_a[1:2, :] = column_sum(gs)
    io.sums_a[2:3, :] = column_sum(gs * n2)
    io.done("sums_a")


def second_norm_outs(rows):
    return Box(
        gz2=("v", shape(rows, D)),
        gb2=("v", shape(rows, D, dtype=BF)),
        gb2t=("v", shape(D, rows, dtype=BF)),
        sums_a=("h", shape(8, D)),
    )


def layer_forward(layer, recv, x, x_mode, inner, weights, vecs, cs, cotangent, deps):
    rows = x.shape[0]
    last = cotangent is not None

    def body(io):
        lane = lane_of(rows)
        lo = lane < HEAD_DIM
        lo_state = lane_of(LANES) < HEAD_DIM
        before = sum_states(io, len(recv))
        io.before[...] = low(before)
        io.done("before")
        totals = state_totals(before)
        for pair in range(PAIRS):
            here = slice(pair * LANES, (pair + 1) * LANES)
            sq = up(io.sq[:, here])
            other = swap(sq)
            state = before[here]
            cs_now = io.cs[...]
            feats = beside(
                low(jnp.where(lo, sq, other) * cs_now), low(jnp.where(lo, other, sq) * cs_now)
            )
            both = nn(
                feats,
                diagonal(
                    low(jnp.where(lo_state, state, totals_column(totals, 2 * pair))),
                    low(jnp.where(lo_state, totals_column(totals, 2 * pair + 1), state)),
                ),
            )
            n0 = both[:, :LANES]
            n1 = both[:, LANES:]
            num = io.num[:, here] + jnp.where(lo, n0, n1)
            inv = 1.0 / (io.den[:, here] + swap(jnp.where(lo, n1, n0)))
            mixed = num * inv
            io.inv[:, here] = inv
            io.mixed[:, here] = low(mixed)
            io.mixt[here, :] = low(mixed.T)
        io.done("inv")
        io.done("mixed")
        io.done("mixt")
        shifts = up(io.shifts[layer])
        gains = up(io.gains[layer])
        bias = vector(io, "ffn_bias", layer)
        branch = nn(io.mixed[...], io.part("wo", 0)[...]) + shifts[0:1]
        middle, n1, r1 = norm_apply(up(io.x[...]) + branch, gains[0:1], shifts[2:3])
        io.n1[...] = n1
        io.done("n1")
        io.r1[...] = jnp.broadcast_to(r1, (rows, LANES))
        io.done("r1")
        io.midt[...] = low(middle.T)
        io.done("midt")
        mid = low(middle)
        total = middle + shifts[1:2]
        for j in range(FF // D):
            here = slice(D * j, D * (j + 1))
            pre = nn(mid, io.part("w1", j)[...]) + bias[:, here]
            cdf = 0.5 * (1.0 + lax.erf(pre * (1.0 / math.sqrt(2.0))))
            hid = low(pre * cdf)
            io.hid[:, here] = hid
            io.slope[:, here] = low(
                cdf + pre * jnp.exp(-0.5 * pre * pre) * (1.0 / math.sqrt(2.0 * math.pi))
            )
            total = total + nn(hid, io.part("w2", j)[...])
        io.done("hid")
        io.done("slope")
        s_next, n2, r2 = norm_apply(total, gains[1:2], shifts[3:4])
        if last:
            io.output[...] = low(s_next)
            io.done("output")
            second_norm_back(io, up(io.cot[...]), n2, r2, gains[1:2])
        else:
            io.s_next[...] = s_next
            io.n2[...] = n2
            io.done("n2")
            io.r2[...] = jnp.broadcast_to(r2, (rows, LANES))
            io.done("r2")

    ins = Box({"recv%d" % i: ("v", recv[i]) for i in range(len(recv))})
    ins.update(
        Box(
            x=(x_mode, x),
            num=("v", inner.num),
            den=("v", inner.den),
            sq=("v", inner.sq),
            wo=("v", weights.wo),
            w1=("v", weights.w1),
            w2=("v", weights.w2),
            cs=("d", cs),
            **vecs,
        )
    )
    if last:
        ins.cot = ("d", cotangent)
    mode = "v" if last else "h"
    outs = Box(
        before=("h", shape(STATE_ROWS, LANES, dtype=BF)),
        mixed=(mode, shape(rows, D, dtype=BF)),
        mixt=("h", shape(D, rows, dtype=BF)),
        inv=(mode, shape(rows, D)),
        n1=(mode, shape(rows, D)),
        r1=(mode, shape(rows, LANES)),
        midt=(mode, shape(D, rows, dtype=BF)),
        hid=(mode, shape(rows, FF, dtype=BF)),
        slope=(mode, shape(rows, FF, dtype=BF)),
    )
    if last:
        outs.output = ("h", shape(rows, D, dtype=BF))
        outs.update(second_norm_outs(rows))
    else:
        outs.s_next = ("v", shape(rows, D))
        outs.n2 = ("h", shape(rows, D))
        outs.r2 = ("h", shape(rows, LANES))
    return run(
        body,
        ins,
        outs,
        deps,
        limit=20,
        flops=2 * rows * D * (D + 2 * FF),
        nbytes=2 * D * (D + 2 * FF),
    )


def layer_back(layer, top, kept, mode, weights, vecs, cs, fetches, deps):
    rows = top.gz2.shape[0]

    def body(io):
        lane = lane_of(rows)
        lo = lane < HEAD_DIM
        lane_state = lane_of(LANES)
        lo_state = lane_state < HEAD_DIM
        left_rows = lax.broadcasted_iota(jnp.int32, (LANES, LANES), 0) < HEAD_DIM
        same = low(jnp.where(lo_state == left_rows, 1.0, 0.0))
        gb2 = io.gb2[...]
        gmid = io.gz2[...]
        sums = io.sums_b
        sums[...] = jnp.zeros((8, D), F32)
        for j in range(FF // D):
            here = slice(D * j, D * (j + 1))
            gpre = low(nt(gb2, io.part("w2", j)[...]) * up(io.slope[:, here]))
            io.gpre[:, here] = gpre
            sums[j : j + 1, :] = column_sum(up(gpre))
            gmid = gmid + nt(gpre, io.part("w1", j)[...])
        n1 = io.n1[...]
        gz1 = norm_back(gmid, n1, io.r1[:, :1], up(io.gains[layer])[0:1])
        gb1 = low(gz1)
        io.gz1[...] = gz1
        io.gb1[...] = gb1
        sums[4:5, :] = column_sum(up(gb1))
        sums[5:6, :] = column_sum(gmid)
        sums[6:7, :] = column_sum(gmid * n1)
        io.done("sums_b")
        gmixed = up(low(nt(gb1, io.part("wo", 0)[...])))
        totals = jnp.zeros((LANES, LANES), F32)
        for pair in range(PAIRS):
            here = slice(pair * LANES, (pair + 1) * LANES)
            u = gmixed[:, here] * io.inv[:, here]
            dd = -nn(low(u * up(io.mixed[:, here])), same)
            io.u[:, here] = low(u)
            io.dd[:, here] = low(dd)
            ds = swap(dd)
            sq = up(io.sq[:, here])
            other = swap(sq)
            cs_now = io.cs[...]
            s0 = tn(low(jnp.where(lo, sq, other) * cs_now), low(jnp.where(lo, u, ds)))
            s1 = tn(low(jnp.where(lo, other, sq) * cs_now), low(jnp.where(lo, ds, u)))
            io.state[here, :] = low(jnp.where(lo_state, s0, s1))
            totals = jnp.where(lane_state == 2 * pair, swap(s0), totals)
            totals = jnp.where(lane_state == 2 * pair + 1, s1, totals)
        io.state[PAIRS * LANES :, :] = low(totals.T[:16])

    ins = Box(
        gz2=("v", top.gz2),
        gb2=("v", top.gb2),
        wo=("v", weights.wo),
        w1=("v", weights.w1),
        w2=("v", weights.w2),
    )
    for name in ("slope", "n1", "r1", "inv", "mixed", "sq"):
        ins[name] = (mode, kept[name])
    ins.gains = vecs.gains
    ins.cs = ("d", cs)
    outs = Box(
        gpre=("v", shape(rows, FF, dtype=BF)),
        gb1=("v", shape(rows, D, dtype=BF)),
        gz1=("v", shape(rows, D)),
        u=("v", shape(rows, D, dtype=BF)),
        dd=("v", shape(rows, D, dtype=BF)),
        state=("v", shape(STATE_ROWS, LANES, dtype=BF)),
        sums_b=("h", shape(8, D)),
    )
    outs.update(fetches)
    return run(
        body,
        ins,
        outs,
        deps,
        limit=20,
        flops=2 * rows * D * (D + 2 * FF),
        nbytes=2 * D * (D + 2 * FF),
    )


def mix_back(layer, recv, spot, low_part, kept, cs, cm, wq, below, fetches, deps):
    rows = low_part.u.shape[0]

    def body(io):
        lane = lane_of(rows)
        lo = lane < HEAD_DIM
        lane_state = lane_of(LANES)
        lo_state = lane_state < HEAD_DIM
        one_left = jnp.where(lane == 0, 1.0, 0.0)
        one_right = jnp.where(lane == HEAD_DIM, 1.0, 0.0)
        later = sum_states(io, len(recv))
        later_totals = state_totals(later)
        before = up(io.before[...])
        before_totals = state_totals(before)

        def halves(state, totals, pair):
            first = jnp.where(
                lo_state,
                state,
                jnp.where(lane_state == HEAD_DIM, totals_column(totals, 2 * pair), 0.0),
            )
            second = jnp.where(
                lo_state,
                jnp.where(lane_state == 0, totals_column(totals, 2 * pair + 1), 0.0),
                state,
            )
            return diagonal(low(first), low(second))

        def fold(v, cs_now):
            first = v[:, :LANES] * cs_now
            second = v[:, LANES:] * cs_now
            return jnp.where(lo, first + swap(first), second + swap(second))

        for pair in range(PAIRS):
            here = slice(pair * LANES, (pair + 1) * LANES)
            at = pair * 3 * LANES
            t0, t1, t2 = (
                up(io.packed[:, at + i * LANES : at + (i + 1) * LANES]) for i in range(3)
            )
            cs_now = io.cs[...]
            mask = io.cm[...]
            sp0, sp1, sp2 = softplus(t0), softplus(t1), softplus(t2)
            sw0 = swap(sp0)
            sw2 = swap(sp2)
            q0 = low(jnp.where(lo, sp0, 0.0))
            k0 = low(jnp.where(lo, sw0, 0.0))
            q1 = low(jnp.where(lo, 0.0, sp1))
            k1 = low(jnp.where(lo, 0.0, sw2))
            kf = beside(
                low(jnp.where(lo, sw0, sp0) * cs_now), low(jnp.where(lo, sp2, sw2) * cs_now)
            )
            v0 = low(jnp.where(lo, t1, one_right))
            v1 = low(jnp.where(lo, one_left, t2))
            uf = up(io.u[:, here])
            ds = swap(up(io.dd[:, here]))
            u0 = low(jnp.where(lo, uf, ds))
            u1 = low(jnp.where(lo, ds, uf))
            ua = low(jnp.where(lo, uf, 0.0))
            ub = low(jnp.where(lo, 0.0, uf))
            p0 = low(nt(q0, k0) * mask)
            p1 = low(nt(q1, k1) * mask)
            d0 = low(nt(u0, v0) * mask)
            d1 = low(nt(u1, v1) * mask)
            after = later[here]
            eq = nt(beside(u0, u1), halves(before[here], before_totals, pair))
            ek = nt(beside(v0, v1), halves(after, later_totals, pair))
            after_split = above(
                low(jnp.where(lo_state, after, 0.0)), low(jnp.where(lo_state, 0.0, after))
            )
            dq = fold(eq, cs_now) + nn(d0, k0) + nn(d1, k1)
            dk = fold(ek, cs_now) + tn(d0, q0) + tn(d1, q1)
            dv = nn(kf, after_split) + tn(p0, ua) + tn(p1, ub)
            dks = swap(dk)
            gpk = io.gpk
            gpk[:, at : at + LANES] = low(jnp.where(lo, dq, dks) * sigmoid(t0))
            gpk[:, at + LANES : at + 2 * LANES] = low(jnp.where(lo, dv, dq * sigmoid(t1)))
            gpk[:, at + 2 * LANES : at + 3 * LANES] = low(jnp.where(lo, dks * sigmoid(t2), dv))
        grad = io.gz1[...]
        io.sums_c[...] = jnp.zeros((8, D), F32)
        for j in range(3):
            gpk = io.gpk[:, D * j : D * (j + 1)]
            io.sums_c[j : j + 1, :] = column_sum(up(gpk))
            grad = grad + nt(gpk, io.part("wq", j)[...])
        io.done("sums_c")
        if below is None:
            io.grad[...] = grad
            io.done("grad")
        else:
            gain = up(io.gains[layer - 1])[1:2]
            second_norm_back(io, grad, io.n2[...], io.r2[:, :1], gain)
        near = io.spot[3]
        far = io.spot[4]
        gpk = up(io.gpk[...])
        gb1 = up(io.gb1[...])
        for low_bit in range(2):
            slot = low_bit ^ near
            for source, start in ((gb1, 0), (gpk, D // 2)):
                width = source.shape[1] // 4
                first = source[:, low_bit * width : (low_bit + 1) * width]
                second = source[:, (low_bit + 2) * width : (low_bit + 3) * width]
                both = beside(
                    jnp.where(far == 0, first, second), jnp.where(far == 0, second, first)
                )
                io.gcol[slot, :, start : start + 2 * width] = low(both)

    ins = Box({"recv%d" % i: ("v", recv[i]) for i in range(len(recv))})
    ins.update(
        Box(
            spot=("s", spot),
            u=("v", low_part.u),
            dd=("v", low_part.dd),
            gb1=("v", low_part.gb1),
            gz1=("v", low_part.gz1),
            packed=("d", kept.packed),
            cs=("d", cs),
            cm=("d", cm),
            before=("d", kept.before),
            wq=wq,
        )
    )
    outs = Box(
        gcol=("v", shape(2, rows, 2 * D, dtype=BF)),
        sums_c=("h", shape(8, D)),
    )
    if below is None:
        outs.grad = ("h", shape(rows, D))
    else:
        ins.n2 = ("d", below.n2)
        ins.r2 = ("d", below.r2)
        ins.gains = below.vecs.gains
        outs.update(second_norm_outs(rows))
    outs.update(fetches)
    return run(
        body,
        ins,
        outs,
        deps,
        scratch=Box(gpk=pltpu.VMEM((rows, 3 * D), BF)),
        limit=20,
        flops=2 * rows * D * 3 * D + 12 * HEADS * rows * rows * LANES,
        nbytes=2 * D * 3 * D,
    )


def owners(spot, core):
    return [
        ((spot[1] ^ along) * 2 + (spot[2] ^ across)) * 2 + core
        for across in range(2)
        for along in range(2)
    ]


def out_terms(io, core, put):
    near, far = io.spot[3], io.spot[4]
    for at, block in enumerate(owners(io.spot, core)):
        lanes = pl.ds(pl.multiple_of(block * (FF // 8), LANES), FF // 8)
        io.rhs[:, at * (FF // 8) : (at + 1) * (FF // 8)] = io.hid[:, lanes]
    lhs = io.gb2t[...]
    for half in range(2):
        grad = nn(lhs, io.rhs[:, half * D : (half + 1) * D])
        for sub in range(2):
            at = 2 * half + sub
            for n in range(4):
                lanes = pl.ds(pl.multiple_of(((n // 2) ^ far) * (D // 2), LANES), D // 2)
                put(
                    at,
                    (n % 2) ^ near,
                    None,
                    lanes,
                    grad[n * 192 : (n + 1) * 192, sub * (D // 2) : (sub + 1) * (D // 2)],
                )


def gather_rows(io, name, target, core):
    for at, block in enumerate(owners(io.spot, core)):
        io[target][at * 96 : (at + 1) * 96, :] = io[name][
            pl.ds(pl.multiple_of(block * 96, 16), 96), :
        ]


def in_terms(io, core, put):
    near, far = io.spot[3], io.spot[4]
    gather_rows(io, "midt", "lhs", core)
    for n in range(4):
        grad = nn(io.lhs[...], io.gpre[:, n * D : (n + 1) * D])
        for at in range(4):
            put(at, (n % 2) ^ near, (n // 2) ^ far, slice(None), grad[at * 96 : (at + 1) * 96])


def mix_terms(io, core, put):
    gather_rows(io, "mixt", "lhs", core)
    gather_rows(io, "xt", "lhs_two", core)
    for slot in range(2):
        for lhs, start, stop in (("lhs", 0, D // 2), ("lhs_two", D // 2, 2 * D)):
            grad = nn(io[lhs][...], io.gcol[slot, :, start:stop])
            for at in range(4):
                put(
                    at,
                    slot,
                    None,
                    slice(start, stop),
                    grad[at * 96 : (at + 1) * 96],
                )


def part_rows(part, count):
    if part is None:
        return slice(None)
    return pl.ds(pl.multiple_of(part * count, 16), count)


TERMS = Box(out=out_terms, inner=in_terms, mix=mix_terms)


def grad_setup(kind, spot, operands):
    ins = Box(spot=("s", spot))
    if kind == "out":
        gb2t, hid = operands
        tokens = gb2t.shape[1]
        ins.gb2t = ("v", gb2t)
        ins.hid = ("v", hid)
        return ins, Box(rhs=pltpu.VMEM((tokens, FF // 2), BF)), (192, D), tokens
    lhs = pltpu.VMEM((D // 2, operands[0].shape[1]), BF)
    if kind == "inner":
        midt, gpre = operands
        ins.midt = ("v", midt)
        ins.gpre = ("v", gpre)
        return ins, Box(lhs=lhs), (192, D), midt.shape[1]
    mixt, xt, gcol = operands
    ins.mixt = ("d", mixt)
    ins.xt = ("d", xt)
    ins.gcol = ("v", gcol)
    return ins, Box(lhs=lhs, lhs_two=lhs), (96, 2 * D), xt.shape[1]


def grad_send(kind, spot, operands, deps):
    ins, scratch, block, tokens = grad_setup(kind, spot, operands)

    def body(io):
        def put(at, slot, part, lanes, value):
            io.send[at, slot, part_rows(part, value.shape[0]), lanes] = low(value)

        TERMS[kind](io, 1 - io.spot[0], put)

    outs, token = run(
        body,
        ins,
        Box(send=("v", shape(4, 2, *block, dtype=BF))),
        deps,
        scratch=scratch,
        flops=2 * tokens * 8 * block[0] * block[1],
        nbytes=4 * 2 * 2 * block[0] * block[1],
    )
    return outs.send, token


def grad_keep(kind, spot, operands, got, order, deps):
    ins, scratch, block, tokens = grad_setup(kind, spot, operands)
    ins.got = ("v", got)
    rows_all = block[0]
    if order == "both":
        half = (rows_all // 2, block[1])
    else:
        half = block

    def body(io):
        def put(at, slot, part, lanes, value):
            count = value.shape[0]
            rows = part_rows(part, count)
            value = low(value + up(io.got[at, slot, rows, lanes]))
            across, along = at // 2, at % 2
            if order == "x":
                io["send0" if across else "keep0"][along, slot, rows, lanes] = value
            elif order == "y":
                io["send0" if along else "keep0"][across, slot, rows, lanes] = value
            else:
                rows = part_rows(part, count // 2)
                first, second = value[: count // 2], value[count // 2 :]
                io["send0" if across else "keep0"][along, slot, rows, lanes] = first
                io["send1" if along else "keep1"][across, slot, rows, lanes] = second

        TERMS[kind](io, io.spot[0], put)

    names = ["send0", "keep0"] + (["send1", "keep1"] if order == "both" else [])
    return run(
        body,
        ins,
        {name: ("v", shape(2, 2, *half, dtype=BF)) for name in names},
        deps,
        scratch=scratch,
        flops=2 * tokens * 8 * block[0] * block[1],
        nbytes=4 * 2 * 4 * block[0] * block[1],
    )


def grad_pass(groups, deps):
    pairs = [
        (group["keep%d" % at], group["got%d" % at]) for group in groups for at in halves_of(group)
    ]
    ins, outs = Box(), Box()
    for at, (keep, got) in enumerate(pairs):
        ins["keep%d" % at] = ("v", keep)
        ins["got%d" % at] = ("v", got)
        outs["next%d" % at] = ("v", shape(*keep.shape[1:], dtype=BF))

    def body(io):
        for at in range(len(pairs)):
            io["next%d" % at][...] = low(
                up(io["keep%d" % at][1]) + up(io["got%d" % at][1])
            )

    outs, token = run(body, ins, outs, deps)
    return [outs["next%d" % at] for at in range(len(pairs))], token


def halves_of(group):
    return [at for at in range(2) if "keep%d" % at in group]


def group_ins(groups):
    ins = Box()
    for which, group in enumerate(groups):
        for at in halves_of(group):
            for name in ("keep", "got", "come"):
                ins["%s%d_%d" % (name, which, at)] = ("v", group["%s%d" % (name, at)])
    return ins


def group_sum(io, which, at, slot):
    return (
        up(io["keep%d_%d" % (which, at)][0, slot])
        + up(io["got%d_%d" % (which, at)][0, slot])
        + up(io["come%d_%d" % (which, at)][slot])
    )


def grad_near(groups, deps):
    ins = group_ins(groups)
    places = [(which, at) for which, group in enumerate(groups) for at in halves_of(group)]
    total = sum(group["keep%d" % at].shape[2] for group in groups for at in halves_of(group))
    lanes = groups[0].keep0.shape[3]

    def body(io):
        start = 0
        for which, at in places:
            rows = groups[which]["keep%d" % at].shape[2]
            here = slice(start, start + rows)
            io.near[here, :] = low(group_sum(io, which, at, 1))
            io.stay[here, :] = low(group_sum(io, which, at, 0))
            start += rows

    return run(
        body,
        ins,
        Box(
            near=("v", shape(total, lanes, dtype=BF)),
            stay=("v", shape(total, lanes, dtype=BF)),
        ),
        deps,
    )


def grad_collect(kinds, groups, deps):
    ins = group_ins(groups)
    ins.spot = ("s", groups[0].spot)

    def body(io):
        near, far = io.spot[3], io.spot[4]
        for which, kind in enumerate(kinds):
            for slot in range(2):
                full = [group_sum(io, which, at, slot) for at in halves_of(groups[which])]
                if kind == "mix":
                    both = above(full[0], full[1])
                    quarter = D // 4
                    parts = [
                        beside(both[:, :quarter], both[:, 2 * quarter : 5 * quarter]),
                        beside(both[:, quarter : 2 * quarter], both[:, 5 * quarter :]),
                    ]
                elif kind == "inner":
                    parts = [full[0][:96], full[0][96:]]
                else:
                    parts = [
                        beside(full[0][:96, : D // 2], full[0][96:, : D // 2]),
                        beside(full[0][:96, D // 2 :], full[0][96:, D // 2 :]),
                    ]
                for half in range(2):
                    owner = (slot ^ near) + 2 * (half ^ far)
                    io.blocks[owner, which * 96 : (which + 1) * 96, :] = low(parts[half])

    outs, token = run(
        body, ins, Box(blocks=("v", shape(4, 96 * len(kinds), D, dtype=BF))), deps
    )
    return outs.blocks, token


def grad_far(kinds, stay, near, deps):
    count = len(kinds)

    def body(io):
        full = up(io.stay[...]) + up(io.near[...])
        if kinds[0] == "mix":
            quarter = D // 4
            io.own[...] = beside(full[:, :quarter], full[:, 2 * quarter : 5 * quarter])
            io.far[...] = low(
                beside(full[:, quarter : 2 * quarter], full[:, 5 * quarter : 8 * quarter])
            )
            return
        for at, kind in enumerate(kinds):
            part = full[192 * at : 192 * (at + 1)]
            here = slice(96 * at, 96 * (at + 1))
            if kind == "out":
                io.own[here, :] = beside(part[:96, : D // 2], part[96:, : D // 2])
                io.far[here, :] = low(beside(part[:96, D // 2 :], part[96:, D // 2 :]))
            else:
                io.own[here, :] = part[:96]
                io.far[here, :] = low(part[96:])

    return run(
        body,
        Box(stay=("v", stay), near=("v", near)),
        Box(
            own=("v", shape(count * 96, D)),
            far=("v", shape(count * 96, D, dtype=BF)),
        ),
        deps,
    )


def grad_last(kind, terms, deps):
    ins = Box()
    for layer in range(LAYERS):
        for at, term in enumerate(terms[layer]):
            ins["term%d_%d" % (layer, at)] = ("v", term)
    if kind == "mix":
        outs = Box(
            first=("h", shape(LAYERS, 96, 3 * D // 4)),
            second=("h", shape(LAYERS, 96, D // 4)),
        )
    else:
        outs = Box(
            first=("h", shape(LAYERS, 96, D)),
            second=("h", shape(LAYERS, FF // 8, D // 4)),
        )

    def body(io):
        for layer in range(LAYERS):
            full = up(io["term%d_0" % layer][...])
            for at in range(1, len(terms[layer])):
                full = full + up(io["term%d_%d" % (layer, at)][...])
            if kind == "mix":
                io.first[layer] = full[:, D // 4 :]
                io.second[layer] = full[:, : D // 4]
            else:
                io.first[layer] = full[96:]
                io.second[layer, :, :96] = full[:96, : D // 2].T
                io.second[layer, :, 96:] = full[:96, D // 2 :].T
        io.done("first")
        io.done("second")

    return run(body, ins, outs, deps)


def wide_swap(v, bit):
    size = lax.axis_size("wide")
    return lax.ppermute(v, "wide", [(i, i ^ bit) for i in range(size)])


def narrow_swap(v, bit):
    size = lax.axis_size("narrow")
    return lax.ppermute(v, "narrow", [(i, i ^ bit) for i in range(size)])


CORE, ACROSS, ALONG = 1, 2, 4
NEAR, FAR = 1, 2


def reduce_plain(left, right):
    term = low(tn(left, right))
    part = lax.psum_scatter(term, "narrow", scatter_dimension=1, tiled=True)
    return lax.psum_scatter(up(part), "wide", scatter_dimension=0, tiled=True)


def move(v, shift):
    size = lax.axis_size("narrow")
    pairs = [(i, i + shift) for i in range(size) if 0 <= i + shift < size]
    return lax.ppermute(v, "narrow", pairs)


def travel(state, step):
    return [move(state, step * shift) for shift in range(1, lax.axis_size("narrow"))]


def add_up(a, b, deps):
    def body(io):
        io.sum[...] = (up(io.a[...]) + up(io.b[...])).astype(a.dtype)

    outs, token = run(
        body,
        Box(a=("v", a), b=("v", b)),
        Box(sum=("v", shape(*a.shape, dtype=a.dtype))),
        deps,
    )
    return outs.sum, token


def shards(
    tokens,
    cotangent,
    horizons,
    qkv_weight,
    out_weight,
    ffn_in_weight,
    ffn_out_weight,
    qkv_bias,
    ffn_in_bias,
    model_biases,
    norm_gains,
):
    Counter.at = 0
    rows = tokens.shape[0]
    wide = lax.axis_size("wide")
    narrow = lax.axis_size("narrow")
    wide_at = lax.axis_index("wide")
    narrow_at = lax.axis_index("narrow")
    fast = wide == 8 and narrow == 4
    place = [wide_at % 2, (wide_at // 4) % 2, (wide_at // 2) % 2, narrow_at % 2, narrow_at // 2]
    if not fast:
        place = [wide_at * 0] * 5
    place.append(narrow_at)
    spot = jnp.stack(place).astype(jnp.int32)
    step = 0.5 * math.pi / up(horizons[0])
    places = up(narrow_at * rows + jnp.arange(rows)) * step
    cs = beside(
        jnp.broadcast_to(jnp.cos(places)[:, None], (rows, HEAD_DIM)),
        jnp.broadcast_to(jnp.sin(places)[:, None], (rows, HEAD_DIM)),
    )

    def mask(step):
        apart = jnp.arange(rows)[:, None] - jnp.arange(rows)[None, :]
        return jnp.where(apart >= 0, jnp.cos(up(apart) * step), 0.0)

    vecs = Box(
        ffn_bias=("d", ffn_in_bias),
        shifts=("d", model_biases),
        gains=("d", norm_gains),
    )
    wq_cuts = [("d", qkv_weight, columns_of(layer, 3)) for layer in range(LAYERS)]

    def weight_fetch(layer):
        return Box(
            wo=("f", out_weight) + layer_of(layer, (D, D)),
            w1=("f", ffn_in_weight) + columns_of(layer, 4),
            w2=("f", ffn_out_weight) + rows_of(layer, 4),
        )

    x = tokens
    wq = wq_cuts[0]
    saved = []
    deps = ()
    for layer in range(LAYERS):
        last = layer == LAYERS - 1
        first, token = project(
            layer, x, "v" if layer else "d", wq, Box(qkv_bias=("d", qkv_bias)), cs, True, deps
        )
        if not layer:
            cm = mask(step + token[0, 0])
        recv = travel(first.state, 1)
        fetches = weight_fetch(layer)
        if not last:
            fetches.wq = ("f", qkv_weight) + columns_of(layer + 1, 3)
        inner, token = inside(first.packed, cm, not last, fetches, (token,))
        weights = inner
        kept, token = layer_forward(
            layer,
            recv,
            x,
            "v" if layer else "d",
            inner,
            weights,
            vecs,
            cs,
            cotangent if last else None,
            (token,),
        )
        kept.packed = first.kept
        kept.xt = first.xt
        kept.sq = inner.sq if last else inner.sq_kept
        kept.vecs = vecs
        saved.append(kept)
        deps = (token,)
        if not last:
            x = kept.s_next
            wq = ("v", inner.wq)

    output = saved[1].output
    one, zero = saved[1], saved[0]
    if not fast:
        grads = [None] * LAYERS
        sums = [None] * LAYERS
        top = one
        for layer in (1, 0):
            kept = saved[layer]
            fetch = Box() if layer == 1 else Box()
            back, token = layer_back(
                layer, top, kept, "v" if layer else "d", weights, vecs, cs, fetch, (token,)
            )
            recv = travel(back.state, -1)
            below = saved[0] if layer == 1 else None
            fetch = weight_fetch(0) if layer == 1 else Box()
            mix, token = mix_back(
                layer, recv, spot, back, kept, cs, cm, wq_cuts[layer], below, fetch, (token,)
            )
            gcol = mix.gcol
            gpk = jnp.concatenate(
                [gcol[n % 2, :, 384 + 576 * (n // 2) : 960 + 576 * (n // 2)] for n in range(4)],
                axis=1,
            )
            grads[layer] = (
                reduce_plain(kept.xt.T, gpk),
                reduce_plain(kept.mixt.T, back.gb1),
                reduce_plain(kept.midt.T, back.gpre),
                reduce_plain(kept.hid, top.gb2),
            )
            sums[layer] = jnp.concatenate(
                [top.sums_a[:3], back.sums_b[:7], mix.sums_c[:3]], axis=0
            )
            top = mix
            weights = mix
        sums = lax.psum(jnp.stack(sums), ("wide", "narrow"))
        grad_qkv, grad_o, grad_in, grad_out = (
            jnp.stack([grads[l][k] for l in range(LAYERS)]) for k in range(4)
        )
        input_grad = mix.grad
    else:
        group = Box()
        ops = Box()

        def send(name, kind, operands, token):
            ops[name] = (kind, operands)
            sent, token = grad_send(kind, spot, operands, (token,))
            ops[name] += (wide_swap(sent, CORE),)
            return token

        def keep(name, order, token):
            kind, operands, got = ops[name]
            found, token = grad_keep(kind, spot, operands, got, order, (token,))
            axes = Box(x=(ACROSS,), y=(ALONG,), both=(ACROSS, ALONG))[order]
            for at, axis in enumerate(axes):
                found["got%d" % at] = wide_swap(found["send%d" % at], axis)
            found.axes = axes
            group[name] = found
            return token

        def forward(names, token):
            sent, token = grad_pass([group[name] for name in names], (token,))
            for name in names:
                for at in halves_of(group[name]):
                    axis = ACROSS + ALONG - group[name].axes[at]
                    group[name]["come%d" % at] = wide_swap(sent.pop(0), axis)
            return token

        def near(names, token):
            found, token = grad_near([group[name] for name in names], (token,))
            return (found.stay, narrow_swap(found.near, NEAR)), token

        def far(kinds, pair, token):
            found, token = grad_far(kinds, *pair, (token,))
            return (found.own, narrow_swap(found.far, FAR)), token

        def gather(kinds, names, token):
            for name in names:
                group[name].spot = spot
            blocks, token = grad_collect(kinds, [group[name] for name in names], (token,))
            mine = lax.psum_scatter(blocks, "narrow", scatter_dimension=0, tiled=True)
            return (mine.reshape(mine.shape[1:]),), token

        token = send("o1", "out", (one.gb2t, one.hid), token)
        back1, token = layer_back(1, one, one, "v", weights, vecs, cs, Box(), (token,))
        later1 = [move(back1.state, -1)]
        token = send("i1", "inner", (one.midt, back1.gpre), token)
        token = keep("o1", "y", token)
        both, token = add_up(back1.state, later1[0], (token,))
        later1.append(move(both, -2))
        token = keep("i1", "x", token)
        mix1, token = mix_back(
            1, later1, spot, back1, one, cs, cm, wq_cuts[1], zero, weight_fetch(0), (token,)
        )
        token = send("m1", "mix", (one.mixt, one.xt, mix1.gcol), token)
        token = forward(["o1"], token)
        token = forward(["i1"], token)
        fetch = Box(
            hid=("f", zero.hid, [whole_cut], (rows, FF)),
            midt=("f", zero.midt, [whole_cut], (D, rows)),
        )
        weights = mix1
        back0, token = layer_back(0, mix1, zero, "d", weights, vecs, cs, fetch, (token,))
        later0 = [move(back0.state, -1)]
        token = keep("m1", "both", token)
        f1, token = gather(["out", "inner"], ["o1", "i1"], token)
        both, token = add_up(back0.state, later0[0], (token,))
        later0.append(move(both, -2))
        token = send("o0", "out", (mix1.gb2t, back0.hid.reshape(rows, FF)), token)
        token = send("i0", "inner", (back0.midt.reshape(D, rows), back0.gpre), token)
        token = forward(["m1"], token)
        token = keep("o0", "y", token)
        token = keep("i0", "x", token)
        mix0, token = mix_back(
            0, later0, spot, back0, zero, cs, cm, wq_cuts[0], None, Box(), (token,)
        )
        input_grad = mix0.grad
        sums = jnp.concatenate(
            [
                mix1.sums_a[:3],
                back0.sums_b[:7],
                mix0.sums_c[:3],
                one.sums_a[:3],
                back1.sums_b[:7],
                mix1.sums_c[:3],
                jnp.zeros((6, D), F32),
            ],
            axis=0,
        )
        token = send("m0", "mix", (zero.mixt, zero.xt, mix0.gcol), token)
        come = wide_swap(sums, CORE)
        sums, token = add_up(sums, come, (token,))
        come = wide_swap(sums, ACROSS)
        mg1, token = gather(["mix"], ["m1"], token)
        sums, token = add_up(sums, come, (token,))
        come = wide_swap(sums, ALONG)
        token = forward(["o0"], token)
        token = forward(["i0"], token)
        sums, token = add_up(sums, come, (token,))
        come = narrow_swap(sums, NEAR)
        token = keep("m0", "both", token)
        sums, token = add_up(sums, come, (token,))
        come = narrow_swap(sums, FAR)
        near_f0, token = near(["o0", "i0"], token)
        sums, token = add_up(sums, come, (token,))
        token = forward(["m0"], token)
        far_f0, token = far(["out", "inner"], near_f0, token)
        near_m0, token = near(["m0"], token)
        far_m0, token = far(["mix"], near_m0, token)
        ffn_grads, token = grad_last("ffn", [far_f0, f1], (token,))
        mix_grads, token = grad_last("mix", [far_m0, mg1], (token,))
        sums = sums[:26].reshape(LAYERS, 13, D)
        grad_qkv, grad_o = mix_grads.first, mix_grads.second
        grad_in, grad_out = ffn_grads.first, ffn_grads.second

    def columns(v):
        width = v.shape[-1] // narrow
        return lax.dynamic_slice_in_dim(v, narrow_at * width, width, axis=v.ndim - 1)

    return (
        output,
        input_grad,
        grad_qkv,
        grad_o,
        grad_in,
        grad_out,
        columns(sums[:, 10:13].reshape(LAYERS, 3 * D)),
        columns(sums[:, 3:7].reshape(LAYERS, FF)),
        columns(jnp.stack([sums[:, 7], sums[:, 0], sums[:, 8], sums[:, 1]], axis=1)),
        columns(jnp.stack([sums[:, 9], sums[:, 2]], axis=1)),
    )


def solution(mesh):
    rows = P(("wide", "narrow"), None)
    placed = (rows, rows, P("wide")) + (P(),) * 8
    return jax.shard_map(
        shards,
        mesh=mesh,
        in_specs=placed,
        out_specs=(rows, rows)
        + (P(None, "wide", "narrow"),) * 4
        + (P(None, "narrow"),) * 2
        + (P(None, None, "narrow"),) * 2,
        check_vma=False,
    )
```

time: 1530 us -> 297 us (0.19)
  local copies, waits for them, and re-layouts: 696 us -> 11.1 us
  waiting for transfers between devices: 482 us -> 96.8 us
  matrix products: 173 us -> 0 us
  Pallas kernels: 0 us -> 116 us
  other arithmetic: 84 us -> 3.55 us
  blocking collectives: 24.7 us -> 0 us
    unnamed x323 -> x83, local copies, waits for them, and re-layouts: 569 us -> 7.75 us
    all_to_all x8 -> x0, waiting for transfers between devices: 224 us -> none  [the longest x2 139 us: shards(): lax.all_to_all(grad_packed_heads, 'narrow', split_axis=0, concat_axis=1,...]
    unnamed x19 -> x2, waiting for transfers between devices: 224 us -> 0.03 us
    dot_general x62 -> x0, matrix products: 173 us -> none  [the longest x8 33.2 us: matmul_low(): return jnp.dot(left, right, preferred_element_type=jnp.float32)]
    pallas_call x0 -> x43, Pallas kernels: none -> 116 us  [run(): pl.pallas_call(kernel, out_shape=tuple(out_shapes), in_specs=in_specs, ou...]
    ppermute x0 -> x41, waiting for transfers between devices: none -> 96.7 us  [the longest x25 45 us: wide_swap(): return lax.ppermute(v, 'wide', [(i, i ^ bit) for i in range(size)])]
    ppermute x0 -> x41, starting transfers between devices: none -> 48.9 us  [the longest x10 28.2 us: move(): return lax.ppermute(v, 'narrow', pairs)]
    another operation x30 -> x2, other arithmetic: 38.7 us -> 1.37 us  [the longest x1 0.69 us: shards(): jnp.stack([sums[:, 7], sums[:, 0], sums[:, 8], sums[:, 1]], axis=1)]
  transfers between devices with their start and end apart: 19 -> 43, of which waited for: 10 -> 17; matrix products, arithmetic and copies ran while one was open for 45% -> 3% of each run, Pallas kernels for 0% -> 30%
where the time goes in v2:
time: 297 us; the launch traced here: 293 us
  Pallas kernels  116 us (39%)
  waiting for transfers between devices  96.8 us (33%)
  starting transfers between devices  48.9 us (16%)
  between operations  17 us (6%)
  local copies, waits for them, and re-layouts  11.1 us (4%)
  other arithmetic  3.55 us (1%)
    pallas_call x43, Pallas kernels, run(): pl.pallas_call(kernel, out_shape=tuple(out_shapes), in_specs=in_specs, ou...  116 us
    ppermute x25, waiting for transfers between devices, wide_swap(): return lax.ppermute(v, 'wide', [(i, i ^ bit) for i in range(size)])  45 us
    ppermute x10, waiting for transfers between devices, move(): return lax.ppermute(v, 'narrow', pairs)  33.2 us
    ppermute x10, starting transfers between devices, move(): return lax.ppermute(v, 'narrow', pairs)  28.2 us
    ppermute x25, starting transfers between devices, wide_swap(): return lax.ppermute(v, 'wide', [(i, i ^ bit) for i in range(size)])  20.3 us
    ppermute x6, waiting for transfers between devices, narrow_swap(): return lax.ppermute(v, 'narrow', [(i, i ^ bit) for i in range(size)])  18.6 us
    unnamed x83, local copies, waits for them, and re-layouts  7.75 us
  transfers between devices with their start and end apart: 43, of which 17 were waited for; matrix products, arithmetic and copies ran while one was open for 3% of the time, Pallas kernels for 30%

profile of v2, /device:TPU:0, one launch (start us, length us, event | category | flops | bytes accessed | tf_op | source)
XLA Modules:
  0.0 293.0 jit_solution(9458717908923028090)
XLA Ops:
  8.9 6.0 %shard_map.186 = (bf16[256,2304]{1,0:T(8,128)(2,1)S(1)}, bf16[768,256]{1,0:T(8,128)(2,1)}, bf16[784,128]{1,0:T(8,128)(2,1)S(1)}, bf16[256,2304]{1,0:T(8,128)(2,1)}, f32[8,128]{1,0:T(8,128)S(1)}) custom-call(bf16[256,768]{1,0:T(8,128)(2,1)} %refs_3_.7, bf16[2,768,2304]{2,1,0:T(8,128)(2,1)} %refs_11_.11, ...), custom_call_target="tpu_custom_call" | custom-call | flops 120000004096 | bytes 100000000 | tf_op jit(solution)/shard_map/pallas_call | solution.py:245
  15.0 7.0 %collective-permute-start.2 = (bf16[784,128]{1,0:T(8,128)(2,1)S(1)}, bf16[784,128]{1,0:T(8,128)(2,1)S(1)}, u32[]{:S(2)}, u32[]{:S(2)}) collective-permute-start(bf16[784,128]{1,0:T(8,128)(2,1)S(1)} %get-tuple-element.179), channel_id=1, source_target_pairs={{0,3},{4,7},{8,11},{12,15},{16,19},{20,23},{24,27},{28,31}} | collective-permute-start | bytes 602120 | tf_op jit(solution)/shard_map/ppermute | solution.py:1120
  21.9 1.3 collective-permute-start.1
  23.3 2.7 collective-permute-start
  27.1 1.4 cosine_select_fusion.refs_1_.refs_9_
  28.5 5.5 %shard_map.187 = (f32[256,768]{1,0:T(8,128)S(1)}, f32[256,768]{1,0:T(8,128)S(1)}, bf16[256,768]{1,0:T(8,128)(2,1)S(1)}, bf16[256,768]{1,0:T(8,128)(2,1)}, bf16[1...) custom-call(bf16[256,2304]{1,0:T(8,128)(2,1)S(1)} %get-tuple-element, ...), custom_call_target="tpu_custom_call" | custom-call | flops 10000000000 | bytes 100000000 | tf_op jit(solution)/shard_map/pallas_call | solution.py:245
  34.8 8.3 %shard_map.188 = (bf16[784,128]{1,0:T(8,128)(2,1)}, bf16[256,768]{1,0:T(8,128)(2,1)}, bf16[768,256]{1,0:T(8,128)(2,1)}, f32[256,768]{1,0:T(8,128)}, f32[256,768]...) custom-call(bf16[784,128]{1,0:T(8,128)(2,1)S(1)} %collective-permute, ...), custom_call_target="tpu_custom_call" | custom-call | flops 15000000512 | bytes 100000000 | tf_op jit(solution)/shard_map/pallas_call | solution.py:245
  43.1 4.2 %shard_map.189 = (bf16[256,2304]{1,0:T(8,128)(2,1)S(1)}, bf16[768,256]{1,0:T(8,128)(2,1)}, bf16[784,128]{1,0:T(8,128)(2,1)S(1)}, bf16[256,2304]{1,0:T(8,128)(2,1)}, f32[8,128]{1,0:T(8,128)S(1)}) custom-call(f32[256,768]{1,0:T(8,128)S(1)} %get-tuple-element.189.refs_0_.refs_3_, bf16[3,768,768]{2,1,0:T(8,128)(2,1)S(1)} %get-tuple-element.190.refs_1_, ...), custom_call_target="tpu_custom_call" | custom-call | flops 60000002048 | bytes 100000000 | tf_op jit(solution)/shard_map/pallas_call | solution.py:245
  47.4 6.3 %collective-permute-start.5 = (bf16[784,128]{1,0:T(8,128)(2,1)S(1)}, bf16[784,128]{1,0:T(8,128)(2,1)S(1)}, u32[]{:S(2)}, u32[]{:S(2)}) collective-permute-start(bf16[784,128]{1,0:T(8,128)(2,1)S(1)} %get-tuple-element.192), channel_id=1, source_target_pairs={{0,3},{4,7},{8,11},{12,15},{16,19},{20,23},{24,27},{28,31}} | collective-permute-start | bytes 602120 | tf_op jit(solution)/shard_map/ppermute | solution.py:1120
  53.6 4.0 %collective-permute-start.4 = (bf16[784,128]{1,0:T(8,128)(2,1)S(1)}, bf16[784,128]{1,0:T(8,128)(2,1)S(1)}, u32[]{:S(2)}, u32[]{:S(2)}) collective-permute-start(bf16[784,128]{1,0:T(8,128)(2,1)S(1)} %get-tuple-element.192), channel_id=1, source_target_pairs={{0,2},{1,3},{4,6},{5,7},{8,10},{9,11},{12,14},{13,15},{16,18},{17,... | collective-permute-start | bytes 602120 | tf_op jit(solution)/shard_map/ppermute | solution.py:1120
  57.6 1.8 collective-permute-start.3
  59.6 4.3 %shard_map.190 = (f32[256,768]{1,0:T(8,128)S(1)}, f32[256,768]{1,0:T(8,128)S(1)}, bf16[256,768]{1,0:T(8,128)(2,1)S(1)}, bf16[1,768,768]{2,1,0:T(8,128)(2,1)S(1)}...) custom-call(bf16[256,2304]{1,0:T(8,128)(2,1)S(1)} %get-tuple-element.193.refs_0_, ...), custom_call_target="tpu_custom_call" | custom-call | flops 300000000 | bytes 100000000 | tf_op jit(solution)/shard_map/pallas_call | solution.py:245
  63.9 2.7 collective-permute-done.3.refs_0_
  66.6 7.3 %shard_map.191 = (bf16[784,128]{1,0:T(8,128)(2,1)}, bf16[256,768]{1,0:T(8,128)(2,1)S(1)}, bf16[768,256]{1,0:T(8,128)(2,1)}, f32[256,768]{1,0:T(8,128)S(1)}, f32[...) custom-call(bf16[784,128]{1,0:T(8,128)(2,1)S(1)} %collective-permute, ...), custom_call_target="tpu_custom_call" | custom-call | flops 30000001024 | bytes 100000000 | tf_op jit(solution)/shard_map/pallas_call | solution.py:245
  73.9 1.4 shard_map.192
  75.4 5.4 %shard_map.193 = (bf16[256,3072]{1,0:T(8,128)(2,1)S(1)}, bf16[256,768]{1,0:T(8,128)(2,1)S(1)}, f32[256,768]{1,0:T(8,128)S(1)}, bf16[256,768]{1,0:T(8,128)(2,1)S(...) custom-call(f32[256,768]{1,0:T(8,128)S(1)} %get-tuple-element.203.ref, ...), custom_call_target="tpu_custom_call" | custom-call | flops 120000004096 | bytes 100000000 | tf_op jit(solution)/shard_map/pallas_call | solution.py:245
  80.8 1.4 shard_map.194
  82.8 1.3 collective-permute-start.6
  84.1 1.4 shard_map.195
  85.5 10.1 %collective-permute-done.6.refs_1_.refs_0_ = bf16[784,128]{1,0:T(8,128)(2,1)S(1)} collective-permute-done((bf16[784,128]{1,0:T(8,128)(2,1)S(1)}, bf16[784,128]{1,0:T(8,128)(2,1)S(1)}, u32[]{:S(2)}, u32[]{:S(2)}) %collective-permute-start.6) | collective-permute-done | bytes 200736 | tf_op jit(solution)/shard_map/ppermute | solution.py:1120
  95.6 1.3 collective-permute-start.8
  96.9 1.3 shard_map.197
  98.3 1.6 collective-permute-start.10
  99.8 1.5 collective-permute-start.11
  101.4 7.8 %collective-permute-done.8.refs_1_ = bf16[784,128]{1,0:T(8,128)(2,1)S(1)} collective-permute-done((bf16[784,128]{1,0:T(8,128)(2,1)S(1)}, bf16[784,128]{1,0:T(8,128)(2,1)S(1)}, u32[]{:S(2)}, u32[]{:S(2)}) %collective-permute-start.8) | collective-permute-done | bytes 200736 | tf_op jit(solution)/shard_map/ppermute | solution.py:1120
  109.2 10.4 %shard_map.198 = (bf16[2,256,1536]{2,1,0:T(8,128)(2,1)S(1)}, f32[8,768]{1,0:T(8,128)}, f32[256,768]{1,0:T(8,128)S(1)}, bf16[256,768]{1,0:T(8,128)(2,1)S(1)}, bf1...) custom-call(bf16[784,128]{1,0:T(8,128)(2,1)S(1)} %collective-permute, ...), custom_call_target="tpu_custom_call" | custom-call | flops 120000004096 | bytes 100000000 | tf_op jit(solution)/shard_map/pallas_call | solution.py:245
  119.6 2.6 shard_map.199
  122.3 4.7 %collective-permute-done.11.refs_1_ = bf16[2,2,192,768]{3,2,1,0:T(8,128)(2,1)S(1)} collective-permute-done((bf16[2,2,192,768]{3,2,1,0:T(8,128)(2,1)S(1)}, bf16[2,2,192,768]{3,2,1,0:T(8,128)(2,1)S(1)}, u32[]{:S(2)}, u32[]{:S(2)}) %collective-permute-start.11) | collective-permute-done | bytes 1179680 | tf_op jit(solution)/shard_map/ppermute | solution.py:1099
  127.3 1.6 collective-permute-start.14
  129.4 7.5 %shard_map.202 = (bf16[256,3072]{1,0:T(8,128)(2,1)S(1)}, bf16[256,768]{1,0:T(8,128)(2,1)S(1)}, f32[256,768]{1,0:T(8,128)S(1)}, bf16[256,768]{1,0:T(8,128)(2,1)S(...) custom-call(f32[256,768]{1,0:T(8,128)S(1)} %get-tuple-element.233.re, ...), custom_call_target="tpu_custom_call" | custom-call | flops 15000000512 | bytes 100000000 | tf_op jit(solution)/shard_map/pallas_call | solution.py:245
  136.9 1.3 collective-permute-start.12
  138.2 3.6 %shard_map.203 = (bf16[2,2,48,1536]{3,2,1,0:T(8,128)(2,1)}, bf16[2,2,48,1536]{3,2,1,0:T(8,128)(2,1)S(1)}, bf16[2,2,48,1536]{3,2,1,0:T(8,128)(2,1)}, bf16[2,2,48,1536]{3,2,1,0:T(8,128)(2,1)S(1)}, f32[8,128]{1,0:T(8,128)S(1)}) custom-call(s32[6]{0:T(128)S(1)} %stack.33.refs_0_.refs_2_.refs_6_, bf16[768,256]{1,0:T(8,128)(2,1)} %get-tuple-element.250.refs_1_, ...), custom_call_target="tpu_custom_call" | custom-call | flops 6000000000 | bytes 100000000 | tf_op jit(solution)/shard_map/pallas_call | solution.py:245
  142.7 1.5 collective-permute-start.19
  144.7 2.0 shard_map.204
  147.5 2.8 shard_map.206
  150.6 1.4 collective-permute-start.16
  152.0 1.4 shard_map.207
  153.9 1.9 collective-permute-done.19.refs_1_
  159.2 2.6 shard_map.209
  161.8 2.5 shard_map.210
  164.3 11.7 %collective-permute-done.16.refs_1_ = bf16[784,128]{1,0:T(8,128)(2,1)S(1)} collective-permute-done((bf16[784,128]{1,0:T(8,128)(2,1)}, bf16[784,128]{1,0:T(8,128)(2,1)S(1)}, u32[]{:S(2)}, u32[]{:S(2)}) %collective-permute-start.16) | collective-permute-done | bytes 200736 | tf_op jit(solution)/shard_map/ppermute | solution.py:1120
  176.1 9.6 %shard_map.211 = (bf16[2,256,1536]{2,1,0:T(8,128)(2,1)S(1)}, f32[8,768]{1,0:T(8,128)}, f32[256,768]{1,0:T(8,128)}, f32[8,128]{1,0:T(8,128)S(1)}) custom-call(bf16[784,128]{1,0:T(8,128)(2,1)S(1)} %collective-permute-done.12.refs_1_.refs_0_, bf16[784,128]{1,0:T(8,128)(2,1)S(1)} %collective-permute-done.16.refs_1_, s32[6]{0:T(128)S(1)} %stack.33.refs_0_.refs_2_.refs_6_, ...), custom_call_target="tpu_custom_call" | custom-call | flops 22000001024 | bytes 100000000 | tf_op jit(solution)/shard_map/pallas_call | solution.py:245
  187.7 1.5 collective-permute-start.28
  189.2 4.0 %shard_map.212 = (bf16[4,2,96,1536]{3,2,1,0:T(8,128)(2,1)}, f32[8,128]{1,0:T(8,128)S(1)}) custom-call(s32[6]{0:T(128)S(1)} %stack.33.refs_0_.refs_2_.refs_6_, bf16[768,256]{1,0:T(8,128)(2,1)} %get-tuple-element.288.refs_1_, bf16[768,256]{1,0:T(8,128)(2,1)} %get-tuple-element.289.refs_2_, bf16[2,256,1536]{2,1,0:T(8,128)(2,1)S(1)} %get-tuple-element.290.refs_3_, ...), custom_call_target="tpu_custom_call" | custom-call | flops 3000000000 | bytes 100000000 | tf_op jit(solution)/shard_map/pallas_call | solution.py:245
  193.4 1.6 collective-permute-start.23
  195.0 2.2 shard_map.214
  197.1 20.7 %collective-permute-done.23.refs_1_ = f32[32,768]{1,0:T(8,128)S(1)} collective-permute-done((f32[32,768]{1,0:T(8,128)S(1)}, f32[32,768]{1,0:T(8,128)S(1)}, u32[]{:S(2)}, u32[]{:S(2)}) %collective-permute-start.23) | collective-permute-done | bytes 98336 | tf_op jit(solution)/shard_map/ppermute | solution.py:1099
  217.8 1.6 collective-permute-start.26
  220.9 2.2 shard_map.217
  223.2 1.2 collective-permute-start.34
  225.1 4.7 %shard_map.219 = (bf16[2,2,48,1536]{3,2,1,0:T(8,128)(2,1)}, bf16[2,2,48,1536]{3,2,1,0:T(8,128)(2,1)S(1)}, bf16[2,2,48,1536]{3,2,1,0:T(8,128)(2,1)}, bf16[2,2,48,1536]{3,2,1,0:T(8,128)(2,1)S(1)}, f32[8,128]{1,0:T(8,128)S(1)}) custom-call(s32[6]{0:T(128)S(1)} %stack.33.refs_0_.refs_2_.refs_6_, bf16[768,256]{1,0:T(8,128)(2,1)} %get-tuple-element.288.refs_1_, ...), custom_call_target="tpu_custom_call" | custom-call | flops 300000000 | bytes 100000000 | tf_op jit(solution)/shard_map/pallas_call | solution.py:245
  230.6 1.5 collective-permute-start.29
  233.0 6.8 %collective-permute-done.34.refs_5_ = bf16[2,192,768]{2,1,0:T(8,128)(2,1)} collective-permute-done((bf16[2,192,768]{2,1,0:T(8,128)(2,1)}, bf16[2,192,768]{2,1,0:T(8,128)(2,1)}, u32[]{:S(2)}, u32[]{:S(2)}) %collective-permute-start.34) | collective-permute-done | bytes 589856 | tf_op jit(solution)/shard_map/ppermute | solution.py:1099
  241.0 2.6 shard_map.221
  245.2 6.6 %collective-permute-done.29.refs_1_ = bf16[2,2,48,1536]{3,2,1,0:T(8,128)(2,1)S(1)} collective-permute-done((bf16[2,2,48,1536]{3,2,1,0:T(8,128)(2,1)}, bf16[2,2,48,1536]{3,2,1,0:T(8,128)(2,1)S(1)}, u32[]{:S(2)}, u32[]{:S(2)}) %collective-permute-start.29) | collective-permute-done | bytes 589856 | tf_op jit(solution)/shard_map/ppermute | solution.py:1099
  251.9 1.3 shard_map.223
  254.3 4.6 %collective-permute-done.37.refs_1_ = bf16[384,768]{1,0:T(8,128)(2,1)S(1)} collective-permute-done((bf16[384,768]{1,0:T(8,128)(2,1)}, bf16[384,768]{1,0:T(8,128)(2,1)S(1)}, u32[]{:S(2)}, u32[]{:S(2)}) %collective-permute-start.37) | collective-permute-done | bytes 589856 | tf_op jit(solution)/shard_map/ppermute | solution.py:1104
  259.2 1.5 collective-permute-done.35.refs_2_
  261.0 1.3 shard_map.225
  264.4 12.0 %collective-permute-done.38.refs_1_ = bf16[96,1536]{1,0:T(8,128)(2,1)S(1)} collective-permute-done((bf16[96,1536]{1,0:T(8,128)(2,1)S(1)}, bf16[96,1536]{1,0:T(8,128)(2,1)S(1)}, u32[]{:S(2)}, u32[]{:S(2)}) %collective-permute-start.38) | collective-permute-done | bytes 294944 | tf_op jit(solution)/shard_map/ppermute | solution.py:1104
  277.6 1.4 shard_map.227
  279.1 2.2 copy.22
  281.3 1.9 collective-permute-done.39.refs_1_
  284.1 1.6 shard_map.228
  (169 shorter events, 24.5 us)
Async XLA Ops:
  7.2 269.5 %reduce-scatter.5.cloned.1.call-start = ((), (), s32[]{:S(2)}) async-start(), calls=%async_computation.3 | async-start | bytes 1474560 | tf_op jit(solution)/shard_map/reduce_scatter | solution.py:1308
  15.0 19.0 %collective-permute-start.2 = (bf16[784,128]{1,0:T(8,128)(2,1)S(1)}, bf16[784,128]{1,0:T(8,128)(2,1)S(1)}, u32[]{:S(2)}, u32[]{:S(2)}) collective-permute-start(bf16[784,128]{1,0:T(8,128)(2,1)S(1)} %get-tuple-element.179), channel_id=1, source_target_pairs={{0,3},{4,7},{8,11},{12,15},{16,19},{20,23},{24,27},{28,31}} | collective-permute-start | bytes 602120 | tf_op jit(solution)/shard_map/ppermute | solution.py:1120
  21.9 12.1 %collective-permute-start.1 = (bf16[784,128]{1,0:T(8,128)(2,1)S(1)}, bf16[784,128]{1,0:T(8,128)(2,1)S(1)}, u32[]{:S(2)}, u32[]{:S(2)}) collective-permute-start(bf16[784,128]{1,0:T(8,128)(2,1)S(1)} %get-tuple-element.179), channel_id=1, source_target_pairs={{0,2},{1,3},{4,6},{5,7},{8,10},{9,11},{12,14},{13,15},{16,18},{17,... | collective-permute-start | bytes 602120 | tf_op jit(solution)/shard_map/ppermute | solution.py:1120
  23.3 11.6 %collective-permute-start = (bf16[784,128]{1,0:T(8,128)(2,1)S(1)}, bf16[784,128]{1,0:T(8,128)(2,1)S(1)}, u32[]{:S(2)}, u32[]{:S(2)}) collective-permute-start(bf16[784,128]{1,0:T(8,128)(2,1)S(1)} %get-tuple-element.179), channel_id=1, source_target_pairs={{0,1},{1,2},{2,3},{4,5},{5,6},{6,7},{8,9},{9,10},{10,11},{12,13},{... | collective-permute-start | bytes 602120 | tf_op jit(solution)/shard_map/ppermute | solution.py:1120
  47.4 16.5 %collective-permute-start.5 = (bf16[784,128]{1,0:T(8,128)(2,1)S(1)}, bf16[784,128]{1,0:T(8,128)(2,1)S(1)}, u32[]{:S(2)}, u32[]{:S(2)}) collective-permute-start(bf16[784,128]{1,0:T(8,128)(2,1)S(1)} %get-tuple-element.192), channel_id=1, source_target_pairs={{0,3},{4,7},{8,11},{12,15},{16,19},{20,23},{24,27},{28,31}} | collective-permute-start | bytes 602120 | tf_op jit(solution)/shard_map/ppermute | solution.py:1120
  53.6 10.2 %collective-permute-start.4 = (bf16[784,128]{1,0:T(8,128)(2,1)S(1)}, bf16[784,128]{1,0:T(8,128)(2,1)S(1)}, u32[]{:S(2)}, u32[]{:S(2)}) collective-permute-start(bf16[784,128]{1,0:T(8,128)(2,1)S(1)} %get-tuple-element.192), channel_id=1, source_target_pairs={{0,2},{1,3},{4,6},{5,7},{8,10},{9,11},{12,14},{13,15},{16,18},{17,... | collective-permute-start | bytes 602120 | tf_op jit(solution)/shard_map/ppermute | solution.py:1120
  57.6 9.0 %collective-permute-start.3 = (bf16[784,128]{1,0:T(8,128)(2,1)S(1)}, bf16[784,128]{1,0:T(8,128)(2,1)S(1)}, u32[]{:S(2)}, u32[]{:S(2)}) collective-permute-start(bf16[784,128]{1,0:T(8,128)(2,1)S(1)} %get-tuple-element.192), channel_id=1, source_target_pairs={{0,1},{1,2},{2,3},{4,5},{5,6},{6,7},{8,9},{9,10},{10,11},{12,13},{... | collective-permute-start | bytes 602120 | tf_op jit(solution)/shard_map/ppermute | solution.py:1120
  75.3 8.7 %collective-permute-start.7 = (bf16[4,2,192,768]{3,2,1,0:T(8,128)(2,1)S(1)}, bf16[4,2,192,768]{3,2,1,0:T(8,128)(2,1)S(1)}, u32[]{:S(2)}, u32[]{:S(2)}) collective-permute-start(bf16[4,2,192,768]{3,2,1,0:T(8,128)(2,1)S(1)} %get-tuple-element.215), channel_id=1, source_target_pairs={{0,4},{4,0},{8,12},{12,8},{16,20},{20,16},{24,28},{28,24},{1,5},{5... | collective-permute-start | bytes 7077896 | tf_op jit(solution)/shard_map/ppermute | solution.py:1099
  82.2 14.7 %collective-permute-start.9 = (bf16[4,2,192,768]{3,2,1,0:T(8,128)(2,1)S(1)}, bf16[4,2,192,768]{3,2,1,0:T(8,128)(2,1)S(1)}, u32[]{:S(2)}, u32[]{:S(2)}) collective-permute-start(bf16[4,2,192,768]{3,2,1,0:T(8,128)(2,1)S(1)} %get-tuple-element.230), channel_id=1, source_target_pairs={{0,4},{4,0},{8,12},{12,8},{16,20},{20,16},{24,28},{28,24},{1,5},{5... | collective-permute-start | bytes 7077896 | tf_op jit(solution)/shard_map/ppermute | solution.py:1099
  82.8 12.8 %collective-permute-start.6 = (bf16[784,128]{1,0:T(8,128)(2,1)S(1)}, bf16[784,128]{1,0:T(8,128)(2,1)S(1)}, u32[]{:S(2)}, u32[]{:S(2)}) collective-permute-start(bf16[784,128]{1,0:T(8,128)(2,1)S(1)} %get-tuple-element.214.refs_0_), channel_id=1, source_target_pairs={{1,0},{2,1},{3,2},{5,4},{6,5},{7,6},{9,8},{10,9},{11,10},{13,12},{... | collective-permute-start | bytes 602120 | tf_op jit(solution)/shard_map/ppermute | solution.py:1120
  95.6 13.6 %collective-permute-start.8 = (bf16[784,128]{1,0:T(8,128)(2,1)S(1)}, bf16[784,128]{1,0:T(8,128)(2,1)S(1)}, u32[]{:S(2)}, u32[]{:S(2)}) collective-permute-start(bf16[784,128]{1,0:T(8,128)(2,1)S(1)} %get-tuple-element.221), channel_id=1, source_target_pairs={{2,0},{3,1},{6,4},{7,5},{10,8},{11,9},{14,12},{15,13},{18,16},{19,... | collective-permute-start | bytes 602120 | tf_op jit(solution)/shard_map/ppermute | solution.py:1120
  98.3 28.8 %collective-permute-start.10 = (bf16[2,2,192,768]{3,2,1,0:T(8,128)(2,1)S(1)}, bf16[2,2,192,768]{3,2,1,0:T(8,128)(2,1)S(1)}, u32[]{:S(2)}, u32[]{:S(2)}) collective-permute-start(bf16[2,2,192,768]{3,2,1,0:T(8,128)(2,1)S(1)} %get-tuple-element.247), channel_id=1, source_target_pairs={{0,8},{4,12},{8,0},{12,4},{16,24},{20,28},{24,16},{28,20},{1,9},{5... | collective-permute-start | bytes 3538952 | tf_op jit(solution)/shard_map/ppermute | solution.py:1099
  99.8 27.1 %collective-permute-start.11 = (bf16[2,2,192,768]{3,2,1,0:T(8,128)(2,1)S(1)}, bf16[2,2,192,768]{3,2,1,0:T(8,128)(2,1)S(1)}, u32[]{:S(2)}, u32[]{:S(2)}) collective-permute-start(bf16[2,2,192,768]{3,2,1,0:T(8,128)(2,1)S(1)} %get-tuple-element.249), channel_id=1, source_target_pairs={{0,16},{4,20},{8,24},{12,28},{16,0},{20,4},{24,8},{28,12},{1,17},{... | collective-permute-start | bytes 3538952 | tf_op jit(solution)/shard_map/ppermute | solution.py:1099
  119.6 27.9 %copy-start.13 = (bf16[768,256]{1,0:T(8,128)(2,1)}, bf16[768,256]{1,0:T(8,128)(2,1)S(1)}, u32[]{:S(2)}) copy-start(bf16[768,256]{1,0:T(8,128)(2,1)S(1)} %get-tuple-element.273.refs_1_) | copy-start | bytes 1179652
  122.2 16.0 %collective-permute-start.15 = (bf16[4,2,96,1536]{3,2,1,0:T(8,128)(2,1)S(1)}, bf16[4,2,96,1536]{3,2,1,0:T(8,128)(2,1)S(1)}, u32[]{:S(2)}, u32[]{:S(2)}) collective-permute-start(bf16[4,2,96,1536]{3,2,1,0:T(8,128)(2,1)S(1)} %get-tuple-element.260), channel_id=1, source_target_pairs={{0,4},{4,0},{8,12},{12,8},{16,20},{20,16},{24,28},{28,24},{1,5},{5... | collective-permute-start | bytes 7077896 | tf_op jit(solution)/shard_map/ppermute | solution.py:1099
  127.3 17.5 %collective-permute-start.14 = (bf16[2,192,768]{2,1,0:T(8,128)(2,1)S(1)}, bf16[2,192,768]{2,1,0:T(8,128)(2,1)S(1)}, u32[]{:S(2)}, u32[]{:S(2)}) collective-permute-start(bf16[2,192,768]{2,1,0:T(8,128)(2,1)S(1)} %get-tuple-element.259), channel_id=1, source_target_pairs={{0,16},{4,20},{8,24},{12,28},{16,0},{20,4},{24,8},{28,12},{1,17},{... | collective-permute-start | bytes 1769480 | tf_op jit(solution)/shard_map/ppermute | solution.py:1099
  128.8 15.9 %collective-permute-start.13 = (bf16[2,192,768]{2,1,0:T(8,128)(2,1)S(1)}, bf16[2,192,768]{2,1,0:T(8,128)(2,1)S(1)}, u32[]{:S(2)}, u32[]{:S(2)}) collective-permute-start(bf16[2,192,768]{2,1,0:T(8,128)(2,1)S(1)} %get-tuple-element.258), channel_id=1, source_target_pairs={{0,8},{4,12},{8,0},{12,4},{16,24},{20,28},{24,16},{28,20},{1,9},{5... | collective-permute-start | bytes 1769480 | tf_op jit(solution)/shard_map/ppermute | solution.py:1099
  136.9 4.9 %copy-start.26 = (f32[256,768]{1,0:T(8,128)}, f32[256,768]{1,0:T(8,128)S(1)}, u32[]{:S(2)}) copy-start(f32[256,768]{1,0:T(8,128)S(1)} %get-tuple-element.268.refs_6_) | copy-start | bytes 2359300
  136.9 4.9 %copy-start.28 = (bf16[256,768]{1,0:T(8,128)(2,1)}, bf16[256,768]{1,0:T(8,128)(2,1)S(1)}, u32[]{:S(2)}) copy-start(bf16[256,768]{1,0:T(8,128)(2,1)S(1)} %get-tuple-element.267.refs_5_) | copy-start | bytes 1179652
  136.9 4.9 %copy-start.30 = (bf16[256,768]{1,0:T(8,128)(2,1)}, bf16[256,768]{1,0:T(8,128)(2,1)S(1)}, u32[]{:S(2)}) copy-start(bf16[256,768]{1,0:T(8,128)(2,1)S(1)} %get-tuple-element.265.refs_3_) | copy-start | bytes 1179652
  136.9 4.9 %copy-start.32 = (bf16[256,768]{1,0:T(8,128)(2,1)}, bf16[256,768]{1,0:T(8,128)(2,1)S(1)}, u32[]{:S(2)}) copy-start(bf16[256,768]{1,0:T(8,128)(2,1)S(1)} %get-tuple-element.266.refs_4_) | copy-start | bytes 1179652
  136.9 10.6 %copy-start.8 = (bf16[1,256,3072]{2,1,0:T(8,128)(2,1)}, bf16[1,256,3072]{2,1,0:T(8,128)(2,1)S(1)}, u32[]{:S(2)}) copy-start(bf16[1,256,3072]{2,1,0:T(8,128)(2,1)S(1)} %get-tuple-element.274) | copy-start | bytes 4718596
  136.9 9.8 %collective-permute-start.12 = (bf16[784,128]{1,0:T(8,128)(2,1)S(1)}, bf16[784,128]{1,0:T(8,128)(2,1)S(1)}, u32[]{:S(2)}, u32[]{:S(2)}) collective-permute-start(bf16[784,128]{1,0:T(8,128)(2,1)S(1)} %get-tuple-element.257.refs_0_), channel_id=1, source_target_pairs={{1,0},{2,1},{3,2},{5,4},{6,5},{7,6},{9,8},{10,9},{11,10},{13,12},{... | collective-permute-start | bytes 602120 | tf_op jit(solution)/shard_map/ppermute | solution.py:1120
  142.7 4.0 %copy-start.15 = (bf16[2,2,48,1536]{3,2,1,0:T(8,128)(2,1)}, bf16[2,2,48,1536]{3,2,1,0:T(8,128)(2,1)S(1)}, u32[]{:S(2)}) copy-start(bf16[2,2,48,1536]{3,2,1,0:T(8,128)(2,1)S(1)} %get-tuple-element.279.refs_0_) | copy-start | bytes 1769476
  142.7 13.2 %collective-permute-start.19 = (bf16[2,2,48,1536]{3,2,1,0:T(8,128)(2,1)}, bf16[2,2,48,1536]{3,2,1,0:T(8,128)(2,1)S(1)}, u32[]{:S(2)}, u32[]{:S(2)}) collective-permute-start(bf16[2,2,48,1536]{3,2,1,0:T(8,128)(2,1)} %get-tuple-element.280), channel_id=1, source_target_pairs={{0,8},{4,12},{8,0},{12,4},{16,24},{20,28},{24,16},{28,20},{1,9},{5... | collective-permute-start | bytes 1769480 | tf_op jit(solution)/shard_map/ppermute | solution.py:1099
  144.2 12.9 %collective-permute-start.20 = (bf16[2,2,48,1536]{3,2,1,0:T(8,128)(2,1)}, bf16[2,2,48,1536]{3,2,1,0:T(8,128)(2,1)S(1)}, u32[]{:S(2)}, u32[]{:S(2)}) collective-permute-start(bf16[2,2,48,1536]{3,2,1,0:T(8,128)(2,1)} %get-tuple-element.282), channel_id=1, source_target_pairs={{0,16},{4,20},{8,24},{12,28},{16,0},{20,4},{24,8},{28,12},{1,17},{... | collective-permute-start | bytes 1769480 | tf_op jit(solution)/shard_map/ppermute | solution.py:1099
  147.5 3.0 %copy-start.37 = (f32[8,768]{1,0:T(8,128)S(1)}, f32[8,768]{1,0:T(8,128)}, u32[]{:S(2)}) copy-start(f32[8,768]{1,0:T(8,128)} %get-tuple-element.298) | copy-start | bytes 73732
  150.4 8.8 %collective-permute-start.18 = (bf16[4,2,192,768]{3,2,1,0:T(8,128)(2,1)}, bf16[4,2,192,768]{3,2,1,0:T(8,128)(2,1)}, u32[]{:S(2)}, u32[]{:S(2)}) collective-permute-start(bf16[4,2,192,768]{3,2,1,0:T(8,128)(2,1)} %get-tuple-element.278), channel_id=1, source_target_pairs={{0,4},{4,0},{8,12},{12,8},{16,20},{20,16},{24,28},{28,24},{1,5},{5... | collective-permute-start | bytes 7077896 | tf_op jit(solution)/shard_map/ppermute | solution.py:1099
  150.5 130.7 %reduce-scatter.3.cloned.1.call-start = ((), (), s32[]{:S(2)}) async-start(), calls=%async_computation.2 | async-start | bytes 737280 | tf_op jit(solution)/shard_map/reduce_scatter | solution.py:1308
  150.6 6.5 %copy-start.16 = (bf16[2,2,48,1536]{3,2,1,0:T(8,128)(2,1)S(1)}, bf16[2,2,48,1536]{3,2,1,0:T(8,128)(2,1)}, u32[]{:S(2)}) copy-start(bf16[2,2,48,1536]{3,2,1,0:T(8,128)(2,1)} %copy-done.15) | copy-start | bytes 1769476
  150.6 6.5 %copy-start.19 = (bf16[2,2,48,1536]{3,2,1,0:T(8,128)(2,1)S(1)}, bf16[2,2,48,1536]{3,2,1,0:T(8,128)(2,1)}, u32[]{:S(2)}) copy-start(bf16[2,2,48,1536]{3,2,1,0:T(8,128)(2,1)} %copy-done.18) | copy-start | bytes 1769476
  150.6 25.5 %collective-permute-start.16 = (bf16[784,128]{1,0:T(8,128)(2,1)}, bf16[784,128]{1,0:T(8,128)(2,1)S(1)}, u32[]{:S(2)}, u32[]{:S(2)}) collective-permute-start(bf16[784,128]{1,0:T(8,128)(2,1)} %copy-done.6), channel_id=1, source_target_pairs={{2,0},{3,1},{6,4},{7,5},{10,8},{11,9},{14,12},{15,13},{18,16},{19,... | collective-permute-start | bytes 602120 | tf_op jit(solution)/shard_map/ppermute | solution.py:1120
  153.4 8.4 %collective-permute-start.17 = (bf16[4,2,192,768]{3,2,1,0:T(8,128)(2,1)S(1)}, bf16[4,2,192,768]{3,2,1,0:T(8,128)(2,1)S(1)}, u32[]{:S(2)}, u32[]{:S(2)}) collective-permute-start(bf16[4,2,192,768]{3,2,1,0:T(8,128)(2,1)S(1)} %get-tuple-element.277), channel_id=1, source_target_pairs={{0,4},{4,0},{8,12},{12,8},{16,20},{20,16},{24,28},{28,24},{1,5},{5... | collective-permute-start | bytes 7077896 | tf_op jit(solution)/shard_map/ppermute | solution.py:1099
  158.1 35.2 %collective-permute-start.24 = (bf16[2,48,1536]{2,1,0:T(8,128)(2,1)}, bf16[2,48,1536]{2,1,0:T(8,128)(2,1)}, u32[]{:S(2)}, u32[]{:S(2)}) collective-permute-start(bf16[2,48,1536]{2,1,0:T(8,128)(2,1)} %get-tuple-element.301), channel_id=1, source_target_pairs={{0,16},{4,20},{8,24},{12,28},{16,0},{20,4},{24,8},{28,12},{1,17},{... | collective-permute-start | bytes 884744 | tf_op jit(solution)/shard_map/ppermute | solution.py:1099
  158.6 36.3 %collective-permute-start.25 = (bf16[2,48,1536]{2,1,0:T(8,128)(2,1)}, bf16[2,48,1536]{2,1,0:T(8,128)(2,1)}, u32[]{:S(2)}, u32[]{:S(2)}) collective-permute-start(bf16[2,48,1536]{2,1,0:T(8,128)(2,1)} %get-tuple-element.302), channel_id=1, source_target_pairs={{0,8},{4,12},{8,0},{12,4},{16,24},{20,28},{24,16},{28,20},{1,9},{5... | collective-permute-start | bytes 884744 | tf_op jit(solution)/shard_map/ppermute | solution.py:1099
  161.8 14.3 %copy-start.27 = (f32[256,768]{1,0:T(8,128)S(1)}, f32[256,768]{1,0:T(8,128)}, u32[]{:S(2)}) copy-start(f32[256,768]{1,0:T(8,128)} %copy-done.26) | copy-start | bytes 2359300
  161.8 14.3 %copy-start.29 = (bf16[256,768]{1,0:T(8,128)(2,1)S(1)}, bf16[256,768]{1,0:T(8,128)(2,1)}, u32[]{:S(2)}) copy-start(bf16[256,768]{1,0:T(8,128)(2,1)} %copy-done.28) | copy-start | bytes 1179652
  161.8 14.3 %copy-start.31 = (bf16[256,768]{1,0:T(8,128)(2,1)S(1)}, bf16[256,768]{1,0:T(8,128)(2,1)}, u32[]{:S(2)}) copy-start(bf16[256,768]{1,0:T(8,128)(2,1)} %copy-done.30) | copy-start | bytes 1179652
  161.8 14.3 %copy-start.33 = (bf16[256,768]{1,0:T(8,128)(2,1)S(1)}, bf16[256,768]{1,0:T(8,128)(2,1)}, u32[]{:S(2)}) copy-start(bf16[256,768]{1,0:T(8,128)(2,1)} %copy-done.32) | copy-start | bytes 1179652
  164.3 21.4 %copy-start.10 = (bf16[2,2,192,768]{3,2,1,0:T(8,128)(2,1)}, bf16[2,2,192,768]{3,2,1,0:T(8,128)(2,1)S(1)}, u32[]{:S(2)}) copy-start(bf16[2,2,192,768]{3,2,1,0:T(8,128)(2,1)S(1)} %get-tuple-element.306.refs_0_.refs_3_) | copy-start | bytes 3538948
  176.1 10.4 %copy-start.34 = (f32[8,768]{1,0:T(8,128)S(1)}, f32[8,768]{1,0:T(8,128)}, u32[]{:S(2)}) copy-start(f32[8,768]{1,0:T(8,128)} %get-tuple-element.297) | copy-start | bytes 73732
  176.1 10.4 %copy-start.35 = (f32[8,768]{1,0:T(8,128)S(1)}, f32[8,768]{1,0:T(8,128)}, u32[]{:S(2)}) copy-start(f32[8,768]{1,0:T(8,128)} %get-tuple-element.294) | copy-start | bytes 73732
  187.0 6.2 %collective-permute-start.22 = (f32[32,768]{1,0:T(8,128)S(1)}, f32[32,768]{1,0:T(8,128)S(1)}, u32[]{:S(2)}, u32[]{:S(2)}) collective-permute-start(f32[32,768]{1,0:T(8,128)S(1)} %concatenate.7.refs_0_), channel_id=1, source_target_pairs={{0,4},{4,0},{8,12},{12,8},{16,20},{20,16},{24,28},{28,24},{1,5},{5... | collective-permute-start | bytes 294920 | tf_op jit(solution)/shard_map/ppermute | solution.py:1099
  187.1 33.3 %collective-permute-start.27 = (bf16[2,2,192,768]{3,2,1,0:T(8,128)(2,1)}, bf16[2,2,192,768]{3,2,1,0:T(8,128)(2,1)}, u32[]{:S(2)}, u32[]{:S(2)}) collective-permute-start(bf16[2,2,192,768]{3,2,1,0:T(8,128)(2,1)} %get-tuple-element.307), channel_id=1, source_target_pairs={{0,8},{4,12},{8,0},{12,4},{16,24},{20,28},{24,16},{28,20},{1,9},{5... | collective-permute-start | bytes 3538952 | tf_op jit(solution)/shard_map/ppermute | solution.py:1099
  187.7 31.7 %collective-permute-start.28 = (bf16[2,2,192,768]{3,2,1,0:T(8,128)(2,1)}, bf16[2,2,192,768]{3,2,1,0:T(8,128)(2,1)S(1)}, u32[]{:S(2)}, u32[]{:S(2)}) collective-permute-start(bf16[2,2,192,768]{3,2,1,0:T(8,128)(2,1)} %copy-done), channel_id=1, source_target_pairs={{0,16},{4,20},{8,24},{12,28},{16,0},{20,4},{24,8},{28,12},{1,17},{... | collective-permute-start | bytes 3538952 | tf_op jit(solution)/shard_map/ppermute | solution.py:1099
  193.2 31.9 %collective-permute-start.21 = (bf16[4,2,96,1536]{3,2,1,0:T(8,128)(2,1)}, bf16[4,2,96,1536]{3,2,1,0:T(8,128)(2,1)}, u32[]{:S(2)}, u32[]{:S(2)}) collective-permute-start(bf16[4,2,96,1536]{3,2,1,0:T(8,128)(2,1)} %get-tuple-element.292), channel_id=1, source_target_pairs={{0,4},{4,0},{8,12},{12,8},{16,20},{20,16},{24,28},{28,24},{1,5},{5... | collective-permute-start | bytes 7077896 | tf_op jit(solution)/shard_map/ppermute | solution.py:1099
  193.4 24.5 %collective-permute-start.23 = (f32[32,768]{1,0:T(8,128)S(1)}, f32[32,768]{1,0:T(8,128)S(1)}, u32[]{:S(2)}, u32[]{:S(2)}) collective-permute-start(f32[32,768]{1,0:T(8,128)S(1)} %get-tuple-element.300.refs_0_), channel_id=1, source_target_pairs={{0,8},{4,12},{8,0},{12,4},{16,24},{20,28},{24,16},{28,20},{1,9},{5... | collective-permute-start | bytes 294920 | tf_op jit(solution)/shard_map/ppermute | solution.py:1099
  217.8 7.1 %collective-permute-start.26 = (f32[32,768]{1,0:T(8,128)S(1)}, f32[32,768]{1,0:T(8,128)S(1)}, u32[]{:S(2)}, u32[]{:S(2)}) collective-permute-start(f32[32,768]{1,0:T(8,128)S(1)} %get-tuple-element.305.refs_0_), channel_id=1, source_target_pairs={{0,16},{4,20},{8,24},{12,28},{16,0},{20,4},{24,8},{28,12},{1,17},{... | collective-permute-start | bytes 294920 | tf_op jit(solution)/shard_map/ppermute | solution.py:1099
  223.2 16.6 %collective-permute-start.34 = (bf16[2,192,768]{2,1,0:T(8,128)(2,1)}, bf16[2,192,768]{2,1,0:T(8,128)(2,1)}, u32[]{:S(2)}, u32[]{:S(2)}) collective-permute-start(bf16[2,192,768]{2,1,0:T(8,128)(2,1)} %get-tuple-element.322), channel_id=1, source_target_pairs={{0,16},{4,20},{8,24},{12,28},{16,0},{20,4},{24,8},{28,12},{1,17},{... | collective-permute-start | bytes 1769480 | tf_op jit(solution)/shard_map/ppermute | solution.py:1099
  224.4 16.6 %collective-permute-start.33 = (bf16[2,192,768]{2,1,0:T(8,128)(2,1)}, bf16[2,192,768]{2,1,0:T(8,128)(2,1)}, u32[]{:S(2)}, u32[]{:S(2)}) collective-permute-start(bf16[2,192,768]{2,1,0:T(8,128)(2,1)} %get-tuple-element.321), channel_id=1, source_target_pairs={{0,8},{4,12},{8,0},{12,4},{16,24},{20,28},{24,16},{28,20},{1,9},{5... | collective-permute-start | bytes 1769480 | tf_op jit(solution)/shard_map/ppermute | solution.py:1099
  225.0 4.9 %collective-permute-start.31 = (f32[32,768]{1,0:T(8,128)S(1)}, f32[32,768]{1,0:T(8,128)S(1)}, u32[]{:S(2)}, u32[]{:S(2)}) collective-permute-start(f32[32,768]{1,0:T(8,128)S(1)} %get-tuple-element.318.refs_0_), channel_id=1, source_target_pairs={{0,1},{1,0},{2,3},{3,2},{4,5},{5,4},{6,7},{7,6},{8,9},{9,8},{10,11... | collective-permute-start | bytes 294920 | tf_op jit(solution)/shard_map/ppermute | solution.py:1104
  229.8 11.2 %copy-start.12 = (bf16[2,2,192,768]{3,2,1,0:T(8,128)(2,1)S(1)}, bf16[2,2,192,768]{3,2,1,0:T(8,128)(2,1)}, u32[]{:S(2)}) copy-start(bf16[2,2,192,768]{3,2,1,0:T(8,128)(2,1)} %copy-done.10) | copy-start | bytes 3538948
  229.8 11.2 %copy-start.23 = (bf16[2,2,192,768]{3,2,1,0:T(8,128)(2,1)S(1)}, bf16[2,2,192,768]{3,2,1,0:T(8,128)(2,1)}, u32[]{:S(2)}) copy-start(bf16[2,2,192,768]{3,2,1,0:T(8,128)(2,1)} %copy-done.21) | copy-start | bytes 3538948
  230.6 13.1 %collective-permute-start.32 = (f32[32,768]{1,0:T(8,128)S(1)}, f32[32,768]{1,0:T(8,128)S(1)}, u32[]{:S(2)}, u32[]{:S(2)}) collective-permute-start(f32[32,768]{1,0:T(8,128)S(1)} %get-tuple-element.320.refs_0_), channel_id=1, source_target_pairs={{0,2},{1,3},{2,0},{3,1},{4,6},{5,7},{6,4},{7,5},{8,10},{9,11},{10,... | collective-permute-start | bytes 294920 | tf_op jit(solution)/shard_map/ppermute | solution.py:1104
  230.6 21.2 %collective-permute-start.29 = (bf16[2,2,48,1536]{3,2,1,0:T(8,128)(2,1)}, bf16[2,2,48,1536]{3,2,1,0:T(8,128)(2,1)S(1)}, u32[]{:S(2)}, u32[]{:S(2)}) collective-permute-start(bf16[2,2,48,1536]{3,2,1,0:T(8,128)(2,1)} %get-tuple-element.315), channel_id=1, source_target_pairs={{0,8},{4,12},{8,0},{12,4},{16,24},{20,28},{24,16},{28,20},{1,9},{5... | collective-permute-start | bytes 1769480 | tf_op jit(solution)/shard_map/ppermute | solution.py:1099
  232.2 19.7 %collective-permute-start.30 = (bf16[2,2,48,1536]{3,2,1,0:T(8,128)(2,1)}, bf16[2,2,48,1536]{3,2,1,0:T(8,128)(2,1)}, u32[]{:S(2)}, u32[]{:S(2)}) collective-permute-start(bf16[2,2,48,1536]{3,2,1,0:T(8,128)(2,1)} %get-tuple-element.317), channel_id=1, source_target_pairs={{0,16},{4,20},{8,24},{12,28},{16,0},{20,4},{24,8},{28,12},{1,17},{... | collective-permute-start | bytes 1769480 | tf_op jit(solution)/shard_map/ppermute | solution.py:1099
  243.7 15.3 %collective-permute-start.37 = (bf16[384,768]{1,0:T(8,128)(2,1)}, bf16[384,768]{1,0:T(8,128)(2,1)S(1)}, u32[]{:S(2)}, u32[]{:S(2)}) collective-permute-start(bf16[384,768]{1,0:T(8,128)(2,1)} %get-tuple-element.329), channel_id=1, source_target_pairs={{0,1},{1,0},{2,3},{3,2},{4,5},{5,4},{6,7},{7,6},{8,9},{9,8},{10,11... | collective-permute-start | bytes 1769480 | tf_op jit(solution)/shard_map/ppermute | solution.py:1104
  243.8 8.1 %copy-start.4 = (bf16[2,2,48,1536]{3,2,1,0:T(8,128)(2,1)S(1)}, bf16[2,2,48,1536]{3,2,1,0:T(8,128)(2,1)}, u32[]{:S(2)}) copy-start(bf16[2,2,48,1536]{3,2,1,0:T(8,128)(2,1)} %copy-done.3) | copy-start | bytes 1769476
  251.9 7.1 %copy-start.25 = (bf16[384,768]{1,0:T(8,128)(2,1)S(1)}, bf16[384,768]{1,0:T(8,128)(2,1)}, u32[]{:S(2)}) copy-start(bf16[384,768]{1,0:T(8,128)(2,1)} %copy-done.24) | copy-start | bytes 1769476
  253.2 7.5 %collective-permute-start.35 = (bf16[2,48,1536]{2,1,0:T(8,128)(2,1)S(1)}, bf16[2,48,1536]{2,1,0:T(8,128)(2,1)S(1)}, u32[]{:S(2)}, u32[]{:S(2)}) collective-permute-start(bf16[2,48,1536]{2,1,0:T(8,128)(2,1)S(1)} %get-tuple-element.326), channel_id=1, source_target_pairs={{0,16},{4,20},{8,24},{12,28},{16,0},{20,4},{24,8},{28,12},{1,17},{... | collective-permute-start | bytes 884744 | tf_op jit(solution)/shard_map/ppermute | solution.py:1099
  253.8 7.2 %collective-permute-start.36 = (bf16[2,48,1536]{2,1,0:T(8,128)(2,1)S(1)}, bf16[2,48,1536]{2,1,0:T(8,128)(2,1)S(1)}, u32[]{:S(2)}, u32[]{:S(2)}) collective-permute-start(bf16[2,48,1536]{2,1,0:T(8,128)(2,1)S(1)} %get-tuple-element.327), channel_id=1, source_target_pairs={{0,8},{4,12},{8,0},{12,4},{16,24},{20,28},{24,16},{28,20},{1,9},{5... | collective-permute-start | bytes 884744 | tf_op jit(solution)/shard_map/ppermute | solution.py:1099
  259.1 17.5 %collective-permute-start.40 = (bf16[192,768]{1,0:T(8,128)(2,1)S(1)}, bf16[192,768]{1,0:T(8,128)(2,1)S(1)}, u32[]{:S(2)}, u32[]{:S(2)}) collective-permute-start(bf16[192,768]{1,0:T(8,128)(2,1)S(1)} %get-tuple-element.339), channel_id=1, source_target_pairs={{0,2},{1,3},{2,0},{3,1},{4,6},{5,7},{6,4},{7,5},{8,10},{9,11},{10,... | collective-permute-start | bytes 884744 | tf_op jit(solution)/shard_map/ppermute | solution.py:1104
  262.3 14.1 %collective-permute-start.38 = (bf16[96,1536]{1,0:T(8,128)(2,1)S(1)}, bf16[96,1536]{1,0:T(8,128)(2,1)S(1)}, u32[]{:S(2)}, u32[]{:S(2)}) collective-permute-start(bf16[96,1536]{1,0:T(8,128)(2,1)S(1)} %get-tuple-element.333), channel_id=1, source_target_pairs={{0,1},{1,0},{2,3},{3,2},{4,5},{5,4},{6,7},{7,6},{8,9},{9,8},{10,11... | collective-permute-start | bytes 884744 | tf_op jit(solution)/shard_map/ppermute | solution.py:1104
  276.5 6.7 %collective-permute-start.39 = (bf16[96,768]{1,0:T(8,128)(2,1)S(1)}, bf16[96,768]{1,0:T(8,128)(2,1)S(1)}, u32[]{:S(2)}, u32[]{:S(2)}) collective-permute-start(bf16[96,768]{1,0:T(8,128)(2,1)S(1)} %get-tuple-element.336), channel_id=1, source_target_pairs={{0,2},{1,3},{2,0},{3,1},{4,6},{5,7},{6,4},{7,5},{8,10},{9,11},{10,... | collective-permute-start | bytes 442376 | tf_op jit(solution)/shard_map/ppermute | solution.py:1104
  (18 other events, 29.3 us)
Sparse Core Ops, SparseCore 0:
  150.7 35.4 reduce-scatter.4
  225.2 23.7 reduce-scatter.2

commit v3 on v2

--- a/solution.py
+++ b/solution.py
@@ -143,8 +143,8 @@
     smem = pl.BlockSpec(memory_space=pltpu.SMEM)
     for name in in_names:
         mode, array = ins[name][:2]
-        operands.append(Box(d=in_hbm, v=in_vmem).get(mode, whole_cut)(array))
-        in_specs.append(Box(v=vmem, s=smem, d=hbm)[mode])
+        operands.append(Box(d=in_hbm, r=in_hbm, v=in_vmem).get(mode, whole_cut)(array))
+        in_specs.append(Box(v=vmem, s=smem, d=hbm, r=hbm)[mode])
     fetch_names = [name for name in out_names if outs[name][0] == "f"]
     for name in fetch_names:
         operands.append(in_hbm(outs[name][1]))
@@ -166,7 +166,7 @@
     for name in out_names:
         mode = outs[name][0]
         if mode == "f":
-            array, cuts, block = outs[name][1:]
+            array, cuts, block = outs[name][1:4]
             out_shapes.append(pltpu.VMEM((len(cuts),) + block, array.dtype))
             copy_count += len(cuts)
         else:
@@ -219,7 +219,9 @@
             mode = outs[name][0]
             if mode == "f":
                 for at, cut in enumerate(outs[name][2]):
-                    fetches.append(make(cut(fetch_refs[name]), out_refs[name].at[at]))
+                    source = fetch_refs[name]
+                    source = cut(source, io) if len(outs[name]) > 4 else cut(source)
+                    fetches.append(make(source, out_refs[name].at[at]))
                 io.refs[name] = out_refs[name]
             elif mode == "h":
                 buffer = spare.pop(0)
@@ -264,18 +266,26 @@
     return [lambda ref, j=j: ref.at[layer, pl.ds(D * j, D), :] for j in range(parts)], (D, D)
 
 
+def half_of(rows, own):
+    def cut(ref, io):
+        along = io.spot[1] if own else 1 - io.spot[1]
+        return ref.at[:, pl.ds(pl.multiple_of(along * (FF // 2), LANES), FF // 2)]
+
+    return [cut], (rows, FF // 2), True
+
+
 def layer_of(layer, block):
     return [lambda ref: ref.at[layer]], block
 
 
-COSTS = [120, 10, 15, 60, 0.3, 30, 30, 120, 0.3, 0.3, 1, 30, 120, 3, 10, 6, 15, 6, 1, 6, 3, 0.3, 22, 30, 22, 22, 3, 6, 22, 10, 120, 3, 10, 0.3, 3, 10, 120, 3, 10, 60, 0.3, 30, 0.3]
+COSTS = [10, 10, 10, 10, 10, 10, 10, 3, 120, 30, 10, 3, 30, 120, 60, 10, 60, 1, 3, 0.3, 60, 30, 6, 120, 0.3, 3, 120, 3, 1, 10, 6, 10, 6, 3, 22, 30, 30, 15, 60, 3, 10, 3]
 
 
 class Counter:
     at = 0
 
 
-def project(layer, x, x_mode, wq, vecs, cs, long, deps):
+def project(layer, spot, x, x_mode, wq, vecs, cs, fetches, deps):
     rows = x.shape[0]
 
     def body(io):
@@ -293,8 +303,7 @@
             bias = vector(io, "qkv_bias", layer)[:, D * j : D * (j + 1)]
             pk = low(nn(xb, w[...]) + bias)
             io.packed[:, D * j : D * (j + 1)] = pk
-            if long:
-                io.kept[:, D * j : D * (j + 1)] = pk
+            io.kept[:, D * j : D * (j + 1)] = pk
             pf = up(pk)
             cs_now = io.cs[...]
             for p in range(2):
@@ -314,19 +323,18 @@
                 totals = jnp.where(lane_state == 2 * pair, swap(s0), totals)
                 totals = jnp.where(lane_state == 2 * pair + 1, s1, totals)
         io.state[PAIRS * LANES :, :] = low(totals.T[:16])
-        if long:
-            io.done("kept")
+        io.done("kept")
 
     outs = Box(
         packed=("v", shape(rows, 3 * D, dtype=BF)),
         xt=("h", shape(D, rows, dtype=BF)),
         state=("v", shape(STATE_ROWS, LANES, dtype=BF)),
     )
-    if long:
-        outs.kept = ("h", shape(rows, 3 * D, dtype=BF))
+    outs.kept = ("h", shape(rows, 3 * D, dtype=BF))
+    outs.update(fetches)
     return run(
         body,
-        Box(x=(x_mode, x), wq=wq, cs=("d", cs), **vecs),
+        Box(spot=("s", spot), x=(x_mode, x), wq=wq, cs=("d", cs), **vecs),
         outs,
         deps,
         flops=2 * rows * D * 3 * D,
@@ -334,7 +342,7 @@
     )
 
 
-def inside(packed, cm, long, fetches, deps):
+def inside(spot, packed, cm, long, fetches, deps):
     rows = packed.shape[0]
 
     def body(io):
@@ -374,7 +382,7 @@
     outs.update(fetches)
     return run(
         body_all,
-        Box(packed=("v", packed), cm=("d", cm)),
+        Box(spot=("s", spot), packed=("v", packed), cm=("d", cm)),
         outs,
         deps,
         flops=4 * HEADS * rows * rows * LANES,
@@ -552,7 +560,7 @@
     )
 
 
-def layer_back(layer, top, kept, mode, weights, vecs, cs, fetches, deps):
+def layer_back(layer, spot, top, kept, mode, weights, vecs, cs, fetches, deps, after=None):
     rows = top.gz2.shape[0]
 
     def body(io):
@@ -609,6 +617,9 @@
     )
     for name in ("slope", "n1", "r1", "inv", "mixed", "sq"):
         ins[name] = (mode, kept[name])
+    if after is not None:
+        ins.after = ("r", after)
+    ins.spot = ("s", spot)
     ins.gains = vecs.gains
     ins.cs = ("d", cs)
     outs = Box(
@@ -805,6 +816,30 @@
                 )
 
 
+def pair_terms(io, core, put):
+    near, far = io.spot[3], io.spot[4]
+    tokens = io.hid.shape[1]
+    width = FF // 8
+    io.lhs[:, :tokens] = io.gb2t[...]
+    io.lhs[:, tokens:] = io.gb2t_got[...]
+    for across in range(2):
+        block = (io.spot[2] ^ across) * 2 + core
+        lanes = pl.ds(pl.multiple_of(block * width, LANES), width)
+        io.rhs[:tokens, across * width : (across + 1) * width] = io.hid[0, :, lanes]
+        io.rhs[tokens:, across * width : (across + 1) * width] = io.hid_got[0, :, lanes]
+    grad = nn(io.lhs[...], io.rhs[...])
+    for across in range(2):
+        for n in range(4):
+            lanes = pl.ds(pl.multiple_of(((n // 2) ^ far) * width, LANES), width)
+            put(
+                across,
+                (n % 2) ^ near,
+                None,
+                lanes,
+                grad[n * 192 : (n + 1) * 192, across * width : (across + 1) * width],
+            )
+
+
 def gather_rows(io, name, target, core):
     for at, block in enumerate(owners(io.spot, core)):
         io[target][at * 96 : (at + 1) * 96, :] = io[name][
@@ -843,7 +878,7 @@
     return pl.ds(pl.multiple_of(part * count, 16), count)
 
 
-TERMS = Box(out=out_terms, inner=in_terms, mix=mix_terms)
+TERMS = Box(pair=pair_terms, out=out_terms, inner=in_terms, mix=mix_terms)
 
 
 def grad_setup(kind, spot, operands):
@@ -854,6 +889,12 @@
         ins.gb2t = ("v", gb2t)
         ins.hid = ("v", hid)
         return ins, Box(rhs=pltpu.VMEM((tokens, FF // 2), BF)), (192, D), tokens
+    if kind == "pair":
+        for name, array in zip(("gb2t", "gb2t_got", "hid", "hid_got"), operands):
+            ins[name] = ("v", array)
+        tokens = 2 * operands[0].shape[1]
+        both = Box(lhs=pltpu.VMEM((D, tokens), BF), rhs=pltpu.VMEM((tokens, D), BF))
+        return ins, both, (192, D), tokens
     lhs = pltpu.VMEM((D // 2, operands[0].shape[1]), BF)
     if kind == "inner":
         midt, gpre = operands
@@ -879,7 +920,7 @@
     outs, token = run(
         body,
         ins,
-        Box(send=("v", shape(4, 2, *block, dtype=BF))),
+        Box(send=("v", shape(2 if kind == "pair" else 4, 2, *block, dtype=BF))),
         deps,
         scratch=scratch,
         flops=2 * tokens * 8 * block[0] * block[1],
@@ -903,7 +944,9 @@
             rows = part_rows(part, count)
             value = low(value + up(io.got[at, slot, rows, lanes]))
             across, along = at // 2, at % 2
-            if order == "x":
+            if kind == "pair":
+                io["send0" if at else "keep0"][slot, rows, lanes] = value
+            elif order == "x":
                 io["send0" if across else "keep0"][along, slot, rows, lanes] = value
             elif order == "y":
                 io["send0" if along else "keep0"][across, slot, rows, lanes] = value
@@ -919,7 +962,10 @@
     return run(
         body,
         ins,
-        {name: ("v", shape(2, 2, *half, dtype=BF)) for name in names},
+        {
+            name: ("v", shape(*((2,) if kind == "pair" else (2, 2)), *half, dtype=BF))
+            for name in names
+        },
         deps,
         scratch=scratch,
         flops=2 * tokens * 8 * block[0] * block[1],
@@ -956,11 +1002,14 @@
     for which, group in enumerate(groups):
         for at in halves_of(group):
             for name in ("keep", "got", "come"):
-                ins["%s%d_%d" % (name, which, at)] = ("v", group["%s%d" % (name, at)])
+                if "%s%d" % (name, at) in group:
+                    ins["%s%d_%d" % (name, which, at)] = ("v", group["%s%d" % (name, at)])
     return ins
 
 
 def group_sum(io, which, at, slot):
+    if "come%d_%d" % (which, at) not in io.refs:
+        return up(io["keep%d_%d" % (which, at)][slot]) + up(io["got%d_%d" % (which, at)][slot])
     return (
         up(io["keep%d_%d" % (which, at)][0, slot])
         + up(io["got%d_%d" % (which, at)][0, slot])
@@ -971,13 +1020,13 @@
 def grad_near(groups, deps):
     ins = group_ins(groups)
     places = [(which, at) for which, group in enumerate(groups) for at in halves_of(group)]
-    total = sum(group["keep%d" % at].shape[2] for group in groups for at in halves_of(group))
-    lanes = groups[0].keep0.shape[3]
+    total = sum(group["keep%d" % at].shape[-2] for group in groups for at in halves_of(group))
+    lanes = groups[0].keep0.shape[-1]
 
     def body(io):
         start = 0
         for which, at in places:
-            rows = groups[which]["keep%d" % at].shape[2]
+            rows = groups[which]["keep%d" % at].shape[-2]
             here = slice(start, start + rows)
             io.near[here, :] = low(group_sum(io, which, at, 1))
             io.stay[here, :] = low(group_sum(io, which, at, 0))
@@ -1045,9 +1094,12 @@
             if kind == "out":
                 io.own[here, :] = beside(part[:96, : D // 2], part[96:, : D // 2])
                 io.far[here, :] = low(beside(part[:96, D // 2 :], part[96:, D // 2 :]))
-            else:
+            elif kind == "inner":
                 io.own[here, :] = part[:96]
                 io.far[here, :] = low(part[96:])
+            else:
+                io.own[here, :] = above(part[:48], part[96:144])
+                io.far[here, :] = low(above(part[48:96], part[144:]))
 
     return run(
         body,
@@ -1122,6 +1174,27 @@
 
 def travel(state, step):
     return [move(state, step * shift) for shift in range(1, lax.axis_size("narrow"))]
+
+
+SUM_ROWS = (3, 7, 3)
+
+
+def collect_sums(parts, deps):
+    def body(io):
+        io.sums[...] = jnp.zeros((32, D), F32)
+        start = 0
+        for at in range(len(parts)):
+            rows = SUM_ROWS[at % 3]
+            io.sums[start : start + rows, :] = io["part%d" % at][:rows, :]
+            start += rows
+
+    outs, token = run(
+        body,
+        Box({"part%d" % at: ("d", part) for at, part in enumerate(parts)}),
+        Box(sums=("v", shape(32, D))),
+        deps,
+    )
+    return outs.sums, token
 
 
 def add_up(a, b, deps):
@@ -1193,16 +1266,19 @@
     deps = ()
     for layer in range(LAYERS):
         last = layer == LAYERS - 1
-        first, token = project(
-            layer, x, "v" if layer else "d", wq, Box(qkv_bias=("d", qkv_bias)), cs, True, deps
-        )
+        hidden = last and fast
+        fetches = Box(hid_send=("f", saved[0].hid) + half_of(rows, False)) if hidden else Box()
+        x_mode = "v" if layer else "d"
+        bias = Box(qkv_bias=("d", qkv_bias))
+        first, token = project(layer, spot, x, x_mode, wq, bias, cs, fetches, deps)
+        hid_got = wide_swap(first.hid_send, ALONG) if hidden else None
         if not layer:
             cm = mask(step + token[0, 0])
         recv = travel(first.state, 1)
         fetches = weight_fetch(layer)
         if not last:
             fetches.wq = ("f", qkv_weight) + columns_of(layer + 1, 3)
-        inner, token = inside(first.packed, cm, not last, fetches, (token,))
+        inner, token = inside(spot, first.packed, cm, not last, fetches, (token,))
         weights = inner
         kept, token = layer_forward(
             layer,
@@ -1236,7 +1312,7 @@
             kept = saved[layer]
             fetch = Box() if layer == 1 else Box()
             back, token = layer_back(
-                layer, top, kept, "v" if layer else "d", weights, vecs, cs, fetch, (token,)
+                layer, spot, top, kept, "v" if layer else "d", weights, vecs, cs, fetch, (token,)
             )
             recv = travel(back.state, -1)
             below = saved[0] if layer == 1 else None
@@ -1301,20 +1377,21 @@
             found, token = grad_far(kinds, *pair, (token,))
             return (found.own, narrow_swap(found.far, FAR)), token
 
-        def gather(kinds, names, token):
+        def gather(kinds, names, token, *after):
             for name in names:
                 group[name].spot = spot
-            blocks, token = grad_collect(kinds, [group[name] for name in names], (token,))
+            groups = [group[name] for name in names]
+            blocks, token = grad_collect(kinds, groups, (token, *after))
             mine = lax.psum_scatter(blocks, "narrow", scatter_dimension=0, tiled=True)
             return (mine.reshape(mine.shape[1:]),), token
 
         token = send("o1", "out", (one.gb2t, one.hid), token)
-        back1, token = layer_back(1, one, one, "v", weights, vecs, cs, Box(), (token,))
-        later1 = [move(back1.state, -1)]
+        back1, token = layer_back(
+            1, spot, one, one, "v", weights, vecs, cs, Box(), (token,), hid_got
+        )
+        later1 = travel(back1.state, -1)
         token = send("i1", "inner", (one.midt, back1.gpre), token)
         token = keep("o1", "y", token)
-        both, token = add_up(back1.state, later1[0], (token,))
-        later1.append(move(both, -2))
         token = keep("i1", "x", token)
         mix1, token = mix_back(
             1, later1, spot, back1, one, cs, cm, wq_cuts[1], zero, weight_fetch(0), (token,)
@@ -1322,59 +1399,51 @@
         token = send("m1", "mix", (one.mixt, one.xt, mix1.gcol), token)
         token = forward(["o1"], token)
         token = forward(["i1"], token)
+        gb2t_got = wide_swap(mix1.gb2t, ALONG)
         fetch = Box(
-            hid=("f", zero.hid, [whole_cut], (rows, FF)),
+            hid=("f", zero.hid) + half_of(rows, True),
+            hid_got=("f", hid_got, [lambda ref: ref.at[0]], (rows, FF // 2)),
             midt=("f", zero.midt, [whole_cut], (D, rows)),
         )
         weights = mix1
-        back0, token = layer_back(0, mix1, zero, "d", weights, vecs, cs, fetch, (token,))
+        back0, token = layer_back(0, spot, mix1, zero, "d", weights, vecs, cs, fetch, (token,))
         later0 = [move(back0.state, -1)]
         token = keep("m1", "both", token)
-        f1, token = gather(["out", "inner"], ["o1", "i1"], token)
+        pair = (mix1.gb2t, gb2t_got, back0.hid, back0.hid_got)
+        token = send("o0", "pair", pair, token)
         both, token = add_up(back0.state, later0[0], (token,))
         later0.append(move(both, -2))
-        token = send("o0", "out", (mix1.gb2t, back0.hid.reshape(rows, FF)), token)
         token = send("i0", "inner", (back0.midt.reshape(D, rows), back0.gpre), token)
         token = forward(["m1"], token)
-        token = keep("o0", "y", token)
-        token = keep("i0", "x", token)
+        token = keep("o0", "x", token)
+        token = keep("i0", "both", token)
+        f1, token = gather(["out", "inner"], ["o1", "i1"], token, later0[1])
         mix0, token = mix_back(
             0, later0, spot, back0, zero, cs, cm, wq_cuts[0], None, Box(), (token,)
         )
         input_grad = mix0.grad
-        sums = jnp.concatenate(
-            [
-                mix1.sums_a[:3],
-                back0.sums_b[:7],
-                mix0.sums_c[:3],
-                one.sums_a[:3],
-                back1.sums_b[:7],
-                mix1.sums_c[:3],
-                jnp.zeros((6, D), F32),
-            ],
-            axis=0,
-        )
+        parts = (mix1.sums_a, back0.sums_b, mix0.sums_c, one.sums_a, back1.sums_b, mix1.sums_c)
         token = send("m0", "mix", (zero.mixt, zero.xt, mix0.gcol), token)
+        token = forward(["i0"], token)
+        token = keep("m0", "both", token)
+        near_f0, token = near(["o0", "i0"], token)
+        sums, token = collect_sums(parts, (token,))
         come = wide_swap(sums, CORE)
+        mg1, token = gather(["mix"], ["m1"], token)
         sums, token = add_up(sums, come, (token,))
         come = wide_swap(sums, ACROSS)
-        mg1, token = gather(["mix"], ["m1"], token)
+        token = forward(["m0"], token)
         sums, token = add_up(sums, come, (token,))
         come = wide_swap(sums, ALONG)
-        token = forward(["o0"], token)
-        token = forward(["i0"], token)
+        far_f0, token = far(["out", "inner both"], near_f0, token)
         sums, token = add_up(sums, come, (token,))
         come = narrow_swap(sums, NEAR)
-        token = keep("m0", "both", token)
+        near_m0, token = near(["m0"], token)
         sums, token = add_up(sums, come, (token,))
         come = narrow_swap(sums, FAR)
-        near_f0, token = near(["o0", "i0"], token)
-        sums, token = add_up(sums, come, (token,))
-        token = forward(["m0"], token)
-        far_f0, token = far(["out", "inner"], near_f0, token)
-        near_m0, token = near(["m0"], token)
         far_m0, token = far(["mix"], near_m0, token)
         ffn_grads, token = grad_last("ffn", [far_f0, f1], (token,))
+        sums, token = add_up(sums, come, (token,))
         mix_grads, token = grad_last("mix", [far_m0, mg1], (token,))
         sums = sums[:26].reshape(LAYERS, 13, D)
         grad_qkv, grad_o = mix_grads.first, mix_grads.second

time: 297 us -> 285 us (0.960)
  waiting for transfers between devices: 96.8 us -> 60.8 us
  starting transfers between devices: 48.9 us -> 72.1 us
  Pallas kernels: 116 us -> 119 us
    ppermute x10 -> x11, waiting for transfers between devices: 33.2 us -> 13.7 us  [move(): return lax.ppermute(v, 'narrow', pairs)]
    ppermute x25 -> x28, waiting for transfers between devices: 45 us -> 27.5 us  [wide_swap(): return lax.ppermute(v, 'wide', [(i, i ^ bit) for i in range(size)])]
    ppermute x6, starting transfers between devices: 0.36 us -> 15.6 us  [narrow_swap(): return lax.ppermute(v, 'narrow', [(i, i ^ bit) for i in range(size)])]
    ppermute x25 -> x28, starting transfers between devices: 20.3 us -> 25.5 us  [wide_swap(): return lax.ppermute(v, 'wide', [(i, i ^ bit) for i in range(size)])]
    pallas_call x43 -> x42, Pallas kernels: 116 us -> 119 us  [run(): pl.pallas_call(kernel, out_shape=tuple(out_shapes), in_specs=in_specs, ou...]
    ppermute x10 -> x11, starting transfers between devices: 28.2 us -> 30.7 us  [move(): return lax.ppermute(v, 'narrow', pairs)]
    unnamed x83 -> x65, local copies, waits for them, and re-layouts: 7.75 us -> 6.74 us
  transfers between devices with their start and end apart: 43 -> 47, of which waited for: 17 -> 17; matrix products, arithmetic and copies ran while one was open for 3% -> 2% of each run, Pallas kernels for 30% -> 35%
where the time goes in v3:
time: 285 us; the launch traced here: 281 us
  Pallas kernels  119 us (42%)
  starting transfers between devices  72.1 us (25%)
  waiting for transfers between devices  60.8 us (21%)
  between operations  16.9 us (6%)
  local copies, waits for them, and re-layouts  8.83 us (3%)
  other arithmetic  3.54 us (1%)
    pallas_call x42, Pallas kernels, run(): pl.pallas_call(kernel, out_shape=tuple(out_shapes), in_specs=in_specs, ou...  119 us
    ppermute x11, starting transfers between devices, move(): return lax.ppermute(v, 'narrow', pairs)  30.7 us
    ppermute x28, waiting for transfers between devices, wide_swap(): return lax.ppermute(v, 'wide', [(i, i ^ bit) for i in range(size)])  27.5 us
    ppermute x28, starting transfers between devices, wide_swap(): return lax.ppermute(v, 'wide', [(i, i ^ bit) for i in range(size)])  25.5 us
    ppermute x6, waiting for transfers between devices, narrow_swap(): return lax.ppermute(v, 'narrow', [(i, i ^ bit) for i in range(size)])  19.5 us
    ppermute x6, starting transfers between devices, narrow_swap(): return lax.ppermute(v, 'narrow', [(i, i ^ bit) for i in range(size)])  15.6 us
    ppermute x11, waiting for transfers between devices, move(): return lax.ppermute(v, 'narrow', pairs)  13.7 us
    unnamed x65, local copies, waits for them, and re-layouts  6.74 us
  transfers between devices with their start and end apart: 47, of which 17 were waited for; matrix products, arithmetic and copies ran while one was open for 2% of the time, Pallas kernels for 35%

profile of v3, /device:TPU:0, one launch (start us, length us, event | category | flops | bytes accessed | tf_op | source)
XLA Modules:
  0.0 281.2 jit_solution(3889957137988735825)
XLA Ops:
  9.1 6.6 %shard_map.186 = (bf16[256,2304]{1,0:T(8,128)(2,1)S(1)}, bf16[768,256]{1,0:T(8,128)(2,1)}, bf16[784,128]{1,0:T(8,128)(2,1)S(1)}, bf16[256,2304]{1,0:T(8,128)(2,1)}, f32[8,128]{1,0:T(8,128)S(1)}) custom-call(s32[6]{0:T(128)S(1)} %stack.33.refs_0_.refs_12_.refs_3_.refs_11_.refs_6_.refs_2_, bf16[256,768]{1,0:T(8,128)(2,1)} %refs_3_.4, ...), custom_call_target="tpu_custom_call" | custom-call | flops 10000000000 | bytes 100000000 | tf_op jit(solution)/shard_map/pallas_call | solution.py:247
  15.7 4.9 %collective-permute-start = (bf16[784,128]{1,0:T(8,128)(2,1)S(1)}, bf16[784,128]{1,0:T(8,128)(2,1)S(1)}, u32[]{:S(2)}, u32[]{:S(2)}) collective-permute-start(bf16[784,128]{1,0:T(8,128)(2,1)S(1)} %get-tuple-element.182), channel_id=1, source_target_pairs={{0,1},{1,2},{2,3},{4,5},{5,6},{6,7},{8,9},{9,10},{10,11},{12,13},{... | collective-permute-start | bytes 602120 | tf_op jit(solution)/shard_map/ppermute | solution.py:1172
  20.6 4.5 %collective-permute-start.1 = (bf16[784,128]{1,0:T(8,128)(2,1)S(1)}, bf16[784,128]{1,0:T(8,128)(2,1)S(1)}, u32[]{:S(2)}, u32[]{:S(2)}) collective-permute-start(bf16[784,128]{1,0:T(8,128)(2,1)S(1)} %get-tuple-element.182), channel_id=1, source_target_pairs={{0,2},{1,3},{4,6},{5,7},{8,10},{9,11},{12,14},{13,15},{16,18},{17,... | collective-permute-start | bytes 602120 | tf_op jit(solution)/shard_map/ppermute | solution.py:1172
  25.1 1.5 collective-permute-start.2
  29.2 6.0 %shard_map.187 = (f32[256,768]{1,0:T(8,128)S(1)}, f32[256,768]{1,0:T(8,128)S(1)}, bf16[256,768]{1,0:T(8,128)(2,1)S(1)}, bf16[256,768]{1,0:T(8,128)(2,1)}, bf16[1...) custom-call(s32[6]{0:T(128)S(1)} %stack.33.refs_0_.refs_12_.refs_3_., ...), custom_call_target="tpu_custom_call" | custom-call | flops 10000000000 | bytes 100000000 | tf_op jit(solution)/shard_map/pallas_call | solution.py:247
  35.2 8.2 %shard_map.188 = (bf16[784,128]{1,0:T(8,128)(2,1)}, bf16[256,768]{1,0:T(8,128)(2,1)}, bf16[768,256]{1,0:T(8,128)(2,1)}, f32[256,768]{1,0:T(8,128)}, f32[256,768]...) custom-call(bf16[784,128]{1,0:T(8,128)(2,1)S(1)} %collective-permute, ...), custom_call_target="tpu_custom_call" | custom-call | flops 10000000000 | bytes 100000000 | tf_op jit(solution)/shard_map/pallas_call | solution.py:247
  43.4 4.8 %shard_map.189 = (bf16[256,2304]{1,0:T(8,128)(2,1)S(1)}, bf16[768,256]{1,0:T(8,128)(2,1)}, bf16[784,128]{1,0:T(8,128)(2,1)S(1)}, bf16[256,2304]{1,0:T(8,128)(2,1...) custom-call(s32[6]{0:T(128)S(1)} %stack.33.refs_0_.refs_12_.refs_3_.refs_11_.refs_6_.refs_2_, ...), custom_call_target="tpu_custom_call" | custom-call | flops 10000000000 | bytes 100000000 | tf_op jit(solution)/shard_map/pallas_call | solution.py:247
  48.2 6.0 %collective-permute-start.3 = (bf16[784,128]{1,0:T(8,128)(2,1)S(1)}, bf16[784,128]{1,0:T(8,128)(2,1)S(1)}, u32[]{:S(2)}, u32[]{:S(2)}) collective-permute-start(bf16[784,128]{1,0:T(8,128)(2,1)S(1)} %get-tuple-element.196), channel_id=1, source_target_pairs={{0,1},{1,2},{2,3},{4,5},{5,6},{6,7},{8,9},{9,10},{10,11},{12,13},{... | collective-permute-start | bytes 602120 | tf_op jit(solution)/shard_map/ppermute | solution.py:1172
  54.2 5.3 %collective-permute-start.4 = (bf16[784,128]{1,0:T(8,128)(2,1)S(1)}, bf16[784,128]{1,0:T(8,128)(2,1)S(1)}, u32[]{:S(2)}, u32[]{:S(2)}) collective-permute-start(bf16[784,128]{1,0:T(8,128)(2,1)S(1)} %get-tuple-element.196), channel_id=1, source_target_pairs={{0,2},{1,3},{4,6},{5,7},{8,10},{9,11},{12,14},{13,15},{16,18},{17,... | collective-permute-start | bytes 602120 | tf_op jit(solution)/shard_map/ppermute | solution.py:1172
  59.5 1.7 collective-permute-start.5
  61.2 1.6 collective-permute-start.6
  62.8 4.8 %shard_map.190 = (f32[256,768]{1,0:T(8,128)S(1)}, f32[256,768]{1,0:T(8,128)S(1)}, bf16[256,768]{1,0:T(8,128)(2,1)S(1)}, bf16[1,768,768]{2,1,0:T(8,128)(2,1)S(1)}...) custom-call(s32[6]{0:T(128)S(1)} %stack.33.refs_0_.refs_12_.refs_3_.refs_11_.refs_6_.refs_, ...), custom_call_target="tpu_custom_call" | custom-call | flops 10000000000 | bytes 100000000 | tf_op jit(solution)/shard_map/pallas_call | solution.py:247
  67.6 7.4 %shard_map.191 = (bf16[784,128]{1,0:T(8,128)(2,1)}, bf16[256,768]{1,0:T(8,128)(2,1)S(1)}, bf16[768,256]{1,0:T(8,128)(2,1)}, f32[256,768]{1,0:T(8,128)S(1)}, f32[...) custom-call(bf16[784,128]{1,0:T(8,128)(2,1)S(1)} %collective-permute, ...), custom_call_target="tpu_custom_call" | custom-call | flops 10000000000 | bytes 100000000 | tf_op jit(solution)/shard_map/pallas_call | solution.py:247
  75.0 1.4 shard_map.192
  76.5 2.6 collective-permute-done.6.refs_11_.refs_15_
  80.1 6.6 %shard_map.193 = (bf16[256,3072]{1,0:T(8,128)(2,1)S(1)}, bf16[256,768]{1,0:T(8,128)(2,1)S(1)}, f32[256,768]{1,0:T(8,128)S(1)}, bf16[256,768]{1,0:T(8,128)(2,1)S(...) custom-call(f32[256,768]{1,0:T(8,128)S(1)} %get-tuple-element.207.refs_0_, ...), custom_call_target="tpu_custom_call" | custom-call | flops 3000000000 | bytes 100000000 | tf_op jit(solution)/shard_map/pallas_call | solution.py:247
  92.0 1.4 shard_map.195
  93.5 1.6 collective-permute-start.13
  95.1 1.5 collective-permute-done.10.refs_3_
  96.6 2.4 shard_map.196
  99.0 1.5 collective-permute-start.12
  100.5 8.8 %collective-permute-done.8.refs_1_ = bf16[784,128]{1,0:T(8,128)(2,1)} collective-permute-done((bf16[784,128]{1,0:T(8,128)(2,1)}, bf16[784,128]{1,0:T(8,128)(2,1)}, u32[]{:S(2)}, u32[]{:S(2)}) %collective-permute-start.8) | collective-permute-done | bytes 200736 | tf_op jit(solution)/shard_map/ppermute | solution.py:1172
  109.3 11.8 %shard_map.197 = (bf16[2,256,1536]{2,1,0:T(8,128)(2,1)S(1)}, f32[8,768]{1,0:T(8,128)}, f32[256,768]{1,0:T(8,128)S(1)}, bf16[256,768]{1,0:T(8,128)(2,1)S(1)}, bf1...) custom-call(bf16[784,128]{1,0:T(8,128)(2,1)} %collective-permute-don, ...), custom_call_target="tpu_custom_call" | custom-call | flops 3000000000 | bytes 100000000 | tf_op jit(solution)/shard_map/pallas_call | solution.py:247
  121.1 4.0 %shard_map.198 = (bf16[4,2,96,1536]{3,2,1,0:T(8,128)(2,1)}, f32[8,128]{1,0:T(8,128)S(1)}) custom-call(s32[6]{0:T(128)S(1)} %stack.33.refs_0_.refs_12_.refs_3_.refs_11_.refs_6_.refs_2_, bf16[768,256]{1,0:T(8,128)(2,1)} %get-tuple-element.252.refs_1_, bf16[768,256]{1,0:T(8,128)(2,1)} %get-tuple-element.253.refs_2_, ...), custom_call_target="tpu_custom_call" | custom-call | flops 30000001024 | bytes 100000000 | tf_op jit(solution)/shard_map/pallas_call | solution.py:247
  125.2 1.6 collective-permute-start.15
  127.8 1.4 shard_map.200
  129.2 7.7 %shard_map.201 = (bf16[256,3072]{1,0:T(8,128)(2,1)S(1)}, bf16[256,768]{1,0:T(8,128)(2,1)S(1)}, f32[256,768]{1,0:T(8,128)S(1)}, bf16[256,768]{1,0:T(8,128)(2,1)S(...) custom-call(f32[256,768]{1,0:T(8,128)S(1)} %get-tuple-element.236.re, ...), custom_call_target="tpu_custom_call" | custom-call | flops 10000000000 | bytes 100000000 | tf_op jit(solution)/shard_map/pallas_call | solution.py:247
  136.9 3.7 %shard_map.202 = (bf16[2,2,48,1536]{3,2,1,0:T(8,128)(2,1)S(1)}, bf16[2,2,48,1536]{3,2,1,0:T(8,128)(2,1)S(1)}, bf16[2,2,48,1536]{3,2,1,0:T(8,128)(2,1)S(1)}, bf16...) custom-call(s32[6]{0:T(128)S(1)} %stack.33.refs_0_.refs_12_.refs_3_.refs_11_.refs_6_.refs_2_, ...), custom_call_target="tpu_custom_call" | custom-call | flops 60000002048 | bytes 100000000 | tf_op jit(solution)/shard_map/pallas_call | solution.py:247
  140.7 1.5 collective-permute-start.22
  146.1 2.0 shard_map.203
  148.2 3.6 %collective-permute-done.14.refs_1_.refs_0_ = bf16[784,128]{1,0:T(8,128)(2,1)S(1)} collective-permute-done((bf16[784,128]{1,0:T(8,128)(2,1)S(1)}, bf16[784,128]{1,0:T(8,128)(2,1)S(1)}, u32[]{:S(2)}, u32[]{:S(2)}) %collective-permute-start.14) | collective-permute-done | bytes 200736 | tf_op jit(solution)/shard_map/ppermute | solution.py:1172
  153.2 3.7 %collective-permute-done.22.refs_1_ = bf16[2,2,48,1536]{3,2,1,0:T(8,128)(2,1)S(1)} collective-permute-done((bf16[2,2,48,1536]{3,2,1,0:T(8,128)(2,1)S(1)}, bf16[2,2,48,1536]{3,2,1,0:T(8,128)(2,1)S(1)}, u32[]{:S(2)}, u32[]{:S(2)}) %collective-permute-start.22) | collective-permute-done | bytes 589856 | tf_op jit(solution)/shard_map/ppermute | solution.py:1151
  156.9 1.5 collective-permute-done.23.refs_3_.refs_4_
  158.4 1.5 collective-permute-start.17
  160.6 2.8 shard_map.207
  164.1 2.3 shard_map.208
  166.4 1.5 collective-permute-start.25
  168.0 1.6 collective-permute-done.18.refs_2_
  172.1 2.8 %shard_map.209 = (bf16[4,192,768]{2,1,0:T(8,128)(2,1)}, f32[8,128]{1,0:T(8,128)S(1)}) custom-call(bf16[2,2,192,768]{3,2,1,0:T(8,128)(2,1)S(1)} %get-tuple-element.250.refs_0_, bf16[2,2,192,768]{3,2,1,0:T(8,128)(2,1)S(1)} %copy-done.7, bf16[2,192,768]{2,1,0:T(8,128)(2,1)S(1)} %collective-permute-done.18.refs_2_, bf16[2,2,192,768]{3,2,1,0:T(8,128)(2,1)S(1)} %copy-done.27, ...), custom_call_target="tpu_custom_call" | custom-call | flops 120000004096 | bytes 100000000 | tf_op jit(solution)/shard_map/pallas_call | solution.py:247
  174.9 9.6 %shard_map.210 = (bf16[2,256,1536]{2,1,0:T(8,128)(2,1)S(1)}, f32[8,768]{1,0:T(8,128)}, f32[256,768]{1,0:T(8,128)}, f32[8,128]{1,0:T(8,128)S(1)}) custom-call(bf16[784,128]{1,0:T(8,128)(2,1)S(1)} %collective-permute-done.14.refs_1_.refs_0_, bf16[784,128]{1,0:T(8,128)(2,1)S(1)} %collective-permute-done.17.refs_8_.refs_1_, s32[6]{0:T(128)S(1)} %copy-done.1, ...), custom_call_target="tpu_custom_call" | custom-call | flops 300000000 | bytes 100000000 | tf_op jit(solution)/shard_map/pallas_call | solution.py:247
  184.5 4.0 %shard_map.211 = (bf16[4,2,96,1536]{3,2,1,0:T(8,128)(2,1)}, f32[8,128]{1,0:T(8,128)S(1)}) custom-call(s32[6]{0:T(128)S(1)} %copy-done.1, bf16[768,256]{1,0:T(8,128)(2,1)} %get-tuple-element.291.refs_1_, bf16[768,256]{1,0:T(8,128)(2,1)} %get-tuple-element.292.refs_2_, bf16[2,256,1536]{2,1,0:T(8,128)(2,1)S(1)} %get-tuple-element.293.refs_3_, ...), custom_call_target="tpu_custom_call" | custom-call | flops 3000000000 | bytes 100000000 | tf_op jit(solution)/shard_map/pallas_call | solution.py:247
  189.0 5.1 %collective-permute-done.25.refs_1_.refs_3_ = bf16[2,2,96,768]{3,2,1,0:T(8,128)(2,1)S(1)} collective-permute-done((bf16[2,2,96,768]{3,2,1,0:T(8,128)(2,1)}, bf16[2,2,96,768]{3,2,1,0:T(8,128)(2,1)S(1)}, u32[]{:S(2)}, u32[]{:S(2)}) %collective-permute-start.25) | collective-permute-done | bytes 589856 | tf_op jit(solution)/shard_map/ppermute | solution.py:1151
  195.5 1.5 collective-permute-start.31
  197.0 1.5 collective-permute-start.33
  199.1 1.4 copy-done.3
  200.5 4.7 %shard_map.213 = (bf16[2,2,48,1536]{3,2,1,0:T(8,128)(2,1)}, bf16[2,2,48,1536]{3,2,1,0:T(8,128)(2,1)S(1)}, bf16[2,2,48,1536]{3,2,1,0:T(8,128)(2,1)}, bf16[2,2,48,1536]{3,2,1,0:T(8,128)(2,1)S(1)}, f32[8,128]{1,0:T(8,128)S(1)}) custom-call(s32[6]{0:T(128)S(1)} %copy-done.1, bf16[768,256]{1,0:T(8,128)(2,1)} %get-tuple-element.291.refs_1_, ...), custom_call_target="tpu_custom_call" | custom-call | flops 3000000000 | bytes 100000000 | tf_op jit(solution)/shard_map/pallas_call | solution.py:247
  205.7 2.1 shard_map.214
  209.0 1.5 collective-permute-start.27
  210.6 1.5 collective-permute-start.28
  212.1 1.4 collective-permute-start.39
  213.5 1.6 shard_map.216
  215.9 9.6 %collective-permute-done.27.refs_1_ = bf16[2,2,48,1536]{3,2,1,0:T(8,128)(2,1)S(1)} collective-permute-done((bf16[2,2,48,1536]{3,2,1,0:T(8,128)(2,1)}, bf16[2,2,48,1536]{3,2,1,0:T(8,128)(2,1)S(1)}, u32[]{:S(2)}, u32[]{:S(2)}) %collective-permute-start.27) | collective-permute-done | bytes 589856 | tf_op jit(solution)/shard_map/ppermute | solution.py:1151
  227.1 1.6 collective-permute-start.38
  229.2 1.5 collective-permute-start.36
  231.0 3.9 %collective-permute-start.44 = (bf16[192,768]{1,0:T(8,128)(2,1)S(1)}, bf16[192,768]{1,0:T(8,128)(2,1)S(1)}, u32[]{:S(2)}, u32[]{:S(2)}) collective-permute-start(bf16[192,768]{1,0:T(8,128)(2,1)S(1)} %get-tuple-element.344), channel_id=1, source_target_pairs={{0,2},{1,3},{2,0},{3,1},{4,6},{5,7},{6,4},{7,5},{8,10},{9,11},{10,... | collective-permute-start | bytes 884744 | tf_op jit(solution)/shard_map/ppermute | solution.py:1156
  234.9 3.3 %collective-permute-start.41 = (f32[32,768]{1,0:T(8,128)S(1)}, f32[32,768]{1,0:T(8,128)S(1)}, u32[]{:S(2)}, u32[]{:S(2)}) collective-permute-start(f32[32,768]{1,0:T(8,128)S(1)} %get-tuple-element.336.refs_0_), channel_id=1, source_target_pairs={{0,1},{1,0},{2,3},{3,2},{4,5},{5,4},{6,7},{7,6},{8,9},{9,8},{10,11... | collective-permute-start | bytes 294920 | tf_op jit(solution)/shard_map/ppermute | solution.py:1156
  238.5 2.1 collective-permute-start.40
  240.6 9.7 %collective-permute-done.41.refs_1_ = f32[32,768]{1,0:T(8,128)S(1)} collective-permute-done((f32[32,768]{1,0:T(8,128)S(1)}, f32[32,768]{1,0:T(8,128)S(1)}, u32[]{:S(2)}, u32[]{:S(2)}) %collective-permute-start.41) | collective-permute-done | bytes 98336 | tf_op jit(solution)/shard_map/ppermute | solution.py:1156
  250.3 3.3 %collective-permute-start.43 = (f32[32,768]{1,0:T(8,128)S(1)}, f32[32,768]{1,0:T(8,128)S(1)}, u32[]{:S(2)}, u32[]{:S(2)}) collective-permute-start(f32[32,768]{1,0:T(8,128)S(1)} %get-tuple-element.342.refs_0_), channel_id=1, source_target_pairs={{0,2},{1,3},{2,0},{3,1},{4,6},{5,7},{6,4},{7,5},{8,10},{9,11},{10,... | collective-permute-start | bytes 294920 | tf_op jit(solution)/shard_map/ppermute | solution.py:1156
  253.6 5.7 %collective-permute-done.40.refs_1_ = bf16[96,1536]{1,0:T(8,128)(2,1)S(1)} collective-permute-done((bf16[96,1536]{1,0:T(8,128)(2,1)S(1)}, bf16[96,1536]{1,0:T(8,128)(2,1)S(1)}, u32[]{:S(2)}, u32[]{:S(2)}) %collective-permute-start.40) | collective-permute-done | bytes 294944 | tf_op jit(solution)/shard_map/ppermute | solution.py:1156
  260.4 1.4 shard_map.225
  261.9 1.5 collective-permute-start.42
  267.3 4.1 %collective-permute-done.42.refs_1_ = bf16[96,768]{1,0:T(8,128)(2,1)S(1)} collective-permute-done((bf16[96,768]{1,0:T(8,128)(2,1)S(1)}, bf16[96,768]{1,0:T(8,128)(2,1)S(1)}, u32[]{:S(2)}, u32[]{:S(2)}) %collective-permute-start.42) | collective-permute-done | bytes 147488 | tf_op jit(solution)/shard_map/ppermute | solution.py:1156
  272.3 1.6 shard_map.227
  (152 shorter events, 32.9 us)
Async XLA Ops:
  7.2 252.3 %reduce-scatter.5.cloned.1.call-start = ((), (), s32[]{:S(2)}) async-start(), calls=%async_computation.3 | async-start | bytes 1474560 | tf_op jit(solution)/shard_map/reduce_scatter | solution.py:1385
  9.1 142.8 %copy-start = (s32[6]{0:T(128)}, s32[6]{0:T(128)S(1)}, u32[]{:S(2)}) copy-start(s32[6]{0:T(128)S(1)} %stack.33.refs_0_.refs_12_.refs_3_.refs_11_.refs_6_.refs_2_) | copy-start | bytes 76
  15.7 19.5 %collective-permute-start = (bf16[784,128]{1,0:T(8,128)(2,1)S(1)}, bf16[784,128]{1,0:T(8,128)(2,1)S(1)}, u32[]{:S(2)}, u32[]{:S(2)}) collective-permute-start(bf16[784,128]{1,0:T(8,128)(2,1)S(1)} %get-tuple-element.182), channel_id=1, source_target_pairs={{0,1},{1,2},{2,3},{4,5},{5,6},{6,7},{8,9},{9,10},{10,11},{12,13},{... | collective-permute-start | bytes 602120 | tf_op jit(solution)/shard_map/ppermute | solution.py:1172
  20.6 14.6 %collective-permute-start.1 = (bf16[784,128]{1,0:T(8,128)(2,1)S(1)}, bf16[784,128]{1,0:T(8,128)(2,1)S(1)}, u32[]{:S(2)}, u32[]{:S(2)}) collective-permute-start(bf16[784,128]{1,0:T(8,128)(2,1)S(1)} %get-tuple-element.182), channel_id=1, source_target_pairs={{0,2},{1,3},{4,6},{5,7},{8,10},{9,11},{12,14},{13,15},{16,18},{17,... | collective-permute-start | bytes 602120 | tf_op jit(solution)/shard_map/ppermute | solution.py:1172
  25.1 10.1 %collective-permute-start.2 = (bf16[784,128]{1,0:T(8,128)(2,1)S(1)}, bf16[784,128]{1,0:T(8,128)(2,1)S(1)}, u32[]{:S(2)}, u32[]{:S(2)}) collective-permute-start(bf16[784,128]{1,0:T(8,128)(2,1)S(1)} %get-tuple-element.182), channel_id=1, source_target_pairs={{0,3},{4,7},{8,11},{12,15},{16,19},{20,23},{24,27},{28,31}} | collective-permute-start | bytes 602120 | tf_op jit(solution)/shard_map/ppermute | solution.py:1172
  48.2 19.4 %collective-permute-start.3 = (bf16[784,128]{1,0:T(8,128)(2,1)S(1)}, bf16[784,128]{1,0:T(8,128)(2,1)S(1)}, u32[]{:S(2)}, u32[]{:S(2)}) collective-permute-start(bf16[784,128]{1,0:T(8,128)(2,1)S(1)} %get-tuple-element.196), channel_id=1, source_target_pairs={{0,1},{1,2},{2,3},{4,5},{5,6},{6,7},{8,9},{9,10},{10,11},{12,13},{... | collective-permute-start | bytes 602120 | tf_op jit(solution)/shard_map/ppermute | solution.py:1172
  54.2 13.4 %collective-permute-start.4 = (bf16[784,128]{1,0:T(8,128)(2,1)S(1)}, bf16[784,128]{1,0:T(8,128)(2,1)S(1)}, u32[]{:S(2)}, u32[]{:S(2)}) collective-permute-start(bf16[784,128]{1,0:T(8,128)(2,1)S(1)} %get-tuple-element.196), channel_id=1, source_target_pairs={{0,2},{1,3},{4,6},{5,7},{8,10},{9,11},{12,14},{13,15},{16,18},{17,... | collective-permute-start | bytes 602120 | tf_op jit(solution)/shard_map/ppermute | solution.py:1172
  59.5 8.1 %collective-permute-start.5 = (bf16[784,128]{1,0:T(8,128)(2,1)S(1)}, bf16[784,128]{1,0:T(8,128)(2,1)S(1)}, u32[]{:S(2)}, u32[]{:S(2)}) collective-permute-start(bf16[784,128]{1,0:T(8,128)(2,1)S(1)} %get-tuple-element.196), channel_id=1, source_target_pairs={{0,3},{4,7},{8,11},{12,15},{16,19},{20,23},{24,27},{28,31}} | collective-permute-start | bytes 602120 | tf_op jit(solution)/shard_map/ppermute | solution.py:1172
  61.2 17.9 %collective-permute-start.6 = (bf16[1,256,1536]{2,1,0:T(8,128)(2,1)S(1)}, bf16[1,256,1536]{2,1,0:T(8,128)(2,1)S(1)}, u32[]{:S(2)}, u32[]{:S(2)}) collective-permute-start(bf16[1,256,1536]{2,1,0:T(8,128)(2,1)S(1)} %get-tuple-element.214), channel_id=1, source_target_pairs={{0,16},{4,20},{8,24},{12,28},{16,0},{20,4},{24,8},{28,12},{1,17},{... | collective-permute-start | bytes 2359304 | tf_op jit(solution)/shard_map/ppermute | solution.py:1151
  76.5 15.6 %collective-permute-start.11 = (bf16[4,2,192,768]{3,2,1,0:T(8,128)(2,1)S(1)}, bf16[4,2,192,768]{3,2,1,0:T(8,128)(2,1)S(1)}, u32[]{:S(2)}, u32[]{:S(2)}) collective-permute-start(bf16[4,2,192,768]{3,2,1,0:T(8,128)(2,1)S(1)} %get-tuple-element.232), channel_id=1, source_target_pairs={{0,4},{4,0},{8,12},{12,8},{16,20},{20,16},{24,28},{28,24},{1,5},{5... | collective-permute-start | bytes 7077896 | tf_op jit(solution)/shard_map/ppermute | solution.py:1151
  86.7 13.8 %collective-permute-start.7 = (bf16[784,128]{1,0:T(8,128)(2,1)}, bf16[784,128]{1,0:T(8,128)(2,1)}, u32[]{:S(2)}, u32[]{:S(2)}) collective-permute-start(bf16[784,128]{1,0:T(8,128)(2,1)} %get-tuple-element.219), channel_id=1, source_target_pairs={{1,0},{2,1},{3,2},{5,4},{6,5},{7,6},{9,8},{10,9},{11,10},{13,12},{... | collective-permute-start | bytes 602120 | tf_op jit(solution)/shard_map/ppermute | solution.py:1172
  88.0 21.3 %collective-permute-start.8 = (bf16[784,128]{1,0:T(8,128)(2,1)}, bf16[784,128]{1,0:T(8,128)(2,1)}, u32[]{:S(2)}, u32[]{:S(2)}) collective-permute-start(bf16[784,128]{1,0:T(8,128)(2,1)} %get-tuple-element.219), channel_id=1, source_target_pairs={{2,0},{3,1},{6,4},{7,5},{10,8},{11,9},{14,12},{15,13},{18,16},{19,... | collective-permute-start | bytes 602120 | tf_op jit(solution)/shard_map/ppermute | solution.py:1172
  89.3 20.0 %collective-permute-start.9 = (bf16[784,128]{1,0:T(8,128)(2,1)}, bf16[784,128]{1,0:T(8,128)(2,1)}, u32[]{:S(2)}, u32[]{:S(2)}) collective-permute-start(bf16[784,128]{1,0:T(8,128)(2,1)} %get-tuple-element.219), channel_id=1, source_target_pairs={{3,0},{7,4},{11,8},{15,12},{19,16},{23,20},{27,24},{31,28}} | collective-permute-start | bytes 602120 | tf_op jit(solution)/shard_map/ppermute | solution.py:1172
  92.0 4.6 %collective-permute-start.10 = (bf16[4,2,192,768]{3,2,1,0:T(8,128)(2,1)S(1)}, bf16[4,2,192,768]{3,2,1,0:T(8,128)(2,1)S(1)}, u32[]{:S(2)}, u32[]{:S(2)}) collective-permute-start(bf16[4,2,192,768]{3,2,1,0:T(8,128)(2,1)S(1)} %get-tuple-element.231), channel_id=1, source_target_pairs={{0,4},{4,0},{8,12},{12,8},{16,20},{20,16},{24,28},{28,24},{1,5},{5... | collective-permute-start | bytes 7077896 | tf_op jit(solution)/shard_map/ppermute | solution.py:1151
  93.5 33.3 %collective-permute-start.13 = (bf16[2,2,192,768]{3,2,1,0:T(8,128)(2,1)S(1)}, bf16[2,2,192,768]{3,2,1,0:T(8,128)(2,1)S(1)}, u32[]{:S(2)}, u32[]{:S(2)}) collective-permute-start(bf16[2,2,192,768]{3,2,1,0:T(8,128)(2,1)S(1)} %get-tuple-element.251), channel_id=1, source_target_pairs={{0,16},{4,20},{8,24},{12,28},{16,0},{20,4},{24,8},{28,12},{1,17},{... | collective-permute-start | bytes 3538952 | tf_op jit(solution)/shard_map/ppermute | solution.py:1151
  99.0 28.8 %copy-start.26 = (bf16[2,2,192,768]{3,2,1,0:T(8,128)(2,1)}, bf16[2,2,192,768]{3,2,1,0:T(8,128)(2,1)S(1)}, u32[]{:S(2)}) copy-start(bf16[2,2,192,768]{3,2,1,0:T(8,128)(2,1)S(1)} %get-tuple-element.248.refs_0_.refs_3_) | copy-start | bytes 3538948
  99.0 28.8 %collective-permute-start.12 = (bf16[2,2,192,768]{3,2,1,0:T(8,128)(2,1)}, bf16[2,2,192,768]{3,2,1,0:T(8,128)(2,1)}, u32[]{:S(2)}, u32[]{:S(2)}) collective-permute-start(bf16[2,2,192,768]{3,2,1,0:T(8,128)(2,1)} %get-tuple-element.249), channel_id=1, source_target_pairs={{0,8},{4,12},{8,0},{12,4},{16,24},{20,28},{24,16},{28,20},{1,9},{5... | collective-permute-start | bytes 3538952 | tf_op jit(solution)/shard_map/ppermute | solution.py:1151
  121.1 4.0 %copy-start.4 = (bf16[2,256,1536]{2,1,0:T(8,128)(2,1)}, bf16[2,256,1536]{2,1,0:T(8,128)(2,1)S(1)}, u32[]{:S(2)}) copy-start(bf16[2,256,1536]{2,1,0:T(8,128)(2,1)S(1)} %get-tuple-element.254.refs_3_) | copy-start | bytes 4718596
  125.1 11.8 %collective-permute-start.16 = (bf16[4,2,96,1536]{3,2,1,0:T(8,128)(2,1)}, bf16[4,2,96,1536]{3,2,1,0:T(8,128)(2,1)}, u32[]{:S(2)}, u32[]{:S(2)}) collective-permute-start(bf16[4,2,96,1536]{3,2,1,0:T(8,128)(2,1)} %get-tuple-element.263), channel_id=1, source_target_pairs={{0,4},{4,0},{8,12},{12,8},{16,20},{20,16},{24,28},{28,24},{1,5},{5... | collective-permute-start | bytes 7077896 | tf_op jit(solution)/shard_map/ppermute | solution.py:1151
  125.2 20.1 %collective-permute-start.15 = (bf16[768,256]{1,0:T(8,128)(2,1)}, bf16[768,256]{1,0:T(8,128)(2,1)}, u32[]{:S(2)}, u32[]{:S(2)}) collective-permute-start(bf16[768,256]{1,0:T(8,128)(2,1)} %get-tuple-element.260.refs_1_), channel_id=1, source_target_pairs={{0,16},{4,20},{8,24},{12,28},{16,0},{20,4},{24,8},{28,12},{1,17},{... | collective-permute-start | bytes 1179656 | tf_op jit(solution)/shard_map/ppermute | solution.py:1151
  129.2 7.7 %copy-start.5 = (bf16[2,256,1536]{2,1,0:T(8,128)(2,1)S(1)}, bf16[2,256,1536]{2,1,0:T(8,128)(2,1)}, u32[]{:S(2)}) copy-start(bf16[2,256,1536]{2,1,0:T(8,128)(2,1)} %copy-done.4) | copy-start | bytes 4718596
  140.7 19.3 %copy-start.22 = (bf16[2,2,48,1536]{3,2,1,0:T(8,128)(2,1)}, bf16[2,2,48,1536]{3,2,1,0:T(8,128)(2,1)S(1)}, u32[]{:S(2)}) copy-start(bf16[2,2,48,1536]{3,2,1,0:T(8,128)(2,1)S(1)} %get-tuple-element.281.refs_0_) | copy-start | bytes 1769476
  140.7 19.3 %copy-start.24 = (bf16[2,2,48,1536]{3,2,1,0:T(8,128)(2,1)}, bf16[2,2,48,1536]{3,2,1,0:T(8,128)(2,1)S(1)}, u32[]{:S(2)}) copy-start(bf16[2,2,48,1536]{3,2,1,0:T(8,128)(2,1)S(1)} %get-tuple-element.283.refs_2_.refs_3_) | copy-start | bytes 1769476
  140.7 16.2 %collective-permute-start.22 = (bf16[2,2,48,1536]{3,2,1,0:T(8,128)(2,1)S(1)}, bf16[2,2,48,1536]{3,2,1,0:T(8,128)(2,1)S(1)}, u32[]{:S(2)}, u32[]{:S(2)}) collective-permute-start(bf16[2,2,48,1536]{3,2,1,0:T(8,128)(2,1)S(1)} %get-tuple-element.282), channel_id=1, source_target_pairs={{0,8},{4,12},{8,0},{12,4},{16,24},{20,28},{24,16},{28,20},{1,9},{5... | collective-permute-start | bytes 1769480 | tf_op jit(solution)/shard_map/ppermute | solution.py:1151
  142.2 16.2 %collective-permute-start.23 = (bf16[2,2,48,1536]{3,2,1,0:T(8,128)(2,1)S(1)}, bf16[2,2,48,1536]{3,2,1,0:T(8,128)(2,1)S(1)}, u32[]{:S(2)}, u32[]{:S(2)}) collective-permute-start(bf16[2,2,48,1536]{3,2,1,0:T(8,128)(2,1)S(1)} %get-tuple-element.284), channel_id=1, source_target_pairs={{0,16},{4,20},{8,24},{12,28},{16,0},{20,4},{24,8},{28,12},{1,17},{... | collective-permute-start | bytes 1769480 | tf_op jit(solution)/shard_map/ppermute | solution.py:1151
  143.3 8.5 %collective-permute-start.14 = (bf16[784,128]{1,0:T(8,128)(2,1)S(1)}, bf16[784,128]{1,0:T(8,128)(2,1)S(1)}, u32[]{:S(2)}, u32[]{:S(2)}) collective-permute-start(bf16[784,128]{1,0:T(8,128)(2,1)S(1)} %get-tuple-element.259.refs_0_), channel_id=1, source_target_pairs={{1,0},{2,1},{3,2},{5,4},{6,5},{7,6},{9,8},{10,9},{11,10},{13,12},{... | collective-permute-start | bytes 602120 | tf_op jit(solution)/shard_map/ppermute | solution.py:1172
  144.6 24.9 %collective-permute-start.18 = (bf16[2,192,768]{2,1,0:T(8,128)(2,1)S(1)}, bf16[2,192,768]{2,1,0:T(8,128)(2,1)S(1)}, u32[]{:S(2)}, u32[]{:S(2)}) collective-permute-start(bf16[2,192,768]{2,1,0:T(8,128)(2,1)S(1)} %get-tuple-element.274), channel_id=1, source_target_pairs={{0,8},{4,12},{8,0},{12,4},{16,24},{20,28},{24,16},{28,20},{1,9},{5... | collective-permute-start | bytes 1769480 | tf_op jit(solution)/shard_map/ppermute | solution.py:1151
  145.2 25.5 %collective-permute-start.19 = (bf16[2,192,768]{2,1,0:T(8,128)(2,1)S(1)}, bf16[2,192,768]{2,1,0:T(8,128)(2,1)S(1)}, u32[]{:S(2)}, u32[]{:S(2)}) collective-permute-start(bf16[2,192,768]{2,1,0:T(8,128)(2,1)S(1)} %get-tuple-element.275), channel_id=1, source_target_pairs={{0,16},{4,20},{8,24},{12,28},{16,0},{20,4},{24,8},{28,12},{1,17},{... | collective-permute-start | bytes 1769480 | tf_op jit(solution)/shard_map/ppermute | solution.py:1151
  151.8 8.4 %collective-permute-start.21 = (bf16[2,2,192,768]{3,2,1,0:T(8,128)(2,1)S(1)}, bf16[2,2,192,768]{3,2,1,0:T(8,128)(2,1)S(1)}, u32[]{:S(2)}, u32[]{:S(2)}) collective-permute-start(bf16[2,2,192,768]{3,2,1,0:T(8,128)(2,1)S(1)} %get-tuple-element.280), channel_id=1, source_target_pairs={{0,4},{4,0},{8,12},{12,8},{16,20},{20,16},{24,28},{28,24},{1,5},{5... | collective-permute-start | bytes 3538952 | tf_op jit(solution)/shard_map/ppermute | solution.py:1151
  156.9 7.2 %collective-permute-start.20 = (bf16[4,2,192,768]{3,2,1,0:T(8,128)(2,1)S(1)}, bf16[4,2,192,768]{3,2,1,0:T(8,128)(2,1)S(1)}, u32[]{:S(2)}, u32[]{:S(2)}) collective-permute-start(bf16[4,2,192,768]{3,2,1,0:T(8,128)(2,1)S(1)} %get-tuple-element.279), channel_id=1, source_target_pairs={{0,4},{4,0},{8,12},{12,8},{16,20},{20,16},{24,28},{28,24},{1,5},{5... | collective-permute-start | bytes 7077896 | tf_op jit(solution)/shard_map/ppermute | solution.py:1151
  158.4 13.6 %collective-permute-start.17 = (bf16[784,128]{1,0:T(8,128)(2,1)S(1)}, bf16[784,128]{1,0:T(8,128)(2,1)S(1)}, u32[]{:S(2)}, u32[]{:S(2)}) collective-permute-start(bf16[784,128]{1,0:T(8,128)(2,1)S(1)} %get-tuple-element.267), channel_id=1, source_target_pairs={{2,0},{3,1},{6,4},{7,5},{10,8},{11,9},{14,12},{15,13},{18,16},{19,... | collective-permute-start | bytes 602120 | tf_op jit(solution)/shard_map/ppermute | solution.py:1172
  163.5 41.8 %collective-permute-start.29 = (bf16[2,192,768]{2,1,0:T(8,128)(2,1)}, bf16[2,192,768]{2,1,0:T(8,128)(2,1)}, u32[]{:S(2)}, u32[]{:S(2)}) collective-permute-start(bf16[2,192,768]{2,1,0:T(8,128)(2,1)} %get-tuple-element.313), channel_id=1, source_target_pairs={{0,8},{4,12},{8,0},{12,4},{16,24},{20,28},{24,16},{28,20},{1,9},{5... | collective-permute-start | bytes 1769480 | tf_op jit(solution)/shard_map/ppermute | solution.py:1151
  164.1 8.0 %copy-start.7 = (bf16[2,2,192,768]{3,2,1,0:T(8,128)(2,1)S(1)}, bf16[2,2,192,768]{3,2,1,0:T(8,128)(2,1)}, u32[]{:S(2)}) copy-start(bf16[2,2,192,768]{3,2,1,0:T(8,128)(2,1)} %copy-done.6) | copy-start | bytes 3538948
  164.1 8.0 %copy-start.27 = (bf16[2,2,192,768]{3,2,1,0:T(8,128)(2,1)S(1)}, bf16[2,2,192,768]{3,2,1,0:T(8,128)(2,1)}, u32[]{:S(2)}) copy-start(bf16[2,2,192,768]{3,2,1,0:T(8,128)(2,1)} %copy-done.26) | copy-start | bytes 3538948
  166.4 27.6 %collective-permute-start.25 = (bf16[2,2,96,768]{3,2,1,0:T(8,128)(2,1)}, bf16[2,2,96,768]{3,2,1,0:T(8,128)(2,1)S(1)}, u32[]{:S(2)}, u32[]{:S(2)}) collective-permute-start(bf16[2,2,96,768]{3,2,1,0:T(8,128)(2,1)} %get-tuple-element.297), channel_id=1, source_target_pairs={{0,8},{4,12},{8,0},{12,4},{16,24},{20,28},{24,16},{28,20},{1,9},{5... | collective-permute-start | bytes 1769480 | tf_op jit(solution)/shard_map/ppermute | solution.py:1151
  169.5 24.5 %collective-permute-start.26 = (bf16[2,2,96,768]{3,2,1,0:T(8,128)(2,1)}, bf16[2,2,96,768]{3,2,1,0:T(8,128)(2,1)S(1)}, u32[]{:S(2)}, u32[]{:S(2)}) collective-permute-start(bf16[2,2,96,768]{3,2,1,0:T(8,128)(2,1)} %get-tuple-element.299), channel_id=1, source_target_pairs={{0,16},{4,20},{8,24},{12,28},{16,0},{20,4},{24,8},{28,12},{1,17},{... | collective-permute-start | bytes 1769480 | tf_op jit(solution)/shard_map/ppermute | solution.py:1151
  184.5 4.0 %copy-start.2 = (bf16[2,256,1536]{2,1,0:T(8,128)(2,1)}, bf16[2,256,1536]{2,1,0:T(8,128)(2,1)S(1)}, u32[]{:S(2)}) copy-start(bf16[2,256,1536]{2,1,0:T(8,128)(2,1)S(1)} %get-tuple-element.293.refs_3_) | copy-start | bytes 4718596
  188.5 10.0 %collective-permute-start.24 = (bf16[4,2,96,1536]{3,2,1,0:T(8,128)(2,1)}, bf16[4,2,96,1536]{3,2,1,0:T(8,128)(2,1)}, u32[]{:S(2)}, u32[]{:S(2)}) collective-permute-start(bf16[4,2,96,1536]{3,2,1,0:T(8,128)(2,1)} %get-tuple-element.295), channel_id=1, source_target_pairs={{0,4},{4,0},{8,12},{12,8},{16,20},{20,16},{24,28},{28,24},{1,5},{5... | collective-permute-start | bytes 7077896 | tf_op jit(solution)/shard_map/ppermute | solution.py:1151
  188.6 78.7 %reduce-scatter.3.cloned.1.call-start = ((), (), s32[]{:S(2)}) async-start(), calls=%async_computation.2 | async-start | bytes 737280 | tf_op jit(solution)/shard_map/reduce_scatter | solution.py:1385
  195.0 10.3 %collective-permute-start.30 = (bf16[2,96,768]{2,1,0:T(8,128)(2,1)}, bf16[2,96,768]{2,1,0:T(8,128)(2,1)S(1)}, u32[]{:S(2)}, u32[]{:S(2)}) collective-permute-start(bf16[2,96,768]{2,1,0:T(8,128)(2,1)} %get-tuple-element.314), channel_id=1, source_target_pairs={{0,16},{4,20},{8,24},{12,28},{16,0},{20,4},{24,8},{28,12},{1,17},{... | collective-permute-start | bytes 884744 | tf_op jit(solution)/shard_map/ppermute | solution.py:1151
  195.5 10.2 %collective-permute-start.31 = (bf16[2,96,768]{2,1,0:T(8,128)(2,1)}, bf16[2,96,768]{2,1,0:T(8,128)(2,1)S(1)}, u32[]{:S(2)}, u32[]{:S(2)}) collective-permute-start(bf16[2,96,768]{2,1,0:T(8,128)(2,1)} %get-tuple-element.315), channel_id=1, source_target_pairs={{0,8},{4,12},{8,0},{12,4},{16,24},{20,28},{24,16},{28,20},{1,9},{5... | collective-permute-start | bytes 884744 | tf_op jit(solution)/shard_map/ppermute | solution.py:1151
  197.0 15.1 %collective-permute-start.33 = (bf16[2,48,1536]{2,1,0:T(8,128)(2,1)}, bf16[2,48,1536]{2,1,0:T(8,128)(2,1)S(1)}, u32[]{:S(2)}, u32[]{:S(2)}) collective-permute-start(bf16[2,48,1536]{2,1,0:T(8,128)(2,1)} %copy-done.16), channel_id=1, source_target_pairs={{0,16},{4,20},{8,24},{12,28},{16,0},{20,4},{24,8},{28,12},{1,17},{... | collective-permute-start | bytes 884744 | tf_op jit(solution)/shard_map/ppermute | solution.py:1151
  198.5 15.0 %collective-permute-start.34 = (bf16[2,48,1536]{2,1,0:T(8,128)(2,1)}, bf16[2,48,1536]{2,1,0:T(8,128)(2,1)S(1)}, u32[]{:S(2)}, u32[]{:S(2)}) collective-permute-start(bf16[2,48,1536]{2,1,0:T(8,128)(2,1)} %copy-done.15), channel_id=1, source_target_pairs={{0,8},{4,12},{8,0},{12,4},{16,24},{20,28},{24,16},{28,20},{1,9},{5... | collective-permute-start | bytes 884744 | tf_op jit(solution)/shard_map/ppermute | solution.py:1151
  207.8 5.7 %copy-start.9 = (bf16[2,2,48,1536]{3,2,1,0:T(8,128)(2,1)S(1)}, bf16[2,2,48,1536]{3,2,1,0:T(8,128)(2,1)}, u32[]{:S(2)}) copy-start(bf16[2,2,48,1536]{3,2,1,0:T(8,128)(2,1)} %copy-done.8) | copy-start | bytes 1769476
  207.8 5.7 %copy-start.11 = (bf16[2,2,48,1536]{3,2,1,0:T(8,128)(2,1)S(1)}, bf16[2,2,48,1536]{3,2,1,0:T(8,128)(2,1)}, u32[]{:S(2)}) copy-start(bf16[2,2,48,1536]{3,2,1,0:T(8,128)(2,1)} %copy-done.10) | copy-start | bytes 1769476
  207.8 5.7 %copy-start.23 = (bf16[2,2,48,1536]{3,2,1,0:T(8,128)(2,1)S(1)}, bf16[2,2,48,1536]{3,2,1,0:T(8,128)(2,1)}, u32[]{:S(2)}) copy-start(bf16[2,2,48,1536]{3,2,1,0:T(8,128)(2,1)} %copy-done.22) | copy-start | bytes 1769476
  207.8 5.7 %copy-start.25 = (bf16[2,2,48,1536]{3,2,1,0:T(8,128)(2,1)S(1)}, bf16[2,2,48,1536]{3,2,1,0:T(8,128)(2,1)}, u32[]{:S(2)}) copy-start(bf16[2,2,48,1536]{3,2,1,0:T(8,128)(2,1)} %copy-done.24) | copy-start | bytes 1769476
  209.0 6.2 %collective-permute-start.32 = (f32[32,768]{1,0:T(8,128)S(1)}, f32[32,768]{1,0:T(8,128)S(1)}, u32[]{:S(2)}, u32[]{:S(2)}) collective-permute-start(f32[32,768]{1,0:T(8,128)S(1)} %get-tuple-element.318.refs_0_), channel_id=1, source_target_pairs={{0,4},{4,0},{8,12},{12,8},{16,20},{20,16},{24,28},{28,24},{1,5},{5... | collective-permute-start | bytes 294920 | tf_op jit(solution)/shard_map/ppermute | solution.py:1151
  209.0 16.4 %collective-permute-start.27 = (bf16[2,2,48,1536]{3,2,1,0:T(8,128)(2,1)}, bf16[2,2,48,1536]{3,2,1,0:T(8,128)(2,1)S(1)}, u32[]{:S(2)}, u32[]{:S(2)}) collective-permute-start(bf16[2,2,48,1536]{3,2,1,0:T(8,128)(2,1)} %get-tuple-element.303), channel_id=1, source_target_pairs={{0,8},{4,12},{8,0},{12,4},{16,24},{20,28},{24,16},{28,20},{1,9},{5... | collective-permute-start | bytes 1769480 | tf_op jit(solution)/shard_map/ppermute | solution.py:1151
  210.6 15.6 %collective-permute-start.28 = (bf16[2,2,48,1536]{3,2,1,0:T(8,128)(2,1)}, bf16[2,2,48,1536]{3,2,1,0:T(8,128)(2,1)S(1)}, u32[]{:S(2)}, u32[]{:S(2)}) collective-permute-start(bf16[2,2,48,1536]{3,2,1,0:T(8,128)(2,1)} %get-tuple-element.305), channel_id=1, source_target_pairs={{0,16},{4,20},{8,24},{12,28},{16,0},{20,4},{24,8},{28,12},{1,17},{... | collective-permute-start | bytes 1769480 | tf_op jit(solution)/shard_map/ppermute | solution.py:1151
  212.1 18.7 %collective-permute-start.39 = (bf16[384,768]{1,0:T(8,128)(2,1)}, bf16[384,768]{1,0:T(8,128)(2,1)S(1)}, u32[]{:S(2)}, u32[]{:S(2)}) collective-permute-start(bf16[384,768]{1,0:T(8,128)(2,1)} %get-tuple-element.330), channel_id=1, source_target_pairs={{0,1},{1,0},{2,3},{3,2},{4,5},{5,4},{6,7},{7,6},{8,9},{9,8},{10,11... | collective-permute-start | bytes 1769480 | tf_op jit(solution)/shard_map/ppermute | solution.py:1156
  215.2 11.0 %copy-start.19 = (bf16[2,2,48,1536]{3,2,1,0:T(8,128)(2,1)S(1)}, bf16[2,2,48,1536]{3,2,1,0:T(8,128)(2,1)}, u32[]{:S(2)}) copy-start(bf16[2,2,48,1536]{3,2,1,0:T(8,128)(2,1)} %copy-done.18) | copy-start | bytes 1769476
  215.2 11.0 %copy-start.21 = (bf16[2,2,48,1536]{3,2,1,0:T(8,128)(2,1)S(1)}, bf16[2,2,48,1536]{3,2,1,0:T(8,128)(2,1)}, u32[]{:S(2)}) copy-start(bf16[2,2,48,1536]{3,2,1,0:T(8,128)(2,1)} %copy-done.20) | copy-start | bytes 1769476
  215.3 11.8 %collective-permute-start.37 = (f32[32,768]{1,0:T(8,128)S(1)}, f32[32,768]{1,0:T(8,128)S(1)}, u32[]{:S(2)}, u32[]{:S(2)}) collective-permute-start(f32[32,768]{1,0:T(8,128)S(1)} %get-tuple-element.326.refs_0_), channel_id=1, source_target_pairs={{0,8},{4,12},{8,0},{12,4},{16,24},{20,28},{24,16},{28,20},{1,9},{5... | collective-permute-start | bytes 294920 | tf_op jit(solution)/shard_map/ppermute | solution.py:1151
  227.1 3.7 %copy-start.13 = (bf16[384,768]{1,0:T(8,128)(2,1)S(1)}, bf16[384,768]{1,0:T(8,128)(2,1)}, u32[]{:S(2)}) copy-start(bf16[384,768]{1,0:T(8,128)(2,1)} %copy-done.12) | copy-start | bytes 1769476
  227.1 7.8 %collective-permute-start.38 = (f32[32,768]{1,0:T(8,128)S(1)}, f32[32,768]{1,0:T(8,128)S(1)}, u32[]{:S(2)}, u32[]{:S(2)}) collective-permute-start(f32[32,768]{1,0:T(8,128)S(1)} %get-tuple-element.328.refs_0_), channel_id=1, source_target_pairs={{0,16},{4,20},{8,24},{12,28},{16,0},{20,4},{24,8},{28,12},{1,17},{... | collective-permute-start | bytes 294920 | tf_op jit(solution)/shard_map/ppermute | solution.py:1151
  228.7 9.6 %collective-permute-start.35 = (bf16[2,48,1536]{2,1,0:T(8,128)(2,1)S(1)}, bf16[2,48,1536]{2,1,0:T(8,128)(2,1)S(1)}, u32[]{:S(2)}, u32[]{:S(2)}) collective-permute-start(bf16[2,48,1536]{2,1,0:T(8,128)(2,1)S(1)} %get-tuple-element.324), channel_id=1, source_target_pairs={{0,16},{4,20},{8,24},{12,28},{16,0},{20,4},{24,8},{28,12},{1,17},{... | collective-permute-start | bytes 884744 | tf_op jit(solution)/shard_map/ppermute | solution.py:1151
  229.2 9.1 %collective-permute-start.36 = (bf16[2,48,1536]{2,1,0:T(8,128)(2,1)S(1)}, bf16[2,48,1536]{2,1,0:T(8,128)(2,1)S(1)}, u32[]{:S(2)}, u32[]{:S(2)}) collective-permute-start(bf16[2,48,1536]{2,1,0:T(8,128)(2,1)S(1)} %get-tuple-element.325), channel_id=1, source_target_pairs={{0,8},{4,12},{8,0},{12,4},{16,24},{20,28},{24,16},{28,20},{1,9},{5... | collective-permute-start | bytes 884744 | tf_op jit(solution)/shard_map/ppermute | solution.py:1151
  231.0 28.5 %collective-permute-start.44 = (bf16[192,768]{1,0:T(8,128)(2,1)S(1)}, bf16[192,768]{1,0:T(8,128)(2,1)S(1)}, u32[]{:S(2)}, u32[]{:S(2)}) collective-permute-start(bf16[192,768]{1,0:T(8,128)(2,1)S(1)} %get-tuple-element.344), channel_id=1, source_target_pairs={{0,2},{1,3},{2,0},{3,1},{4,6},{5,7},{6,4},{7,5},{8,10},{9,11},{10,... | collective-permute-start | bytes 884744 | tf_op jit(solution)/shard_map/ppermute | solution.py:1156
  234.9 15.3 %collective-permute-start.41 = (f32[32,768]{1,0:T(8,128)S(1)}, f32[32,768]{1,0:T(8,128)S(1)}, u32[]{:S(2)}, u32[]{:S(2)}) collective-permute-start(f32[32,768]{1,0:T(8,128)S(1)} %get-tuple-element.336.refs_0_), channel_id=1, source_target_pairs={{0,1},{1,0},{2,3},{3,2},{4,5},{5,4},{6,7},{7,6},{8,9},{9,8},{10,11... | collective-permute-start | bytes 294920 | tf_op jit(solution)/shard_map/ppermute | solution.py:1156
  238.5 20.8 %collective-permute-start.40 = (bf16[96,1536]{1,0:T(8,128)(2,1)S(1)}, bf16[96,1536]{1,0:T(8,128)(2,1)S(1)}, u32[]{:S(2)}, u32[]{:S(2)}) collective-permute-start(bf16[96,1536]{1,0:T(8,128)(2,1)S(1)} %get-tuple-element.335), channel_id=1, source_target_pairs={{0,1},{1,0},{2,3},{3,2},{4,5},{5,4},{6,7},{7,6},{8,9},{9,8},{10,11... | collective-permute-start | bytes 884744 | tf_op jit(solution)/shard_map/ppermute | solution.py:1156
  250.3 11.6 %collective-permute-start.43 = (f32[32,768]{1,0:T(8,128)S(1)}, f32[32,768]{1,0:T(8,128)S(1)}, u32[]{:S(2)}, u32[]{:S(2)}) collective-permute-start(f32[32,768]{1,0:T(8,128)S(1)} %get-tuple-element.342.refs_0_), channel_id=1, source_target_pairs={{0,2},{1,3},{2,0},{3,1},{4,6},{5,7},{6,4},{7,5},{8,10},{9,11},{10,... | collective-permute-start | bytes 294920 | tf_op jit(solution)/shard_map/ppermute | solution.py:1156
  261.9 3.6 %copy-start.29 = (f32[2,384,192]{2,1,0:T(8,128)S(1)}, f32[2,384,192]{2,1,0:T(8,128)}, u32[]{:S(2)}) copy-start(f32[2,384,192]{2,1,0:T(8,128)} %get-tuple-element.369) | copy-start | bytes 1769476
  261.9 9.4 %collective-permute-start.42 = (bf16[96,768]{1,0:T(8,128)(2,1)S(1)}, bf16[96,768]{1,0:T(8,128)(2,1)S(1)}, u32[]{:S(2)}, u32[]{:S(2)}) collective-permute-start(bf16[96,768]{1,0:T(8,128)(2,1)S(1)} %get-tuple-element.340), channel_id=1, source_target_pairs={{0,2},{1,3},{2,0},{3,1},{4,6},{5,7},{6,4},{7,5},{8,10},{9,11},{10,... | collective-permute-start | bytes 442376 | tf_op jit(solution)/shard_map/ppermute | solution.py:1156
  (13 other events, 23.7 us)
Sparse Core Ops, SparseCore 0:
  188.7 32.0 reduce-scatter.4
  223.1 35.4 reduce-scatter.2

commit v4 on v3

--- a/solution.py
+++ b/solution.py
@@ -278,7 +278,7 @@
     return [lambda ref: ref.at[layer]], block
 
 
-COSTS = [10, 10, 10, 10, 10, 10, 10, 3, 120, 30, 10, 3, 30, 120, 60, 10, 60, 1, 3, 0.3, 60, 30, 6, 120, 0.3, 3, 120, 3, 1, 10, 6, 10, 6, 3, 22, 30, 30, 15, 60, 3, 10, 3]
+COSTS = [10, 10, 10, 10, 10, 10, 0.3, 0.3, 0.3, 1, 0.3, 0.3, 0.3, 0.3, 0.3, 15, 1, 0.3, 1, 3, 0.3, 10, 15, 1, 6, 0.3, 0.3, 22, 10, 3, 1, 3, 1, 0.3, 0.3, 6, 3, 0.3, 0.3, 0.3, 0.3, 1]
 
 
 class Counter:
@@ -676,6 +676,7 @@
             second = v[:, LANES:] * cs_now
             return jnp.where(lo, first + swap(first), second + swap(second))
 
+        io.cmt[...] = io.cm[...].T
         for pair in range(PAIRS):
             here = slice(pair * LANES, (pair + 1) * LANES)
             at = pair * 3 * LANES
@@ -702,19 +703,19 @@
             u1 = low(jnp.where(lo, ds, uf))
             ua = low(jnp.where(lo, uf, 0.0))
             ub = low(jnp.where(lo, 0.0, uf))
-            p0 = low(nt(q0, k0) * mask)
-            p1 = low(nt(q1, k1) * mask)
-            d0 = low(nt(u0, v0) * mask)
-            d1 = low(nt(u1, v1) * mask)
+            mask_t = io.cmt[...]
+            pt = beside(low(nt(k0, q0) * mask_t), low(nt(k1, q1) * mask_t))
+            d = beside(low(nt(u0, v0) * mask), low(nt(u1, v1) * mask))
+            dt = beside(low(nt(v0, u0) * mask_t), low(nt(v1, u1) * mask_t))
             after = later[here]
             eq = nt(beside(u0, u1), halves(before[here], before_totals, pair))
             ek = nt(beside(v0, v1), halves(after, later_totals, pair))
             after_split = above(
                 low(jnp.where(lo_state, after, 0.0)), low(jnp.where(lo_state, 0.0, after))
             )
-            dq = fold(eq, cs_now) + nn(d0, k0) + nn(d1, k1)
-            dk = fold(ek, cs_now) + tn(d0, q0) + tn(d1, q1)
-            dv = nn(kf, after_split) + tn(p0, ua) + tn(p1, ub)
+            dq = fold(eq, cs_now) + nn(d, above(k0, k1))
+            dk = fold(ek, cs_now) + nn(dt, above(q0, q1))
+            dv = nn(beside(kf, pt), jnp.concatenate([after_split, ua, ub], axis=0))
             dks = swap(dk)
             gpk = io.gpk
             gpk[:, at : at + LANES] = low(jnp.where(lo, dq, dks) * sigmoid(t0))
@@ -780,7 +781,7 @@
         ins,
         outs,
         deps,
-        scratch=Box(gpk=pltpu.VMEM((rows, 3 * D), BF)),
+        scratch=Box(gpk=pltpu.VMEM((rows, 3 * D), BF), cmt=pltpu.VMEM((rows, rows), F32)),
         limit=20,
         flops=2 * rows * D * 3 * D + 12 * HEADS * rows * rows * LANES,
         nbytes=2 * D * 3 * D,
@@ -902,8 +903,8 @@
         ins.gpre = ("v", gpre)
         return ins, Box(lhs=lhs), (192, D), midt.shape[1]
     mixt, xt, gcol = operands
-    ins.mixt = ("d", mixt)
-    ins.xt = ("d", xt)
+    ins.mixt = ("v", mixt)
+    ins.xt = ("v", xt)
     ins.gcol = ("v", gcol)
     return ins, Box(lhs=lhs, lhs_two=lhs), (96, 2 * D), xt.shape[1]
 
@@ -1020,24 +1021,26 @@
 def grad_near(groups, deps):
     ins = group_ins(groups)
     places = [(which, at) for which, group in enumerate(groups) for at in halves_of(group)]
-    total = sum(group["keep%d" % at].shape[-2] for group in groups for at in halves_of(group))
-    lanes = groups[0].keep0.shape[-1]
+    sizes = [groups[which]["keep%d" % at].shape[-2:] for which, at in places]
+    total = sum(rows * lanes // D for rows, lanes in sizes)
 
     def body(io):
         start = 0
         for which, at in places:
-            rows = groups[which]["keep%d" % at].shape[-2]
-            here = slice(start, start + rows)
-            io.near[here, :] = low(group_sum(io, which, at, 1))
-            io.stay[here, :] = low(group_sum(io, which, at, 0))
-            start += rows
+            rows, lanes = groups[which]["keep%d" % at].shape[-2:]
+            for slot, target in ((1, io.near), (0, io.stay)):
+                value = low(group_sum(io, which, at, slot))
+                for part in range(lanes // D):
+                    here = slice(start + part * rows, start + (part + 1) * rows)
+                    target[here, :] = value[:, part * D : (part + 1) * D]
+            start += rows * lanes // D
 
     return run(
         body,
         ins,
         Box(
-            near=("v", shape(total, lanes, dtype=BF)),
-            stay=("v", shape(total, lanes, dtype=BF)),
+            near=("v", shape(total, D, dtype=BF)),
+            stay=("v", shape(total, D, dtype=BF)),
         ),
         deps,
     )
@@ -1053,7 +1056,7 @@
             for slot in range(2):
                 full = [group_sum(io, which, at, slot) for at in halves_of(groups[which])]
                 if kind == "mix":
-                    both = above(full[0], full[1])
+                    both = full[0]
                     quarter = D // 4
                     parts = [
                         beside(both[:, :quarter], both[:, 2 * quarter : 5 * quarter]),
@@ -1076,34 +1079,41 @@
     return outs.blocks, token
 
 
-def grad_far(kinds, stay, near, deps):
+def grad_far(kinds, pairs, deps):
     count = len(kinds)
+    ins = Box()
+    for at, (stay, near) in enumerate(pairs):
+        ins["stay%d" % at] = ("v", stay)
+        ins["near%d" % at] = ("v", near)
 
     def body(io):
-        full = up(io.stay[...]) + up(io.near[...])
-        if kinds[0] == "mix":
-            quarter = D // 4
-            io.own[...] = beside(full[:, :quarter], full[:, 2 * quarter : 5 * quarter])
-            io.far[...] = low(
-                beside(full[:, quarter : 2 * quarter], full[:, 5 * quarter : 8 * quarter])
-            )
-            return
+        sums = [
+            up(io["stay%d" % at][...]) + up(io["near%d" % at][...]) for at in range(len(pairs))
+        ]
+        full = jnp.concatenate(sums, axis=0)
         for at, kind in enumerate(kinds):
             part = full[192 * at : 192 * (at + 1)]
             here = slice(96 * at, 96 * (at + 1))
-            if kind == "out":
+            if kind in ("mix", "mix both"):
+                if kind == "mix":
+                    both = beside(part[:96], part[96:])
+                else:
+                    both = above(beside(part[:48], part[48:96]), beside(part[96:144], part[144:]))
+                quarter = D // 4
+                io.own[here, :] = beside(both[:, :quarter], both[:, 2 * quarter : 5 * quarter])
+                io.far[here, :] = low(
+                    beside(both[:, quarter : 2 * quarter], both[:, 5 * quarter : 8 * quarter])
+                )
+            elif kind == "out":
                 io.own[here, :] = beside(part[:96, : D // 2], part[96:, : D // 2])
                 io.far[here, :] = low(beside(part[:96, D // 2 :], part[96:, D // 2 :]))
-            elif kind == "inner":
-                io.own[here, :] = part[:96]
-                io.far[here, :] = low(part[96:])
             else:
                 io.own[here, :] = above(part[:48], part[96:144])
                 io.far[here, :] = low(above(part[48:96], part[144:]))
 
     return run(
         body,
-        Box(stay=("v", stay), near=("v", near)),
+        ins,
         Box(
             own=("v", shape(count * 96, D)),
             far=("v", shape(count * 96, D, dtype=BF)),
@@ -1112,7 +1122,8 @@
     )
 
 
-def grad_last(kind, terms, deps):
+def grad_last(kind, terms, starts, deps):
+    size = 96 if kind == "mix" else 192
     ins = Box()
     for layer in range(LAYERS):
         for at, term in enumerate(terms[layer]):
@@ -1130,16 +1141,17 @@
 
     def body(io):
         for layer in range(LAYERS):
-            full = up(io["term%d_0" % layer][...])
+            here = slice(starts[layer], starts[layer] + size)
+            full = up(io["term%d_0" % layer][here, :])
             for at in range(1, len(terms[layer])):
-                full = full + up(io["term%d_%d" % (layer, at)][...])
+                full = full + up(io["term%d_%d" % (layer, at)][here, :])
             if kind == "mix":
                 io.first[layer] = full[:, D // 4 :]
                 io.second[layer] = full[:, : D // 4]
             else:
-                io.first[layer] = full[96:]
-                io.second[layer, :, :96] = full[:96, : D // 2].T
-                io.second[layer, :, 96:] = full[:96, D // 2 :].T
+                io.first[layer] = full[:96]
+                io.second[layer, :, :96] = full[96:, : D // 2].T
+                io.second[layer, :, 96:] = full[96:, D // 2 :].T
         io.done("first")
         io.done("second")
 
@@ -1373,8 +1385,8 @@
             found, token = grad_near([group[name] for name in names], (token,))
             return (found.stay, narrow_swap(found.near, NEAR)), token
 
-        def far(kinds, pair, token):
-            found, token = grad_far(kinds, *pair, (token,))
+        def far(kinds, pairs, token):
+            found, token = grad_far(kinds, pairs, (token,))
             return (found.own, narrow_swap(found.far, FAR)), token
 
         def gather(kinds, names, token, *after):
@@ -1393,10 +1405,21 @@
         token = send("i1", "inner", (one.midt, back1.gpre), token)
         token = keep("o1", "y", token)
         token = keep("i1", "x", token)
+        def features(kept):
+            return Box(
+                mixt=("f", kept.mixt, [whole_cut], (D, rows)),
+                xt=("f", kept.xt, [whole_cut], (D, rows)),
+            )
+
+        def mix_operands(mix):
+            return mix.mixt.reshape(D, rows), mix.xt.reshape(D, rows), mix.gcol
+
+        fetch = weight_fetch(0)
+        fetch.update(features(one))
         mix1, token = mix_back(
-            1, later1, spot, back1, one, cs, cm, wq_cuts[1], zero, weight_fetch(0), (token,)
+            1, later1, spot, back1, one, cs, cm, wq_cuts[1], zero, fetch, (token,)
         )
-        token = send("m1", "mix", (one.mixt, one.xt, mix1.gcol), token)
+        token = send("m1", "mix", mix_operands(mix1), token)
         token = forward(["o1"], token)
         token = forward(["i1"], token)
         gb2t_got = wide_swap(mix1.gb2t, ALONG)
@@ -1413,38 +1436,38 @@
         token = send("o0", "pair", pair, token)
         both, token = add_up(back0.state, later0[0], (token,))
         later0.append(move(both, -2))
+        f1, token = gather(["inner", "out"], ["i1", "o1"], token)
         token = send("i0", "inner", (back0.midt.reshape(D, rows), back0.gpre), token)
         token = forward(["m1"], token)
         token = keep("o0", "x", token)
         token = keep("i0", "both", token)
-        f1, token = gather(["out", "inner"], ["o1", "i1"], token, later0[1])
         mix0, token = mix_back(
-            0, later0, spot, back0, zero, cs, cm, wq_cuts[0], None, Box(), (token,)
+            0, later0, spot, back0, zero, cs, cm, wq_cuts[0], None, features(zero), (token,)
         )
         input_grad = mix0.grad
         parts = (mix1.sums_a, back0.sums_b, mix0.sums_c, one.sums_a, back1.sums_b, mix1.sums_c)
-        token = send("m0", "mix", (zero.mixt, zero.xt, mix0.gcol), token)
+        token = send("m0", "mix", mix_operands(mix0), token)
+        near_a, token = near(["o0", "m1"], token)
         token = forward(["i0"], token)
         token = keep("m0", "both", token)
-        near_f0, token = near(["o0", "i0"], token)
+        near_b, token = near(["i0"], token)
         sums, token = collect_sums(parts, (token,))
         come = wide_swap(sums, CORE)
-        mg1, token = gather(["mix"], ["m1"], token)
         sums, token = add_up(sums, come, (token,))
         come = wide_swap(sums, ACROSS)
         token = forward(["m0"], token)
         sums, token = add_up(sums, come, (token,))
         come = wide_swap(sums, ALONG)
-        far_f0, token = far(["out", "inner both"], near_f0, token)
+        far_f0, token = far(["inner both", "out", "mix both"], [near_b, near_a], token)
         sums, token = add_up(sums, come, (token,))
         come = narrow_swap(sums, NEAR)
         near_m0, token = near(["m0"], token)
         sums, token = add_up(sums, come, (token,))
         come = narrow_swap(sums, FAR)
-        far_m0, token = far(["mix"], near_m0, token)
-        ffn_grads, token = grad_last("ffn", [far_f0, f1], (token,))
+        far_m0, token = far(["mix both"], [near_m0], token)
+        ffn_grads, token = grad_last("ffn", [far_f0, f1], (0, 0), (token,))
         sums, token = add_up(sums, come, (token,))
-        mix_grads, token = grad_last("mix", [far_m0, mg1], (token,))
+        mix_grads, token = grad_last("mix", [far_m0, far_f0], (0, 192), (token,))
         sums = sums[:26].reshape(LAYERS, 13, D)
         grad_qkv, grad_o = mix_grads.first, mix_grads.second
         grad_in, grad_out = ffn_grads.first, ffn_grads.second

time: 285 us -> 277 us (0.972)
  Pallas kernels: 119 us -> 107 us
  waiting for transfers between devices: 60.8 us -> 68.8 us
  starting transfers between devices: 72.1 us -> 66.1 us
    pallas_call x42, Pallas kernels: 119 us -> 107 us  [run(): pl.pallas_call(kernel, out_shape=tuple(out_shapes), in_specs=in_specs, ou...]
    ppermute x6 -> x7, starting transfers between devices: 15.6 us -> 9.36 us  [narrow_swap(): return lax.ppermute(v, 'narrow', [(i, i ^ bit) for i in range(size)])]
    ppermute x6 -> x7, waiting for transfers between devices: 19.5 us -> 24.8 us  [narrow_swap(): return lax.ppermute(v, 'narrow', [(i, i ^ bit) for i in range(size)])]
    unnamed x65 -> x39, local copies, waits for them, and re-layouts: 6.74 us -> 9.24 us
  transfers between devices with their start and end apart: 47 -> 47, of which waited for: 17 -> 18; matrix products, arithmetic and copies ran while one was open for 2% -> 2% of each run, Pallas kernels for 35% -> 31%
where the time goes in v4:
time: 277 us; the launch traced here: 273 us
  Pallas kernels  107 us (39%)
  waiting for transfers between devices  68.8 us (25%)
  starting transfers between devices  66.1 us (24%)
  between operations  16.7 us (6%)
  local copies, waits for them, and re-layouts  11.3 us (4%)
  other arithmetic  3.55 us (1%)
    pallas_call x42, Pallas kernels, run(): pl.pallas_call(kernel, out_shape=tuple(out_shapes), in_specs=in_specs, ou...  107 us
    ppermute x11, starting transfers between devices, move(): return lax.ppermute(v, 'narrow', pairs)  30.5 us
    ppermute x28, waiting for transfers between devices, wide_swap(): return lax.ppermute(v, 'wide', [(i, i ^ bit) for i in range(size)])  29.4 us
    ppermute x28, starting transfers between devices, wide_swap(): return lax.ppermute(v, 'wide', [(i, i ^ bit) for i in range(size)])  26.2 us
    ppermute x7, waiting for transfers between devices, narrow_swap(): return lax.ppermute(v, 'narrow', [(i, i ^ bit) for i in range(size)])  24.8 us
    ppermute x11, waiting for transfers between devices, move(): return lax.ppermute(v, 'narrow', pairs)  14.6 us
    ppermute x7, starting transfers between devices, narrow_swap(): return lax.ppermute(v, 'narrow', [(i, i ^ bit) for i in range(size)])  9.36 us
    unnamed x39, local copies, waits for them, and re-layouts  9.24 us
  transfers between devices with their start and end apart: 47, of which 18 were waited for; matrix products, arithmetic and copies ran while one was open for 2% of the time, Pallas kernels for 31%

profile of v4, /device:TPU:0, one launch (start us, length us, event | category | flops | bytes accessed | tf_op | source)
XLA Modules:
  0.0 273.4 jit_solution(4890153386810338327)
XLA Ops:
  9.1 6.6 %shard_map.186 = (bf16[256,2304]{1,0:T(8,128)(2,1)S(1)}, bf16[768,256]{1,0:T(8,128)(2,1)}, bf16[784,128]{1,0:T(8,128)(2,1)S(1)}, bf16[256,2304]{1,0:T(8,128)(2,1)}, f32[8,128]{1,0:T(8,128)S(1)}) custom-call(s32[6]{0:T(128)S(1)} %stack.33.refs_0_.refs_12_.refs_3_.refs_11_.refs_6_.refs_2_, bf16[256,768]{1,0:T(8,128)(2,1)} %refs_3_.4, ...), custom_call_target="tpu_custom_call" | custom-call | flops 10000000000 | bytes 100000000 | tf_op jit(solution)/shard_map/pallas_call | solution.py:247
  15.7 4.9 %collective-permute-start = (bf16[784,128]{1,0:T(8,128)(2,1)S(1)}, bf16[784,128]{1,0:T(8,128)(2,1)S(1)}, u32[]{:S(2)}, u32[]{:S(2)}) collective-permute-start(bf16[784,128]{1,0:T(8,128)(2,1)S(1)} %get-tuple-element.187), channel_id=1, source_target_pairs={{0,1},{1,2},{2,3},{4,5},{5,6},{6,7},{8,9},{9,10},{10,11},{12,13},{... | collective-permute-start | bytes 602120 | tf_op jit(solution)/shard_map/ppermute | solution.py:1184
  20.7 4.5 %collective-permute-start.1 = (bf16[784,128]{1,0:T(8,128)(2,1)S(1)}, bf16[784,128]{1,0:T(8,128)(2,1)S(1)}, u32[]{:S(2)}, u32[]{:S(2)}) collective-permute-start(bf16[784,128]{1,0:T(8,128)(2,1)S(1)} %get-tuple-element.187), channel_id=1, source_target_pairs={{0,2},{1,3},{4,6},{5,7},{8,10},{9,11},{12,14},{13,15},{16,18},{17,... | collective-permute-start | bytes 602120 | tf_op jit(solution)/shard_map/ppermute | solution.py:1184
  25.2 1.5 collective-permute-start.2
  27.9 1.4 cosine_select_fusion.refs_2_.refs_10_.refs_9_
  29.2 6.0 %shard_map.187 = (f32[256,768]{1,0:T(8,128)S(1)}, f32[256,768]{1,0:T(8,128)S(1)}, bf16[256,768]{1,0:T(8,128)(2,1)S(1)}, bf16[256,768]{1,0:T(8,128)(2,1)}, bf16[1...) custom-call(s32[6]{0:T(128)S(1)} %stack.33.refs_0_.refs_12_.refs_3_., ...), custom_call_target="tpu_custom_call" | custom-call | flops 10000000000 | bytes 100000000 | tf_op jit(solution)/shard_map/pallas_call | solution.py:247
  35.3 8.5 %shard_map.188 = (bf16[784,128]{1,0:T(8,128)(2,1)}, bf16[256,768]{1,0:T(8,128)(2,1)}, bf16[768,256]{1,0:T(8,128)(2,1)}, f32[256,768]{1,0:T(8,128)}, f32[256,768]...) custom-call(bf16[784,128]{1,0:T(8,128)(2,1)S(1)} %collective-permute, ...), custom_call_target="tpu_custom_call" | custom-call | flops 10000000000 | bytes 100000000 | tf_op jit(solution)/shard_map/pallas_call | solution.py:247
  43.7 4.8 %shard_map.189 = (bf16[256,2304]{1,0:T(8,128)(2,1)S(1)}, bf16[768,256]{1,0:T(8,128)(2,1)}, bf16[784,128]{1,0:T(8,128)(2,1)S(1)}, bf16[256,2304]{1,0:T(8,128)(2,1...) custom-call(s32[6]{0:T(128)S(1)} %stack.33.refs_0_.refs_12_.refs_3_.refs_11_.refs_6_.refs_2_, ...), custom_call_target="tpu_custom_call" | custom-call | flops 10000000000 | bytes 100000000 | tf_op jit(solution)/shard_map/pallas_call | solution.py:247
  48.5 6.0 %collective-permute-start.3 = (bf16[784,128]{1,0:T(8,128)(2,1)S(1)}, bf16[784,128]{1,0:T(8,128)(2,1)S(1)}, u32[]{:S(2)}, u32[]{:S(2)}) collective-permute-start(bf16[784,128]{1,0:T(8,128)(2,1)S(1)} %get-tuple-element.201), channel_id=1, source_target_pairs={{0,1},{1,2},{2,3},{4,5},{5,6},{6,7},{8,9},{9,10},{10,11},{12,13},{... | collective-permute-start | bytes 602120 | tf_op jit(solution)/shard_map/ppermute | solution.py:1184
  54.5 5.3 %collective-permute-start.4 = (bf16[784,128]{1,0:T(8,128)(2,1)S(1)}, bf16[784,128]{1,0:T(8,128)(2,1)S(1)}, u32[]{:S(2)}, u32[]{:S(2)}) collective-permute-start(bf16[784,128]{1,0:T(8,128)(2,1)S(1)} %get-tuple-element.201), channel_id=1, source_target_pairs={{0,2},{1,3},{4,6},{5,7},{8,10},{9,11},{12,14},{13,15},{16,18},{17,... | collective-permute-start | bytes 602120 | tf_op jit(solution)/shard_map/ppermute | solution.py:1184
  59.8 1.8 collective-permute-start.5
  61.6 1.6 collective-permute-start.6
  63.1 4.8 %shard_map.190 = (f32[256,768]{1,0:T(8,128)S(1)}, f32[256,768]{1,0:T(8,128)S(1)}, bf16[256,768]{1,0:T(8,128)(2,1)S(1)}, bf16[1,768,768]{2,1,0:T(8,128)(2,1)S(1)}...) custom-call(s32[6]{0:T(128)S(1)} %stack.33.refs_0_.refs_12_.refs_3_.refs_11_.refs_6_.refs_, ...), custom_call_target="tpu_custom_call" | custom-call | flops 10000000000 | bytes 100000000 | tf_op jit(solution)/shard_map/pallas_call | solution.py:247
  68.0 7.5 %shard_map.191 = (bf16[784,128]{1,0:T(8,128)(2,1)}, bf16[256,768]{1,0:T(8,128)(2,1)S(1)}, bf16[768,256]{1,0:T(8,128)(2,1)}, f32[256,768]{1,0:T(8,128)S(1)}, f32[...) custom-call(bf16[784,128]{1,0:T(8,128)(2,1)S(1)} %collective-permute, ...), custom_call_target="tpu_custom_call" | custom-call | flops 10000000000 | bytes 100000000 | tf_op jit(solution)/shard_map/pallas_call | solution.py:247
  75.5 1.4 shard_map.192
  77.0 2.4 collective-permute-done.6.refs_11_.refs_15_
  80.5 6.0 %shard_map.193 = (bf16[256,3072]{1,0:T(8,128)(2,1)S(1)}, bf16[256,768]{1,0:T(8,128)(2,1)S(1)}, f32[256,768]{1,0:T(8,128)S(1)}, bf16[256,768]{1,0:T(8,128)(2,1)S(...) custom-call(f32[256,768]{1,0:T(8,128)S(1)} %get-tuple-element.212.ref, ...), custom_call_target="tpu_custom_call" | custom-call | flops 300000000 | bytes 100000000 | tf_op jit(solution)/shard_map/pallas_call | solution.py:247
  86.5 1.4 shard_map.194
  88.0 1.3 collective-permute-start.7
  90.6 1.4 shard_map.195
  92.0 1.6 collective-permute-start.13
  94.9 1.4 shard_map.196
  96.3 1.6 collective-permute-start.12
  97.9 12.4 %collective-permute-done.8.refs_1_ = bf16[784,128]{1,0:T(8,128)(2,1)S(1)} collective-permute-done((bf16[784,128]{1,0:T(8,128)(2,1)S(1)}, bf16[784,128]{1,0:T(8,128)(2,1)S(1)}, u32[]{:S(2)}, u32[]{:S(2)}) %collective-permute-start.8) | collective-permute-done | bytes 200736 | tf_op jit(solution)/shard_map/ppermute | solution.py:1184
  110.3 10.8 %shard_map.197 = (bf16[2,256,1536]{2,1,0:T(8,128)(2,1)S(1)}, f32[8,768]{1,0:T(8,128)}, f32[256,768]{1,0:T(8,128)S(1)}, bf16[256,768]{1,0:T(8,128)(2,1)S(1)}, bf1...) custom-call(bf16[784,128]{1,0:T(8,128)(2,1)S(1)} %collective-permute, ...), custom_call_target="tpu_custom_call" | custom-call | flops 300000000 | bytes 100000000 | tf_op jit(solution)/shard_map/pallas_call | solution.py:247
  121.1 1.4 shard_map.198
  122.6 1.6 collective-permute-start.15
  124.3 1.6 collective-permute-start.19
  126.6 7.7 %shard_map.201 = (bf16[256,3072]{1,0:T(8,128)(2,1)S(1)}, bf16[256,768]{1,0:T(8,128)(2,1)S(1)}, f32[256,768]{1,0:T(8,128)S(1)}, bf16[256,768]{1,0:T(8,128)(2,1)S(...) custom-call(f32[256,768]{1,0:T(8,128)S(1)} %get-tuple-element.243.re, ...), custom_call_target="tpu_custom_call" | custom-call | flops 15000000512 | bytes 100000000 | tf_op jit(solution)/shard_map/pallas_call | solution.py:247
  135.6 1.4 shard_map.202
  137.7 1.5 collective-permute-start.23
  139.2 1.4 shard_map.203
  140.6 2.1 collective-permute-done.14.refs_1_.refs_0_
  142.8 4.4 %collective-permute-done.18.refs_2_ = bf16[2,192,768]{2,1,0:T(8,128)(2,1)S(1)} collective-permute-done((bf16[2,192,768]{2,1,0:T(8,128)(2,1)S(1)}, bf16[2,192,768]{2,1,0:T(8,128)(2,1)S(1)}, u32[]{:S(2)}, u32[]{:S(2)}) %collective-permute-start.18) | collective-permute-done | bytes 589856 | tf_op jit(solution)/shard_map/ppermute | solution.py:1163
  147.2 2.0 shard_map.205
  149.3 1.4 shard_map.206
  152.4 7.0 %collective-permute-done.23.refs_3_.refs_6_ = bf16[2,2,48,1536]{3,2,1,0:T(8,128)(2,1)S(1)} collective-permute-done((bf16[2,2,48,1536]{3,2,1,0:T(8,128)(2,1)S(1)}, bf16[2,2,48,1536]{3,2,1,0:T(8,128)(2,1)S(1)}, u32[]{:S(2)}, u32[]{:S(2)}) %collective-permute-start.23) | collective-permute-done | bytes 589856 | tf_op jit(solution)/shard_map/ppermute | solution.py:1163
  160.3 1.6 collective-permute-start.28
  161.9 1.5 collective-permute-start.29
  163.4 2.2 shard_map.208
  167.0 2.4 shard_map.209
  170.2 1.5 collective-permute-start.25
  172.2 9.9 %shard_map.210 = (bf16[2,256,1536]{2,1,0:T(8,128)(2,1)S(1)}, f32[8,768]{1,0:T(8,128)}, f32[256,768]{1,0:T(8,128)}, bf16[1,768,256]{2,1,0:T(8,128)(2,1)S(1)}, bf1...) custom-call(bf16[784,128]{1,0:T(8,128)(2,1)S(1)} %collective-permute-done.14.refs_1_.refs_0_, ...), custom_call_target="tpu_custom_call" | custom-call | flops 6000000000 | bytes 100000000 | tf_op jit(solution)/shard_map/pallas_call | solution.py:247
  182.2 2.8 %shard_map.211 = (bf16[4,2,96,1536]{3,2,1,0:T(8,128)(2,1)}, f32[8,128]{1,0:T(8,128)S(1)}) custom-call(s32[6]{0:T(128)S(1)} %stack.33.refs_0_.refs_12_.refs_3_.refs_11_.refs_6_.refs_2_, bf16[768,256]{1,0:T(8,128)(2,1)S(1)} %bitcast.27, bf16[768,256]{1,0:T(8,128)(2,1)S(1)} %bitcast.29, bf16[2,256,1536]{2,1,0:T(8,128)(2,1)S(1)} %get-tuple-element.302.refs_3_, ...), custom_call_target="tpu_custom_call" | custom-call | flops 300000000 | bytes 100000000 | tf_op jit(solution)/shard_map/pallas_call | solution.py:247
  189.6 1.7 shard_map.212
  191.4 4.4 %collective-permute-done.25.refs_1_ = bf16[2,2,96,768]{3,2,1,0:T(8,128)(2,1)} collective-permute-done((bf16[2,2,96,768]{3,2,1,0:T(8,128)(2,1)}, bf16[2,2,96,768]{3,2,1,0:T(8,128)(2,1)}, u32[]{:S(2)}, u32[]{:S(2)}) %collective-permute-start.25) | collective-permute-done | bytes 589856 | tf_op jit(solution)/shard_map/ppermute | solution.py:1163
  195.8 1.5 shard_map.213
  197.9 1.5 collective-permute-start.33
  199.4 2.6 shard_map.214
  202.6 1.5 collective-permute-start.31
  204.2 2.5 collective-permute-done.32.refs_2_
  207.4 1.5 shard_map.215
  211.3 2.0 collective-permute-start.37
  213.2 5.5 %collective-permute-done.30.refs_1_ = bf16[2,2,48,1536]{3,2,1,0:T(8,128)(2,1)S(1)} collective-permute-done((bf16[2,2,48,1536]{3,2,1,0:T(8,128)(2,1)S(1)}, bf16[2,2,48,1536]{3,2,1,0:T(8,128)(2,1)S(1)}, u32[]{:S(2)}, u32[]{:S(2)}) %collective-permute-start.30) | collective-permute-done | bytes 589856 | tf_op jit(solution)/shard_map/ppermute | solution.py:1163
  219.8 1.6 collective-permute-start.38
  221.9 1.5 collective-permute-start.36
  223.4 6.5 %collective-permute-done.39.refs_1_ = bf16[192,768]{1,0:T(8,128)(2,1)S(1)} collective-permute-done((bf16[192,768]{1,0:T(8,128)(2,1)S(1)}, bf16[192,768]{1,0:T(8,128)(2,1)S(1)}, u32[]{:S(2)}, u32[]{:S(2)}) %collective-permute-start.39) | collective-permute-done | bytes 294944 | tf_op jit(solution)/shard_map/ppermute | solution.py:1168
  230.2 2.1 collective-permute-start.44
  234.7 14.7 %collective-permute-done.42.refs_1_ = f32[32,768]{1,0:T(8,128)S(1)} collective-permute-done((f32[32,768]{1,0:T(8,128)S(1)}, f32[32,768]{1,0:T(8,128)S(1)}, u32[]{:S(2)}, u32[]{:S(2)}) %collective-permute-start.42) | collective-permute-done | bytes 98336 | tf_op jit(solution)/shard_map/ppermute | solution.py:1168
  249.4 2.8 %collective-permute-start.45 = (f32[32,768]{1,0:T(8,128)S(1)}, f32[32,768]{1,0:T(8,128)S(1)}, u32[]{:S(2)}, u32[]{:S(2)}) collective-permute-start(f32[32,768]{1,0:T(8,128)S(1)} %get-tuple-element.354.refs_0_), channel_id=1, source_target_pairs={{0,2},{1,3},{2,0},{3,1},{4,6},{5,7},{6,4},{7,5},{8,10},{9,11},{10,... | collective-permute-start | bytes 294920 | tf_op jit(solution)/shard_map/ppermute | solution.py:1168
  253.7 1.4 shard_map.225
  255.9 2.2 collective-permute-start.43
  261.8 2.7 collective-permute-done.43.refs_1_
  264.5 1.6 shard_map.227
  (125 shorter events, 32.8 us)
Async XLA Ops:
  7.2 245.3 %reduce-scatter.2.cloned.1.call-start = ((), (), s32[]{:S(2)}) async-start(), calls=%async_computation.1 | async-start | bytes 1474560 | tf_op jit(solution)/shard_map/reduce_scatter | solution.py:1397
  15.7 19.5 %collective-permute-start = (bf16[784,128]{1,0:T(8,128)(2,1)S(1)}, bf16[784,128]{1,0:T(8,128)(2,1)S(1)}, u32[]{:S(2)}, u32[]{:S(2)}) collective-permute-start(bf16[784,128]{1,0:T(8,128)(2,1)S(1)} %get-tuple-element.187), channel_id=1, source_target_pairs={{0,1},{1,2},{2,3},{4,5},{5,6},{6,7},{8,9},{9,10},{10,11},{12,13},{... | collective-permute-start | bytes 602120 | tf_op jit(solution)/shard_map/ppermute | solution.py:1184
  20.7 14.6 %collective-permute-start.1 = (bf16[784,128]{1,0:T(8,128)(2,1)S(1)}, bf16[784,128]{1,0:T(8,128)(2,1)S(1)}, u32[]{:S(2)}, u32[]{:S(2)}) collective-permute-start(bf16[784,128]{1,0:T(8,128)(2,1)S(1)} %get-tuple-element.187), channel_id=1, source_target_pairs={{0,2},{1,3},{4,6},{5,7},{8,10},{9,11},{12,14},{13,15},{16,18},{17,... | collective-permute-start | bytes 602120 | tf_op jit(solution)/shard_map/ppermute | solution.py:1184
  25.2 10.1 %collective-permute-start.2 = (bf16[784,128]{1,0:T(8,128)(2,1)S(1)}, bf16[784,128]{1,0:T(8,128)(2,1)S(1)}, u32[]{:S(2)}, u32[]{:S(2)}) collective-permute-start(bf16[784,128]{1,0:T(8,128)(2,1)S(1)} %get-tuple-element.187), channel_id=1, source_target_pairs={{0,3},{4,7},{8,11},{12,15},{16,19},{20,23},{24,27},{28,31}} | collective-permute-start | bytes 602120 | tf_op jit(solution)/shard_map/ppermute | solution.py:1184
  48.5 19.5 %collective-permute-start.3 = (bf16[784,128]{1,0:T(8,128)(2,1)S(1)}, bf16[784,128]{1,0:T(8,128)(2,1)S(1)}, u32[]{:S(2)}, u32[]{:S(2)}) collective-permute-start(bf16[784,128]{1,0:T(8,128)(2,1)S(1)} %get-tuple-element.201), channel_id=1, source_target_pairs={{0,1},{1,2},{2,3},{4,5},{5,6},{6,7},{8,9},{9,10},{10,11},{12,13},{... | collective-permute-start | bytes 602120 | tf_op jit(solution)/shard_map/ppermute | solution.py:1184
  54.5 13.5 %collective-permute-start.4 = (bf16[784,128]{1,0:T(8,128)(2,1)S(1)}, bf16[784,128]{1,0:T(8,128)(2,1)S(1)}, u32[]{:S(2)}, u32[]{:S(2)}) collective-permute-start(bf16[784,128]{1,0:T(8,128)(2,1)S(1)} %get-tuple-element.201), channel_id=1, source_target_pairs={{0,2},{1,3},{4,6},{5,7},{8,10},{9,11},{12,14},{13,15},{16,18},{17,... | collective-permute-start | bytes 602120 | tf_op jit(solution)/shard_map/ppermute | solution.py:1184
  59.8 8.2 %collective-permute-start.5 = (bf16[784,128]{1,0:T(8,128)(2,1)S(1)}, bf16[784,128]{1,0:T(8,128)(2,1)S(1)}, u32[]{:S(2)}, u32[]{:S(2)}) collective-permute-start(bf16[784,128]{1,0:T(8,128)(2,1)S(1)} %get-tuple-element.201), channel_id=1, source_target_pairs={{0,3},{4,7},{8,11},{12,15},{16,19},{20,23},{24,27},{28,31}} | collective-permute-start | bytes 602120 | tf_op jit(solution)/shard_map/ppermute | solution.py:1184
  61.6 17.9 %collective-permute-start.6 = (bf16[1,256,1536]{2,1,0:T(8,128)(2,1)S(1)}, bf16[1,256,1536]{2,1,0:T(8,128)(2,1)S(1)}, u32[]{:S(2)}, u32[]{:S(2)}) collective-permute-start(bf16[1,256,1536]{2,1,0:T(8,128)(2,1)S(1)} %get-tuple-element.219), channel_id=1, source_target_pairs={{0,16},{4,20},{8,24},{12,28},{16,0},{20,4},{24,8},{28,12},{1,17},{... | collective-permute-start | bytes 2359304 | tf_op jit(solution)/shard_map/ppermute | solution.py:1163
  77.0 13.6 %collective-permute-start.11 = (bf16[4,2,192,768]{3,2,1,0:T(8,128)(2,1)S(1)}, bf16[4,2,192,768]{3,2,1,0:T(8,128)(2,1)S(1)}, u32[]{:S(2)}, u32[]{:S(2)}) collective-permute-start(bf16[4,2,192,768]{3,2,1,0:T(8,128)(2,1)S(1)} %get-tuple-element.239), channel_id=1, source_target_pairs={{0,4},{4,0},{8,12},{12,8},{16,20},{20,16},{24,28},{28,24},{1,5},{5... | collective-permute-start | bytes 7077896 | tf_op jit(solution)/shard_map/ppermute | solution.py:1163
  79.5 1.0 copy-start.15
  87.9 7.0 %collective-permute-start.10 = (bf16[4,2,192,768]{3,2,1,0:T(8,128)(2,1)S(1)}, bf16[4,2,192,768]{3,2,1,0:T(8,128)(2,1)S(1)}, u32[]{:S(2)}, u32[]{:S(2)}) collective-permute-start(bf16[4,2,192,768]{3,2,1,0:T(8,128)(2,1)S(1)} %get-tuple-element.238), channel_id=1, source_target_pairs={{0,4},{4,0},{8,12},{12,8},{16,20},{20,16},{24,28},{28,24},{1,5},{5... | collective-permute-start | bytes 7077896 | tf_op jit(solution)/shard_map/ppermute | solution.py:1163
  88.0 10.0 %collective-permute-start.7 = (bf16[784,128]{1,0:T(8,128)(2,1)S(1)}, bf16[784,128]{1,0:T(8,128)(2,1)S(1)}, u32[]{:S(2)}, u32[]{:S(2)}) collective-permute-start(bf16[784,128]{1,0:T(8,128)(2,1)S(1)} %get-tuple-element.224), channel_id=1, source_target_pairs={{1,0},{2,1},{3,2},{5,4},{6,5},{7,6},{9,8},{10,9},{11,10},{13,12},{... | collective-permute-start | bytes 602120 | tf_op jit(solution)/shard_map/ppermute | solution.py:1184
  89.3 21.0 %collective-permute-start.8 = (bf16[784,128]{1,0:T(8,128)(2,1)S(1)}, bf16[784,128]{1,0:T(8,128)(2,1)S(1)}, u32[]{:S(2)}, u32[]{:S(2)}) collective-permute-start(bf16[784,128]{1,0:T(8,128)(2,1)S(1)} %get-tuple-element.224), channel_id=1, source_target_pairs={{2,0},{3,1},{6,4},{7,5},{10,8},{11,9},{14,12},{15,13},{18,16},{19,... | collective-permute-start | bytes 602120 | tf_op jit(solution)/shard_map/ppermute | solution.py:1184
  92.0 32.2 %collective-permute-start.13 = (bf16[2,2,192,768]{3,2,1,0:T(8,128)(2,1)S(1)}, bf16[2,2,192,768]{3,2,1,0:T(8,128)(2,1)S(1)}, u32[]{:S(2)}, u32[]{:S(2)}) collective-permute-start(bf16[2,2,192,768]{3,2,1,0:T(8,128)(2,1)S(1)} %get-tuple-element.258), channel_id=1, source_target_pairs={{0,16},{4,20},{8,24},{12,28},{16,0},{20,4},{24,8},{28,12},{1,17},{... | collective-permute-start | bytes 3538952 | tf_op jit(solution)/shard_map/ppermute | solution.py:1163
  93.6 16.7 %collective-permute-start.9 = (bf16[784,128]{1,0:T(8,128)(2,1)S(1)}, bf16[784,128]{1,0:T(8,128)(2,1)S(1)}, u32[]{:S(2)}, u32[]{:S(2)}) collective-permute-start(bf16[784,128]{1,0:T(8,128)(2,1)S(1)} %get-tuple-element.224), channel_id=1, source_target_pairs={{3,0},{7,4},{11,8},{15,12},{19,16},{23,20},{27,24},{31,28}} | collective-permute-start | bytes 602120 | tf_op jit(solution)/shard_map/ppermute | solution.py:1184
  96.3 29.6 %collective-permute-start.12 = (bf16[2,2,192,768]{3,2,1,0:T(8,128)(2,1)S(1)}, bf16[2,2,192,768]{3,2,1,0:T(8,128)(2,1)S(1)}, u32[]{:S(2)}, u32[]{:S(2)}) collective-permute-start(bf16[2,2,192,768]{3,2,1,0:T(8,128)(2,1)S(1)} %get-tuple-element.256), channel_id=1, source_target_pairs={{0,8},{4,12},{8,0},{12,4},{16,24},{20,28},{24,16},{28,20},{1,9},{5... | collective-permute-start | bytes 3538952 | tf_op jit(solution)/shard_map/ppermute | solution.py:1163
  122.5 13.1 %collective-permute-start.16 = (bf16[4,2,96,1536]{3,2,1,0:T(8,128)(2,1)S(1)}, bf16[4,2,96,1536]{3,2,1,0:T(8,128)(2,1)S(1)}, u32[]{:S(2)}, u32[]{:S(2)}) collective-permute-start(bf16[4,2,96,1536]{3,2,1,0:T(8,128)(2,1)S(1)} %get-tuple-element.270), channel_id=1, source_target_pairs={{0,4},{4,0},{8,12},{12,8},{16,20},{20,16},{24,28},{28,24},{1,5},{5... | collective-permute-start | bytes 7077896 | tf_op jit(solution)/shard_map/ppermute | solution.py:1163
  122.6 15.1 %collective-permute-start.15 = (bf16[768,256]{1,0:T(8,128)(2,1)S(1)}, bf16[768,256]{1,0:T(8,128)(2,1)S(1)}, u32[]{:S(2)}, u32[]{:S(2)}) collective-permute-start(bf16[768,256]{1,0:T(8,128)(2,1)S(1)} %get-tuple-element.267.refs_1_), channel_id=1, source_target_pairs={{0,16},{4,20},{8,24},{12,28},{16,0},{20,4},{24,8},{28,12},{1,17},{... | collective-permute-start | bytes 1179656 | tf_op jit(solution)/shard_map/ppermute | solution.py:1163
  124.3 18.4 %collective-permute-start.19 = (bf16[2,192,768]{2,1,0:T(8,128)(2,1)S(1)}, bf16[2,192,768]{2,1,0:T(8,128)(2,1)S(1)}, u32[]{:S(2)}, u32[]{:S(2)}) collective-permute-start(bf16[2,192,768]{2,1,0:T(8,128)(2,1)S(1)} %get-tuple-element.286), channel_id=1, source_target_pairs={{0,8},{4,12},{8,0},{12,4},{16,24},{20,28},{24,16},{28,20},{1,9},{5... | collective-permute-start | bytes 1769480 | tf_op jit(solution)/shard_map/ppermute | solution.py:1163
  126.1 21.2 %collective-permute-start.18 = (bf16[2,192,768]{2,1,0:T(8,128)(2,1)S(1)}, bf16[2,192,768]{2,1,0:T(8,128)(2,1)S(1)}, u32[]{:S(2)}, u32[]{:S(2)}) collective-permute-start(bf16[2,192,768]{2,1,0:T(8,128)(2,1)S(1)} %get-tuple-element.285), channel_id=1, source_target_pairs={{0,16},{4,20},{8,24},{12,28},{16,0},{20,4},{24,8},{28,12},{1,17},{... | collective-permute-start | bytes 1769480 | tf_op jit(solution)/shard_map/ppermute | solution.py:1163
  134.3 8.4 %collective-permute-start.14 = (bf16[784,128]{1,0:T(8,128)(2,1)S(1)}, bf16[784,128]{1,0:T(8,128)(2,1)S(1)}, u32[]{:S(2)}, u32[]{:S(2)}) collective-permute-start(bf16[784,128]{1,0:T(8,128)(2,1)S(1)} %get-tuple-element.266.refs_0_), channel_id=1, source_target_pairs={{1,0},{2,1},{3,2},{5,4},{6,5},{7,6},{9,8},{10,9},{11,10},{13,12},{... | collective-permute-start | bytes 602120 | tf_op jit(solution)/shard_map/ppermute | solution.py:1184
  137.1 15.4 %collective-permute-start.22 = (bf16[2,2,48,1536]{3,2,1,0:T(8,128)(2,1)S(1)}, bf16[2,2,48,1536]{3,2,1,0:T(8,128)(2,1)S(1)}, u32[]{:S(2)}, u32[]{:S(2)}) collective-permute-start(bf16[2,2,48,1536]{3,2,1,0:T(8,128)(2,1)S(1)} %get-tuple-element.292), channel_id=1, source_target_pairs={{0,8},{4,12},{8,0},{12,4},{16,24},{20,28},{24,16},{28,20},{1,9},{5... | collective-permute-start | bytes 1769480 | tf_op jit(solution)/shard_map/ppermute | solution.py:1163
  137.7 21.7 %collective-permute-start.23 = (bf16[2,2,48,1536]{3,2,1,0:T(8,128)(2,1)S(1)}, bf16[2,2,48,1536]{3,2,1,0:T(8,128)(2,1)S(1)}, u32[]{:S(2)}, u32[]{:S(2)}) collective-permute-start(bf16[2,2,48,1536]{3,2,1,0:T(8,128)(2,1)S(1)} %get-tuple-element.294), channel_id=1, source_target_pairs={{0,16},{4,20},{8,24},{12,28},{16,0},{20,4},{24,8},{28,12},{1,17},{... | collective-permute-start | bytes 1769480 | tf_op jit(solution)/shard_map/ppermute | solution.py:1163
  142.7 20.7 %collective-permute-start.21 = (bf16[2,2,192,768]{3,2,1,0:T(8,128)(2,1)S(1)}, bf16[2,2,192,768]{3,2,1,0:T(8,128)(2,1)S(1)}, u32[]{:S(2)}, u32[]{:S(2)}) collective-permute-start(bf16[2,2,192,768]{3,2,1,0:T(8,128)(2,1)S(1)} %get-tuple-element.290), channel_id=1, source_target_pairs={{0,4},{4,0},{8,12},{12,8},{16,20},{20,16},{24,28},{28,24},{1,5},{5... | collective-permute-start | bytes 3538952 | tf_op jit(solution)/shard_map/ppermute | solution.py:1163
  150.6 16.3 %collective-permute-start.20 = (bf16[4,2,192,768]{3,2,1,0:T(8,128)(2,1)S(1)}, bf16[4,2,192,768]{3,2,1,0:T(8,128)(2,1)S(1)}, u32[]{:S(2)}, u32[]{:S(2)}) collective-permute-start(bf16[4,2,192,768]{3,2,1,0:T(8,128)(2,1)S(1)} %get-tuple-element.289), channel_id=1, source_target_pairs={{0,4},{4,0},{8,12},{12,8},{16,20},{20,16},{24,28},{28,24},{1,5},{5... | collective-permute-start | bytes 7077896 | tf_op jit(solution)/shard_map/ppermute | solution.py:1163
  150.7 21.0 %collective-permute-start.17 = (bf16[784,128]{1,0:T(8,128)(2,1)S(1)}, bf16[784,128]{1,0:T(8,128)(2,1)S(1)}, u32[]{:S(2)}, u32[]{:S(2)}) collective-permute-start(bf16[784,128]{1,0:T(8,128)(2,1)S(1)} %get-tuple-element.274), channel_id=1, source_target_pairs={{2,0},{3,1},{6,4},{7,5},{10,8},{11,9},{14,12},{15,13},{18,16},{19,... | collective-permute-start | bytes 602120 | tf_op jit(solution)/shard_map/ppermute | solution.py:1184
  159.4 0.9 copy-start
  160.3 25.4 %collective-permute-start.28 = (bf16[2,48,1536]{2,1,0:T(8,128)(2,1)S(1)}, bf16[2,48,1536]{2,1,0:T(8,128)(2,1)S(1)}, u32[]{:S(2)}, u32[]{:S(2)}) collective-permute-start(bf16[2,48,1536]{2,1,0:T(8,128)(2,1)S(1)} %get-tuple-element.311), channel_id=1, source_target_pairs={{0,16},{4,20},{8,24},{12,28},{16,0},{20,4},{24,8},{28,12},{1,17},{... | collective-permute-start | bytes 884744 | tf_op jit(solution)/shard_map/ppermute | solution.py:1163
  161.9 24.6 %collective-permute-start.29 = (bf16[2,48,1536]{2,1,0:T(8,128)(2,1)}, bf16[2,48,1536]{2,1,0:T(8,128)(2,1)}, u32[]{:S(2)}, u32[]{:S(2)}) collective-permute-start(bf16[2,48,1536]{2,1,0:T(8,128)(2,1)} %get-tuple-element.312), channel_id=1, source_target_pairs={{0,8},{4,12},{8,0},{12,4},{16,24},{20,28},{24,16},{28,20},{1,9},{5... | collective-permute-start | bytes 884744 | tf_op jit(solution)/shard_map/ppermute | solution.py:1163
  165.6 0.8 copy-start.2
  166.4 20.1 %collective-permute-start.27 = (bf16[2,192,768]{2,1,0:T(8,128)(2,1)}, bf16[2,192,768]{2,1,0:T(8,128)(2,1)}, u32[]{:S(2)}, u32[]{:S(2)}) collective-permute-start(bf16[2,192,768]{2,1,0:T(8,128)(2,1)} %get-tuple-element.310), channel_id=1, source_target_pairs={{0,8},{4,12},{8,0},{12,4},{16,24},{20,28},{24,16},{28,20},{1,9},{5... | collective-permute-start | bytes 1769480 | tf_op jit(solution)/shard_map/ppermute | solution.py:1163
  169.4 0.8 copy-start.11
  170.2 12.0 %copy-start.13 = (bf16[2,2,96,768]{3,2,1,0:T(8,128)(2,1)}, bf16[2,2,96,768]{3,2,1,0:T(8,128)(2,1)S(1)}, u32[]{:S(2)}) copy-start(bf16[2,2,96,768]{3,2,1,0:T(8,128)(2,1)S(1)} %get-tuple-element.307.refs_2_.refs_3_) | copy-start | bytes 1769476
  170.2 25.6 %collective-permute-start.25 = (bf16[2,2,96,768]{3,2,1,0:T(8,128)(2,1)}, bf16[2,2,96,768]{3,2,1,0:T(8,128)(2,1)}, u32[]{:S(2)}, u32[]{:S(2)}) collective-permute-start(bf16[2,2,96,768]{3,2,1,0:T(8,128)(2,1)} %get-tuple-element.306), channel_id=1, source_target_pairs={{0,8},{4,12},{8,0},{12,4},{16,24},{20,28},{24,16},{28,20},{1,9},{5... | collective-permute-start | bytes 1769480 | tf_op jit(solution)/shard_map/ppermute | solution.py:1163
  171.7 24.1 %collective-permute-start.26 = (bf16[2,2,96,768]{3,2,1,0:T(8,128)(2,1)}, bf16[2,2,96,768]{3,2,1,0:T(8,128)(2,1)}, u32[]{:S(2)}, u32[]{:S(2)}) collective-permute-start(bf16[2,2,96,768]{3,2,1,0:T(8,128)(2,1)} %get-tuple-element.308), channel_id=1, source_target_pairs={{0,16},{4,20},{8,24},{12,28},{16,0},{20,4},{24,8},{28,12},{1,17},{... | collective-permute-start | bytes 1769480 | tf_op jit(solution)/shard_map/ppermute | solution.py:1163
  182.2 2.8 %copy-start.6 = (bf16[1,768,256]{2,1,0:T(8,128)(2,1)}, bf16[1,768,256]{2,1,0:T(8,128)(2,1)S(1)}, u32[]{:S(2)}) copy-start(bf16[1,768,256]{2,1,0:T(8,128)(2,1)S(1)} %get-tuple-element.301) | copy-start | bytes 1179652
  185.0 0.7 copy-start.4
  185.8 0.7 copy-start.8
  186.5 12.9 %collective-permute-start.24 = (bf16[4,2,96,1536]{3,2,1,0:T(8,128)(2,1)}, bf16[4,2,96,1536]{3,2,1,0:T(8,128)(2,1)}, u32[]{:S(2)}, u32[]{:S(2)}) collective-permute-start(bf16[4,2,96,1536]{3,2,1,0:T(8,128)(2,1)} %get-tuple-element.304), channel_id=1, source_target_pairs={{0,4},{4,0},{8,12},{12,8},{16,20},{20,16},{24,28},{28,24},{1,5},{5... | collective-permute-start | bytes 7077896 | tf_op jit(solution)/shard_map/ppermute | solution.py:1163
  186.5 1.1 copy-start.1
  187.6 1.1 copy-start.3
  188.7 1.0 copy-start.9
  189.6 6.2 %copy-start.12 = (bf16[2,2,96,768]{3,2,1,0:T(8,128)(2,1)S(1)}, bf16[2,2,96,768]{3,2,1,0:T(8,128)(2,1)}, u32[]{:S(2)}) copy-start(bf16[2,2,96,768]{3,2,1,0:T(8,128)(2,1)} %copy-done.11) | copy-start | bytes 1769476
  189.6 6.2 %copy-start.14 = (bf16[2,2,96,768]{3,2,1,0:T(8,128)(2,1)S(1)}, bf16[2,2,96,768]{3,2,1,0:T(8,128)(2,1)}, u32[]{:S(2)}) copy-start(bf16[2,2,96,768]{3,2,1,0:T(8,128)(2,1)} %copy-done.13) | copy-start | bytes 1769476
  191.3 32.1 %collective-permute-start.40 = (bf16[384,768]{1,0:T(8,128)(2,1)S(1)}, bf16[384,768]{1,0:T(8,128)(2,1)S(1)}, u32[]{:S(2)}, u32[]{:S(2)}) collective-permute-start(bf16[384,768]{1,0:T(8,128)(2,1)S(1)} %get-tuple-element.341), channel_id=1, source_target_pairs={{0,1},{1,0},{2,3},{3,2},{4,5},{5,4},{6,7},{7,6},{8,9},{9,8},{10,11... | collective-permute-start | bytes 1769480 | tf_op jit(solution)/shard_map/ppermute | solution.py:1168
  195.8 3.6 %copy-start.5 = (bf16[1,768,256]{2,1,0:T(8,128)(2,1)S(1)}, bf16[1,768,256]{2,1,0:T(8,128)(2,1)}, u32[]{:S(2)}) copy-start(bf16[1,768,256]{2,1,0:T(8,128)(2,1)} %copy-done.4) | copy-start | bytes 1179652
  195.8 3.6 %copy-start.7 = (bf16[1,768,256]{2,1,0:T(8,128)(2,1)S(1)}, bf16[1,768,256]{2,1,0:T(8,128)(2,1)}, u32[]{:S(2)}) copy-start(bf16[1,768,256]{2,1,0:T(8,128)(2,1)} %copy-done.6) | copy-start | bytes 1179652
  197.4 9.3 %collective-permute-start.32 = (bf16[2,96,768]{2,1,0:T(8,128)(2,1)S(1)}, bf16[2,96,768]{2,1,0:T(8,128)(2,1)S(1)}, u32[]{:S(2)}, u32[]{:S(2)}) collective-permute-start(bf16[2,96,768]{2,1,0:T(8,128)(2,1)S(1)} %get-tuple-element.326), channel_id=1, source_target_pairs={{0,16},{4,20},{8,24},{12,28},{16,0},{20,4},{24,8},{28,12},{1,17},{... | collective-permute-start | bytes 884744 | tf_op jit(solution)/shard_map/ppermute | solution.py:1163
  197.9 9.5 %collective-permute-start.33 = (bf16[2,96,768]{2,1,0:T(8,128)(2,1)S(1)}, bf16[2,96,768]{2,1,0:T(8,128)(2,1)S(1)}, u32[]{:S(2)}, u32[]{:S(2)}) collective-permute-start(bf16[2,96,768]{2,1,0:T(8,128)(2,1)S(1)} %get-tuple-element.327), channel_id=1, source_target_pairs={{0,8},{4,12},{8,0},{12,4},{16,24},{20,28},{24,16},{28,20},{1,9},{5... | collective-permute-start | bytes 884744 | tf_op jit(solution)/shard_map/ppermute | solution.py:1163
  202.0 16.7 %collective-permute-start.30 = (bf16[2,2,48,1536]{3,2,1,0:T(8,128)(2,1)S(1)}, bf16[2,2,48,1536]{3,2,1,0:T(8,128)(2,1)S(1)}, u32[]{:S(2)}, u32[]{:S(2)}) collective-permute-start(bf16[2,2,48,1536]{3,2,1,0:T(8,128)(2,1)S(1)} %get-tuple-element.317), channel_id=1, source_target_pairs={{0,8},{4,12},{8,0},{12,4},{16,24},{20,28},{24,16},{28,20},{1,9},{5... | collective-permute-start | bytes 1769480 | tf_op jit(solution)/shard_map/ppermute | solution.py:1163
  202.6 16.1 %collective-permute-start.31 = (bf16[2,2,48,1536]{3,2,1,0:T(8,128)(2,1)S(1)}, bf16[2,2,48,1536]{3,2,1,0:T(8,128)(2,1)S(1)}, u32[]{:S(2)}, u32[]{:S(2)}) collective-permute-start(bf16[2,2,48,1536]{3,2,1,0:T(8,128)(2,1)S(1)} %get-tuple-element.319), channel_id=1, source_target_pairs={{0,16},{4,20},{8,24},{12,28},{16,0},{20,4},{24,8},{28,12},{1,17},{... | collective-permute-start | bytes 1769480 | tf_op jit(solution)/shard_map/ppermute | solution.py:1163
  209.9 1.4 collective-permute-start.34
  209.9 19.9 %collective-permute-start.39 = (bf16[192,768]{1,0:T(8,128)(2,1)S(1)}, bf16[192,768]{1,0:T(8,128)(2,1)S(1)}, u32[]{:S(2)}, u32[]{:S(2)}) collective-permute-start(bf16[192,768]{1,0:T(8,128)(2,1)S(1)} %get-tuple-element.339), channel_id=1, source_target_pairs={{0,1},{1,0},{2,3},{3,2},{4,5},{5,4},{6,7},{7,6},{8,9},{9,8},{10,11... | collective-permute-start | bytes 884744 | tf_op jit(solution)/shard_map/ppermute | solution.py:1168
  211.3 8.5 %collective-permute-start.37 = (f32[32,768]{1,0:T(8,128)S(1)}, f32[32,768]{1,0:T(8,128)S(1)}, u32[]{:S(2)}, u32[]{:S(2)}) collective-permute-start(f32[32,768]{1,0:T(8,128)S(1)} %get-tuple-element.335.refs_0_), channel_id=1, source_target_pairs={{0,8},{4,12},{8,0},{12,4},{16,24},{20,28},{24,16},{28,20},{1,9},{5... | collective-permute-start | bytes 294920 | tf_op jit(solution)/shard_map/ppermute | solution.py:1163
  219.8 12.5 %collective-permute-start.38 = (f32[32,768]{1,0:T(8,128)S(1)}, f32[32,768]{1,0:T(8,128)S(1)}, u32[]{:S(2)}, u32[]{:S(2)}) collective-permute-start(f32[32,768]{1,0:T(8,128)S(1)} %get-tuple-element.337.refs_0_), channel_id=1, source_target_pairs={{0,16},{4,20},{8,24},{12,28},{16,0},{20,4},{24,8},{28,12},{1,17},{... | collective-permute-start | bytes 294920 | tf_op jit(solution)/shard_map/ppermute | solution.py:1163
  221.4 10.9 %collective-permute-start.35 = (bf16[2,48,1536]{2,1,0:T(8,128)(2,1)S(1)}, bf16[2,48,1536]{2,1,0:T(8,128)(2,1)S(1)}, u32[]{:S(2)}, u32[]{:S(2)}) collective-permute-start(bf16[2,48,1536]{2,1,0:T(8,128)(2,1)S(1)} %get-tuple-element.333), channel_id=1, source_target_pairs={{0,16},{4,20},{8,24},{12,28},{16,0},{20,4},{24,8},{28,12},{1,17},{... | collective-permute-start | bytes 884744 | tf_op jit(solution)/shard_map/ppermute | solution.py:1163
  221.9 10.4 %collective-permute-start.36 = (bf16[2,48,1536]{2,1,0:T(8,128)(2,1)S(1)}, bf16[2,48,1536]{2,1,0:T(8,128)(2,1)S(1)}, u32[]{:S(2)}, u32[]{:S(2)}) collective-permute-start(bf16[2,48,1536]{2,1,0:T(8,128)(2,1)S(1)} %get-tuple-element.334), channel_id=1, source_target_pairs={{0,8},{4,12},{8,0},{12,4},{16,24},{20,28},{24,16},{28,20},{1,9},{5... | collective-permute-start | bytes 884744 | tf_op jit(solution)/shard_map/ppermute | solution.py:1163
  230.2 22.5 %collective-permute-start.44 = (bf16[288,768]{1,0:T(8,128)(2,1)S(1)}, bf16[288,768]{1,0:T(8,128)(2,1)S(1)}, u32[]{:S(2)}, u32[]{:S(2)}) collective-permute-start(bf16[288,768]{1,0:T(8,128)(2,1)S(1)} %get-tuple-element.353), channel_id=1, source_target_pairs={{0,2},{1,3},{2,0},{3,1},{4,6},{5,7},{6,4},{7,5},{8,10},{9,11},{10,... | collective-permute-start | bytes 1327112 | tf_op jit(solution)/shard_map/ppermute | solution.py:1168
  232.6 19.7 %collective-permute-start.41 = (bf16[192,768]{1,0:T(8,128)(2,1)S(1)}, bf16[192,768]{1,0:T(8,128)(2,1)S(1)}, u32[]{:S(2)}, u32[]{:S(2)}) collective-permute-start(bf16[192,768]{1,0:T(8,128)(2,1)S(1)} %get-tuple-element.346), channel_id=1, source_target_pairs={{0,1},{1,0},{2,3},{3,2},{4,5},{5,4},{6,7},{7,6},{8,9},{9,8},{10,11... | collective-permute-start | bytes 884744 | tf_op jit(solution)/shard_map/ppermute | solution.py:1168
  233.4 16.0 %collective-permute-start.42 = (f32[32,768]{1,0:T(8,128)S(1)}, f32[32,768]{1,0:T(8,128)S(1)}, u32[]{:S(2)}, u32[]{:S(2)}) collective-permute-start(f32[32,768]{1,0:T(8,128)S(1)} %get-tuple-element.347.refs_0_), channel_id=1, source_target_pairs={{0,1},{1,0},{2,3},{3,2},{4,5},{5,4},{6,7},{7,6},{8,9},{9,8},{10,11... | collective-permute-start | bytes 294920 | tf_op jit(solution)/shard_map/ppermute | solution.py:1168
  249.4 6.3 %collective-permute-start.45 = (f32[32,768]{1,0:T(8,128)S(1)}, f32[32,768]{1,0:T(8,128)S(1)}, u32[]{:S(2)}, u32[]{:S(2)}) collective-permute-start(f32[32,768]{1,0:T(8,128)S(1)} %get-tuple-element.354.refs_0_), channel_id=1, source_target_pairs={{0,2},{1,3},{2,0},{3,1},{4,6},{5,7},{6,4},{7,5},{8,10},{9,11},{10,... | collective-permute-start | bytes 294920 | tf_op jit(solution)/shard_map/ppermute | solution.py:1168
  252.7 1.0 copy-start.10
  255.1 5.0 %copy-start.16 = (f32[2,384,192]{2,1,0:T(8,128)S(1)}, f32[2,384,192]{2,1,0:T(8,128)}, u32[]{:S(2)}) copy-start(f32[2,384,192]{2,1,0:T(8,128)} %get-tuple-element.379) | copy-start | bytes 1769476
  255.9 8.6 %collective-permute-start.43 = (bf16[96,768]{1,0:T(8,128)(2,1)S(1)}, bf16[96,768]{1,0:T(8,128)(2,1)S(1)}, u32[]{:S(2)}, u32[]{:S(2)}) collective-permute-start(bf16[96,768]{1,0:T(8,128)(2,1)S(1)} %get-tuple-element.351), channel_id=1, source_target_pairs={{0,2},{1,3},{2,0},{3,1},{4,6},{5,7},{6,4},{7,5},{8,10},{9,11},{10,... | collective-permute-start | bytes 442376 | tf_op jit(solution)/shard_map/ppermute | solution.py:1168
Sparse Core Ops, SparseCore 0:
  186.6 44.4 reduce-scatter.1

commit v5 on v4

--- a/solution.py
+++ b/solution.py
@@ -1142,9 +1142,13 @@
     def body(io):
         for layer in range(LAYERS):
             here = slice(starts[layer], starts[layer] + size)
-            full = up(io["term%d_0" % layer][here, :])
-            for at in range(1, len(terms[layer])):
-                full = full + up(io["term%d_%d" % (layer, at)][here, :])
+            full = 0.0
+            for at, term in enumerate(terms[layer]):
+                ref = io["term%d_%d" % (layer, at)]
+                if len(term.shape) == 2:
+                    full = full + up(ref[here, :])
+                else:
+                    full = full + sum(up(ref[part]) for part in range(term.shape[0]))
             if kind == "mix":
                 io.first[layer] = full[:, D // 4 :]
                 io.second[layer] = full[:, : D // 4]
@@ -1191,7 +1195,7 @@
 SUM_ROWS = (3, 7, 3)
 
 
-def collect_sums(parts, deps):
+def collect_sums(parts, after, deps):
     def body(io):
         io.sums[...] = jnp.zeros((32, D), F32)
         start = 0
@@ -1202,7 +1206,7 @@
 
     outs, token = run(
         body,
-        Box({"part%d" % at: ("d", part) for at, part in enumerate(parts)}),
+        Box({"part%d" % at: ("d", part) for at, part in enumerate(parts)}, after=("r", after)),
         Box(sums=("v", shape(32, D))),
         deps,
     )
@@ -1394,8 +1398,8 @@
                 group[name].spot = spot
             groups = [group[name] for name in names]
             blocks, token = grad_collect(kinds, groups, (token, *after))
-            mine = lax.psum_scatter(blocks, "narrow", scatter_dimension=0, tiled=True)
-            return (mine.reshape(mine.shape[1:]),), token
+            parts = lax.all_to_all(blocks, "narrow", split_axis=0, concat_axis=0, tiled=True)
+            return (parts,), token
 
         token = send("o1", "out", (one.gb2t, one.hid), token)
         back1, token = layer_back(
@@ -1451,7 +1455,7 @@
         token = forward(["i0"], token)
         token = keep("m0", "both", token)
         near_b, token = near(["i0"], token)
-        sums, token = collect_sums(parts, (token,))
+        sums, token = collect_sums(parts, f1[0], (token,))
         come = wide_swap(sums, CORE)
         sums, token = add_up(sums, come, (token,))
         come = wide_swap(sums, ACROSS)

time: 277 us -> 271 us (0.978)
  between operations: 16.7 us -> 3.45 us
  local copies, waits for them, and re-layouts: 11.3 us -> 15.3 us
    all_to_all x0 -> x1, waiting for transfers between devices: none -> 5.52 us  [gather(): lax.all_to_all(blocks, 'narrow', split_axis=0, concat_axis=0, tiled=True)]
    ppermute x28, waiting for transfers between devices: 29.4 us -> 24.9 us  [wide_swap(): return lax.ppermute(v, 'wide', [(i, i ^ bit) for i in range(size)])]
    unnamed x39 -> x75, local copies, waits for them, and re-layouts: 9.24 us -> 13.2 us
    all_to_all x0 -> x1, starting transfers between devices: none -> 3.78 us  [gather(): lax.all_to_all(blocks, 'narrow', split_axis=0, concat_axis=0, tiled=True)]
  transfers between devices with their start and end apart: 47 -> 47, of which waited for: 18 -> 18; matrix products, arithmetic and copies ran while one was open for 2% -> 2% of each run, Pallas kernels for 31% -> 33%
where the time goes in v5:
time: 271 us; the launch traced here: 267 us
  Pallas kernels  109 us (40%)
  waiting for transfers between devices  70.3 us (26%)
  starting transfers between devices  65 us (24%)
  local copies, waits for them, and re-layouts  15.3 us (6%)
  other arithmetic  3.55 us (1%)
  between operations  3.45 us (1%)
    pallas_call x42, Pallas kernels, run(): pl.pallas_call(kernel, out_shape=tuple(out_shapes), in_specs=in_specs, ou...  109 us
    ppermute x11, starting transfers between devices, move(): return lax.ppermute(v, 'narrow', pairs)  30.5 us
    ppermute x7, waiting for transfers between devices, narrow_swap(): return lax.ppermute(v, 'narrow', [(i, i ^ bit) for i in range(size)])  25.6 us
    ppermute x28, waiting for transfers between devices, wide_swap(): return lax.ppermute(v, 'wide', [(i, i ^ bit) for i in range(size)])  24.9 us
    ppermute x28, starting transfers between devices, wide_swap(): return lax.ppermute(v, 'wide', [(i, i ^ bit) for i in range(size)])  24 us
    ppermute x11, waiting for transfers between devices, move(): return lax.ppermute(v, 'narrow', pairs)  14.4 us
    unnamed x75, local copies, waits for them, and re-layouts  13.2 us
    ppermute x7, starting transfers between devices, narrow_swap(): return lax.ppermute(v, 'narrow', [(i, i ^ bit) for i in range(size)])  6.81 us
  transfers between devices with their start and end apart: 47, of which 18 were waited for; matrix products, arithmetic and copies ran while one was open for 2% of the time, Pallas kernels for 33%

profile of v5, /device:TPU:0, one launch (start us, length us, event | category | flops | bytes accessed | tf_op | source)
XLA Modules:
  0.0 267.2 jit_solution(17308243911479826003)
XLA Ops:
  2.5 6.6 %shard_map.186 = (bf16[256,2304]{1,0:T(8,128)(2,1)S(1)}, bf16[768,256]{1,0:T(8,128)(2,1)}, bf16[784,128]{1,0:T(8,128)(2,1)S(1)}, bf16[256,2304]{1,0:T(8,128)(2,1)}, f32[8,128]{1,0:T(8,128)S(1)}) custom-call(s32[6]{0:T(128)S(1)} %stack.33.refs_0_.refs_12_.refs_3_.refs_11_.refs_6_.refs_2_, bf16[256,768]{1,0:T(8,128)(2,1)} %refs_3_.4, ...), custom_call_target="tpu_custom_call" | custom-call | flops 10000000000 | bytes 100000000 | tf_op jit(solution)/shard_map/pallas_call | solution.py:247
  9.1 4.9 %collective-permute-start = (bf16[784,128]{1,0:T(8,128)(2,1)S(1)}, bf16[784,128]{1,0:T(8,128)(2,1)S(1)}, u32[]{:S(2)}, u32[]{:S(2)}) collective-permute-start(bf16[784,128]{1,0:T(8,128)(2,1)S(1)} %get-tuple-element.187), channel_id=1, source_target_pairs={{0,1},{1,2},{2,3},{4,5},{5,6},{6,7},{8,9},{9,10},{10,11},{12,13},{... | collective-permute-start | bytes 602120 | tf_op jit(solution)/shard_map/ppermute | solution.py:1188
  14.0 4.5 %collective-permute-start.1 = (bf16[784,128]{1,0:T(8,128)(2,1)S(1)}, bf16[784,128]{1,0:T(8,128)(2,1)S(1)}, u32[]{:S(2)}, u32[]{:S(2)}) collective-permute-start(bf16[784,128]{1,0:T(8,128)(2,1)S(1)} %get-tuple-element.187), channel_id=1, source_target_pairs={{0,2},{1,3},{4,6},{5,7},{8,10},{9,11},{12,14},{13,15},{16,18},{17,... | collective-permute-start | bytes 602120 | tf_op jit(solution)/shard_map/ppermute | solution.py:1188
  18.6 1.5 collective-permute-start.2
  21.2 1.4 cosine_select_fusion.refs_2_.refs_10_.refs_9_
  22.6 6.0 %shard_map.187 = (f32[256,768]{1,0:T(8,128)S(1)}, f32[256,768]{1,0:T(8,128)S(1)}, bf16[256,768]{1,0:T(8,128)(2,1)S(1)}, bf16[256,768]{1,0:T(8,128)(2,1)}, bf16[1...) custom-call(s32[6]{0:T(128)S(1)} %stack.33.refs_0_.refs_12_.refs_3_., ...), custom_call_target="tpu_custom_call" | custom-call | flops 10000000000 | bytes 100000000 | tf_op jit(solution)/shard_map/pallas_call | solution.py:247
  28.7 8.3 %shard_map.188 = (bf16[784,128]{1,0:T(8,128)(2,1)}, bf16[256,768]{1,0:T(8,128)(2,1)}, bf16[768,256]{1,0:T(8,128)(2,1)}, f32[256,768]{1,0:T(8,128)}, f32[256,768]...) custom-call(bf16[784,128]{1,0:T(8,128)(2,1)S(1)} %collective-permute, ...), custom_call_target="tpu_custom_call" | custom-call | flops 10000000000 | bytes 100000000 | tf_op jit(solution)/shard_map/pallas_call | solution.py:247
  37.0 4.7 %shard_map.189 = (bf16[256,2304]{1,0:T(8,128)(2,1)S(1)}, bf16[768,256]{1,0:T(8,128)(2,1)}, bf16[784,128]{1,0:T(8,128)(2,1)S(1)}, bf16[256,2304]{1,0:T(8,128)(2,1...) custom-call(s32[6]{0:T(128)S(1)} %stack.33.refs_0_.refs_12_.refs_3_.refs_11_.refs_6_.refs_2_, ...), custom_call_target="tpu_custom_call" | custom-call | flops 10000000000 | bytes 100000000 | tf_op jit(solution)/shard_map/pallas_call | solution.py:247
  41.7 6.0 %collective-permute-start.3 = (bf16[784,128]{1,0:T(8,128)(2,1)S(1)}, bf16[784,128]{1,0:T(8,128)(2,1)S(1)}, u32[]{:S(2)}, u32[]{:S(2)}) collective-permute-start(bf16[784,128]{1,0:T(8,128)(2,1)S(1)} %get-tuple-element.201), channel_id=1, source_target_pairs={{0,1},{1,2},{2,3},{4,5},{5,6},{6,7},{8,9},{9,10},{10,11},{12,13},{... | collective-permute-start | bytes 602120 | tf_op jit(solution)/shard_map/ppermute | solution.py:1188
  47.7 5.3 %collective-permute-start.4 = (bf16[784,128]{1,0:T(8,128)(2,1)S(1)}, bf16[784,128]{1,0:T(8,128)(2,1)S(1)}, u32[]{:S(2)}, u32[]{:S(2)}) collective-permute-start(bf16[784,128]{1,0:T(8,128)(2,1)S(1)} %get-tuple-element.201), channel_id=1, source_target_pairs={{0,2},{1,3},{4,6},{5,7},{8,10},{9,11},{12,14},{13,15},{16,18},{17,... | collective-permute-start | bytes 602120 | tf_op jit(solution)/shard_map/ppermute | solution.py:1188
  53.0 1.8 collective-permute-start.5
  54.8 1.6 collective-permute-start.6
  56.4 4.8 %shard_map.190 = (f32[256,768]{1,0:T(8,128)S(1)}, f32[256,768]{1,0:T(8,128)S(1)}, bf16[256,768]{1,0:T(8,128)(2,1)S(1)}, bf16[1,768,768]{2,1,0:T(8,128)(2,1)S(1)}...) custom-call(s32[6]{0:T(128)S(1)} %stack.33.refs_0_.refs_12_.refs_3_.refs_11_.refs_6_.refs_, ...), custom_call_target="tpu_custom_call" | custom-call | flops 10000000000 | bytes 100000000 | tf_op jit(solution)/shard_map/pallas_call | solution.py:247
  61.2 7.3 %shard_map.191 = (bf16[784,128]{1,0:T(8,128)(2,1)}, bf16[256,768]{1,0:T(8,128)(2,1)S(1)}, bf16[768,256]{1,0:T(8,128)(2,1)}, f32[256,768]{1,0:T(8,128)S(1)}, f32[...) custom-call(bf16[784,128]{1,0:T(8,128)(2,1)S(1)} %collective-permute, ...), custom_call_target="tpu_custom_call" | custom-call | flops 10000000000 | bytes 100000000 | tf_op jit(solution)/shard_map/pallas_call | solution.py:247
  68.6 1.4 shard_map.192
  70.1 2.6 collective-permute-done.6.refs_11_.refs_15_
  73.6 5.9 %shard_map.193 = (bf16[256,3072]{1,0:T(8,128)(2,1)S(1)}, bf16[256,768]{1,0:T(8,128)(2,1)S(1)}, f32[256,768]{1,0:T(8,128)S(1)}, bf16[256,768]{1,0:T(8,128)(2,1)S(...) custom-call(f32[256,768]{1,0:T(8,128)S(1)} %get-tuple-element.212.ref, ...), custom_call_target="tpu_custom_call" | custom-call | flops 300000000 | bytes 100000000 | tf_op jit(solution)/shard_map/pallas_call | solution.py:247
  79.6 1.4 shard_map.194
  81.0 1.3 collective-permute-start.7
  82.3 1.3 collective-permute-start.8
  83.6 1.4 shard_map.195
  85.0 1.6 collective-permute-start.13
  87.9 1.3 shard_map.196
  89.3 1.6 collective-permute-start.12
  91.1 12.1 %collective-permute-done.8.refs_1_ = bf16[784,128]{1,0:T(8,128)(2,1)S(1)} collective-permute-done((bf16[784,128]{1,0:T(8,128)(2,1)S(1)}, bf16[784,128]{1,0:T(8,128)(2,1)S(1)}, u32[]{:S(2)}, u32[]{:S(2)}) %collective-permute-start.8) | collective-permute-done | bytes 200736 | tf_op jit(solution)/shard_map/ppermute | solution.py:1188
  103.2 10.7 %shard_map.197 = (bf16[2,256,1536]{2,1,0:T(8,128)(2,1)S(1)}, f32[8,768]{1,0:T(8,128)}, f32[256,768]{1,0:T(8,128)S(1)}, bf16[256,768]{1,0:T(8,128)(2,1)S(1)}, bf1...) custom-call(bf16[784,128]{1,0:T(8,128)(2,1)S(1)} %collective-permute, ...), custom_call_target="tpu_custom_call" | custom-call | flops 300000000 | bytes 100000000 | tf_op jit(solution)/shard_map/pallas_call | solution.py:247
  113.9 1.4 shard_map.198
  115.4 1.6 collective-permute-start.15
  117.2 1.6 collective-permute-start.19
  119.4 7.6 %shard_map.201 = (bf16[256,3072]{1,0:T(8,128)(2,1)S(1)}, bf16[256,768]{1,0:T(8,128)(2,1)S(1)}, f32[256,768]{1,0:T(8,128)S(1)}, bf16[256,768]{1,0:T(8,128)(2,1)S(...) custom-call(f32[256,768]{1,0:T(8,128)S(1)} %get-tuple-element.243.re, ...), custom_call_target="tpu_custom_call" | custom-call | flops 15000000512 | bytes 100000000 | tf_op jit(solution)/shard_map/pallas_call | solution.py:247
  127.0 1.3 collective-permute-start.14
  128.3 1.4 shard_map.202
  130.4 1.5 collective-permute-start.23
  131.9 1.4 shard_map.203
  133.4 2.1 collective-permute-done.14.refs_1_.refs_0_
  135.5 4.5 %collective-permute-done.18.refs_2_ = bf16[2,192,768]{2,1,0:T(8,128)(2,1)S(1)} collective-permute-done((bf16[2,192,768]{2,1,0:T(8,128)(2,1)S(1)}, bf16[2,192,768]{2,1,0:T(8,128)(2,1)S(1)}, u32[]{:S(2)}, u32[]{:S(2)}) %collective-permute-start.18) | collective-permute-done | bytes 589856 | tf_op jit(solution)/shard_map/ppermute | solution.py:1167
  141.0 1.4 shard_map.206
  143.8 1.5 collective-permute-done.22.refs_1_.refs_3_
  145.3 6.9 %collective-permute-done.23.refs_3_.refs_6_ = bf16[2,2,48,1536]{3,2,1,0:T(8,128)(2,1)S(1)} collective-permute-done((bf16[2,2,48,1536]{3,2,1,0:T(8,128)(2,1)S(1)}, bf16[2,2,48,1536]{3,2,1,0:T(8,128)(2,1)S(1)}, u32[]{:S(2)}, u32[]{:S(2)}) %collective-permute-start.23) | collective-permute-done | bytes 589856 | tf_op jit(solution)/shard_map/ppermute | solution.py:1167
  153.1 1.6 collective-permute-start.28
  154.7 1.5 collective-permute-start.29
  156.2 2.2 shard_map.208
  159.0 2.3 shard_map.209
  161.4 1.6 collective-permute-start.25
  163.5 9.9 %shard_map.210 = (bf16[2,256,1536]{2,1,0:T(8,128)(2,1)S(1)}, f32[8,768]{1,0:T(8,128)}, f32[256,768]{1,0:T(8,128)}, bf16[1,768,256]{2,1,0:T(8,128)(2,1)S(1)}, bf1...) custom-call(bf16[784,128]{1,0:T(8,128)(2,1)S(1)} %collective-permute-done.14.refs_1_.refs_0_, ...), custom_call_target="tpu_custom_call" | custom-call | flops 6000000000 | bytes 100000000 | tf_op jit(solution)/shard_map/pallas_call | solution.py:247
  173.4 2.9 %shard_map.211 = (bf16[4,2,96,1536]{3,2,1,0:T(8,128)(2,1)}, f32[8,128]{1,0:T(8,128)S(1)}) custom-call(s32[6]{0:T(128)S(1)} %stack.33.refs_0_.refs_12_.refs_3_.refs_11_.refs_6_.refs_2_, bf16[768,256]{1,0:T(8,128)(2,1)S(1)} %bitcast.26, bf16[768,256]{1,0:T(8,128)(2,1)S(1)} %bitcast.28, bf16[2,256,1536]{2,1,0:T(8,128)(2,1)S(1)} %get-tuple-element.302.refs_3_, ...), custom_call_target="tpu_custom_call" | custom-call | flops 300000000 | bytes 100000000 | tf_op jit(solution)/shard_map/pallas_call | solution.py:247
  177.8 3.8 %all-to-all-start = ((bf16[4,192,768]{2,1,0:T(8,128)(2,1)}), bf16[4,192,768]{2,1,0:T(8,128)(2,1)S(1)}, u32[]{:S(2)}, u32[]{:S(2)}) async-start(bf16[4,192,768]{2,1,0:T(8,128)(2,1)} %copy-done.2), calls=%async_computation | async-start | bytes 2359296 | tf_op jit(solution)/shard_map/all_to_all | solution.py:1401
  186.8 2.2 shard_map.212
  189.9 2.0 collective-permute-start.40
  191.9 1.5 shard_map.213
  193.4 1.6 collective-permute-start.32
  195.5 3.6 %shard_map.214 = (bf16[2,2,48,1536]{3,2,1,0:T(8,128)(2,1)}, bf16[2,2,48,1536]{3,2,1,0:T(8,128)(2,1)S(1)}, bf16[2,2,48,1536]{3,2,1,0:T(8,128)(2,1)}, bf16[2,2,48,1536]{3,2,1,0:T(8,128)(2,1)S(1)}, f32[8,128]{1,0:T(8,128)S(1)}) custom-call(s32[6]{0:T(128)S(1)} %stack.33.refs_0_.refs_12_.refs_3_.refs_11_.refs_6_.refs_2_, bf16[768,256]{1,0:T(8,128)(2,1)S(1)} %bitcast.27, ...), custom_call_target="tpu_custom_call" | custom-call | flops 10000000000 | bytes 100000000 | tf_op jit(solution)/shard_map/pallas_call | solution.py:247
  200.7 1.5 collective-permute-start.30
  202.7 1.4 collective-permute-done.33.refs_5_
  204.1 1.5 shard_map.215
  205.6 5.5 %all-to-all-done.refs_6_.refs_2_ = bf16[4,192,768]{2,1,0:T(8,128)(2,1)S(1)} async-done(((bf16[4,192,768]{2,1,0:T(8,128)(2,1)}), bf16[4,192,768]{2,1,0:T(8,128)(2,1)S(1)}, u32[]{:S(2)}, u32[]{:S(2)}) %all-to-all-start) | async-done | bytes 1179680 | tf_op jit(solution)/shard_map/all_to_all | solution.py:1401
  219.4 1.6 collective-permute-start.38
  223.9 2.5 collective-permute-start.44
  226.4 3.6 %collective-permute-done.35.refs_2_ = bf16[2,48,1536]{2,1,0:T(8,128)(2,1)S(1)} collective-permute-done((bf16[2,48,1536]{2,1,0:T(8,128)(2,1)S(1)}, bf16[2,48,1536]{2,1,0:T(8,128)(2,1)S(1)}, u32[]{:S(2)}, u32[]{:S(2)}) %collective-permute-start.35) | collective-permute-done | bytes 294944 | tf_op jit(solution)/shard_map/ppermute | solution.py:1167
  233.4 17.1 %collective-permute-done.42.refs_1_ = f32[32,768]{1,0:T(8,128)S(1)} collective-permute-done((f32[32,768]{1,0:T(8,128)S(1)}, f32[32,768]{1,0:T(8,128)S(1)}, u32[]{:S(2)}, u32[]{:S(2)}) %collective-permute-start.42) | collective-permute-done | bytes 98336 | tf_op jit(solution)/shard_map/ppermute | solution.py:1172
  251.8 1.6 shard_map.225
  253.4 5.0 %collective-permute-done.45.refs_1_ = f32[32,768]{1,0:T(8,128)S(1)} collective-permute-done((f32[32,768]{1,0:T(8,128)S(1)}, f32[32,768]{1,0:T(8,128)S(1)}, u32[]{:S(2)}, u32[]{:S(2)}) %collective-permute-start.45) | collective-permute-done | bytes 98336 | tf_op jit(solution)/shard_map/ppermute | solution.py:1172
  262.3 2.8 %collective-permute-done.43.refs_1_ = bf16[96,768]{1,0:T(8,128)(2,1)S(1)} collective-permute-done((bf16[96,768]{1,0:T(8,128)(2,1)S(1)}, bf16[96,768]{1,0:T(8,128)(2,1)S(1)}, u32[]{:S(2)}, u32[]{:S(2)}) %collective-permute-start.43) | collective-permute-done | bytes 147488 | tf_op jit(solution)/shard_map/ppermute | solution.py:1172
  265.1 1.6 shard_map.227
  (160 shorter events, 40.0 us)
Async XLA Ops:
  9.1 19.5 %collective-permute-start = (bf16[784,128]{1,0:T(8,128)(2,1)S(1)}, bf16[784,128]{1,0:T(8,128)(2,1)S(1)}, u32[]{:S(2)}, u32[]{:S(2)}) collective-permute-start(bf16[784,128]{1,0:T(8,128)(2,1)S(1)} %get-tuple-element.187), channel_id=1, source_target_pairs={{0,1},{1,2},{2,3},{4,5},{5,6},{6,7},{8,9},{9,10},{10,11},{12,13},{... | collective-permute-start | bytes 602120 | tf_op jit(solution)/shard_map/ppermute | solution.py:1188
  14.0 14.6 %collective-permute-start.1 = (bf16[784,128]{1,0:T(8,128)(2,1)S(1)}, bf16[784,128]{1,0:T(8,128)(2,1)S(1)}, u32[]{:S(2)}, u32[]{:S(2)}) collective-permute-start(bf16[784,128]{1,0:T(8,128)(2,1)S(1)} %get-tuple-element.187), channel_id=1, source_target_pairs={{0,2},{1,3},{4,6},{5,7},{8,10},{9,11},{12,14},{13,15},{16,18},{17,... | collective-permute-start | bytes 602120 | tf_op jit(solution)/shard_map/ppermute | solution.py:1188
  18.6 10.1 %collective-permute-start.2 = (bf16[784,128]{1,0:T(8,128)(2,1)S(1)}, bf16[784,128]{1,0:T(8,128)(2,1)S(1)}, u32[]{:S(2)}, u32[]{:S(2)}) collective-permute-start(bf16[784,128]{1,0:T(8,128)(2,1)S(1)} %get-tuple-element.187), channel_id=1, source_target_pairs={{0,3},{4,7},{8,11},{12,15},{16,19},{20,23},{24,27},{28,31}} | collective-permute-start | bytes 602120 | tf_op jit(solution)/shard_map/ppermute | solution.py:1188
  41.7 19.5 %collective-permute-start.3 = (bf16[784,128]{1,0:T(8,128)(2,1)S(1)}, bf16[784,128]{1,0:T(8,128)(2,1)S(1)}, u32[]{:S(2)}, u32[]{:S(2)}) collective-permute-start(bf16[784,128]{1,0:T(8,128)(2,1)S(1)} %get-tuple-element.201), channel_id=1, source_target_pairs={{0,1},{1,2},{2,3},{4,5},{5,6},{6,7},{8,9},{9,10},{10,11},{12,13},{... | collective-permute-start | bytes 602120 | tf_op jit(solution)/shard_map/ppermute | solution.py:1188
  47.7 13.5 %collective-permute-start.4 = (bf16[784,128]{1,0:T(8,128)(2,1)S(1)}, bf16[784,128]{1,0:T(8,128)(2,1)S(1)}, u32[]{:S(2)}, u32[]{:S(2)}) collective-permute-start(bf16[784,128]{1,0:T(8,128)(2,1)S(1)} %get-tuple-element.201), channel_id=1, source_target_pairs={{0,2},{1,3},{4,6},{5,7},{8,10},{9,11},{12,14},{13,15},{16,18},{17,... | collective-permute-start | bytes 602120 | tf_op jit(solution)/shard_map/ppermute | solution.py:1188
  53.0 8.2 %collective-permute-start.5 = (bf16[784,128]{1,0:T(8,128)(2,1)S(1)}, bf16[784,128]{1,0:T(8,128)(2,1)S(1)}, u32[]{:S(2)}, u32[]{:S(2)}) collective-permute-start(bf16[784,128]{1,0:T(8,128)(2,1)S(1)} %get-tuple-element.201), channel_id=1, source_target_pairs={{0,3},{4,7},{8,11},{12,15},{16,19},{20,23},{24,27},{28,31}} | collective-permute-start | bytes 602120 | tf_op jit(solution)/shard_map/ppermute | solution.py:1188
  54.8 17.9 %collective-permute-start.6 = (bf16[1,256,1536]{2,1,0:T(8,128)(2,1)S(1)}, bf16[1,256,1536]{2,1,0:T(8,128)(2,1)S(1)}, u32[]{:S(2)}, u32[]{:S(2)}) collective-permute-start(bf16[1,256,1536]{2,1,0:T(8,128)(2,1)S(1)} %get-tuple-element.219), channel_id=1, source_target_pairs={{0,16},{4,20},{8,24},{12,28},{16,0},{20,4},{24,8},{28,12},{1,17},{... | collective-permute-start | bytes 2359304 | tf_op jit(solution)/shard_map/ppermute | solution.py:1167
  70.0 13.6 %collective-permute-start.11 = (bf16[4,2,192,768]{3,2,1,0:T(8,128)(2,1)S(1)}, bf16[4,2,192,768]{3,2,1,0:T(8,128)(2,1)S(1)}, u32[]{:S(2)}, u32[]{:S(2)}) collective-permute-start(bf16[4,2,192,768]{3,2,1,0:T(8,128)(2,1)S(1)} %get-tuple-element.239), channel_id=1, source_target_pairs={{0,4},{4,0},{8,12},{12,8},{16,20},{20,16},{24,28},{28,24},{1,5},{5... | collective-permute-start | bytes 7077896 | tf_op jit(solution)/shard_map/ppermute | solution.py:1167
  80.9 7.0 %collective-permute-start.10 = (bf16[4,2,192,768]{3,2,1,0:T(8,128)(2,1)S(1)}, bf16[4,2,192,768]{3,2,1,0:T(8,128)(2,1)S(1)}, u32[]{:S(2)}, u32[]{:S(2)}) collective-permute-start(bf16[4,2,192,768]{3,2,1,0:T(8,128)(2,1)S(1)} %get-tuple-element.238), channel_id=1, source_target_pairs={{0,4},{4,0},{8,12},{12,8},{16,20},{20,16},{24,28},{28,24},{1,5},{5... | collective-permute-start | bytes 7077896 | tf_op jit(solution)/shard_map/ppermute | solution.py:1167
  81.0 10.1 %collective-permute-start.7 = (bf16[784,128]{1,0:T(8,128)(2,1)S(1)}, bf16[784,128]{1,0:T(8,128)(2,1)S(1)}, u32[]{:S(2)}, u32[]{:S(2)}) collective-permute-start(bf16[784,128]{1,0:T(8,128)(2,1)S(1)} %get-tuple-element.224), channel_id=1, source_target_pairs={{1,0},{2,1},{3,2},{5,4},{6,5},{7,6},{9,8},{10,9},{11,10},{13,12},{... | collective-permute-start | bytes 602120 | tf_op jit(solution)/shard_map/ppermute | solution.py:1188
  82.3 20.8 %collective-permute-start.8 = (bf16[784,128]{1,0:T(8,128)(2,1)S(1)}, bf16[784,128]{1,0:T(8,128)(2,1)S(1)}, u32[]{:S(2)}, u32[]{:S(2)}) collective-permute-start(bf16[784,128]{1,0:T(8,128)(2,1)S(1)} %get-tuple-element.224), channel_id=1, source_target_pairs={{2,0},{3,1},{6,4},{7,5},{10,8},{11,9},{14,12},{15,13},{18,16},{19,... | collective-permute-start | bytes 602120 | tf_op jit(solution)/shard_map/ppermute | solution.py:1188
  85.0 32.0 %collective-permute-start.13 = (bf16[2,2,192,768]{3,2,1,0:T(8,128)(2,1)S(1)}, bf16[2,2,192,768]{3,2,1,0:T(8,128)(2,1)S(1)}, u32[]{:S(2)}, u32[]{:S(2)}) collective-permute-start(bf16[2,2,192,768]{3,2,1,0:T(8,128)(2,1)S(1)} %get-tuple-element.258), channel_id=1, source_target_pairs={{0,16},{4,20},{8,24},{12,28},{16,0},{20,4},{24,8},{28,12},{1,17},{... | collective-permute-start | bytes 3538952 | tf_op jit(solution)/shard_map/ppermute | solution.py:1167
  86.6 16.5 %collective-permute-start.9 = (bf16[784,128]{1,0:T(8,128)(2,1)S(1)}, bf16[784,128]{1,0:T(8,128)(2,1)S(1)}, u32[]{:S(2)}, u32[]{:S(2)}) collective-permute-start(bf16[784,128]{1,0:T(8,128)(2,1)S(1)} %get-tuple-element.224), channel_id=1, source_target_pairs={{3,0},{7,4},{11,8},{15,12},{19,16},{23,20},{27,24},{31,28}} | collective-permute-start | bytes 602120 | tf_op jit(solution)/shard_map/ppermute | solution.py:1188
  89.3 29.4 %collective-permute-start.12 = (bf16[2,2,192,768]{3,2,1,0:T(8,128)(2,1)S(1)}, bf16[2,2,192,768]{3,2,1,0:T(8,128)(2,1)S(1)}, u32[]{:S(2)}, u32[]{:S(2)}) collective-permute-start(bf16[2,2,192,768]{3,2,1,0:T(8,128)(2,1)S(1)} %get-tuple-element.256), channel_id=1, source_target_pairs={{0,8},{4,12},{8,0},{12,4},{16,24},{20,28},{24,16},{28,20},{1,9},{5... | collective-permute-start | bytes 3538952 | tf_op jit(solution)/shard_map/ppermute | solution.py:1167
  115.3 13.0 %collective-permute-start.16 = (bf16[4,2,96,1536]{3,2,1,0:T(8,128)(2,1)S(1)}, bf16[4,2,96,1536]{3,2,1,0:T(8,128)(2,1)S(1)}, u32[]{:S(2)}, u32[]{:S(2)}) collective-permute-start(bf16[4,2,96,1536]{3,2,1,0:T(8,128)(2,1)S(1)} %get-tuple-element.270), channel_id=1, source_target_pairs={{0,4},{4,0},{8,12},{12,8},{16,20},{20,16},{24,28},{28,24},{1,5},{5... | collective-permute-start | bytes 7077896 | tf_op jit(solution)/shard_map/ppermute | solution.py:1167
  115.4 15.0 %collective-permute-start.15 = (bf16[768,256]{1,0:T(8,128)(2,1)S(1)}, bf16[768,256]{1,0:T(8,128)(2,1)S(1)}, u32[]{:S(2)}, u32[]{:S(2)}) collective-permute-start(bf16[768,256]{1,0:T(8,128)(2,1)S(1)} %get-tuple-element.267.refs_1_), channel_id=1, source_target_pairs={{0,16},{4,20},{8,24},{12,28},{16,0},{20,4},{24,8},{28,12},{1,17},{... | collective-permute-start | bytes 1179656 | tf_op jit(solution)/shard_map/ppermute | solution.py:1167
  117.2 18.3 %collective-permute-start.19 = (bf16[2,192,768]{2,1,0:T(8,128)(2,1)S(1)}, bf16[2,192,768]{2,1,0:T(8,128)(2,1)S(1)}, u32[]{:S(2)}, u32[]{:S(2)}) collective-permute-start(bf16[2,192,768]{2,1,0:T(8,128)(2,1)S(1)} %get-tuple-element.286), channel_id=1, source_target_pairs={{0,8},{4,12},{8,0},{12,4},{16,24},{20,28},{24,16},{28,20},{1,9},{5... | collective-permute-start | bytes 1769480 | tf_op jit(solution)/shard_map/ppermute | solution.py:1167
  118.9 21.1 %collective-permute-start.18 = (bf16[2,192,768]{2,1,0:T(8,128)(2,1)S(1)}, bf16[2,192,768]{2,1,0:T(8,128)(2,1)S(1)}, u32[]{:S(2)}, u32[]{:S(2)}) collective-permute-start(bf16[2,192,768]{2,1,0:T(8,128)(2,1)S(1)} %get-tuple-element.285), channel_id=1, source_target_pairs={{0,16},{4,20},{8,24},{12,28},{16,0},{20,4},{24,8},{28,12},{1,17},{... | collective-permute-start | bytes 1769480 | tf_op jit(solution)/shard_map/ppermute | solution.py:1167
  127.0 8.4 %collective-permute-start.14 = (bf16[784,128]{1,0:T(8,128)(2,1)S(1)}, bf16[784,128]{1,0:T(8,128)(2,1)S(1)}, u32[]{:S(2)}, u32[]{:S(2)}) collective-permute-start(bf16[784,128]{1,0:T(8,128)(2,1)S(1)} %get-tuple-element.266.refs_0_), channel_id=1, source_target_pairs={{1,0},{2,1},{3,2},{5,4},{6,5},{7,6},{9,8},{10,9},{11,10},{13,12},{... | collective-permute-start | bytes 602120 | tf_op jit(solution)/shard_map/ppermute | solution.py:1188
  129.8 22.4 %copy-start.3 = (bf16[2,2,48,1536]{3,2,1,0:T(8,128)(2,1)}, bf16[2,2,48,1536]{3,2,1,0:T(8,128)(2,1)S(1)}, u32[]{:S(2)}) copy-start(bf16[2,2,48,1536]{3,2,1,0:T(8,128)(2,1)S(1)} %get-tuple-element.293.refs_2_.refs_5_) | copy-start | bytes 1769476
  129.8 15.5 %collective-permute-start.22 = (bf16[2,2,48,1536]{3,2,1,0:T(8,128)(2,1)S(1)}, bf16[2,2,48,1536]{3,2,1,0:T(8,128)(2,1)S(1)}, u32[]{:S(2)}, u32[]{:S(2)}) collective-permute-start(bf16[2,2,48,1536]{3,2,1,0:T(8,128)(2,1)S(1)} %get-tuple-element.292), channel_id=1, source_target_pairs={{0,8},{4,12},{8,0},{12,4},{16,24},{20,28},{24,16},{28,20},{1,9},{5... | collective-permute-start | bytes 1769480 | tf_op jit(solution)/shard_map/ppermute | solution.py:1167
  130.4 21.8 %collective-permute-start.23 = (bf16[2,2,48,1536]{3,2,1,0:T(8,128)(2,1)S(1)}, bf16[2,2,48,1536]{3,2,1,0:T(8,128)(2,1)S(1)}, u32[]{:S(2)}, u32[]{:S(2)}) collective-permute-start(bf16[2,2,48,1536]{3,2,1,0:T(8,128)(2,1)S(1)} %get-tuple-element.294), channel_id=1, source_target_pairs={{0,16},{4,20},{8,24},{12,28},{16,0},{20,4},{24,8},{28,12},{1,17},{... | collective-permute-start | bytes 1769480 | tf_op jit(solution)/shard_map/ppermute | solution.py:1167
  135.4 20.8 %collective-permute-start.21 = (bf16[2,2,192,768]{3,2,1,0:T(8,128)(2,1)S(1)}, bf16[2,2,192,768]{3,2,1,0:T(8,128)(2,1)S(1)}, u32[]{:S(2)}, u32[]{:S(2)}) collective-permute-start(bf16[2,2,192,768]{3,2,1,0:T(8,128)(2,1)S(1)} %get-tuple-element.290), channel_id=1, source_target_pairs={{0,4},{4,0},{8,12},{12,8},{16,20},{20,16},{24,28},{28,24},{1,5},{5... | collective-permute-start | bytes 3538952 | tf_op jit(solution)/shard_map/ppermute | solution.py:1167
  142.4 16.6 %collective-permute-start.20 = (bf16[4,2,192,768]{3,2,1,0:T(8,128)(2,1)S(1)}, bf16[4,2,192,768]{3,2,1,0:T(8,128)(2,1)S(1)}, u32[]{:S(2)}, u32[]{:S(2)}) collective-permute-start(bf16[4,2,192,768]{3,2,1,0:T(8,128)(2,1)S(1)} %get-tuple-element.289), channel_id=1, source_target_pairs={{0,4},{4,0},{8,12},{12,8},{16,20},{20,16},{24,28},{28,24},{1,5},{5... | collective-permute-start | bytes 7077896 | tf_op jit(solution)/shard_map/ppermute | solution.py:1167
  142.5 20.5 %collective-permute-start.17 = (bf16[784,128]{1,0:T(8,128)(2,1)S(1)}, bf16[784,128]{1,0:T(8,128)(2,1)S(1)}, u32[]{:S(2)}, u32[]{:S(2)}) collective-permute-start(bf16[784,128]{1,0:T(8,128)(2,1)S(1)} %get-tuple-element.274), channel_id=1, source_target_pairs={{2,0},{3,1},{6,4},{7,5},{10,8},{11,9},{14,12},{15,13},{18,16},{19,... | collective-permute-start | bytes 602120 | tf_op jit(solution)/shard_map/ppermute | solution.py:1188
  145.3 7.8 %copy-start.5 = (bf16[2,2,48,1536]{3,2,1,0:T(8,128)(2,1)}, bf16[2,2,48,1536]{3,2,1,0:T(8,128)(2,1)S(1)}, u32[]{:S(2)}) copy-start(bf16[2,2,48,1536]{3,2,1,0:T(8,128)(2,1)S(1)} %collective-permute-done.22.refs_1_.refs_3_) | copy-start | bytes 1769476
  153.1 23.9 %collective-permute-start.28 = (bf16[2,48,1536]{2,1,0:T(8,128)(2,1)S(1)}, bf16[2,48,1536]{2,1,0:T(8,128)(2,1)S(1)}, u32[]{:S(2)}, u32[]{:S(2)}) collective-permute-start(bf16[2,48,1536]{2,1,0:T(8,128)(2,1)S(1)} %get-tuple-element.311), channel_id=1, source_target_pairs={{0,16},{4,20},{8,24},{12,28},{16,0},{20,4},{24,8},{28,12},{1,17},{... | collective-permute-start | bytes 884744 | tf_op jit(solution)/shard_map/ppermute | solution.py:1167
  154.7 26.8 %collective-permute-start.29 = (bf16[2,48,1536]{2,1,0:T(8,128)(2,1)}, bf16[2,48,1536]{2,1,0:T(8,128)(2,1)}, u32[]{:S(2)}, u32[]{:S(2)}) collective-permute-start(bf16[2,48,1536]{2,1,0:T(8,128)(2,1)} %get-tuple-element.312), channel_id=1, source_target_pairs={{0,8},{4,12},{8,0},{12,4},{16,24},{20,28},{24,16},{28,20},{1,9},{5... | collective-permute-start | bytes 884744 | tf_op jit(solution)/shard_map/ppermute | solution.py:1167
  158.4 3.0 %copy-start.9 = (bf16[2,192,768]{2,1,0:T(8,128)(2,1)}, bf16[2,192,768]{2,1,0:T(8,128)(2,1)S(1)}, u32[]{:S(2)}) copy-start(bf16[2,192,768]{2,1,0:T(8,128)(2,1)S(1)} %get-tuple-element.309.refs_0_) | copy-start | bytes 1769476
  158.4 23.1 %collective-permute-start.27 = (bf16[2,192,768]{2,1,0:T(8,128)(2,1)}, bf16[2,192,768]{2,1,0:T(8,128)(2,1)}, u32[]{:S(2)}, u32[]{:S(2)}) collective-permute-start(bf16[2,192,768]{2,1,0:T(8,128)(2,1)} %get-tuple-element.310), channel_id=1, source_target_pairs={{0,8},{4,12},{8,0},{12,4},{16,24},{20,28},{24,16},{28,20},{1,9},{5... | collective-permute-start | bytes 1769480 | tf_op jit(solution)/shard_map/ppermute | solution.py:1167
  161.4 12.0 %copy-start.21 = (bf16[2,2,96,768]{3,2,1,0:T(8,128)(2,1)}, bf16[2,2,96,768]{3,2,1,0:T(8,128)(2,1)S(1)}, u32[]{:S(2)}) copy-start(bf16[2,2,96,768]{3,2,1,0:T(8,128)(2,1)S(1)} %get-tuple-element.305.refs_0_) | copy-start | bytes 1769476
  161.4 12.0 %copy-start.23 = (bf16[2,2,96,768]{3,2,1,0:T(8,128)(2,1)}, bf16[2,2,96,768]{3,2,1,0:T(8,128)(2,1)S(1)}, u32[]{:S(2)}) copy-start(bf16[2,2,96,768]{3,2,1,0:T(8,128)(2,1)S(1)} %get-tuple-element.307.refs_2_.refs_3_) | copy-start | bytes 1769476
  161.4 30.5 %collective-permute-start.25 = (bf16[2,2,96,768]{3,2,1,0:T(8,128)(2,1)}, bf16[2,2,96,768]{3,2,1,0:T(8,128)(2,1)}, u32[]{:S(2)}, u32[]{:S(2)}) collective-permute-start(bf16[2,2,96,768]{3,2,1,0:T(8,128)(2,1)} %get-tuple-element.306), channel_id=1, source_target_pairs={{0,8},{4,12},{8,0},{12,4},{16,24},{20,28},{24,16},{28,20},{1,9},{5... | collective-permute-start | bytes 1769480 | tf_op jit(solution)/shard_map/ppermute | solution.py:1167
  163.0 28.9 %collective-permute-start.26 = (bf16[2,2,96,768]{3,2,1,0:T(8,128)(2,1)}, bf16[2,2,96,768]{3,2,1,0:T(8,128)(2,1)}, u32[]{:S(2)}, u32[]{:S(2)}) collective-permute-start(bf16[2,2,96,768]{3,2,1,0:T(8,128)(2,1)} %get-tuple-element.308), channel_id=1, source_target_pairs={{0,16},{4,20},{8,24},{12,28},{16,0},{20,4},{24,8},{28,12},{1,17},{... | collective-permute-start | bytes 1769480 | tf_op jit(solution)/shard_map/ppermute | solution.py:1167
  173.4 2.9 %copy-start.15 = (bf16[1,768,256]{2,1,0:T(8,128)(2,1)}, bf16[1,768,256]{2,1,0:T(8,128)(2,1)S(1)}, u32[]{:S(2)}) copy-start(bf16[1,768,256]{2,1,0:T(8,128)(2,1)S(1)} %get-tuple-element.301) | copy-start | bytes 1179652
  177.8 17.7 %collective-permute-start.24 = (bf16[4,2,96,1536]{3,2,1,0:T(8,128)(2,1)}, bf16[4,2,96,1536]{3,2,1,0:T(8,128)(2,1)}, u32[]{:S(2)}, u32[]{:S(2)}) collective-permute-start(bf16[4,2,96,1536]{3,2,1,0:T(8,128)(2,1)} %get-tuple-element.304), channel_id=1, source_target_pairs={{0,4},{4,0},{8,12},{12,8},{16,20},{20,16},{24,28},{28,24},{1,5},{5... | collective-permute-start | bytes 7077896 | tf_op jit(solution)/shard_map/ppermute | solution.py:1167
  177.8 33.3 %all-to-all-start = ((bf16[4,192,768]{2,1,0:T(8,128)(2,1)}), bf16[4,192,768]{2,1,0:T(8,128)(2,1)S(1)}, u32[]{:S(2)}, u32[]{:S(2)}) async-start(bf16[4,192,768]{2,1,0:T(8,128)(2,1)} %copy-done.2), calls=%async_computation | async-start | bytes 2359296 | tf_op jit(solution)/shard_map/all_to_all | solution.py:1401
  186.8 5.1 %copy-start.22 = (bf16[2,2,96,768]{3,2,1,0:T(8,128)(2,1)S(1)}, bf16[2,2,96,768]{3,2,1,0:T(8,128)(2,1)}, u32[]{:S(2)}) copy-start(bf16[2,2,96,768]{3,2,1,0:T(8,128)(2,1)} %copy-done.21) | copy-start | bytes 1769476
  186.8 5.1 %copy-start.24 = (bf16[2,2,96,768]{3,2,1,0:T(8,128)(2,1)S(1)}, bf16[2,2,96,768]{3,2,1,0:T(8,128)(2,1)}, u32[]{:S(2)}) copy-start(bf16[2,2,96,768]{3,2,1,0:T(8,128)(2,1)} %copy-done.23) | copy-start | bytes 1769476
  189.9 32.1 %collective-permute-start.40 = (bf16[384,768]{1,0:T(8,128)(2,1)}, bf16[384,768]{1,0:T(8,128)(2,1)S(1)}, u32[]{:S(2)}, u32[]{:S(2)}) collective-permute-start(bf16[384,768]{1,0:T(8,128)(2,1)} %get-tuple-element.342), channel_id=1, source_target_pairs={{0,1},{1,0},{2,3},{3,2},{4,5},{5,4},{6,7},{7,6},{8,9},{9,8},{10,11... | collective-permute-start | bytes 1769480 | tf_op jit(solution)/shard_map/ppermute | solution.py:1172
  191.9 3.6 %copy-start.14 = (bf16[1,768,256]{2,1,0:T(8,128)(2,1)S(1)}, bf16[1,768,256]{2,1,0:T(8,128)(2,1)}, u32[]{:S(2)}) copy-start(bf16[1,768,256]{2,1,0:T(8,128)(2,1)} %copy-done.13) | copy-start | bytes 1179652
  191.9 3.6 %copy-start.16 = (bf16[1,768,256]{2,1,0:T(8,128)(2,1)S(1)}, bf16[1,768,256]{2,1,0:T(8,128)(2,1)}, u32[]{:S(2)}) copy-start(bf16[1,768,256]{2,1,0:T(8,128)(2,1)} %copy-done.15) | copy-start | bytes 1179652
  193.4 9.3 %collective-permute-start.32 = (bf16[2,96,768]{2,1,0:T(8,128)(2,1)S(1)}, bf16[2,96,768]{2,1,0:T(8,128)(2,1)S(1)}, u32[]{:S(2)}, u32[]{:S(2)}) collective-permute-start(bf16[2,96,768]{2,1,0:T(8,128)(2,1)S(1)} %get-tuple-element.327), channel_id=1, source_target_pairs={{0,16},{4,20},{8,24},{12,28},{16,0},{20,4},{24,8},{28,12},{1,17},{... | collective-permute-start | bytes 884744 | tf_op jit(solution)/shard_map/ppermute | solution.py:1167
  195.0 9.1 %collective-permute-start.33 = (bf16[2,96,768]{2,1,0:T(8,128)(2,1)S(1)}, bf16[2,96,768]{2,1,0:T(8,128)(2,1)S(1)}, u32[]{:S(2)}, u32[]{:S(2)}) collective-permute-start(bf16[2,96,768]{2,1,0:T(8,128)(2,1)S(1)} %get-tuple-element.328), channel_id=1, source_target_pairs={{0,8},{4,12},{8,0},{12,4},{16,24},{20,28},{24,16},{28,20},{1,9},{5... | collective-permute-start | bytes 884744 | tf_op jit(solution)/shard_map/ppermute | solution.py:1167
  200.7 15.5 %collective-permute-start.30 = (bf16[2,2,48,1536]{3,2,1,0:T(8,128)(2,1)}, bf16[2,2,48,1536]{3,2,1,0:T(8,128)(2,1)S(1)}, u32[]{:S(2)}, u32[]{:S(2)}) collective-permute-start(bf16[2,2,48,1536]{3,2,1,0:T(8,128)(2,1)} %get-tuple-element.317), channel_id=1, source_target_pairs={{0,8},{4,12},{8,0},{12,4},{16,24},{20,28},{24,16},{28,20},{1,9},{5... | collective-permute-start | bytes 1769480 | tf_op jit(solution)/shard_map/ppermute | solution.py:1167
  202.2 14.7 %collective-permute-start.31 = (bf16[2,2,48,1536]{3,2,1,0:T(8,128)(2,1)}, bf16[2,2,48,1536]{3,2,1,0:T(8,128)(2,1)}, u32[]{:S(2)}, u32[]{:S(2)}) collective-permute-start(bf16[2,2,48,1536]{3,2,1,0:T(8,128)(2,1)} %get-tuple-element.319), channel_id=1, source_target_pairs={{0,16},{4,20},{8,24},{12,28},{16,0},{20,4},{24,8},{28,12},{1,17},{... | collective-permute-start | bytes 1769480 | tf_op jit(solution)/shard_map/ppermute | solution.py:1167
  213.0 1.4 collective-permute-start.34
  213.1 9.6 %collective-permute-start.39 = (bf16[192,768]{1,0:T(8,128)(2,1)S(1)}, bf16[192,768]{1,0:T(8,128)(2,1)S(1)}, u32[]{:S(2)}, u32[]{:S(2)}) collective-permute-start(bf16[192,768]{1,0:T(8,128)(2,1)S(1)} %get-tuple-element.340), channel_id=1, source_target_pairs={{0,1},{1,0},{2,3},{3,2},{4,5},{5,4},{6,7},{7,6},{8,9},{9,8},{10,11... | collective-permute-start | bytes 884744 | tf_op jit(solution)/shard_map/ppermute | solution.py:1172
  214.4 4.9 %collective-permute-start.37 = (f32[32,768]{1,0:T(8,128)S(1)}, f32[32,768]{1,0:T(8,128)S(1)}, u32[]{:S(2)}, u32[]{:S(2)}) collective-permute-start(f32[32,768]{1,0:T(8,128)S(1)} %get-tuple-element.336.refs_0_), channel_id=1, source_target_pairs={{0,8},{4,12},{8,0},{12,4},{16,24},{20,28},{24,16},{28,20},{1,9},{5... | collective-permute-start | bytes 294920 | tf_op jit(solution)/shard_map/ppermute | solution.py:1167
  216.9 5.9 %copy-start.12 = (bf16[384,768]{1,0:T(8,128)(2,1)S(1)}, bf16[384,768]{1,0:T(8,128)(2,1)}, u32[]{:S(2)}) copy-start(bf16[384,768]{1,0:T(8,128)(2,1)} %copy-done.11) | copy-start | bytes 1769476
  219.4 7.0 %collective-permute-start.38 = (f32[32,768]{1,0:T(8,128)S(1)}, f32[32,768]{1,0:T(8,128)S(1)}, u32[]{:S(2)}, u32[]{:S(2)}) collective-permute-start(f32[32,768]{1,0:T(8,128)S(1)} %get-tuple-element.338.refs_0_), channel_id=1, source_target_pairs={{0,16},{4,20},{8,24},{12,28},{16,0},{20,4},{24,8},{28,12},{1,17},{... | collective-permute-start | bytes 294920 | tf_op jit(solution)/shard_map/ppermute | solution.py:1167
  221.0 9.0 %collective-permute-start.35 = (bf16[2,48,1536]{2,1,0:T(8,128)(2,1)S(1)}, bf16[2,48,1536]{2,1,0:T(8,128)(2,1)S(1)}, u32[]{:S(2)}, u32[]{:S(2)}) collective-permute-start(bf16[2,48,1536]{2,1,0:T(8,128)(2,1)S(1)} %get-tuple-element.334), channel_id=1, source_target_pairs={{0,16},{4,20},{8,24},{12,28},{16,0},{20,4},{24,8},{28,12},{1,17},{... | collective-permute-start | bytes 884744 | tf_op jit(solution)/shard_map/ppermute | solution.py:1167
  221.5 8.5 %collective-permute-start.36 = (bf16[2,48,1536]{2,1,0:T(8,128)(2,1)S(1)}, bf16[2,48,1536]{2,1,0:T(8,128)(2,1)S(1)}, u32[]{:S(2)}, u32[]{:S(2)}) collective-permute-start(bf16[2,48,1536]{2,1,0:T(8,128)(2,1)S(1)} %get-tuple-element.335), channel_id=1, source_target_pairs={{0,8},{4,12},{8,0},{12,4},{16,24},{20,28},{24,16},{28,20},{1,9},{5... | collective-permute-start | bytes 884744 | tf_op jit(solution)/shard_map/ppermute | solution.py:1167
  223.9 27.9 %collective-permute-start.44 = (bf16[288,768]{1,0:T(8,128)(2,1)}, bf16[288,768]{1,0:T(8,128)(2,1)S(1)}, u32[]{:S(2)}, u32[]{:S(2)}) collective-permute-start(bf16[288,768]{1,0:T(8,128)(2,1)} %get-tuple-element.354), channel_id=1, source_target_pairs={{0,2},{1,3},{2,0},{3,1},{4,6},{5,7},{6,4},{7,5},{8,10},{9,11},{10,... | collective-permute-start | bytes 1327112 | tf_op jit(solution)/shard_map/ppermute | solution.py:1172
  226.4 3.6 %copy-start.20 = (bf16[2,2,48,1536]{3,2,1,0:T(8,128)(2,1)S(1)}, bf16[2,2,48,1536]{3,2,1,0:T(8,128)(2,1)}, u32[]{:S(2)}) copy-start(bf16[2,2,48,1536]{3,2,1,0:T(8,128)(2,1)} %copy-done.19) | copy-start | bytes 1769476
  231.3 19.3 %copy-start.27 = (bf16[192,768]{1,0:T(8,128)(2,1)}, bf16[192,768]{1,0:T(8,128)(2,1)S(1)}, u32[]{:S(2)}) copy-start(bf16[192,768]{1,0:T(8,128)(2,1)S(1)} %get-tuple-element.346.refs_0_) | copy-start | bytes 884740
  231.3 20.5 %copy-start.1 = (bf16[4,192,768]{2,1,0:T(8,128)(2,1)S(1)}, bf16[4,192,768]{2,1,0:T(8,128)(2,1)}, u32[]{:S(2)}) copy-start(bf16[4,192,768]{2,1,0:T(8,128)(2,1)} %copy-done) | copy-start | bytes 3538948
  231.3 19.3 %collective-permute-start.41 = (bf16[192,768]{1,0:T(8,128)(2,1)S(1)}, bf16[192,768]{1,0:T(8,128)(2,1)S(1)}, u32[]{:S(2)}, u32[]{:S(2)}) collective-permute-start(bf16[192,768]{1,0:T(8,128)(2,1)S(1)} %get-tuple-element.347), channel_id=1, source_target_pairs={{0,1},{1,0},{2,3},{3,2},{4,5},{5,4},{6,7},{7,6},{8,9},{9,8},{10,11... | collective-permute-start | bytes 884744 | tf_op jit(solution)/shard_map/ppermute | solution.py:1172
  232.2 18.3 %collective-permute-start.42 = (f32[32,768]{1,0:T(8,128)S(1)}, f32[32,768]{1,0:T(8,128)S(1)}, u32[]{:S(2)}, u32[]{:S(2)}) collective-permute-start(f32[32,768]{1,0:T(8,128)S(1)} %get-tuple-element.348.refs_0_), channel_id=1, source_target_pairs={{0,1},{1,0},{2,3},{3,2},{4,5},{5,4},{6,7},{7,6},{8,9},{9,8},{10,11... | collective-permute-start | bytes 294920 | tf_op jit(solution)/shard_map/ppermute | solution.py:1172
  250.6 7.8 %collective-permute-start.45 = (f32[32,768]{1,0:T(8,128)S(1)}, f32[32,768]{1,0:T(8,128)S(1)}, u32[]{:S(2)}, u32[]{:S(2)}) collective-permute-start(f32[32,768]{1,0:T(8,128)S(1)} %get-tuple-element.355.refs_0_), channel_id=1, source_target_pairs={{0,2},{1,3},{2,0},{3,1},{4,6},{5,7},{6,4},{7,5},{8,10},{9,11},{10,... | collective-permute-start | bytes 294920 | tf_op jit(solution)/shard_map/ppermute | solution.py:1172
  251.8 6.6 %copy-start.25 = (f32[96,768]{1,0:T(8,128)}, f32[96,768]{1,0:T(8,128)S(1)}, u32[]{:S(2)}) copy-start(f32[96,768]{1,0:T(8,128)S(1)} %get-tuple-element.351.refs_0_) | copy-start | bytes 884740
  253.4 7.2 %copy-start.34 = (f32[2,384,192]{2,1,0:T(8,128)S(1)}, f32[2,384,192]{2,1,0:T(8,128)}, u32[]{:S(2)}) copy-start(f32[2,384,192]{2,1,0:T(8,128)} %get-tuple-element.379) | copy-start | bytes 1769476
  258.4 6.7 %copy-start.26 = (f32[96,768]{1,0:T(8,128)S(1)}, f32[96,768]{1,0:T(8,128)}, u32[]{:S(2)}) copy-start(f32[96,768]{1,0:T(8,128)} %copy-done.25) | copy-start | bytes 884740
  258.5 6.6 %collective-permute-start.43 = (bf16[96,768]{1,0:T(8,128)(2,1)S(1)}, bf16[96,768]{1,0:T(8,128)(2,1)S(1)}, u32[]{:S(2)}, u32[]{:S(2)}) collective-permute-start(bf16[96,768]{1,0:T(8,128)(2,1)S(1)} %get-tuple-element.352), channel_id=1, source_target_pairs={{0,2},{1,3},{2,0},{3,1},{4,6},{5,7},{6,4},{7,5},{8,10},{9,11},{10,... | collective-permute-start | bytes 442376 | tf_op jit(solution)/shard_map/ppermute | solution.py:1172
  (18 other events, 21.3 us)
